TPU v7x, 32 devices: a whole 2x2x4 slice. The times are simulated.
32 devices in a mesh: gx: 8 (over z, core), gy: 4 (over y, x).
Axes of the slice: x: 2, y: 2, z: 4, core: 2. Of those that a mesh axis runs over, the one named last changes fastest.
Arguments:
- checkpoint: float32 [19, 64, 1024], P(None, 'gx', 'gy'), may hold values from 0.02 to 0.1
- cotangent: float32 [19, 64, 1024], P(None, 'gx', 'gy'), may hold values from -6 to 6
- cell_codes: int32 [4, 64, 1024], P(None, 'gx', 'gy'), may hold values from 0 to 3, as said below
- porosity: float32 [64], replicated, may hold values from 0.2 to 0.9
- baffle_index: int32 [64, 1024], P('gx', 'gy'), may hold values from 0 to 63, as said below
Outputs:
- adjoint_start: float32 [19, 64, 1024], P(None, 'gx', 'gy')
- porosity_grad: float32 [64], replicated
Inputs may be any that keep to these rules, and one draw needn't show every extreme that they name: `cell_codes`: in each step and column, the cells below the surface cell are all 1 or all 3, the surface cell is 2 and the cells above are 0; the surface cell's depth index lies between 8 and 24; the columns of code 3 fill whole tiles of 4 x 4 columns and are the same in all steps. `baffle_index`: constant over each tile of 4 x 4 columns and all depths; each value names exactly two tiles.
All inputs are finite; a program needn't handle non-finite values.
Results may differ from a plain program's by a relative error of at most 0.0003.
Values sent between devices are 32-bit elements; how exact they have to be, the bound alone decides.
No kernel may reach another device: no remote copies, remote signals or barrier semaphores. Data moves between devices by JAX's collectives and lax.ppermute only.
A program may use at most 128 MiB of HBM per device.

v0:
```python
import jax
import jax.numpy as jnp
import numpy as np
from jax import lax
from jax.sharding import PartitionSpec as P

Q = 19
STEPS = 4
NZ = 32


VELOCITIES = [
    (0, 0, 0),
    (1, 0, 0),
    (-1, 0, 0),
    (0, 1, 0),
    (0, -1, 0),
    (0, 0, 1),
    (0, 0, -1),
    (1, 1, 0),
    (-1, -1, 0),
    (1, -1, 0),
    (-1, 1, 0),
    (1, 0, 1),
    (-1, 0, -1),
    (1, 0, -1),
    (-1, 0, 1),
    (0, 1, 1),
    (0, -1, -1),
    (0, 1, -1),
    (0, -1, 1),
]
OPPOSITE = [0, 2, 1, 4, 3, 6, 5, 8, 7, 10, 9, 12, 11, 14, 13, 16, 15, 18, 17]
WEIGHTS = [1.0 / 3.0] + [1.0 / 18.0] * 6 + [1.0 / 36.0] * 12
OMEGA = 1.6
ACCEL = (0.002, 0.0, -0.003)
VELOCITY_TABLE = np.array(VELOCITIES, np.float32)
WEIGHT_TABLE = np.array(WEIGHTS, np.float32)
OPPOSITE_TABLE = np.array(OPPOSITE, np.int32)


def with_halo(value, sides, width):
    for axis, dim in sides:
        size, length = (lax.axis_size(axis), value.shape[dim])
        up = [(i, (i + 1) % size) for i in range(size - 1)]
        down = [(j, i) for i, j in up]
        last = lax.slice_in_dim(value, length - width, length, axis=dim)
        leading = lax.slice_in_dim(value, 0, width, axis=dim)
        before = lax.ppermute(last, axis, up)
        after = lax.ppermute(leading, axis, down)
        value = jnp.concatenate([before, value, after], axis=dim)
    return value


def collide(field, codes, phi):
    extent = (len(VELOCITIES),) + (1,) * (field.ndim - 1)
    density = jnp.sum(field, axis=0)
    velocity = []
    for axis_number in range(3):
        column = jnp.asarray(VELOCITY_TABLE[:, axis_number].reshape(extent), field.dtype)
        velocity.append(jnp.sum(column * field, axis=0) / density + ACCEL[axis_number] / OMEGA)
    square = velocity[0] * velocity[0] + velocity[1] * velocity[1] + velocity[2] * velocity[2]
    along = jnp.zeros_like(field)
    for axis_number in range(3):
        column = jnp.asarray(VELOCITY_TABLE[:, axis_number].reshape(extent), field.dtype)
        along = along + column * velocity[axis_number][None]
    weight = jnp.asarray(WEIGHT_TABLE.reshape(extent), field.dtype)
    equilib = weight * (1.0 + 3.0 * along + 4.5 * along * along - 1.5 * square[None])
    bulk = field - OMEGA * (field - density[None] * equilib)
    surface = field - OMEGA * (field - equilib)
    porous = phi[None] * bulk + (1.0 - phi[None]) * field[OPPOSITE_TABLE]
    gas_value = jnp.zeros_like(field) + weight
    kinds = codes[None]
    return jnp.where(
        kinds == 1, bulk, jnp.where(kinds == 2, surface, jnp.where(kinds == 3, porous, gas_value))
    )


def bounce(padded, field, sign, coords, extents):
    xpos, ypos, zpos = coords
    size_x, size_y, size_z = (field.shape[1], field.shape[2], field.shape[3])
    results = []
    for number, vector in enumerate(VELOCITIES):
        shift_x, shift_y, shift_z = (sign * vector[0], sign * vector[1], sign * vector[2])
        pulled = padded[
            number,
            1 - shift_x : 1 - shift_x + size_x,
            1 - shift_y : 1 - shift_y + size_y,
            1 - shift_z : 1 - shift_z + size_z,
        ]
        outside = (
            (xpos - shift_x < 0)
            | (xpos - shift_x >= extents[0])
            | (ypos - shift_y < 0)
            | (ypos - shift_y >= extents[1])
            | (zpos - shift_z < 0)
            | (zpos - shift_z >= extents[2])
        )
        results.append(jnp.where(outside, field[OPPOSITE[number]], pulled))
    return jnp.stack(results)


def stream(field, sign, coords, extents):
    padded = with_halo(field, (("gx", 1), ("gy", 2)), 1)
    padded = jnp.pad(padded, ((0, 0), (0, 0), (0, 0), (1, 1)))
    return bounce(padded, field, sign, coords, extents)


def run_steps(start, back_start, codes_all, phi, mover):

    def forward_step(state, codes_now):
        return (mover(collide(state, codes_now, phi), 1), state)

    _, saved = lax.scan(forward_step, start, codes_all)

    def backward_step(carry, pieces):
        adjoint, grad_now = carry
        state_now, codes_now = pieces
        incoming = mover(adjoint, -1)
        _, pull = jax.vjp(lambda left, right: collide(left, codes_now, right), state_now, phi)
        back, grad_phi = pull(incoming)
        return ((back, grad_now + grad_phi), None)

    grad_start = jnp.zeros(phi.shape, jnp.float32)
    (adjoint, grad_cells), _ = lax.scan(
        backward_step, (back_start, grad_start), (saved, codes_all), reverse=True
    )
    return (adjoint, grad_cells)


def on_device(checkpoint, cotangent, cell_codes, porosity, baffle_index):
    width_x = checkpoint.shape[1]
    width_y = checkpoint.shape[2] // NZ
    shape_four = (Q, width_x, width_y, NZ)
    field = checkpoint.reshape(shape_four)
    codes_all = cell_codes.reshape(STEPS, width_x, width_y, NZ)
    panels = baffle_index.reshape(width_x, width_y, NZ)
    phi = porosity[panels]
    extents = (width_x * lax.axis_size("gx"), width_y * lax.axis_size("gy"), NZ)
    coords = (
        lax.axis_index("gx") * width_x
        + jnp.arange(width_x, dtype=jnp.int32).reshape(width_x, 1, 1),
        lax.axis_index("gy") * width_y
        + jnp.arange(width_y, dtype=jnp.int32).reshape(1, width_y, 1),
        jnp.arange(NZ, dtype=jnp.int32).reshape(1, 1, NZ),
    )

    def mover_shared(value, sign):
        return stream(value, sign, coords, extents)

    adjoint, grad_cells = run_steps(
        field, cotangent.reshape(shape_four), codes_all, phi, mover_shared
    )
    local_sums = jax.ops.segment_sum(
        grad_cells.reshape(-1), panels.reshape(-1), num_segments=porosity.shape[0]
    )
    totals = lax.psum(local_sums, ("gx", "gy"))
    return (adjoint.reshape(Q, width_x, width_y * NZ), totals)


def solution(mesh):
    in_specs = (P(None, "gx", "gy"), P(None, "gx", "gy"), P(None, "gx", "gy"), P(), P("gx", "gy"))
    out_specs = (P(None, "gx", "gy"), P())
    return jax.shard_map(
        on_device, mesh=mesh, in_specs=in_specs, out_specs=out_specs, check_vma=False
    )
```

profile of v0, /device:TPU:0, one launch (start us, length us, event | category | flops | bytes accessed | tf_op | source)
XLA Modules:
  0.0 261.5 jit_solution(15309259685353302890)
XLA Ops:
  3.6 12.6 %gather_fusion.2 = f32[2048]{0:T(1024)S(1)} fusion(f32[64]{0:T(128)S(1)} %copy-done, s32[2048]{0:T(1024)S(1)} %broadcast_clamp_fusion), kind=kCustom, calls=%fused_computation.2 | custom fusion | bytes 24576 | tf_op jit(solution)/shard_map/gather | solution.py:138
  16.5 88.6 %while.38 = (s32[]{:T(128)}, f32[19,8,8,32]{3,2,1,0:T(8,128)S(1)}, f32[4,19,8,8,32]{4,3,2,1,0:T(8,128)}, s32[4,8,8,32]{3,2,1,0:T(8,128)S(1)}, f32[8,8,32]{2,1,0:...) while((s32[]{:T(128)}, f32[19,8,8,32]{3,2,1,0:T(8,128)S(1)}, ...), condition=%wide.region_5.6_spmd.clone.clone.clone, body=%wide.region_0.5_spmd.sunk.clone.clone.clone.sunk | while | flops 2205058 | bytes 11318961 | solution.py:114
  18.4 2.4 collective-permute-start
  23.2 3.0 %collective-permute-done.1 = f32[19,1,8,32]{3,2,1,0:T(8,128)S(1)} collective-permute-done((f32[19,1,8,32]{3,2,1,0:T(8,128)S(1)}, f32[19,1,8,32]{3,2,1,0:T(8,128)S(1)}, u32[]{:S(2)}, u32[]{:S(2)}) %collective-permute-start.1) | collective-permute-done | bytes 19488 | tf_op jit(solution)/shard_map/while/body/eval_jaxpr/ppermute | solution.py:50
  26.3 3.4 %collective-permute-start.2 = (f32[19,10,1,32]{3,2,1,0:T(1,128)S(1)}, f32[19,10,1,32]{3,2,1,0:T(1,128)S(1)}, u32[]{:S(2)}, u32[]{:S(2)}) collective-permute-start(f32[19,10,1,32]{3,2,1,0:T(1,128)S(1)} %get-tuple-element.1568), channel_id=1, source_target_pairs={{0,1},{1,2},{2,3},{4,5},{5,6},{6,7},{8,9},{9,10},{10,11},{12,13},{... | collective-permute-start | bytes 72968 | tf_op jit(solution)/shard_map/while/body/eval_jaxpr/ppermute | solution.py:49
  31.9 5.0 %collective-permute-done.3 = f32[19,10,1,32]{3,2,1,0:T(1,128)S(1)} collective-permute-done((f32[19,10,1,32]{3,2,1,0:T(1,128)S(1)}, f32[19,10,1,32]{3,2,1,0:T(1,128)S(1)}, u32[]{:S(2)}, u32[]{:S(2)}) %collective-permute-start.3) | collective-permute-done | bytes 24352 | tf_op jit(solution)/shard_map/while/body/eval_jaxpr/ppermute | solution.py:50
  41.0 2.9 %collective-permute-start = (f32[19,1,8,32]{3,2,1,0:T(8,128)S(1)}, f32[19,1,8,32]{3,2,1,0:T(8,128)S(1)}, u32[]{:S(2)}, u32[]{:S(2)}) collective-permute-start(f32[19,1,8,32]{3,2,1,0:T(8,128)S(1)} %get-tuple-element.1556), channel_id=1, source_target_pairs={{0,4},{4,8},{8,12},{12,16},{16,20},{20,24},{24,28},{1,5},{5,9},{9,... | collective-permute-start | bytes 58376 | tf_op jit(solution)/shard_map/while/body/eval_jaxpr/ppermute | solution.py:49
  46.2 2.3 collective-permute-done.1
  48.6 4.3 %collective-permute-start.2 = (f32[19,10,1,32]{3,2,1,0:T(1,128)S(1)}, f32[19,10,1,32]{3,2,1,0:T(1,128)S(1)}, u32[]{:S(2)}, u32[]{:S(2)}) collective-permute-start(f32[19,10,1,32]{3,2,1,0:T(1,128)S(1)} %get-tuple-element.1568), channel_id=1, source_target_pairs={{0,1},{1,2},{2,3},{4,5},{5,6},{6,7},{8,9},{9,10},{10,11},{12,13},{... | collective-permute-start | bytes 72968 | tf_op jit(solution)/shard_map/while/body/eval_jaxpr/ppermute | solution.py:49
  55.1 4.3 %collective-permute-done.3 = f32[19,10,1,32]{3,2,1,0:T(1,128)S(1)} collective-permute-done((f32[19,10,1,32]{3,2,1,0:T(1,128)S(1)}, f32[19,10,1,32]{3,2,1,0:T(1,128)S(1)}, u32[]{:S(2)}, u32[]{:S(2)}) %collective-permute-start.3) | collective-permute-done | bytes 24352 | tf_op jit(solution)/shard_map/while/body/eval_jaxpr/ppermute | solution.py:50
  63.5 3.5 %collective-permute-start = (f32[19,1,8,32]{3,2,1,0:T(8,128)S(1)}, f32[19,1,8,32]{3,2,1,0:T(8,128)S(1)}, u32[]{:S(2)}, u32[]{:S(2)}) collective-permute-start(f32[19,1,8,32]{3,2,1,0:T(8,128)S(1)} %get-tuple-element.1556), channel_id=1, source_target_pairs={{0,4},{4,8},{8,12},{12,16},{16,20},{20,24},{24,28},{1,5},{5,9},{9,... | collective-permute-start | bytes 58376 | tf_op jit(solution)/shard_map/while/body/eval_jaxpr/ppermute | solution.py:49
  69.5 2.2 collective-permute-done.1
  71.9 3.4 %collective-permute-start.2 = (f32[19,10,1,32]{3,2,1,0:T(1,128)S(1)}, f32[19,10,1,32]{3,2,1,0:T(1,128)S(1)}, u32[]{:S(2)}, u32[]{:S(2)}) collective-permute-start(f32[19,10,1,32]{3,2,1,0:T(1,128)S(1)} %get-tuple-element.1568), channel_id=1, source_target_pairs={{0,1},{1,2},{2,3},{4,5},{5,6},{6,7},{8,9},{9,10},{10,11},{12,13},{... | collective-permute-start | bytes 72968 | tf_op jit(solution)/shard_map/while/body/eval_jaxpr/ppermute | solution.py:49
  77.5 4.3 %collective-permute-done.3 = f32[19,10,1,32]{3,2,1,0:T(1,128)S(1)} collective-permute-done((f32[19,10,1,32]{3,2,1,0:T(1,128)S(1)}, f32[19,10,1,32]{3,2,1,0:T(1,128)S(1)}, u32[]{:S(2)}, u32[]{:S(2)}) %collective-permute-start.3) | collective-permute-done | bytes 24352 | tf_op jit(solution)/shard_map/while/body/eval_jaxpr/ppermute | solution.py:50
  85.9 3.5 %collective-permute-start = (f32[19,1,8,32]{3,2,1,0:T(8,128)S(1)}, f32[19,1,8,32]{3,2,1,0:T(8,128)S(1)}, u32[]{:S(2)}, u32[]{:S(2)}) collective-permute-start(f32[19,1,8,32]{3,2,1,0:T(8,128)S(1)} %get-tuple-element.1556), channel_id=1, source_target_pairs={{0,4},{4,8},{8,12},{12,16},{16,20},{20,24},{24,28},{1,5},{5,9},{9,... | collective-permute-start | bytes 58376 | tf_op jit(solution)/shard_map/while/body/eval_jaxpr/ppermute | solution.py:49
  93.8 2.6 collective-permute-start.2
  98.6 4.3 %collective-permute-done.3 = f32[19,10,1,32]{3,2,1,0:T(1,128)S(1)} collective-permute-done((f32[19,10,1,32]{3,2,1,0:T(1,128)S(1)}, f32[19,10,1,32]{3,2,1,0:T(1,128)S(1)}, u32[]{:S(2)}, u32[]{:S(2)}) %collective-permute-start.3) | collective-permute-done | bytes 24352 | tf_op jit(solution)/shard_map/while/body/eval_jaxpr/ppermute | solution.py:50
  105.1 95.7 %while.39 = (s32[]{:T(128)}, f32[19,8,8,32]{3,2,1,0:T(8,128)S(1)}, f32[8,8,32]{2,1,0:T(8,128)S(1)}, s32[4,8,8,32]{3,2,1,0:T(8,128)S(1)}, f32[8,8,32]{2,1,0:T(8,1...) while((s32[]{:T(128)}, f32[19,8,8,32]{3,2,1,0:T(8,128)S(1)}, ...), condition=%wide.region_19.20_spmd.clone.clone.clone, body=%wide.region_6.19_spmd.sunk.clone.clone.clone.sunk | while | flops 3863780 | bytes 13389855 | solution.py:125
  106.5 4.2 %collective-permute-start.5 = (f32[19,1,8,32]{3,2,1,0:T(8,128)S(1)}, f32[19,1,8,32]{3,2,1,0:T(8,128)S(1)}, u32[]{:S(2)}, u32[]{:S(2)}) collective-permute-start(f32[19,1,8,32]{3,2,1,0:T(8,128)S(1)} %get-tuple-element.1597), channel_id=1, source_target_pairs={{0,4},{4,8},{8,12},{12,16},{16,20},{20,24},{24,28},{1,5},{5,9},{9,... | collective-permute-start | bytes 58376 | tf_op jit(solution)/shard_map/while/body/eval_jaxpr/ppermute | solution.py:49
  115.5 4.6 %collective-permute-start.7 = (f32[19,10,1,32]{3,2,1,0:T(1,128)S(1)}, f32[19,10,1,32]{3,2,1,0:T(1,128)S(1)}, u32[]{:S(2)}, u32[]{:S(2)}) collective-permute-start(f32[19,10,1,32]{3,2,1,0:T(1,128)S(1)} %get-tuple-element.1601), channel_id=1, source_target_pairs={{0,1},{1,2},{2,3},{4,5},{5,6},{6,7},{8,9},{9,10},{10,11},{12,13},{... | collective-permute-start | bytes 72968 | tf_op jit(solution)/shard_map/while/body/eval_jaxpr/ppermute | solution.py:49
  127.1 2.2 scatter_fusion
  130.7 3.1 %collective-permute-start.5 = (f32[19,1,8,32]{3,2,1,0:T(8,128)S(1)}, f32[19,1,8,32]{3,2,1,0:T(8,128)S(1)}, u32[]{:S(2)}, u32[]{:S(2)}) collective-permute-start(f32[19,1,8,32]{3,2,1,0:T(8,128)S(1)} %get-tuple-element.1597), channel_id=1, source_target_pairs={{0,4},{4,8},{8,12},{12,16},{16,20},{20,24},{24,28},{1,5},{5,9},{9,... | collective-permute-start | bytes 58376 | tf_op jit(solution)/shard_map/while/body/eval_jaxpr/ppermute | solution.py:49
  138.7 5.0 %collective-permute-start.7 = (f32[19,10,1,32]{3,2,1,0:T(1,128)S(1)}, f32[19,10,1,32]{3,2,1,0:T(1,128)S(1)}, u32[]{:S(2)}, u32[]{:S(2)}) collective-permute-start(f32[19,10,1,32]{3,2,1,0:T(1,128)S(1)} %get-tuple-element.1601), channel_id=1, source_target_pairs={{0,1},{1,2},{2,3},{4,5},{5,6},{6,7},{8,9},{9,10},{10,11},{12,13},{... | collective-permute-start | bytes 72968 | tf_op jit(solution)/shard_map/while/body/eval_jaxpr/ppermute | solution.py:49
  150.3 2.2 scatter_fusion
  153.9 3.4 %collective-permute-start.5 = (f32[19,1,8,32]{3,2,1,0:T(8,128)S(1)}, f32[19,1,8,32]{3,2,1,0:T(8,128)S(1)}, u32[]{:S(2)}, u32[]{:S(2)}) collective-permute-start(f32[19,1,8,32]{3,2,1,0:T(8,128)S(1)} %get-tuple-element.1597), channel_id=1, source_target_pairs={{0,4},{4,8},{8,12},{12,16},{16,20},{20,24},{24,28},{1,5},{5,9},{9,... | collective-permute-start | bytes 58376 | tf_op jit(solution)/shard_map/while/body/eval_jaxpr/ppermute | solution.py:49
  162.2 5.5 %collective-permute-start.7 = (f32[19,10,1,32]{3,2,1,0:T(1,128)S(1)}, f32[19,10,1,32]{3,2,1,0:T(1,128)S(1)}, u32[]{:S(2)}, u32[]{:S(2)}) collective-permute-start(f32[19,10,1,32]{3,2,1,0:T(1,128)S(1)} %get-tuple-element.1601), channel_id=1, source_target_pairs={{0,1},{1,2},{2,3},{4,5},{5,6},{6,7},{8,9},{9,10},{10,11},{12,13},{... | collective-permute-start | bytes 72968 | tf_op jit(solution)/shard_map/while/body/eval_jaxpr/ppermute | solution.py:49
  174.4 2.2 scatter_fusion
  178.0 3.4 %collective-permute-start.5 = (f32[19,1,8,32]{3,2,1,0:T(8,128)S(1)}, f32[19,1,8,32]{3,2,1,0:T(8,128)S(1)}, u32[]{:S(2)}, u32[]{:S(2)}) collective-permute-start(f32[19,1,8,32]{3,2,1,0:T(8,128)S(1)} %get-tuple-element.1597), channel_id=1, source_target_pairs={{0,4},{4,8},{8,12},{12,16},{16,20},{20,24},{24,28},{1,5},{5,9},{9,... | collective-permute-start | bytes 58376 | tf_op jit(solution)/shard_map/while/body/eval_jaxpr/ppermute | solution.py:49
  186.3 5.7 %collective-permute-start.7 = (f32[19,10,1,32]{3,2,1,0:T(1,128)S(1)}, f32[19,10,1,32]{3,2,1,0:T(1,128)S(1)}, u32[]{:S(2)}, u32[]{:S(2)}) collective-permute-start(f32[19,10,1,32]{3,2,1,0:T(1,128)S(1)} %get-tuple-element.1601), channel_id=1, source_target_pairs={{0,1},{1,2},{2,3},{4,5},{5,6},{6,7},{8,9},{9,10},{10,11},{12,13},{... | collective-permute-start | bytes 72968 | tf_op jit(solution)/shard_map/while/body/eval_jaxpr/ppermute | solution.py:49
  198.6 2.2 scatter_fusion
  201.8 14.7 %scatter_custom_fusion.1 = f32[64]{0:T(128)S(1)} fusion(s32[2048]{0:T(1024)S(1)} %bitcast.122, f32[2048]{0:T(1024)S(1)} %reshape.1723, f32[]{:T(128)} %constant.337.clone.1), kind=kCustom, calls=%fused_computation.240 | custom fusion | flops 2048 | bytes 260 | tf_op jit(solution)/shard_map/scatter-add | solution.py:154
  216.5 45.0 %psum.7 = f32[64]{0:T(128)} all-reduce(f32[64]{0:T(128)S(1)} %scatter_custom_fusion.1), channel_id=1, replica_groups=mesh['gx'=8,'gy'=4] {'gx','gy'}, use_global_device_ids=true, to_apply=%region_21.22 | all-reduce | flops 64 | bytes 512 | tf_op jit(solution)/shard_map/psum | solution.py:157
  (406 shorter events, 91.4 us)
Async XLA Ops:
  18.4 4.7 %collective-permute-start = (f32[19,1,8,32]{3,2,1,0:T(8,128)S(1)}, f32[19,1,8,32]{3,2,1,0:T(8,128)S(1)}, u32[]{:S(2)}, u32[]{:S(2)}) collective-permute-start(f32[19,1,8,32]{3,2,1,0:T(8,128)S(1)} %get-tuple-element.1556), channel_id=1, source_target_pairs={{0,4},{4,8},{8,12},{12,16},{16,20},{20,24},{24,28},{1,5},{5,9},{9,... | collective-permute-start | bytes 58376 | tf_op jit(solution)/shard_map/while/body/eval_jaxpr/ppermute | solution.py:49
  20.8 5.4 %collective-permute-start.1 = (f32[19,1,8,32]{3,2,1,0:T(8,128)S(1)}, f32[19,1,8,32]{3,2,1,0:T(8,128)S(1)}, u32[]{:S(2)}, u32[]{:S(2)}) collective-permute-start(f32[19,1,8,32]{3,2,1,0:T(8,128)S(1)} %get-tuple-element.1566), channel_id=1, source_target_pairs={{4,0},{8,4},{12,8},{16,12},{20,16},{24,20},{28,24},{5,1},{9,5},{13... | collective-permute-start | bytes 58376 | tf_op jit(solution)/shard_map/while/body/eval_jaxpr/ppermute | solution.py:50
  26.3 5.6 %collective-permute-start.2 = (f32[19,10,1,32]{3,2,1,0:T(1,128)S(1)}, f32[19,10,1,32]{3,2,1,0:T(1,128)S(1)}, u32[]{:S(2)}, u32[]{:S(2)}) collective-permute-start(f32[19,10,1,32]{3,2,1,0:T(1,128)S(1)} %get-tuple-element.1568), channel_id=1, source_target_pairs={{0,1},{1,2},{2,3},{4,5},{5,6},{6,7},{8,9},{9,10},{10,11},{12,13},{... | collective-permute-start | bytes 72968 | tf_op jit(solution)/shard_map/while/body/eval_jaxpr/ppermute | solution.py:49
  29.7 7.2 %collective-permute-start.3 = (f32[19,10,1,32]{3,2,1,0:T(1,128)S(1)}, f32[19,10,1,32]{3,2,1,0:T(1,128)S(1)}, u32[]{:S(2)}, u32[]{:S(2)}) collective-permute-start(f32[19,10,1,32]{3,2,1,0:T(1,128)S(1)} %get-tuple-element.1570), channel_id=1, source_target_pairs={{1,0},{2,1},{3,2},{5,4},{6,5},{7,6},{9,8},{10,9},{11,10},{13,12},{... | collective-permute-start | bytes 72968 | tf_op jit(solution)/shard_map/while/body/eval_jaxpr/ppermute | solution.py:50
  41.0 5.3 %collective-permute-start = (f32[19,1,8,32]{3,2,1,0:T(8,128)S(1)}, f32[19,1,8,32]{3,2,1,0:T(8,128)S(1)}, u32[]{:S(2)}, u32[]{:S(2)}) collective-permute-start(f32[19,1,8,32]{3,2,1,0:T(8,128)S(1)} %get-tuple-element.1556), channel_id=1, source_target_pairs={{0,4},{4,8},{8,12},{12,16},{16,20},{20,24},{24,28},{1,5},{5,9},{9,... | collective-permute-start | bytes 58376 | tf_op jit(solution)/shard_map/while/body/eval_jaxpr/ppermute | solution.py:49
  43.8 4.7 %collective-permute-start.1 = (f32[19,1,8,32]{3,2,1,0:T(8,128)S(1)}, f32[19,1,8,32]{3,2,1,0:T(8,128)S(1)}, u32[]{:S(2)}, u32[]{:S(2)}) collective-permute-start(f32[19,1,8,32]{3,2,1,0:T(8,128)S(1)} %get-tuple-element.1566), channel_id=1, source_target_pairs={{4,0},{8,4},{12,8},{16,12},{20,16},{24,20},{28,24},{5,1},{9,5},{13... | collective-permute-start | bytes 58376 | tf_op jit(solution)/shard_map/while/body/eval_jaxpr/ppermute | solution.py:50
  48.6 6.5 %collective-permute-start.2 = (f32[19,10,1,32]{3,2,1,0:T(1,128)S(1)}, f32[19,10,1,32]{3,2,1,0:T(1,128)S(1)}, u32[]{:S(2)}, u32[]{:S(2)}) collective-permute-start(f32[19,10,1,32]{3,2,1,0:T(1,128)S(1)} %get-tuple-element.1568), channel_id=1, source_target_pairs={{0,1},{1,2},{2,3},{4,5},{5,6},{6,7},{8,9},{9,10},{10,11},{12,13},{... | collective-permute-start | bytes 72968 | tf_op jit(solution)/shard_map/while/body/eval_jaxpr/ppermute | solution.py:49
  52.9 6.5 %collective-permute-start.3 = (f32[19,10,1,32]{3,2,1,0:T(1,128)S(1)}, f32[19,10,1,32]{3,2,1,0:T(1,128)S(1)}, u32[]{:S(2)}, u32[]{:S(2)}) collective-permute-start(f32[19,10,1,32]{3,2,1,0:T(1,128)S(1)} %get-tuple-element.1570), channel_id=1, source_target_pairs={{1,0},{2,1},{3,2},{5,4},{6,5},{7,6},{9,8},{10,9},{11,10},{13,12},{... | collective-permute-start | bytes 72968 | tf_op jit(solution)/shard_map/while/body/eval_jaxpr/ppermute | solution.py:50
  63.5 5.9 %collective-permute-start = (f32[19,1,8,32]{3,2,1,0:T(8,128)S(1)}, f32[19,1,8,32]{3,2,1,0:T(8,128)S(1)}, u32[]{:S(2)}, u32[]{:S(2)}) collective-permute-start(f32[19,1,8,32]{3,2,1,0:T(8,128)S(1)} %get-tuple-element.1556), channel_id=1, source_target_pairs={{0,4},{4,8},{8,12},{12,16},{16,20},{20,24},{24,28},{1,5},{5,9},{9,... | collective-permute-start | bytes 58376 | tf_op jit(solution)/shard_map/while/body/eval_jaxpr/ppermute | solution.py:49
  67.1 4.7 %collective-permute-start.1 = (f32[19,1,8,32]{3,2,1,0:T(8,128)S(1)}, f32[19,1,8,32]{3,2,1,0:T(8,128)S(1)}, u32[]{:S(2)}, u32[]{:S(2)}) collective-permute-start(f32[19,1,8,32]{3,2,1,0:T(8,128)S(1)} %get-tuple-element.1566), channel_id=1, source_target_pairs={{4,0},{8,4},{12,8},{16,12},{20,16},{24,20},{28,24},{5,1},{9,5},{13... | collective-permute-start | bytes 58376 | tf_op jit(solution)/shard_map/while/body/eval_jaxpr/ppermute | solution.py:50
  71.9 5.6 %collective-permute-start.2 = (f32[19,10,1,32]{3,2,1,0:T(1,128)S(1)}, f32[19,10,1,32]{3,2,1,0:T(1,128)S(1)}, u32[]{:S(2)}, u32[]{:S(2)}) collective-permute-start(f32[19,10,1,32]{3,2,1,0:T(1,128)S(1)} %get-tuple-element.1568), channel_id=1, source_target_pairs={{0,1},{1,2},{2,3},{4,5},{5,6},{6,7},{8,9},{9,10},{10,11},{12,13},{... | collective-permute-start | bytes 72968 | tf_op jit(solution)/shard_map/while/body/eval_jaxpr/ppermute | solution.py:49
  75.3 6.5 %collective-permute-start.3 = (f32[19,10,1,32]{3,2,1,0:T(1,128)S(1)}, f32[19,10,1,32]{3,2,1,0:T(1,128)S(1)}, u32[]{:S(2)}, u32[]{:S(2)}) collective-permute-start(f32[19,10,1,32]{3,2,1,0:T(1,128)S(1)} %get-tuple-element.1570), channel_id=1, source_target_pairs={{1,0},{2,1},{3,2},{5,4},{6,5},{7,6},{9,8},{10,9},{11,10},{13,12},{... | collective-permute-start | bytes 72968 | tf_op jit(solution)/shard_map/while/body/eval_jaxpr/ppermute | solution.py:50
  85.9 5.9 %collective-permute-start = (f32[19,1,8,32]{3,2,1,0:T(8,128)S(1)}, f32[19,1,8,32]{3,2,1,0:T(8,128)S(1)}, u32[]{:S(2)}, u32[]{:S(2)}) collective-permute-start(f32[19,1,8,32]{3,2,1,0:T(8,128)S(1)} %get-tuple-element.1556), channel_id=1, source_target_pairs={{0,4},{4,8},{8,12},{12,16},{16,20},{20,24},{24,28},{1,5},{5,9},{9,... | collective-permute-start | bytes 58376 | tf_op jit(solution)/shard_map/while/body/eval_jaxpr/ppermute | solution.py:49
  89.4 4.3 %collective-permute-start.1 = (f32[19,1,8,32]{3,2,1,0:T(8,128)S(1)}, f32[19,1,8,32]{3,2,1,0:T(8,128)S(1)}, u32[]{:S(2)}, u32[]{:S(2)}) collective-permute-start(f32[19,1,8,32]{3,2,1,0:T(8,128)S(1)} %get-tuple-element.1566), channel_id=1, source_target_pairs={{4,0},{8,4},{12,8},{16,12},{20,16},{24,20},{28,24},{5,1},{9,5},{13... | collective-permute-start | bytes 58376 | tf_op jit(solution)/shard_map/while/body/eval_jaxpr/ppermute | solution.py:50
  93.8 4.8 %collective-permute-start.2 = (f32[19,10,1,32]{3,2,1,0:T(1,128)S(1)}, f32[19,10,1,32]{3,2,1,0:T(1,128)S(1)}, u32[]{:S(2)}, u32[]{:S(2)}) collective-permute-start(f32[19,10,1,32]{3,2,1,0:T(1,128)S(1)} %get-tuple-element.1568), channel_id=1, source_target_pairs={{0,1},{1,2},{2,3},{4,5},{5,6},{6,7},{8,9},{9,10},{10,11},{12,13},{... | collective-permute-start | bytes 72968 | tf_op jit(solution)/shard_map/while/body/eval_jaxpr/ppermute | solution.py:49
  96.4 6.5 %collective-permute-start.3 = (f32[19,10,1,32]{3,2,1,0:T(1,128)S(1)}, f32[19,10,1,32]{3,2,1,0:T(1,128)S(1)}, u32[]{:S(2)}, u32[]{:S(2)}) collective-permute-start(f32[19,10,1,32]{3,2,1,0:T(1,128)S(1)} %get-tuple-element.1570), channel_id=1, source_target_pairs={{1,0},{2,1},{3,2},{5,4},{6,5},{7,6},{9,8},{10,9},{11,10},{13,12},{... | collective-permute-start | bytes 72968 | tf_op jit(solution)/shard_map/while/body/eval_jaxpr/ppermute | solution.py:50
  105.2 8.9 %collective-permute-start.4 = (f32[19,1,8,32]{3,2,1,0:T(8,128)S(1)}, f32[19,1,8,32]{3,2,1,0:T(8,128)S(1)}, u32[]{:S(2)}, u32[]{:S(2)}) collective-permute-start(f32[19,1,8,32]{3,2,1,0:T(8,128)S(1)} %get-tuple-element.1587), channel_id=1, source_target_pairs={{4,0},{8,4},{12,8},{16,12},{20,16},{24,20},{28,24},{5,1},{9,5},{13... | collective-permute-start | bytes 58376 | tf_op jit(solution)/shard_map/while/body/eval_jaxpr/ppermute | solution.py:50
  106.5 7.5 %collective-permute-start.5 = (f32[19,1,8,32]{3,2,1,0:T(8,128)S(1)}, f32[19,1,8,32]{3,2,1,0:T(8,128)S(1)}, u32[]{:S(2)}, u32[]{:S(2)}) collective-permute-start(f32[19,1,8,32]{3,2,1,0:T(8,128)S(1)} %get-tuple-element.1597), channel_id=1, source_target_pairs={{0,4},{4,8},{8,12},{12,16},{16,20},{20,24},{24,28},{1,5},{5,9},{9,... | collective-permute-start | bytes 58376 | tf_op jit(solution)/shard_map/while/body/eval_jaxpr/ppermute | solution.py:49
  114.2 6.8 %collective-permute-start.6 = (f32[19,10,1,32]{3,2,1,0:T(1,128)S(1)}, f32[19,10,1,32]{3,2,1,0:T(1,128)S(1)}, u32[]{:S(2)}, u32[]{:S(2)}) collective-permute-start(f32[19,10,1,32]{3,2,1,0:T(1,128)S(1)} %get-tuple-element.1599), channel_id=1, source_target_pairs={{1,0},{2,1},{3,2},{5,4},{6,5},{7,6},{9,8},{10,9},{11,10},{13,12},{... | collective-permute-start | bytes 72968 | tf_op jit(solution)/shard_map/while/body/eval_jaxpr/ppermute | solution.py:50
  115.5 7.3 %collective-permute-start.7 = (f32[19,10,1,32]{3,2,1,0:T(1,128)S(1)}, f32[19,10,1,32]{3,2,1,0:T(1,128)S(1)}, u32[]{:S(2)}, u32[]{:S(2)}) collective-permute-start(f32[19,10,1,32]{3,2,1,0:T(1,128)S(1)} %get-tuple-element.1601), channel_id=1, source_target_pairs={{0,1},{1,2},{2,3},{4,5},{5,6},{6,7},{8,9},{9,10},{10,11},{12,13},{... | collective-permute-start | bytes 72968 | tf_op jit(solution)/shard_map/while/body/eval_jaxpr/ppermute | solution.py:49
  129.4 7.8 %collective-permute-start.4 = (f32[19,1,8,32]{3,2,1,0:T(8,128)S(1)}, f32[19,1,8,32]{3,2,1,0:T(8,128)S(1)}, u32[]{:S(2)}, u32[]{:S(2)}) collective-permute-start(f32[19,1,8,32]{3,2,1,0:T(8,128)S(1)} %get-tuple-element.1587), channel_id=1, source_target_pairs={{4,0},{8,4},{12,8},{16,12},{20,16},{24,20},{28,24},{5,1},{9,5},{13... | collective-permute-start | bytes 58376 | tf_op jit(solution)/shard_map/while/body/eval_jaxpr/ppermute | solution.py:50
  130.7 6.5 %collective-permute-start.5 = (f32[19,1,8,32]{3,2,1,0:T(8,128)S(1)}, f32[19,1,8,32]{3,2,1,0:T(8,128)S(1)}, u32[]{:S(2)}, u32[]{:S(2)}) collective-permute-start(f32[19,1,8,32]{3,2,1,0:T(8,128)S(1)} %get-tuple-element.1597), channel_id=1, source_target_pairs={{0,4},{4,8},{8,12},{12,16},{16,20},{20,24},{24,28},{1,5},{5,9},{9,... | collective-permute-start | bytes 58376 | tf_op jit(solution)/shard_map/while/body/eval_jaxpr/ppermute | solution.py:49
  137.4 6.9 %collective-permute-start.6 = (f32[19,10,1,32]{3,2,1,0:T(1,128)S(1)}, f32[19,10,1,32]{3,2,1,0:T(1,128)S(1)}, u32[]{:S(2)}, u32[]{:S(2)}) collective-permute-start(f32[19,10,1,32]{3,2,1,0:T(1,128)S(1)} %get-tuple-element.1599), channel_id=1, source_target_pairs={{1,0},{2,1},{3,2},{5,4},{6,5},{7,6},{9,8},{10,9},{11,10},{13,12},{... | collective-permute-start | bytes 72968 | tf_op jit(solution)/shard_map/while/body/eval_jaxpr/ppermute | solution.py:50
  138.7 7.4 %collective-permute-start.7 = (f32[19,10,1,32]{3,2,1,0:T(1,128)S(1)}, f32[19,10,1,32]{3,2,1,0:T(1,128)S(1)}, u32[]{:S(2)}, u32[]{:S(2)}) collective-permute-start(f32[19,10,1,32]{3,2,1,0:T(1,128)S(1)} %get-tuple-element.1601), channel_id=1, source_target_pairs={{0,1},{1,2},{2,3},{4,5},{5,6},{6,7},{8,9},{9,10},{10,11},{12,13},{... | collective-permute-start | bytes 72968 | tf_op jit(solution)/shard_map/while/body/eval_jaxpr/ppermute | solution.py:49
  152.6 8.2 %collective-permute-start.4 = (f32[19,1,8,32]{3,2,1,0:T(8,128)S(1)}, f32[19,1,8,32]{3,2,1,0:T(8,128)S(1)}, u32[]{:S(2)}, u32[]{:S(2)}) collective-permute-start(f32[19,1,8,32]{3,2,1,0:T(8,128)S(1)} %get-tuple-element.1587), channel_id=1, source_target_pairs={{4,0},{8,4},{12,8},{16,12},{20,16},{24,20},{28,24},{5,1},{9,5},{13... | collective-permute-start | bytes 58376 | tf_op jit(solution)/shard_map/while/body/eval_jaxpr/ppermute | solution.py:50
  153.9 6.8 %collective-permute-start.5 = (f32[19,1,8,32]{3,2,1,0:T(8,128)S(1)}, f32[19,1,8,32]{3,2,1,0:T(8,128)S(1)}, u32[]{:S(2)}, u32[]{:S(2)}) collective-permute-start(f32[19,1,8,32]{3,2,1,0:T(8,128)S(1)} %get-tuple-element.1597), channel_id=1, source_target_pairs={{0,4},{4,8},{8,12},{12,16},{16,20},{20,24},{24,28},{1,5},{5,9},{9,... | collective-permute-start | bytes 58376 | tf_op jit(solution)/shard_map/while/body/eval_jaxpr/ppermute | solution.py:49
  160.9 7.5 %collective-permute-start.6 = (f32[19,10,1,32]{3,2,1,0:T(1,128)S(1)}, f32[19,10,1,32]{3,2,1,0:T(1,128)S(1)}, u32[]{:S(2)}, u32[]{:S(2)}) collective-permute-start(f32[19,10,1,32]{3,2,1,0:T(1,128)S(1)} %get-tuple-element.1599), channel_id=1, source_target_pairs={{1,0},{2,1},{3,2},{5,4},{6,5},{7,6},{9,8},{10,9},{11,10},{13,12},{... | collective-permute-start | bytes 72968 | tf_op jit(solution)/shard_map/while/body/eval_jaxpr/ppermute | solution.py:50
  162.2 7.9 %collective-permute-start.7 = (f32[19,10,1,32]{3,2,1,0:T(1,128)S(1)}, f32[19,10,1,32]{3,2,1,0:T(1,128)S(1)}, u32[]{:S(2)}, u32[]{:S(2)}) collective-permute-start(f32[19,10,1,32]{3,2,1,0:T(1,128)S(1)} %get-tuple-element.1601), channel_id=1, source_target_pairs={{0,1},{1,2},{2,3},{4,5},{5,6},{6,7},{8,9},{9,10},{10,11},{12,13},{... | collective-permute-start | bytes 72968 | tf_op jit(solution)/shard_map/while/body/eval_jaxpr/ppermute | solution.py:49
  176.7 8.2 %collective-permute-start.4 = (f32[19,1,8,32]{3,2,1,0:T(8,128)S(1)}, f32[19,1,8,32]{3,2,1,0:T(8,128)S(1)}, u32[]{:S(2)}, u32[]{:S(2)}) collective-permute-start(f32[19,1,8,32]{3,2,1,0:T(8,128)S(1)} %get-tuple-element.1587), channel_id=1, source_target_pairs={{4,0},{8,4},{12,8},{16,12},{20,16},{24,20},{28,24},{5,1},{9,5},{13... | collective-permute-start | bytes 58376 | tf_op jit(solution)/shard_map/while/body/eval_jaxpr/ppermute | solution.py:50
  178.0 6.8 %collective-permute-start.5 = (f32[19,1,8,32]{3,2,1,0:T(8,128)S(1)}, f32[19,1,8,32]{3,2,1,0:T(8,128)S(1)}, u32[]{:S(2)}, u32[]{:S(2)}) collective-permute-start(f32[19,1,8,32]{3,2,1,0:T(8,128)S(1)} %get-tuple-element.1597), channel_id=1, source_target_pairs={{0,4},{4,8},{8,12},{12,16},{16,20},{20,24},{24,28},{1,5},{5,9},{9,... | collective-permute-start | bytes 58376 | tf_op jit(solution)/shard_map/while/body/eval_jaxpr/ppermute | solution.py:49
  185.0 7.7 %collective-permute-start.6 = (f32[19,10,1,32]{3,2,1,0:T(1,128)S(1)}, f32[19,10,1,32]{3,2,1,0:T(1,128)S(1)}, u32[]{:S(2)}, u32[]{:S(2)}) collective-permute-start(f32[19,10,1,32]{3,2,1,0:T(1,128)S(1)} %get-tuple-element.1599), channel_id=1, source_target_pairs={{1,0},{2,1},{3,2},{5,4},{6,5},{7,6},{9,8},{10,9},{11,10},{13,12},{... | collective-permute-start | bytes 72968 | tf_op jit(solution)/shard_map/while/body/eval_jaxpr/ppermute | solution.py:50
  186.3 8.0 %collective-permute-start.7 = (f32[19,10,1,32]{3,2,1,0:T(1,128)S(1)}, f32[19,10,1,32]{3,2,1,0:T(1,128)S(1)}, u32[]{:S(2)}, u32[]{:S(2)}) collective-permute-start(f32[19,10,1,32]{3,2,1,0:T(1,128)S(1)} %get-tuple-element.1601), channel_id=1, source_target_pairs={{0,1},{1,2},{2,3},{4,5},{5,6},{6,7},{8,9},{9,10},{10,11},{12,13},{... | collective-permute-start | bytes 72968 | tf_op jit(solution)/shard_map/while/body/eval_jaxpr/ppermute | solution.py:49
  (8 other events, 177.0 us)
where the time goes:
time: 263 us; the launch traced here: 261 us
  starting transfers between devices  81.5 us (31%)
  other arithmetic  67.2 us (26%)
  blocking collectives  45 us (17%)
  waiting for transfers between devices  39.4 us (15%)
  local copies, waits for them, and re-layouts  25.8 us (10%)
    ppermute x16, starting transfers between devices, with_halo(): before = lax.ppermute(last, axis, up)  60.8 us
    psum x1, blocking collectives, on_device(): totals = lax.psum(local_sums, ('gx', 'gy'))  45 us
    ppermute x16, waiting for transfers between devices, with_halo(): after = lax.ppermute(leading, axis, down)  29.6 us
    ppermute x16, starting transfers between devices, with_halo(): after = lax.ppermute(leading, axis, down)  20.7 us
    scatter-add x1, other arithmetic, on_device(): jax.ops.segment_sum(grad_cells.reshape(-1), panels.reshape(-1), num_segme...  14.7 us
    gather x2, local copies, waits for them, and re-layouts, on_device(): phi = porosity[panels]  12.7 us
    while x136, other arithmetic  10.9 us
    ppermute x16, waiting for transfers between devices, with_halo(): before = lax.ppermute(last, axis, up)  9.8 us
  transfers between devices with their start and end apart: 32, of which 20 were waited for; matrix products, arithmetic and copies ran while one was open for 7% of the time, Pallas kernels for 0%

commit v1 on v0

v1 whole, which is shorter than its diff:
```python
import functools

import jax
import jax.numpy as jnp
import numpy as np
from jax import lax
from jax.experimental import pallas as pl
from jax.experimental.pallas import tpu as pltpu
from jax.sharding import PartitionSpec as P

Q = 19
STEPS = 4
NZ = 32
ROWS = 8
LANES = 128
OMEGA = 1.6
ACCEL = (0.002, 0.0, -0.003)
SHIFT = tuple(a / OMEGA for a in ACCEL)

VELOCITIES = [
    (0, 0, 0),
    (1, 0, 0),
    (-1, 0, 0),
    (0, 1, 0),
    (0, -1, 0),
    (0, 0, 1),
    (0, 0, -1),
    (1, 1, 0),
    (-1, -1, 0),
    (1, -1, 0),
    (-1, 1, 0),
    (1, 0, 1),
    (-1, 0, -1),
    (1, 0, -1),
    (-1, 0, 1),
    (0, 1, 1),
    (0, -1, -1),
    (0, 1, -1),
    (0, -1, 1),
]
OPPOSITE = [0, 2, 1, 4, 3, 6, 5, 8, 7, 10, 9, 12, 11, 14, 13, 16, 15, 18, 17]
PAIRS = [(i, i + 1) for i in range(1, Q, 2)]
W_REST, W_AXIS, W_DIAG = 1.0 / 3.0, 1.0 / 18.0, 1.0 / 36.0

Y_COT, Y_CODE, Y_PHI, Y_HALF = 19, 38, 41, 42
HALVES = Q + 2
Y_TILES = Y_HALF + (HALVES + 1) // 2
X_COT = 5 * Q
X_CODE1 = X_COT + 4 * Q
X_CODE2 = X_CODE1 + 5
X_CODE3 = X_CODE2 + 4
X_PHI = X_CODE3 + 4
X_TILES = X_PHI + 5


def total(values):
    values = list(values)
    while len(values) > 1:
        values = [a + b for a, b in zip(values[::2], values[1::2])] + (
            [values[-1]] if len(values) % 2 else []
        )
    return values[0]


def along(vector, three):
    terms = None
    for c, value in zip(vector, three):
        if c == 0:
            continue
        if terms is None:
            terms = value if c > 0 else -value
        else:
            terms = terms + value if c > 0 else terms - value
    return terms


def moments(f):
    plus = {i: f[i] + f[o] for i, o in PAIRS}
    minus = {i: f[i] - f[o] for i, o in PAIRS}
    rho = total([f[0]] + [plus[i] for i, _ in PAIRS])
    rinv = 1.0 / rho
    u = []
    for axis in range(3):
        terms = [
            minus[i] if VELOCITIES[i][axis] > 0 else -minus[i]
            for i, _ in PAIRS
            if VELOCITIES[i][axis] != 0
        ]
        u.append(total(terms) * rinv + SHIFT[axis])
    return plus, minus, rho, rinv, u


def coefficients(kind, phi, rinv):
    baffle = kind == 3.0
    gas = kind == 0.0
    even = jnp.where(gas, 0.0, jnp.where(baffle, 0.5 - 0.5 * OMEGA * phi, 0.5 * (1.0 - OMEGA)))
    odd = jnp.where(
        gas, 0.0, jnp.where(baffle, (1.0 - 0.5 * OMEGA) * phi - 0.5, 0.5 * (1.0 - OMEGA))
    )
    slope = jnp.where(
        baffle,
        OMEGA * phi,
        jnp.where(kind == 1.0, OMEGA, jnp.where(kind == 2.0, OMEGA * rinv, 0.0)),
    )
    return even, odd, slope


def collide(f, kind, phi, parts):
    plus, minus, rho, rinv, u = parts
    even, odd, slope = coefficients(kind, phi, rinv)
    scale = slope * rho
    rest = 1.0 - 1.5 * (u[0] * u[0] + u[1] * u[1] + u[2] * u[2])
    base = scale * rest + jnp.where(kind == 0.0, 1.0, 0.0)
    out = [None] * Q
    out[0] = 2.0 * even * f[0] + W_REST * base
    for weight, pairs in ((W_AXIS, PAIRS[:3]), (W_DIAG, PAIRS[3:])):
        flat = weight * base
        three = (3.0 * weight) * scale
        for i, o in pairs:
            cu = along(VELOCITIES[i], u)
            lin = three * cu
            ev = even * plus[i] + (flat + 1.5 * lin * cu)
            od = odd * minus[i] + lin
            out[i] = ev + od
            out[o] = ev - od
    return out


def collide_back(b, kind, phi, rho, rinv, u, state=None):
    even, odd, slope = coefficients(kind, phi, rinv)
    plus = {i: b[i] + b[o] for i, o in PAIRS}
    minus = {i: b[i] - b[o] for i, o in PAIRS}
    rest = 1.0 - 1.5 * (u[0] * u[0] + u[1] * u[1] + u[2] * u[2])
    u_half = [1.5 * c for c in u]
    weighted = W_REST * b[0]
    energy = 0.0
    vector = [0.0, 0.0, 0.0]
    for weight, pairs in ((W_AXIS, PAIRS[:3]), (W_DIAG, PAIRS[3:])):
        weighted = weighted + weight * total([plus[i] for i, _ in pairs])
        energies, parts = [], ([], [], [])
        for i, _ in pairs:
            cu = along(VELOCITIES[i], u)
            half = along(VELOCITIES[i], u_half) * plus[i]
            first = minus[i] + half
            energies.append(cu * first)
            second = first + half
            for axis in range(3):
                c = VELOCITIES[i][axis]
                if c:
                    parts[axis].append(second if c > 0 else -second)
        energy = energy + (3.0 * weight) * total(energies)
        vector = [vector[k] + (3.0 * weight) * total(parts[k]) for k in range(3)]
    energy = energy + rest * weighted
    vector = [vector[k] - (3.0 * weighted) * u[k] for k in range(3)]
    push = [slope * v for v in vector]
    inner = total([push[k] * (u[k] - SHIFT[k]) for k in range(3)])
    shared = jnp.where(kind == 2.0, 0.0, slope) * energy - inner
    out = [None] * Q
    out[0] = 2.0 * even * b[0] + shared
    for i, o in PAIRS:
        ev = even * plus[i] + shared
        od = odd * minus[i] + along(VELOCITIES[i], push)
        out[i] = ev + od
        out[o] = ev - od
    if state is None:
        return out, None
    evens = total([plus[i] * (state[i] + state[o]) for i, o in PAIRS])
    odds = total([minus[i] * (state[i] - state[o]) for i, o in PAIRS])
    term = (
        -OMEGA * (b[0] * state[0] + 0.5 * evens)
        + (1.0 - 0.5 * OMEGA) * odds
        + OMEGA * rho * energy
    )
    return out, jnp.where(kind == 3.0, term, 0.0)


def wall_masks(sign_rows, own_low, own_high, edges):
    lane = lax.broadcasted_iota(jnp.int32, (ROWS, LANES), 1)
    row = lax.broadcasted_iota(jnp.int32, (ROWS, LANES), 0)
    x_low, x_high, y_low, y_high = edges
    depth = lane % NZ
    masks = {}
    masks[2, 1] = depth == 0
    masks[2, -1] = depth == NZ - 1
    masks[1, 1] = lane < jnp.where(own_low, y_low * NZ, 0)
    masks[1, -1] = lane >= jnp.where(own_high, LANES - y_high * NZ, LANES)
    if sign_rows:
        masks[0, 1] = row < x_low
        masks[0, -1] = row >= ROWS - x_high
    return masks


def stream_tile(load, sign, masks, lane):
    cross_low, cross_high = lane >= LANES - NZ, lane < NZ
    combined = {}
    out = []
    for i, vector in enumerate(VELOCITIES):
        v = tuple(sign * c for c in vector)
        value = load(i, 0, -v[0])
        if v[1] == 1:
            value = jnp.where(cross_low, load(i, -1, -v[0]), value)
        elif v[1] == -1:
            value = jnp.where(cross_high, load(i, 1, -v[0]), value)
        amount = (v[1] * NZ + v[2]) % LANES
        if amount:
            value = pltpu.roll(value, amount, 1)
        outside = None
        if v not in combined:
            for axis in range(3):
                if v[axis] and (axis, v[axis]) in masks:
                    wall = masks[axis, v[axis]]
                    outside = wall if outside is None else outside | wall
            combined[v] = outside
        outside = combined[v]
        if outside is not None:
            value = jnp.where(outside, load(OPPOSITE[i], 0, 0), value)
        out.append(value)
    return out


def panel_field(porosity_ref, panels_ref, tile):
    row = lax.broadcasted_iota(jnp.int32, (ROWS, LANES), 0)
    upper = porosity_ref[panels_ref[0, tile * LANES]]
    lower = porosity_ref[panels_ref[4, tile * LANES]]
    return jnp.where(row < 4, upper, lower)


def pack_y(porosity_ref, panels_ref, f_ref, cot_ref, codes_ref, up_ref, down_ref, own_ref):
    lane = lax.broadcasted_iota(jnp.int32, (ROWS, LANES), 1)
    high = lane >= LANES // 2
    for tile, out_ref in ((0, down_ref), (1, up_ref)):
        lanes = pl.ds(tile * LANES, LANES)
        phi = panel_field(porosity_ref, panels_ref, tile)
        f = [f_ref[i, :, lanes] for i in range(Q)]
        kinds = [codes_ref[s, :, lanes].astype(jnp.float32) for s in range(STEPS)]
        g = collide(f, kinds[0], phi, moments(f))
        for i in range(Q):
            own_ref[2 * i + tile] = g[i]
            out_ref[i] = g[i]
            out_ref[Y_COT + i] = cot_ref[i, :, lanes]
        for s in range(1, STEPS):
            out_ref[Y_CODE + s - 1] = kinds[s]
        out_ref[Y_PHI] = phi
        outer = g + [kinds[1], phi]
        other_ref = down_ref if tile == 1 else up_ref
        keep = high if tile == 0 else ~high
        for n in range(0, HALVES, 2):
            value = outer[n]
            if n + 1 < HALVES:
                value = jnp.where(keep, value, pltpu.roll(outer[n + 1], LANES // 2, 1))
            other_ref[Y_HALF + n // 2] = value


def pack_x(porosity_ref, panels_ref, own_ref, cot_ref, codes_ref, left_ref, right_ref, out_ref):
    lane = lax.broadcasted_iota(jnp.int32, (ROWS, LANES), 1)
    high = lane >= LANES // 2

    def outer(n):
        left, right = left_ref[Y_HALF + n // 2], right_ref[Y_HALF + n // 2]
        if n % 2 == 0:
            return jnp.where(high, left, right)
        return pltpu.roll(jnp.where(high, right, left), LANES // 2, 1)

    for i in range(Q):
        out_ref[5 * i] = outer(i)
        out_ref[5 * i + 1] = left_ref[i]
        out_ref[5 * i + 2] = own_ref[2 * i]
        out_ref[5 * i + 3] = own_ref[2 * i + 1]
        out_ref[5 * i + 4] = right_ref[i]
        out_ref[X_COT + 4 * i] = left_ref[Y_COT + i]
        out_ref[X_COT + 4 * i + 1] = cot_ref[i, :, pl.ds(0, LANES)]
        out_ref[X_COT + 4 * i + 2] = cot_ref[i, :, pl.ds(LANES, LANES)]
        out_ref[X_COT + 4 * i + 3] = right_ref[Y_COT + i]
    out_ref[X_CODE1] = outer(Q)
    for s, first in ((1, X_CODE1 + 1), (2, X_CODE2), (3, X_CODE3)):
        out_ref[first] = left_ref[Y_CODE + s - 1]
        for tile in range(2):
            out_ref[first + 1 + tile] = codes_ref[s, :, pl.ds(tile * LANES, LANES)].astype(
                jnp.float32
            )
        out_ref[first + 3] = right_ref[Y_CODE + s - 1]
    out_ref[X_PHI] = outer(Q + 1)
    out_ref[X_PHI + 1] = left_ref[Y_PHI]
    for tile in range(2):
        out_ref[X_PHI + 2 + tile] = panel_field(porosity_ref, panels_ref, tile)
    out_ref[X_PHI + 4] = right_ref[Y_PHI]


def steps_kernel(
    sizes,
    panels_ref,
    f_ref,
    codes_ref,
    below_ref,
    mid_ref,
    above_ref,
    adjoint_ref,
    panel_ref,
    pop_a,
    pop_b,
    cot,
    field,
    saved,
    mom,
    grad,
    sems,
):
    size_x, size_y = sizes
    copies = []
    for n, source in enumerate((below_ref, mid_ref, above_ref)):
        rows = pl.ds(ROWS * (n + 1), ROWS)
        for m, (target, first, count) in enumerate(
            (
                (pop_a, 0, X_COT),
                (cot, X_COT, X_CODE1 - X_COT),
                (field, X_CODE1, X_TILES - X_CODE1),
            )
        ):
            copy = pltpu.make_async_copy(
                source.at[pl.ds(first, count)], target.at[:, rows, :], sems.at[n, m]
            )
            copy.start()
            copies.append(copy)
    for copy in copies:
        copy.wait()

    at_x, at_y = lax.axis_index("gx"), lax.axis_index("gy")
    edges = (
        jnp.where(at_x == 0, 1, 0),
        jnp.where(at_x == size_x - 1, 1, 0),
        jnp.where(at_y == 0, 1, 0),
        jnp.where(at_y == size_y - 1, 1, 0),
    )
    lane = lax.broadcasted_iota(jnp.int32, (ROWS, LANES), 1)

    def streamed(ref, tile, tiles, r, sign, masks, four):
        step = {0: tile, -1: lax.rem(tile + tiles - 1, tiles), 1: lax.rem(tile + 1, tiles)}

        def load(i, tile_step, row_step):
            return ref[tiles * i + step[tile_step], pl.ds(ROWS * (r + 1) + row_step, ROWS), :]

        return stream_tile(load, sign, masks, lane)

    def masks_of(tile, first, r):
        return wall_masks(r == 1, tile == first, tile == first + 1, edges)

    def rows_of(r):
        return pl.ds(ROWS * (r + 1), ROWS)

    def forward(source, tiles, own, s, target, target_tiles, offset):
        def body(tile, carry):
            ring = tile - offset if target_tiles != tiles else tile
            for r in range(3):
                f = streamed(source, tile, tiles, r, 1, masks_of(tile, own, r), None)
                parts = moments(f)
                _, _, rho, rinv, u = parts
                place = tile if tiles == 4 else lax.rem(tile + 4, 5)
                for n, value in enumerate((rho, rinv, *u)):
                    mom[s - 1, n, place, pl.ds(ROWS * r, ROWS), :] = value
                if r == 1:
                    for i in range(Q):
                        saved[s - 1, i, place] = f[i]
                if target is not None:
                    at = tile if tiles == 5 else tile + 1
                    first = (X_CODE1 if s == 1 else X_CODE2 - 1) - X_CODE1
                    kind = field[first + at, rows_of(r), :]
                    phi = field[X_PHI - X_CODE1 + at, rows_of(r), :]
                    g = collide(f, kind, phi, parts)
                    for i in range(Q):
                        target[target_tiles * i + ring, rows_of(r), :] = g[i]
            return carry

        start, stop = (0, 5) if target_tiles == 5 else (1, 5)
        if tiles == 4:
            start, stop = 0, 4
        lax.fori_loop(start, stop, body, 0)

    forward(pop_a, 5, 2, 1, pop_b, 5, 0)
    forward(pop_b, 5, 2, 2, pop_a, 4, 1)
    forward(pop_a, 4, 1, 3, None, 4, 0)

    def backward(source, s, target):
        def body(tile, carry):
            for r in range(3):
                b = streamed(source, tile, 4, r, -1, masks_of(tile, 1, r), None)
                rho, rinv, *u = [
                    mom[s - 1, n, tile, pl.ds(ROWS * r, ROWS), :] for n in range(5)
                ]
                first = (X_CODE1 + 1, X_CODE2, X_CODE3)[s - 1] - X_CODE1
                kind = field[first + tile, rows_of(r), :]
                phi = field[X_PHI + 1 - X_CODE1 + tile, rows_of(r), :]
                state = [saved[s - 1, i, tile] for i in range(Q)] if r == 1 else None
                back, term = collide_back(b, kind, phi, rho, rinv, u, state)
                for i in range(Q):
                    target[4 * i + tile, rows_of(r), :] = back[i]
                if r == 1:
                    grad[tile] = term if s == 3 else grad[tile] + term
            return carry

        lax.fori_loop(0, 4, body, 0)

    backward(cot, 3, pop_a)
    backward(pop_a, 2, pop_b)
    backward(pop_b, 1, pop_a)

    row = lax.broadcasted_iota(jnp.int32, (ROWS, LANES), 0)
    panel = lax.broadcasted_iota(jnp.int32, panel_ref.shape, 1)
    sums = jnp.zeros(panel_ref.shape, jnp.float32)
    for tile in range(2):
        lanes = pl.ds(tile * LANES, LANES)
        b = streamed(pop_a, tile + 1, 4, 1, -1, masks_of(tile, 0, 1), None)
        f = [f_ref[i, :, lanes] for i in range(Q)]
        kind = codes_ref[0, :, lanes].astype(jnp.float32)
        phi = field[X_PHI + 2 - X_CODE1 + tile, rows_of(1), :]
        _, _, rho, rinv, u = moments(f)
        back, term = collide_back(b, kind, phi, rho, rinv, u, f)
        for i in range(Q):
            adjoint_ref[i, :, lanes] = back[i]
        term = term + grad[tile + 1]
        for part in range(2):
            inside = (row < 4) if part == 0 else (row >= 4)
            amount = jnp.sum(jnp.where(inside, term, 0.0))
            name = panels_ref[4 * part, tile * LANES]
            sums = sums + jnp.where(panel == name, amount, 0.0)
    panel_ref[...] = sums


VMEM = pl.BlockSpec(memory_space=pltpu.VMEM)
SMEM = pl.BlockSpec(memory_space=pltpu.SMEM)
ANY = pl.BlockSpec(memory_space=pl.ANY)


def shape_of(*dims):
    return jax.ShapeDtypeStruct(dims, jnp.float32)


def on_device(sizes, checkpoint, cotangent, cell_codes, porosity, baffle_index):
    size_x, size_y = sizes
    panels = porosity.shape[0]
    devices = size_x * size_y
    params = pltpu.CompilerParams(vmem_limit_bytes=32 * 1024 * 1024)

    up, down, own = pl.pallas_call(
        pack_y,
        out_shape=(
            shape_of(Y_TILES, ROWS, LANES),
            shape_of(Y_TILES, ROWS, LANES),
            shape_of(2 * Q, ROWS, LANES),
        ),
        in_specs=[SMEM, SMEM, VMEM, VMEM, VMEM],
        out_specs=(VMEM, VMEM, VMEM),
        compiler_params=params,
        name="pack_y",
    )(porosity, baffle_index, checkpoint, cotangent, cell_codes)

    def exchange(to_next, to_last, axis, size):
        ups = [(i, i + 1) for i in range(size - 1)]
        downs = [(i + 1, i) for i in range(size - 1)]
        return lax.ppermute(to_next, axis, ups), lax.ppermute(to_last, axis, downs)

    left, right = exchange(up, down, "gy", size_y)
    ext = pl.pallas_call(
        pack_x,
        out_shape=shape_of(X_TILES, ROWS, LANES),
        in_specs=[SMEM, SMEM, VMEM, VMEM, VMEM, VMEM, VMEM],
        out_specs=VMEM,
        compiler_params=params,
        name="pack_x",
    )(porosity, baffle_index, own, cotangent, cell_codes, left, right)
    below, above = exchange(ext, ext, "gx", size_x)

    adjoint, sums = pl.pallas_call(
        functools.partial(steps_kernel, sizes),
        out_shape=(shape_of(Q, ROWS, 2 * LANES), shape_of(devices, panels)),
        in_specs=[SMEM, VMEM, VMEM, ANY, ANY, ANY],
        out_specs=(VMEM, VMEM),
        scratch_shapes=[
            pltpu.VMEM((5 * Q, 5 * ROWS, LANES), jnp.float32),
            pltpu.VMEM((5 * Q, 5 * ROWS, LANES), jnp.float32),
            pltpu.VMEM((4 * Q, 5 * ROWS, LANES), jnp.float32),
            pltpu.VMEM((X_TILES - X_CODE1, 5 * ROWS, LANES), jnp.float32),
            pltpu.VMEM((3, Q, 5, ROWS, LANES), jnp.float32),
            pltpu.VMEM((3, 5, 5, 3 * ROWS, LANES), jnp.float32),
            pltpu.VMEM((4, ROWS, LANES), jnp.float32),
            pltpu.SemaphoreType.DMA((3, 3)),
        ],
        compiler_params=params,
        name="steps",
    )(baffle_index, checkpoint, cell_codes, below, ext, above)
    gathered = lax.all_to_all(sums, ("gx", "gy"), 0, 0, tiled=True)
    return adjoint, jnp.sum(gathered, axis=0)


def solution(mesh):
    sizes = (mesh.shape["gx"], mesh.shape["gy"])
    in_specs = (P(None, "gx", "gy"), P(None, "gx", "gy"), P(None, "gx", "gy"), P(), P("gx", "gy"))
    out_specs = (P(None, "gx", "gy"), P())
    return jax.shard_map(
        functools.partial(on_device, sizes),
        mesh=mesh,
        in_specs=in_specs,
        out_specs=out_specs,
        check_vma=False,
    )
```

time: 263 us -> 56.2 us (0.21)
  starting transfers between devices: 81.5 us -> 10.5 us
  other arithmetic: 67.2 us -> 0.56 us
  waiting for transfers between devices: 39.4 us -> 11.7 us
  blocking collectives: 45 us -> 20.8 us
  local copies, waits for them, and re-layouts: 25.8 us -> 3.94 us
  Pallas kernels: 0 us -> 7.69 us
    ppermute x32 -> x4, starting transfers between devices: 81.5 us -> 10.5 us  [the longest x2 7.93 us: exchange(): lax.ppermute(to_next, axis, ups)]
    psum x1 -> x0, blocking collectives: 45 us -> none  [on_device(): totals = lax.psum(local_sums, ('gx', 'gy'))]
    ppermute x32 -> x4, waiting for transfers between devices: 39.4 us -> 11.7 us  [the longest x2 6.6 us: exchange(): lax.ppermute(to_last, axis, downs)]
    scatter-add x5 -> x0, other arithmetic: 23.6 us -> none  [the longest x1 14.7 us: on_device(): jax.ops.segment_sum(grad_cells.reshape(-1), panels.reshape(-1), num_segme...]
    all_to_all x0 -> x1, blocking collectives: none -> 20.8 us  [on_device(): gathered = lax.all_to_all(sums, ('gx', 'gy'), 0, 0, tiled=True)]
    gather x10 -> x0, local copies, waits for them, and re-layouts: 17.4 us -> none  [the longest x2 12.7 us: on_device(): phi = porosity[panels]]
    reduce_sum x16 -> x1, other arithmetic: 16.9 us -> 0.56 us  [on_device(): return (adjoint, jnp.sum(gathered, axis=0))]
    while x136 -> x0, other arithmetic: 10.9 us -> none
  transfers between devices with their start and end apart: 32 -> 4, of which waited for: 20 -> 3; matrix products, arithmetic and copies ran while one was open for 7% -> 0% of each run, Pallas kernels for 0% -> 0%
where the time goes in v1:
time: 56.2 us; the launch traced here: 55.9 us
  blocking collectives  20.8 us (37%)
  waiting for transfers between devices  11.7 us (21%)
  starting transfers between devices  10.5 us (19%)
  Pallas kernels  7.69 us (14%)
  local copies, waits for them, and re-layouts  3.94 us (7%)
  between operations  0.7 us (1%)
    all_to_all x1, blocking collectives, on_device(): gathered = lax.all_to_all(sums, ('gx', 'gy'), 0, 0, tiled=True)  20.8 us
    ppermute x2, starting transfers between devices, exchange(): lax.ppermute(to_next, axis, ups)  7.93 us
    ppermute x2, waiting for transfers between devices, exchange(): lax.ppermute(to_last, axis, downs)  6.6 us
    pallas_call x1, Pallas kernels, on_device(): pl.pallas_call(functools.partial(steps_kernel, sizes), out_shape=(shape_o...  6.15 us
    ppermute x2, waiting for transfers between devices, exchange(): lax.ppermute(to_next, axis, ups)  5.08 us
    unnamed x16, local copies, waits for them, and re-layouts  3.94 us
    ppermute x2, starting transfers between devices, exchange(): lax.ppermute(to_last, axis, downs)  2.58 us
  transfers between devices with their start and end apart: 4, of which 3 were waited for; matrix products, arithmetic and copies ran while one was open for 0% of the time, Pallas kernels for 0%

profile of v1, /device:TPU:0, one launch (start us, length us, event | category | flops | bytes accessed | tf_op | source)
XLA Modules:
  0.0 55.9 jit_solution(17194588525572919948)
XLA Ops:
  0.6 0.0 copy-start
  0.6 0.9 %copy-done = f32[19,8,256]{2,1,0:T(8,128)S(1)} copy-done((f32[19,8,256]{2,1,0:T(8,128)S(1)}, f32[19,8,256]{2,1,0:T(8,128)}, u32[]{:S(2)}) %copy-start) | copy-done | bytes 155672
  1.5 0.0 copy-start.2
  1.5 0.9 %copy-done.2 = f32[19,8,256]{2,1,0:T(8,128)S(1)} copy-done((f32[19,8,256]{2,1,0:T(8,128)S(1)}, f32[19,8,256]{2,1,0:T(8,128)}, u32[]{:S(2)}) %copy-start.2) | copy-done | bytes 155672
  2.5 0.0 copy-start.4
  2.5 0.8 %copy-done.4 = s32[4,8,256]{2,1,0:T(8,128)S(1)} copy-done((s32[4,8,256]{2,1,0:T(8,128)S(1)}, s32[4,8,256]{2,1,0:T(8,128)}, u32[]{:S(2)}) %copy-start.4) | copy-done | bytes 32792
  3.2 0.0 copy-start.6
  3.2 0.7 %copy-done.6 = s32[8,256]{1,0:T(8,128)S(1)} copy-done((s32[8,256]{1,0:T(8,128)S(1)}, s32[8,256]{1,0:T(8,128)}, u32[]{:S(2)}) %copy-start.6) | copy-done | bytes 8216
  3.9 0.0 copy-start.7
  3.9 0.7 %copy-done.7 = f32[64]{0:T(128)S(1)} copy-done((f32[64]{0:T(128)S(1)}, f32[64]{0:T(128)}, u32[]{:S(2)}) %copy-start.7) | copy-done | bytes 280
  4.6 0.0 copy-start.3
  4.6 0.0 copy-start.5
  4.6 0.8 %pack_y.1 = (f32[53,8,128]{2,1,0:T(8,128)S(1)}, f32[53,8,128]{2,1,0:T(8,128)S(1)}, f32[38,8,128]{2,1,0:T(8,128)S(1)}) custom-call(f32[64]{0:T(128)S(1)} %copy-done.7, s32[8,256]{1,0:T(8,128)S(1)} %copy-done.6, f32[19,8,256]{2,1,0:T(8,128)S(1)} %copy-done, f32[19,8,256]{2,1,0:T(8,128)S(1)} %copy-done.2, s32[4,8,256]{2,1,0:T(8,128)S(1)} %copy-done.4), custom_call_target="tpu_custom_call" | custom-call | tf_op jit(solution)/shard_map/pack_y/pallas_call | solution.py:443
  5.4 4.9 %collective-permute-start = (f32[53,8,128]{2,1,0:T(8,128)S(1)}, f32[53,8,128]{2,1,0:T(8,128)S(1)}, u32[]{:S(2)}, u32[]{:S(2)}) collective-permute-start(f32[53,8,128]{2,1,0:T(8,128)S(1)} %get-tuple-element.8), channel_id=1, source_target_pairs={{0,1},{1,2},{2,3},{4,5},{5,6},{6,7},{8,9},{9,10},{10,11},{12,13},{... | collective-permute-start | bytes 651272 | tf_op jit(solution)/shard_map/ppermute | solution.py:459
  10.2 1.3 %collective-permute-start.1 = (f32[53,8,128]{2,1,0:T(8,128)S(1)}, f32[53,8,128]{2,1,0:T(8,128)S(1)}, u32[]{:S(2)}, u32[]{:S(2)}) collective-permute-start(f32[53,8,128]{2,1,0:T(8,128)S(1)} %get-tuple-element.9), channel_id=1, source_target_pairs={{1,0},{2,1},{3,2},{5,4},{6,5},{7,6},{9,8},{10,9},{11,10},{13,12},{... | collective-permute-start | bytes 651272 | tf_op jit(solution)/shard_map/ppermute | solution.py:459
  11.5 3.3 %collective-permute-done.left_ref = f32[53,8,128]{2,1,0:T(8,128)S(1)} collective-permute-done((f32[53,8,128]{2,1,0:T(8,128)S(1)}, f32[53,8,128]{2,1,0:T(8,128)S(1)}, u32[]{:S(2)}, u32[]{:S(2)}) %collective-permute-start) | collective-permute-done | bytes 217120 | tf_op jit(solution)/shard_map/ppermute | solution.py:459
  14.8 6.6 %collective-permute-done.1.right_ref = f32[53,8,128]{2,1,0:T(8,128)S(1)} collective-permute-done((f32[53,8,128]{2,1,0:T(8,128)S(1)}, f32[53,8,128]{2,1,0:T(8,128)S(1)}, u32[]{:S(2)}, u32[]{:S(2)}) %collective-permute-start.1) | collective-permute-done | bytes 217120 | tf_op jit(solution)/shard_map/ppermute | solution.py:459
  21.4 0.0 copy-done.3
  21.4 0.0 copy-done.5
  21.4 0.0 copy-start.1
  21.4 0.8 %pack_x.1.mid_ref = f32[189,8,128]{2,1,0:T(8,128)S(1)} custom-call(f32[64]{0:T(128)S(1)} %copy-done.7, s32[8,256]{1,0:T(8,128)S(1)} %copy-done.6, f32[38,8,128]{2,1,0:T(8,128)S(1)} %get-tuple-element.7.own_ref, f32[19,8,256]{2,1,0:T(8,128)S(1)} %copy-done.3, s32[4,8,256]{2,1,0:T(8,128)S(1)} %copy-done.5, f32[53,8,128]{2,1,0:T(8,128)S(1)} %collective-permute-done.left_ref, ...), custom_call_target="tpu_custom_call" | custom-call | tf_op jit(solution)/shard_map/pack_x/pallas_call | solution.py:462
  22.2 1.3 %collective-permute-start.3 = (f32[189,8,128]{2,1,0:T(8,128)S(1)}, f32[189,8,128]{2,1,0:T(8,128)S(1)}, u32[]{:S(2)}, u32[]{:S(2)}) collective-permute-start(f32[189,8,128]{2,1,0:T(8,128)S(1)} %pack_x.1.mid_ref), channel_id=1, source_target_pairs={{4,0},{8,4},{12,8},{16,12},{20,16},{24,20},{28,24},{5,1},{9,5},{13... | collective-permute-start | bytes 2322440 | tf_op jit(solution)/shard_map/ppermute | solution.py:459
  23.5 3.1 %collective-permute-start.2 = (f32[189,8,128]{2,1,0:T(8,128)S(1)}, f32[189,8,128]{2,1,0:T(8,128)S(1)}, u32[]{:S(2)}, u32[]{:S(2)}) collective-permute-start(f32[189,8,128]{2,1,0:T(8,128)S(1)} %pack_x.1.mid_ref), channel_id=1, source_target_pairs={{0,4},{4,8},{8,12},{12,16},{16,20},{20,24},{24,28},{1,5},{5,9},{9,... | collective-permute-start | bytes 2322440 | tf_op jit(solution)/shard_map/ppermute | solution.py:459
  26.5 0.0 collective-permute-done.3.above_ref
  26.6 1.8 %collective-permute-done.2.below_ref = f32[189,8,128]{2,1,0:T(8,128)S(1)} collective-permute-done((f32[189,8,128]{2,1,0:T(8,128)S(1)}, f32[189,8,128]{2,1,0:T(8,128)S(1)}, u32[]{:S(2)}, u32[]{:S(2)}) %collective-permute-start.2) | collective-permute-done | bytes 774176 | tf_op jit(solution)/shard_map/ppermute | solution.py:459
  28.4 0.0 copy-done.1
  28.4 6.1 %steps.1 = (f32[19,8,256]{2,1,0:T(8,128)}, f32[32,64]{1,0:T(8,128)S(1)}) custom-call(s32[8,256]{1,0:T(8,128)S(1)} %copy-done.6, f32[19,8,256]{2,1,0:T(8,128)S(1)} %copy-done.1, s32[4,8,256]{2,1,0:T(8,128)S(1)} %copy-done.5, f32[189,8,128]{2,1,0:T(8,128)S(1)} %collective-permute-done.2.below_ref, f32[189,8,128]{2,1,0:T(8,128)S(1)} %pack_x.1.mid_ref, ...), custom_call_target="tpu_custom_call" | custom-call | tf_op jit(solution)/shard_map/steps/pallas_call | solution.py:472
  34.5 20.8 %all_to_all.9 = f32[32,1,64]{2,1,0:T(1,128)S(1)} all-to-all(f32[32,1,64]{2,1,0:T(1,128)S(1)} %bitcast.3), channel_id=1, replica_groups=mesh['gx'=8,'gy'=4] {'gx','gy'}, dimensions={0} | all-to-all | bytes 16384 | tf_op jit(solution)/shard_map/all_to_all | solution.py:490
  55.3 0.6 %reduce_sum.9 = f32[64]{0:T(128)} reduce(f32[32,1,64]{2,1,0:T(1,128)S(1)} %all_to_all.9, f32[]{:T(128)} %constant.0.clone.1), dimensions={0,1}, to_apply=%region_0.0 | reduce | flops 1984 | bytes 8452 | tf_op jit(solution)/shard_map/reduce_sum | solution.py:491
Async XLA Ops:
  0.6 0.9 %copy-start = (f32[19,8,256]{2,1,0:T(8,128)S(1)}, f32[19,8,256]{2,1,0:T(8,128)}, u32[]{:S(2)}) copy-start(f32[19,8,256]{2,1,0:T(8,128)} %f_ref.3) | copy-start | bytes 466948
  1.5 0.9 %copy-start.2 = (f32[19,8,256]{2,1,0:T(8,128)S(1)}, f32[19,8,256]{2,1,0:T(8,128)}, u32[]{:S(2)}) copy-start(f32[19,8,256]{2,1,0:T(8,128)} %cot_ref.3) | copy-start | bytes 466948
  2.5 0.8 %copy-start.4 = (s32[4,8,256]{2,1,0:T(8,128)S(1)}, s32[4,8,256]{2,1,0:T(8,128)}, u32[]{:S(2)}) copy-start(s32[4,8,256]{2,1,0:T(8,128)} %codes_ref.5) | copy-start | bytes 98308
  3.2 0.7 %copy-start.6 = (s32[8,256]{1,0:T(8,128)S(1)}, s32[8,256]{1,0:T(8,128)}, u32[]{:S(2)}) copy-start(s32[8,256]{1,0:T(8,128)} %panels_ref.5) | copy-start | bytes 24580
  3.9 0.7 %copy-start.7 = (f32[64]{0:T(128)S(1)}, f32[64]{0:T(128)}, u32[]{:S(2)}) copy-start(f32[64]{0:T(128)} %porosity_ref.3) | copy-start | bytes 772
  4.6 16.8 %copy-start.3 = (f32[19,8,256]{2,1,0:T(8,128)S(1)}, f32[19,8,256]{2,1,0:T(8,128)}, u32[]{:S(2)}) copy-start(f32[19,8,256]{2,1,0:T(8,128)} %cot_ref.3) | copy-start | bytes 466948
  4.6 16.8 %copy-start.5 = (s32[4,8,256]{2,1,0:T(8,128)S(1)}, s32[4,8,256]{2,1,0:T(8,128)}, u32[]{:S(2)}) copy-start(s32[4,8,256]{2,1,0:T(8,128)} %codes_ref.5) | copy-start | bytes 98308
  5.4 9.4 %collective-permute-start = (f32[53,8,128]{2,1,0:T(8,128)S(1)}, f32[53,8,128]{2,1,0:T(8,128)S(1)}, u32[]{:S(2)}, u32[]{:S(2)}) collective-permute-start(f32[53,8,128]{2,1,0:T(8,128)S(1)} %get-tuple-element.8), channel_id=1, source_target_pairs={{0,1},{1,2},{2,3},{4,5},{5,6},{6,7},{8,9},{9,10},{10,11},{12,13},{... | collective-permute-start | bytes 651272 | tf_op jit(solution)/shard_map/ppermute | solution.py:459
  10.2 11.2 %collective-permute-start.1 = (f32[53,8,128]{2,1,0:T(8,128)S(1)}, f32[53,8,128]{2,1,0:T(8,128)S(1)}, u32[]{:S(2)}, u32[]{:S(2)}) collective-permute-start(f32[53,8,128]{2,1,0:T(8,128)S(1)} %get-tuple-element.9), channel_id=1, source_target_pairs={{1,0},{2,1},{3,2},{5,4},{6,5},{7,6},{9,8},{10,9},{11,10},{13,12},{... | collective-permute-start | bytes 651272 | tf_op jit(solution)/shard_map/ppermute | solution.py:459
  21.4 7.0 %copy-start.1 = (f32[19,8,256]{2,1,0:T(8,128)S(1)}, f32[19,8,256]{2,1,0:T(8,128)}, u32[]{:S(2)}) copy-start(f32[19,8,256]{2,1,0:T(8,128)} %f_ref.3) | copy-start | bytes 466948
  22.2 4.4 %collective-permute-start.3 = (f32[189,8,128]{2,1,0:T(8,128)S(1)}, f32[189,8,128]{2,1,0:T(8,128)S(1)}, u32[]{:S(2)}, u32[]{:S(2)}) collective-permute-start(f32[189,8,128]{2,1,0:T(8,128)S(1)} %pack_x.1.mid_ref), channel_id=1, source_target_pairs={{4,0},{8,4},{12,8},{16,12},{20,16},{24,20},{28,24},{5,1},{9,5},{13... | collective-permute-start | bytes 2322440 | tf_op jit(solution)/shard_map/ppermute | solution.py:459
  23.5 4.9 %collective-permute-start.2 = (f32[189,8,128]{2,1,0:T(8,128)S(1)}, f32[189,8,128]{2,1,0:T(8,128)S(1)}, u32[]{:S(2)}, u32[]{:S(2)}) collective-permute-start(f32[189,8,128]{2,1,0:T(8,128)S(1)} %pack_x.1.mid_ref), channel_id=1, source_target_pairs={{0,4},{4,8},{8,12},{12,16},{16,20},{20,24},{24,28},{1,5},{5,9},{9,... | collective-permute-start | bytes 2322440 | tf_op jit(solution)/shard_map/ppermute | solution.py:459

commit v2 on v1

--- a/solution.py
+++ b/solution.py
@@ -437,7 +437,6 @@
 def on_device(sizes, checkpoint, cotangent, cell_codes, porosity, baffle_index):
     size_x, size_y = sizes
     panels = porosity.shape[0]
-    devices = size_x * size_y
     params = pltpu.CompilerParams(vmem_limit_bytes=32 * 1024 * 1024)
 
     up, down, own = pl.pallas_call(
@@ -471,7 +470,7 @@
 
     adjoint, sums = pl.pallas_call(
         functools.partial(steps_kernel, sizes),
-        out_shape=(shape_of(Q, ROWS, 2 * LANES), shape_of(devices, panels)),
+        out_shape=(shape_of(Q, ROWS, 2 * LANES), shape_of(size_x, panels)),
         in_specs=[SMEM, VMEM, VMEM, ANY, ANY, ANY],
         out_specs=(VMEM, VMEM),
         scratch_shapes=[
@@ -487,8 +486,10 @@
         compiler_params=params,
         name="steps",
     )(baffle_index, checkpoint, cell_codes, below, ext, above)
-    gathered = lax.all_to_all(sums, ("gx", "gy"), 0, 0, tiled=True)
-    return adjoint, jnp.sum(gathered, axis=0)
+    for axis, size in (("gx", size_x), ("gy", size_y)):
+        gathered = lax.all_to_all(sums, axis, 0, 0, tiled=True)
+        sums = jnp.broadcast_to(jnp.sum(gathered, axis=0), (size_y, panels))
+    return adjoint, sums[0]
 
 
 def solution(mesh):

time: 56.2 us -> 61.8 us (1.100)
  blocking collectives: 20.8 us -> 26.3 us
    all_to_all x1 -> x2, blocking collectives: 20.8 us -> 26.3 us  [on_device(): gathered = lax.all_to_all(sums, axis, 0, 0, tiled=True)]
where the time goes in v2:
time: 61.8 us; the launch traced here: 61.4 us
  blocking collectives  26.3 us (43%)
  waiting for transfers between devices  11.7 us (19%)
  starting transfers between devices  10.5 us (17%)
  Pallas kernels  7.69 us (12%)
  local copies, waits for them, and re-layouts  3.95 us (6%)
  between operations  0.7 us (1%)
    all_to_all x2, blocking collectives, on_device(): gathered = lax.all_to_all(sums, axis, 0, 0, tiled=True)  26.3 us
    ppermute x2, starting transfers between devices, exchange(): lax.ppermute(to_next, axis, ups)  7.93 us
    ppermute x2, waiting for transfers between devices, exchange(): lax.ppermute(to_last, axis, downs)  6.6 us
    pallas_call x1, Pallas kernels, on_device(): pl.pallas_call(functools.partial(steps_kernel, sizes), out_shape=(shape_o...  6.15 us
    ppermute x2, waiting for transfers between devices, exchange(): lax.ppermute(to_next, axis, ups)  5.08 us
    unnamed x16, local copies, waits for them, and re-layouts  3.94 us
    ppermute x2, starting transfers between devices, exchange(): lax.ppermute(to_last, axis, downs)  2.58 us
  transfers between devices with their start and end apart: 4, of which 3 were waited for; matrix products, arithmetic and copies ran while one was open for 0% of the time, Pallas kernels for 0%

profile of v2, /device:TPU:0, one launch (start us, length us, event | category | flops | bytes accessed | tf_op | source)
XLA Modules:
  0.0 61.4 jit_solution(4480141294862735999)
XLA Ops:
  0.6 0.0 copy-start
  0.6 0.9 %copy-done = f32[19,8,256]{2,1,0:T(8,128)S(1)} copy-done((f32[19,8,256]{2,1,0:T(8,128)S(1)}, f32[19,8,256]{2,1,0:T(8,128)}, u32[]{:S(2)}) %copy-start) | copy-done | bytes 155672
  1.5 0.0 copy-start.2
  1.5 0.9 %copy-done.2 = f32[19,8,256]{2,1,0:T(8,128)S(1)} copy-done((f32[19,8,256]{2,1,0:T(8,128)S(1)}, f32[19,8,256]{2,1,0:T(8,128)}, u32[]{:S(2)}) %copy-start.2) | copy-done | bytes 155672
  2.5 0.0 copy-start.4
  2.5 0.8 %copy-done.4 = s32[4,8,256]{2,1,0:T(8,128)S(1)} copy-done((s32[4,8,256]{2,1,0:T(8,128)S(1)}, s32[4,8,256]{2,1,0:T(8,128)}, u32[]{:S(2)}) %copy-start.4) | copy-done | bytes 32792
  3.2 0.0 copy-start.6
  3.2 0.7 %copy-done.6 = s32[8,256]{1,0:T(8,128)S(1)} copy-done((s32[8,256]{1,0:T(8,128)S(1)}, s32[8,256]{1,0:T(8,128)}, u32[]{:S(2)}) %copy-start.6) | copy-done | bytes 8216
  3.9 0.0 copy-start.7
  3.9 0.7 %copy-done.7 = f32[64]{0:T(128)S(1)} copy-done((f32[64]{0:T(128)S(1)}, f32[64]{0:T(128)}, u32[]{:S(2)}) %copy-start.7) | copy-done | bytes 280
  4.6 0.0 copy-start.3
  4.6 0.0 copy-start.5
  4.6 0.8 %pack_y.1 = (f32[53,8,128]{2,1,0:T(8,128)S(1)}, f32[53,8,128]{2,1,0:T(8,128)S(1)}, f32[38,8,128]{2,1,0:T(8,128)S(1)}) custom-call(f32[64]{0:T(128)S(1)} %copy-done.7, s32[8,256]{1,0:T(8,128)S(1)} %copy-done.6, f32[19,8,256]{2,1,0:T(8,128)S(1)} %copy-done, f32[19,8,256]{2,1,0:T(8,128)S(1)} %copy-done.2, s32[4,8,256]{2,1,0:T(8,128)S(1)} %copy-done.4), custom_call_target="tpu_custom_call" | custom-call | tf_op jit(solution)/shard_map/pack_y/pallas_call | solution.py:442
  5.4 4.9 %collective-permute-start = (f32[53,8,128]{2,1,0:T(8,128)S(1)}, f32[53,8,128]{2,1,0:T(8,128)S(1)}, u32[]{:S(2)}, u32[]{:S(2)}) collective-permute-start(f32[53,8,128]{2,1,0:T(8,128)S(1)} %get-tuple-element.8), channel_id=1, source_target_pairs={{0,1},{1,2},{2,3},{4,5},{5,6},{6,7},{8,9},{9,10},{10,11},{12,13},{... | collective-permute-start | bytes 651272 | tf_op jit(solution)/shard_map/ppermute | solution.py:458
  10.2 1.3 %collective-permute-start.1 = (f32[53,8,128]{2,1,0:T(8,128)S(1)}, f32[53,8,128]{2,1,0:T(8,128)S(1)}, u32[]{:S(2)}, u32[]{:S(2)}) collective-permute-start(f32[53,8,128]{2,1,0:T(8,128)S(1)} %get-tuple-element.9), channel_id=1, source_target_pairs={{1,0},{2,1},{3,2},{5,4},{6,5},{7,6},{9,8},{10,9},{11,10},{13,12},{... | collective-permute-start | bytes 651272 | tf_op jit(solution)/shard_map/ppermute | solution.py:458
  11.5 3.3 %collective-permute-done.left_ref = f32[53,8,128]{2,1,0:T(8,128)S(1)} collective-permute-done((f32[53,8,128]{2,1,0:T(8,128)S(1)}, f32[53,8,128]{2,1,0:T(8,128)S(1)}, u32[]{:S(2)}, u32[]{:S(2)}) %collective-permute-start) | collective-permute-done | bytes 217120 | tf_op jit(solution)/shard_map/ppermute | solution.py:458
  14.8 6.6 %collective-permute-done.1.right_ref = f32[53,8,128]{2,1,0:T(8,128)S(1)} collective-permute-done((f32[53,8,128]{2,1,0:T(8,128)S(1)}, f32[53,8,128]{2,1,0:T(8,128)S(1)}, u32[]{:S(2)}, u32[]{:S(2)}) %collective-permute-start.1) | collective-permute-done | bytes 217120 | tf_op jit(solution)/shard_map/ppermute | solution.py:458
  21.4 0.0 copy-done.3
  21.4 0.0 copy-done.5
  21.4 0.0 copy-start.1
  21.4 0.8 %pack_x.1.mid_ref = f32[189,8,128]{2,1,0:T(8,128)S(1)} custom-call(f32[64]{0:T(128)S(1)} %copy-done.7, s32[8,256]{1,0:T(8,128)S(1)} %copy-done.6, f32[38,8,128]{2,1,0:T(8,128)S(1)} %get-tuple-element.7.own_ref, f32[19,8,256]{2,1,0:T(8,128)S(1)} %copy-done.3, s32[4,8,256]{2,1,0:T(8,128)S(1)} %copy-done.5, f32[53,8,128]{2,1,0:T(8,128)S(1)} %collective-permute-done.left_ref, ...), custom_call_target="tpu_custom_call" | custom-call | tf_op jit(solution)/shard_map/pack_x/pallas_call | solution.py:461
  22.2 1.3 %collective-permute-start.3 = (f32[189,8,128]{2,1,0:T(8,128)S(1)}, f32[189,8,128]{2,1,0:T(8,128)S(1)}, u32[]{:S(2)}, u32[]{:S(2)}) collective-permute-start(f32[189,8,128]{2,1,0:T(8,128)S(1)} %pack_x.1.mid_ref), channel_id=1, source_target_pairs={{4,0},{8,4},{12,8},{16,12},{20,16},{24,20},{28,24},{5,1},{9,5},{13... | collective-permute-start | bytes 2322440 | tf_op jit(solution)/shard_map/ppermute | solution.py:458
  23.5 3.1 %collective-permute-start.2 = (f32[189,8,128]{2,1,0:T(8,128)S(1)}, f32[189,8,128]{2,1,0:T(8,128)S(1)}, u32[]{:S(2)}, u32[]{:S(2)}) collective-permute-start(f32[189,8,128]{2,1,0:T(8,128)S(1)} %pack_x.1.mid_ref), channel_id=1, source_target_pairs={{0,4},{4,8},{8,12},{12,16},{16,20},{20,24},{24,28},{1,5},{5,9},{9,... | collective-permute-start | bytes 2322440 | tf_op jit(solution)/shard_map/ppermute | solution.py:458
  26.5 0.0 collective-permute-done.3.above_ref
  26.6 1.8 %collective-permute-done.2.below_ref = f32[189,8,128]{2,1,0:T(8,128)S(1)} collective-permute-done((f32[189,8,128]{2,1,0:T(8,128)S(1)}, f32[189,8,128]{2,1,0:T(8,128)S(1)}, u32[]{:S(2)}, u32[]{:S(2)}) %collective-permute-start.2) | collective-permute-done | bytes 774176 | tf_op jit(solution)/shard_map/ppermute | solution.py:458
  28.4 0.0 copy-done.1
  28.4 6.1 %steps.1 = (f32[19,8,256]{2,1,0:T(8,128)}, f32[8,64]{1,0:T(8,128)S(1)}) custom-call(s32[8,256]{1,0:T(8,128)S(1)} %copy-done.6, f32[19,8,256]{2,1,0:T(8,128)S(1)} %copy-done.1, s32[4,8,256]{2,1,0:T(8,128)S(1)} %copy-done.5, f32[189,8,128]{2,1,0:T(8,128)S(1)} %collective-permute-done.2.below_ref, f32[189,8,128]{2,1,0:T(8,128)S(1)} %pack_x.1.mid_ref, ...), custom_call_target="tpu_custom_call" | custom-call | tf_op jit(solution)/shard_map/steps/pallas_call | solution.py:471
  34.5 19.1 %all_to_all.15 = f32[8,1,64]{2,1,0:T(1,128)S(1)} all-to-all(f32[8,1,64]{2,1,0:T(1,128)S(1)} %bitcast.4), channel_id=1, replica_groups=mesh['gx'=8,'gy'=4] {'gx'}, dimensions={0} | all-to-all | bytes 4096 | tf_op jit(solution)/shard_map/all_to_all | solution.py:490
  53.7 7.2 %all_to_all.16 = f32[4,1,64]{2,1,0:T(1,128)S(1)} all-to-all(f32[4,1,64]{2,1,0:T(1,128)S(1)} %broadcast_in_dim.4), channel_id=1, replica_groups=mesh['gx'=8,'gy'=4] {'gy'}, dimensions={0} | all-to-all | bytes 2048 | tf_op jit(solution)/shard_map/all_to_all | solution.py:490
  60.9 0.5 reduce_sum.19
  (2 shorter events, 0.0 us)
Async XLA Ops:
  0.6 0.9 %copy-start = (f32[19,8,256]{2,1,0:T(8,128)S(1)}, f32[19,8,256]{2,1,0:T(8,128)}, u32[]{:S(2)}) copy-start(f32[19,8,256]{2,1,0:T(8,128)} %f_ref.3) | copy-start | bytes 466948
  1.5 0.9 %copy-start.2 = (f32[19,8,256]{2,1,0:T(8,128)S(1)}, f32[19,8,256]{2,1,0:T(8,128)}, u32[]{:S(2)}) copy-start(f32[19,8,256]{2,1,0:T(8,128)} %cot_ref.3) | copy-start | bytes 466948
  2.5 0.8 %copy-start.4 = (s32[4,8,256]{2,1,0:T(8,128)S(1)}, s32[4,8,256]{2,1,0:T(8,128)}, u32[]{:S(2)}) copy-start(s32[4,8,256]{2,1,0:T(8,128)} %codes_ref.5) | copy-start | bytes 98308
  3.2 0.7 %copy-start.6 = (s32[8,256]{1,0:T(8,128)S(1)}, s32[8,256]{1,0:T(8,128)}, u32[]{:S(2)}) copy-start(s32[8,256]{1,0:T(8,128)} %panels_ref.5) | copy-start | bytes 24580
  3.9 0.7 %copy-start.7 = (f32[64]{0:T(128)S(1)}, f32[64]{0:T(128)}, u32[]{:S(2)}) copy-start(f32[64]{0:T(128)} %porosity_ref.3) | copy-start | bytes 772
  4.6 16.8 %copy-start.3 = (f32[19,8,256]{2,1,0:T(8,128)S(1)}, f32[19,8,256]{2,1,0:T(8,128)}, u32[]{:S(2)}) copy-start(f32[19,8,256]{2,1,0:T(8,128)} %cot_ref.3) | copy-start | bytes 466948
  4.6 16.8 %copy-start.5 = (s32[4,8,256]{2,1,0:T(8,128)S(1)}, s32[4,8,256]{2,1,0:T(8,128)}, u32[]{:S(2)}) copy-start(s32[4,8,256]{2,1,0:T(8,128)} %codes_ref.5) | copy-start | bytes 98308
  5.4 9.4 %collective-permute-start = (f32[53,8,128]{2,1,0:T(8,128)S(1)}, f32[53,8,128]{2,1,0:T(8,128)S(1)}, u32[]{:S(2)}, u32[]{:S(2)}) collective-permute-start(f32[53,8,128]{2,1,0:T(8,128)S(1)} %get-tuple-element.8), channel_id=1, source_target_pairs={{0,1},{1,2},{2,3},{4,5},{5,6},{6,7},{8,9},{9,10},{10,11},{12,13},{... | collective-permute-start | bytes 651272 | tf_op jit(solution)/shard_map/ppermute | solution.py:458
  10.2 11.2 %collective-permute-start.1 = (f32[53,8,128]{2,1,0:T(8,128)S(1)}, f32[53,8,128]{2,1,0:T(8,128)S(1)}, u32[]{:S(2)}, u32[]{:S(2)}) collective-permute-start(f32[53,8,128]{2,1,0:T(8,128)S(1)} %get-tuple-element.9), channel_id=1, source_target_pairs={{1,0},{2,1},{3,2},{5,4},{6,5},{7,6},{9,8},{10,9},{11,10},{13,12},{... | collective-permute-start | bytes 651272 | tf_op jit(solution)/shard_map/ppermute | solution.py:458
  21.4 7.0 %copy-start.1 = (f32[19,8,256]{2,1,0:T(8,128)S(1)}, f32[19,8,256]{2,1,0:T(8,128)}, u32[]{:S(2)}) copy-start(f32[19,8,256]{2,1,0:T(8,128)} %f_ref.3) | copy-start | bytes 466948
  22.2 4.4 %collective-permute-start.3 = (f32[189,8,128]{2,1,0:T(8,128)S(1)}, f32[189,8,128]{2,1,0:T(8,128)S(1)}, u32[]{:S(2)}, u32[]{:S(2)}) collective-permute-start(f32[189,8,128]{2,1,0:T(8,128)S(1)} %pack_x.1.mid_ref), channel_id=1, source_target_pairs={{4,0},{8,4},{12,8},{16,12},{20,16},{24,20},{28,24},{5,1},{9,5},{13... | collective-permute-start | bytes 2322440 | tf_op jit(solution)/shard_map/ppermute | solution.py:458
  23.5 4.9 %collective-permute-start.2 = (f32[189,8,128]{2,1,0:T(8,128)S(1)}, f32[189,8,128]{2,1,0:T(8,128)S(1)}, u32[]{:S(2)}, u32[]{:S(2)}) collective-permute-start(f32[189,8,128]{2,1,0:T(8,128)S(1)} %pack_x.1.mid_ref), channel_id=1, source_target_pairs={{0,4},{4,8},{8,12},{12,16},{16,20},{20,24},{24,28},{1,5},{5,9},{9,... | collective-permute-start | bytes 2322440 | tf_op jit(solution)/shard_map/ppermute | solution.py:458

commit v3 on v1

--- a/solution.py
+++ b/solution.py
@@ -42,15 +42,19 @@
 PAIRS = [(i, i + 1) for i in range(1, Q, 2)]
 W_REST, W_AXIS, W_DIAG = 1.0 / 3.0, 1.0 / 18.0, 1.0 / 36.0
 
-Y_COT, Y_CODE, Y_PHI, Y_HALF = 19, 38, 41, 42
-HALVES = Q + 2
-Y_TILES = Y_HALF + (HALVES + 1) // 2
-X_COT = 5 * Q
-X_CODE1 = X_COT + 4 * Q
-X_CODE2 = X_CODE1 + 5
-X_CODE3 = X_CODE2 + 4
-X_PHI = X_CODE3 + 4
-X_TILES = X_PHI + 5
+Y_CODE1, Y_CODE2, Y_CODE3, Y_POP, Y_COT = 38, 39, 40, 41, 42
+Y_TILES = 43
+X_EXTRA, X_CODE13, X_CODE2 = 19, 20, 21
+X_LANE = 22
+X_RING = 2 * X_LANE
+X_CORNER = X_RING + Q + 1
+F_CODE1, F_CODE2, F_CODE3, F_PHI = 0, 5, 9, 13
+FIELDS = 18
+OWN_PHI = 4
+
+
+def turned(axis, outward):
+    return [i for i, v in enumerate(VELOCITIES) if v[axis] == outward and sum(map(abs, v)) == 2]
 
 
 def total(values):
@@ -218,82 +222,295 @@
     return out
 
 
-def panel_field(porosity_ref, panels_ref, tile):
+def iotas():
     row = lax.broadcasted_iota(jnp.int32, (ROWS, LANES), 0)
-    upper = porosity_ref[panels_ref[0, tile * LANES]]
-    lower = porosity_ref[panels_ref[4, tile * LANES]]
-    return jnp.where(row < 4, upper, lower)
-
-
-def pack_y(porosity_ref, panels_ref, f_ref, cot_ref, codes_ref, up_ref, down_ref, own_ref):
     lane = lax.broadcasted_iota(jnp.int32, (ROWS, LANES), 1)
-    high = lane >= LANES // 2
-    for tile, out_ref in ((0, down_ref), (1, up_ref)):
-        lanes = pl.ds(tile * LANES, LANES)
-        phi = panel_field(porosity_ref, panels_ref, tile)
-        f = [f_ref[i, :, lanes] for i in range(Q)]
-        kinds = [codes_ref[s, :, lanes].astype(jnp.float32) for s in range(STEPS)]
+    return row, lane, lane // NZ, lane % NZ
+
+
+def columns(value, count):
+    amount = (count * NZ) % LANES
+    return pltpu.roll(value, amount, 1) if amount else value
+
+
+def lines(value, count):
+    amount = count % ROWS
+    return pltpu.roll(value, amount, 0) if amount else value
+
+
+def pack_y(
+    f_hbm,
+    cot_hbm,
+    codes_hbm,
+    panels_hbm,
+    porosity_hbm,
+    up_ref,
+    down_ref,
+    own_ref,
+    field_ref,
+    f_ref,
+    cot_ref,
+    codes_ref,
+    panels_ref,
+    porosity_ref,
+    sems,
+):
+    pieces = (
+        (panels_hbm, panels_ref),
+        (porosity_hbm, porosity_ref),
+        (f_hbm, f_ref),
+        (codes_hbm, codes_ref),
+        (cot_hbm, cot_ref),
+    )
+    copies = [
+        pltpu.make_async_copy(source, target, sems.at[n])
+        for n, (source, target) in enumerate(pieces)
+    ]
+    for copy in copies:
+        copy.start()
+    for copy in copies[:4]:
+        copy.wait()
+    row, lane, column, depth = iotas()
+    top = depth == NZ - 1
+
+    def tile_of(ref, i, t):
+        return ref[i, :, pl.ds(t * LANES, LANES)]
+
+    codes, phis = [], []
+    for t in range(2):
+        upper = porosity_ref[panels_ref[0, t * LANES]]
+        lower = porosity_ref[panels_ref[4, t * LANES]]
+        phi = jnp.where(row < 4, upper, lower)
+        kinds = [tile_of(codes_ref, s, t).astype(jnp.float32) for s in range(STEPS)]
+        f = [tile_of(f_ref, i, t) for i in range(Q)]
         g = collide(f, kinds[0], phi, moments(f))
         for i in range(Q):
-            own_ref[2 * i + tile] = g[i]
-            out_ref[i] = g[i]
-            out_ref[Y_COT + i] = cot_ref[i, :, lanes]
-        for s in range(1, STEPS):
-            out_ref[Y_CODE + s - 1] = kinds[s]
-        out_ref[Y_PHI] = phi
-        outer = g + [kinds[1], phi]
-        other_ref = down_ref if tile == 1 else up_ref
-        keep = high if tile == 0 else ~high
-        for n in range(0, HALVES, 2):
-            value = outer[n]
-            if n + 1 < HALVES:
-                value = jnp.where(keep, value, pltpu.roll(outer[n + 1], LANES // 2, 1))
-            other_ref[Y_HALF + n // 2] = value
-
-
-def pack_x(porosity_ref, panels_ref, own_ref, cot_ref, codes_ref, left_ref, right_ref, out_ref):
-    lane = lax.broadcasted_iota(jnp.int32, (ROWS, LANES), 1)
+            own_ref[2 * i + t] = g[i]
+        for s in range(STEPS):
+            field_ref[2 * s + t] = kinds[s]
+        field_ref[2 * OWN_PHI + t] = phi
+        codes.append([jnp.where(top, phi, kinds[1]), kinds[2], kinds[3]])
+    copies[4].wait()
+    for out_ref, way in ((up_ref, 1), (down_ref, -1)):
+        near, far = (1, 0) if way == 1 else (0, 1)
+        for i in range(Q):
+            deep = 3 - way * VELOCITIES[i][1]
+            cot = tile_of(cot_ref, i, near)
+            g_far = own_ref[2 * i + far]
+            if way == 1:
+                mixed = jnp.where(column >= deep, g_far, columns(cot, deep - 4))
+            else:
+                mixed = jnp.where(column < 4 - deep, g_far, columns(cot, 4 - deep))
+            out_ref[2 * i + near] = own_ref[2 * i + near]
+            out_ref[2 * i + far] = mixed
+        outer = 3 if way == 1 else 0
+        out_ref[Y_CODE1] = codes[near][0]
+        out_ref[Y_CODE2] = codes[near][1]
+        out_ref[Y_CODE3] = jnp.where(
+            column == 3 - outer, columns(codes[far][0], 3 - 2 * outer), codes[near][2]
+        )
+        extra = None
+        for k, i in enumerate(turned(1, -way)):
+            value = columns(own_ref[2 * i + far], k - outer)
+            extra = value if extra is None else jnp.where(column == k, value, extra)
+        out_ref[Y_POP] = extra
+        extra = None
+        for k, i in enumerate(turned(1, way)):
+            value = columns(tile_of(cot_ref, i, near), k - (1 if way == 1 else 2))
+            extra = value if extra is None else jnp.where(column == k, value, extra)
+        out_ref[Y_COT] = extra
+
+
+def from_y(left_ref, right_ref):
+    row, lane, column, depth = iotas()
     high = lane >= LANES // 2
 
-    def outer(n):
-        left, right = left_ref[Y_HALF + n // 2], right_ref[Y_HALF + n // 2]
-        if n % 2 == 0:
+    def population(i, c):
+        if c == 1:
+            return left_ref[2 * i + 1]
+        if c == 4:
+            return right_ref[2 * i]
+        along_y = VELOCITIES[i][1]
+        left, right = left_ref[2 * i], right_ref[2 * i + 1]
+        if along_y == 1 and i in turned(1, 1):
+            right = columns(right_ref[Y_POP], -turned(1, 1).index(i))
+        if along_y == -1 and i in turned(1, -1):
+            left = columns(left_ref[Y_POP], 3 - turned(1, -1).index(i))
+        return jnp.where(high, left, right)
+
+    def cotangent(i, c):
+        ref, way, place, far = (left_ref, 1, 1, 0) if c == 1 else (right_ref, -1, 2, 1)
+        deep = 3 - way * VELOCITIES[i][1]
+        value = columns(ref[2 * i + far], way * (4 - deep))
+        if i in turned(1, way):
+            extra = columns(ref[Y_COT], place - turned(1, way).index(i))
+            value = jnp.where(column == place, extra, value)
+        return value
+
+    def codes(s, c):
+        if c == 0:
+            left, right = columns(left_ref[Y_CODE3], 3), columns(right_ref[Y_CODE3], 1)
             return jnp.where(high, left, right)
-        return pltpu.roll(jnp.where(high, right, left), LANES // 2, 1)
+        return (left_ref if c == 1 else right_ref)[(Y_CODE1, Y_CODE2, Y_CODE3)[s - 1]]
+
+    return population, cotangent, codes
+
+
+def pack_lines(out_ref, first, way, population, cotangent, codes):
+    row, lane, column, depth = iotas()
+
+    def mixed(pop, cot, deep):
+        if way == 1:
+            return jnp.where(row >= deep, pop, lines(cot, deep))
+        return jnp.where(row < ROWS - deep, pop, lines(cot, -deep))
 
     for i in range(Q):
-        out_ref[5 * i] = outer(i)
-        out_ref[5 * i + 1] = left_ref[i]
-        out_ref[5 * i + 2] = own_ref[2 * i]
-        out_ref[5 * i + 3] = own_ref[2 * i + 1]
-        out_ref[5 * i + 4] = right_ref[i]
-        out_ref[X_COT + 4 * i] = left_ref[Y_COT + i]
-        out_ref[X_COT + 4 * i + 1] = cot_ref[i, :, pl.ds(0, LANES)]
-        out_ref[X_COT + 4 * i + 2] = cot_ref[i, :, pl.ds(LANES, LANES)]
-        out_ref[X_COT + 4 * i + 3] = right_ref[Y_COT + i]
-    out_ref[X_CODE1] = outer(Q)
-    for s, first in ((1, X_CODE1 + 1), (2, X_CODE2), (3, X_CODE3)):
-        out_ref[first] = left_ref[Y_CODE + s - 1]
-        for tile in range(2):
-            out_ref[first + 1 + tile] = codes_ref[s, :, pl.ds(tile * LANES, LANES)].astype(
-                jnp.float32
+        out_ref[first + i] = mixed(population(i), cotangent(i), 3 - way * VELOCITIES[i][0])
+    extra = None
+    for k, i in enumerate(turned(0, -way)):
+        value = lines(population(i), k - (3 if way == 1 else 4))
+        extra = value if extra is None else jnp.where(row == k, value, extra)
+    for k, i in enumerate(turned(0, way)):
+        value = lines(cotangent(i), 4 + k - (5 if way == 1 else 2))
+        extra = jnp.where(row == 4 + k, value, extra)
+    out_ref[first + X_EXTRA] = extra
+    out_ref[first + X_CODE13] = mixed(codes(1), codes(3), 3)
+    out_ref[first + X_CODE2] = codes(2)
+
+
+def from_x(ref, first, way):
+    row, lane, column, depth = iotas()
+
+    def population(i):
+        value = ref[first + i]
+        if i in turned(0, -way):
+            place = 3 if way == 1 else 4
+            extra = lines(ref[first + X_EXTRA], place - turned(0, -way).index(i))
+            value = jnp.where(row == place, extra, value)
+        return value
+
+    def cotangent(i):
+        value = lines(ref[first + i], -way * (3 - way * VELOCITIES[i][0]))
+        if i in turned(0, way):
+            place = 5 if way == 1 else 2
+            extra = lines(ref[first + X_EXTRA], place - 4 - turned(0, way).index(i))
+            value = jnp.where(row == place, extra, value)
+        return value
+
+    def codes(s):
+        if s == 2:
+            return ref[first + X_CODE2]
+        value = ref[first + X_CODE13]
+        return value if s == 1 else lines(value, -3 * way)
+
+    return population, cotangent, codes
+
+
+def pack_x(own_ref, cot_ref, field_ref, up_ref, down_ref):
+    row, lane, column, depth = iotas()
+    for t in range(2):
+
+        def codes(s):
+            value = field_ref[2 * s + t]
+            return jnp.where(depth == NZ - 1, field_ref[2 * OWN_PHI + t], value) if s == 1 else value
+
+        for out_ref, way in ((up_ref, 1), (down_ref, -1)):
+            pack_lines(
+                out_ref,
+                X_LANE * t,
+                way,
+                lambda i: own_ref[2 * i + t],
+                lambda i: cot_ref[i, :, pl.ds(t * LANES, LANES)],
+                codes,
             )
-        out_ref[first + 3] = right_ref[Y_CODE + s - 1]
-    out_ref[X_PHI] = outer(Q + 1)
-    out_ref[X_PHI + 1] = left_ref[Y_PHI]
-    for tile in range(2):
-        out_ref[X_PHI + 2 + tile] = panel_field(porosity_ref, panels_ref, tile)
-    out_ref[X_PHI + 4] = right_ref[Y_PHI]
+
+
+def pack_corner(left_ref, right_ref, up_ref, down_ref):
+    population, cotangent, codes = from_y(left_ref, right_ref)
+    for n, c in enumerate((1, 4)):
+        for out_ref, way in ((up_ref, 1), (down_ref, -1)):
+            pack_lines(
+                out_ref,
+                X_LANE * n,
+                way,
+                lambda i: population(i, c),
+                lambda i: cotangent(i, c),
+                lambda s: codes(s, c),
+            )
+    for n in range(Q + 1):
+        value = population(n, 0) if n < Q else codes(1, 0)
+        up_ref[X_RING + n] = value
+        down_ref[X_RING + n] = value
+
+
+def add_panels(parts_ref, out_ref):
+    out_ref[...] = jnp.sum(parts_ref[...], axis=0)
+
+
+def fill(
+    left_ref, right_ref, own_ref, field_ref, cot_ref, own_x, corner_x, pop, cot, field
+):
+    row, lane, column, depth = iotas()
+    top = depth == NZ - 1
+    from_left = from_y(left_ref, right_ref)
+
+    def put(c, r, population, cotangent, codes):
+        rows = pl.ds(ROWS * (r + 1), ROWS)
+        for i in range(Q):
+            pop[5 * i + c, rows, :] = population(i)
+            if c:
+                cot[4 * i + c - 1, rows, :] = cotangent(i)
+        code = codes(1)
+        phi = jnp.where(top, code, 0.0)
+        for step in (1, 2, 4, 8, 16):
+            phi = phi + pltpu.roll(phi, LANES - step, 1)
+        field[F_CODE1 + c, rows, :] = jnp.where(top, 0.0, code)
+        field[F_PHI + c, rows, :] = phi
+        if c:
+            field[F_CODE2 + c - 1, rows, :] = codes(2)
+            field[F_CODE3 + c - 1, rows, :] = codes(3)
+
+    for c in (0, 1, 4):
+        put(c, 1, *(functools.partial(lambda g, n: g(n, c), get) for get in from_left))
+    for t in range(2):
+        rows = pl.ds(2 * ROWS, ROWS)
+        for i in range(Q):
+            pop[5 * i + 2 + t, rows, :] = own_ref[2 * i + t]
+            cot[4 * i + 1 + t, rows, :] = cot_ref[i, :, pl.ds(t * LANES, LANES)]
+        field[F_CODE1 + 2 + t, rows, :] = field_ref[2 + t]
+        field[F_CODE2 + 1 + t, rows, :] = field_ref[4 + t]
+        field[F_CODE3 + 1 + t, rows, :] = field_ref[6 + t]
+        field[F_PHI + 2 + t, rows, :] = field_ref[2 * OWN_PHI + t]
+    for way, r, side_ref, corner_ref in (
+        (1, 0, own_x[0], corner_x[0]),
+        (-1, 2, own_x[1], corner_x[1]),
+    ):
+        for t in range(2):
+            put(2 + t, r, *from_x(side_ref, X_LANE * t, way))
+        for n, c in enumerate((1, 4)):
+            put(c, r, *from_x(corner_ref, X_LANE * n, way))
+        put(
+            0,
+            r,
+            lambda i: corner_ref[X_RING + i],
+            None,
+            lambda s: corner_ref[X_RING + Q],
+        )
 
 
 def steps_kernel(
     sizes,
-    panels_ref,
+    panels_hbm,
     f_ref,
-    codes_ref,
+    cot_ref,
+    own_ref,
+    own_field_ref,
+    left_ref,
+    right_ref,
     below_ref,
-    mid_ref,
     above_ref,
+    below_corner_ref,
+    above_corner_ref,
     adjoint_ref,
     panel_ref,
     pop_a,
@@ -303,26 +520,24 @@
     saved,
     mom,
     grad,
-    sems,
+    panels_ref,
+    sem,
 ):
     size_x, size_y = sizes
-    copies = []
-    for n, source in enumerate((below_ref, mid_ref, above_ref)):
-        rows = pl.ds(ROWS * (n + 1), ROWS)
-        for m, (target, first, count) in enumerate(
-            (
-                (pop_a, 0, X_COT),
-                (cot, X_COT, X_CODE1 - X_COT),
-                (field, X_CODE1, X_TILES - X_CODE1),
-            )
-        ):
-            copy = pltpu.make_async_copy(
-                source.at[pl.ds(first, count)], target.at[:, rows, :], sems.at[n, m]
-            )
-            copy.start()
-            copies.append(copy)
-    for copy in copies:
-        copy.wait()
+    names = pltpu.make_async_copy(panels_hbm, panels_ref, sem)
+    names.start()
+    fill(
+        left_ref,
+        right_ref,
+        own_ref,
+        own_field_ref,
+        cot_ref,
+        (below_ref, above_ref),
+        (below_corner_ref, above_corner_ref),
+        pop_a,
+        cot,
+        field,
+    )
 
     at_x, at_y = lax.axis_index("gx"), lax.axis_index("gy")
     edges = (
@@ -362,9 +577,9 @@
                         saved[s - 1, i, place] = f[i]
                 if target is not None:
                     at = tile if tiles == 5 else tile + 1
-                    first = (X_CODE1 if s == 1 else X_CODE2 - 1) - X_CODE1
+                    first = F_CODE1 if s == 1 else F_CODE2 - 1
                     kind = field[first + at, rows_of(r), :]
-                    phi = field[X_PHI - X_CODE1 + at, rows_of(r), :]
+                    phi = field[F_PHI + at, rows_of(r), :]
                     g = collide(f, kind, phi, parts)
                     for i in range(Q):
                         target[target_tiles * i + ring, rows_of(r), :] = g[i]
@@ -386,9 +601,9 @@
                 rho, rinv, *u = [
                     mom[s - 1, n, tile, pl.ds(ROWS * r, ROWS), :] for n in range(5)
                 ]
-                first = (X_CODE1 + 1, X_CODE2, X_CODE3)[s - 1] - X_CODE1
+                first = (F_CODE1 + 1, F_CODE2, F_CODE3)[s - 1]
                 kind = field[first + tile, rows_of(r), :]
-                phi = field[X_PHI + 1 - X_CODE1 + tile, rows_of(r), :]
+                phi = field[F_PHI + 1 + tile, rows_of(r), :]
                 state = [saved[s - 1, i, tile] for i in range(Q)] if r == 1 else None
                 back, term = collide_back(b, kind, phi, rho, rinv, u, state)
                 for i in range(Q):
@@ -403,6 +618,7 @@
     backward(pop_a, 2, pop_b)
     backward(pop_b, 1, pop_a)
 
+    names.wait()
     row = lax.broadcasted_iota(jnp.int32, (ROWS, LANES), 0)
     panel = lax.broadcasted_iota(jnp.int32, panel_ref.shape, 1)
     sums = jnp.zeros(panel_ref.shape, jnp.float32)
@@ -410,8 +626,8 @@
         lanes = pl.ds(tile * LANES, LANES)
         b = streamed(pop_a, tile + 1, 4, 1, -1, masks_of(tile, 0, 1), None)
         f = [f_ref[i, :, lanes] for i in range(Q)]
-        kind = codes_ref[0, :, lanes].astype(jnp.float32)
-        phi = field[X_PHI + 2 - X_CODE1 + tile, rows_of(1), :]
+        kind = own_field_ref[tile]
+        phi = own_field_ref[2 * OWN_PHI + tile]
         _, _, rho, rinv, u = moments(f)
         back, term = collide_back(b, kind, phi, rho, rinv, u, f)
         for i in range(Q):
@@ -426,69 +642,96 @@
 
 
 VMEM = pl.BlockSpec(memory_space=pltpu.VMEM)
-SMEM = pl.BlockSpec(memory_space=pltpu.SMEM)
-ANY = pl.BlockSpec(memory_space=pl.ANY)
+HBM = pl.BlockSpec(memory_space=pltpu.HBM)
 
 
 def shape_of(*dims):
     return jax.ShapeDtypeStruct(dims, jnp.float32)
+
+
+def tiles_of(count):
+    return shape_of(count, ROWS, LANES)
 
 
 def on_device(sizes, checkpoint, cotangent, cell_codes, porosity, baffle_index):
     size_x, size_y = sizes
     panels = porosity.shape[0]
     devices = size_x * size_y
-    params = pltpu.CompilerParams(vmem_limit_bytes=32 * 1024 * 1024)
-
-    up, down, own = pl.pallas_call(
-        pack_y,
-        out_shape=(
-            shape_of(Y_TILES, ROWS, LANES),
-            shape_of(Y_TILES, ROWS, LANES),
-            shape_of(2 * Q, ROWS, LANES),
-        ),
-        in_specs=[SMEM, SMEM, VMEM, VMEM, VMEM],
-        out_specs=(VMEM, VMEM, VMEM),
-        compiler_params=params,
-        name="pack_y",
-    )(porosity, baffle_index, checkpoint, cotangent, cell_codes)
+
+    def call(kernel, out_shape, in_specs, scratch=(), name=None):
+        return pl.pallas_call(
+            kernel,
+            out_shape=out_shape,
+            in_specs=in_specs,
+            out_specs=jax.tree.map(lambda _: VMEM, out_shape),
+            scratch_shapes=scratch,
+            compiler_params=pltpu.CompilerParams(vmem_limit_bytes=32 * 1024 * 1024),
+            name=name,
+        )
 
     def exchange(to_next, to_last, axis, size):
         ups = [(i, i + 1) for i in range(size - 1)]
         downs = [(i + 1, i) for i in range(size - 1)]
         return lax.ppermute(to_next, axis, ups), lax.ppermute(to_last, axis, downs)
 
+    up, down, own, field = call(
+        pack_y,
+        (tiles_of(Y_TILES), tiles_of(Y_TILES), tiles_of(2 * Q), tiles_of(2 * OWN_PHI + 2)),
+        [HBM] * 5,
+        [
+            pltpu.VMEM((Q, ROWS, 2 * LANES), jnp.float32),
+            pltpu.VMEM((Q, ROWS, 2 * LANES), jnp.float32),
+            pltpu.VMEM((STEPS, ROWS, 2 * LANES), jnp.int32),
+            pltpu.SMEM(baffle_index.shape, jnp.int32),
+            pltpu.SMEM(porosity.shape, jnp.float32),
+            pltpu.SemaphoreType.DMA((5,)),
+        ],
+        name="pack_y",
+    )(checkpoint, cotangent, cell_codes, baffle_index, porosity)
     left, right = exchange(up, down, "gy", size_y)
-    ext = pl.pallas_call(
-        pack_x,
-        out_shape=shape_of(X_TILES, ROWS, LANES),
-        in_specs=[SMEM, SMEM, VMEM, VMEM, VMEM, VMEM, VMEM],
-        out_specs=VMEM,
-        compiler_params=params,
-        name="pack_x",
-    )(porosity, baffle_index, own, cotangent, cell_codes, left, right)
-    below, above = exchange(ext, ext, "gx", size_x)
-
-    adjoint, sums = pl.pallas_call(
+    side_up, side_down = call(
+        pack_x, (tiles_of(2 * X_LANE), tiles_of(2 * X_LANE)), [VMEM] * 3, name="pack_x"
+    )(own, cotangent, field)
+    below, above = exchange(side_up, side_down, "gx", size_x)
+    corner_up, corner_down = call(
+        pack_corner, (tiles_of(X_CORNER), tiles_of(X_CORNER)), [VMEM] * 2, name="pack_corner"
+    )(left, right)
+    below_corner, above_corner = exchange(corner_up, corner_down, "gx", size_x)
+
+    adjoint, sums = call(
         functools.partial(steps_kernel, sizes),
-        out_shape=(shape_of(Q, ROWS, 2 * LANES), shape_of(devices, panels)),
-        in_specs=[SMEM, VMEM, VMEM, ANY, ANY, ANY],
-        out_specs=(VMEM, VMEM),
-        scratch_shapes=[
+        (shape_of(Q, ROWS, 2 * LANES), shape_of(devices, panels)),
+        [HBM] + [VMEM] * 10,
+        [
             pltpu.VMEM((5 * Q, 5 * ROWS, LANES), jnp.float32),
             pltpu.VMEM((5 * Q, 5 * ROWS, LANES), jnp.float32),
             pltpu.VMEM((4 * Q, 5 * ROWS, LANES), jnp.float32),
-            pltpu.VMEM((X_TILES - X_CODE1, 5 * ROWS, LANES), jnp.float32),
+            pltpu.VMEM((FIELDS, 5 * ROWS, LANES), jnp.float32),
             pltpu.VMEM((3, Q, 5, ROWS, LANES), jnp.float32),
             pltpu.VMEM((3, 5, 5, 3 * ROWS, LANES), jnp.float32),
             pltpu.VMEM((4, ROWS, LANES), jnp.float32),
-            pltpu.SemaphoreType.DMA((3, 3)),
+            pltpu.SMEM(baffle_index.shape, jnp.int32),
+            pltpu.SemaphoreType.DMA,
         ],
-        compiler_params=params,
         name="steps",
-    )(baffle_index, checkpoint, cell_codes, below, ext, above)
+    )(
+        baffle_index,
+        checkpoint,
+        cotangent,
+        own,
+        field,
+        left,
+        right,
+        below,
+        above,
+        below_corner,
+        above_corner,
+    )
     gathered = lax.all_to_all(sums, ("gx", "gy"), 0, 0, tiled=True)
-    return adjoint, jnp.sum(gathered, axis=0)
+    totals = call(add_panels, shape_of(1, panels), [VMEM], name="add_panels")(
+        gathered.reshape(devices, 1, panels)
+    )
+    return adjoint, totals.reshape(panels)
 
 
 def solution(mesh):

time: 56.2 us -> 53.1 us (0.945)
  blocking collectives: 20.8 us -> 14.5 us
  starting transfers between devices: 10.5 us -> 15 us
    all_to_all x1, blocking collectives: 20.8 us -> 14.5 us  [on_device(): gathered = lax.all_to_all(sums, ('gx', 'gy'), 0, 0, tiled=True)]
    ppermute x2 -> x3, starting transfers between devices: 7.93 us -> 11 us  [exchange(): lax.ppermute(to_next, axis, ups)]
    ppermute x2 -> x3, waiting for transfers between devices: 5.08 us -> 2.25 us  [exchange(): lax.ppermute(to_next, axis, ups)]
    ppermute x2 -> x3, waiting for transfers between devices: 6.6 us -> 8.95 us  [exchange(): lax.ppermute(to_last, axis, downs)]
    ppermute x2 -> x3, starting transfers between devices: 2.58 us -> 4.01 us  [exchange(): lax.ppermute(to_last, axis, downs)]
    pallas_call x3 -> x5, Pallas kernels: 7.69 us -> 7.35 us  [the longest x1 5.69 us: on_device(): call(functools.partial(steps_kernel, sizes), (shape_of(Q, ROWS, 2 * LANES...]
    unnamed x16 -> x12, local copies, waits for them, and re-layouts: 3.94 us -> 3.93 us
  transfers between devices with their start and end apart: 4 -> 6, of which waited for: 3 -> 3; matrix products, arithmetic and copies ran while one was open for 0% -> 0% of each run, Pallas kernels for 0% -> 0%
where the time goes in v3:
time: 53.1 us; the launch traced here: 52.7 us
  starting transfers between devices  15 us (28%)
  blocking collectives  14.5 us (27%)
  waiting for transfers between devices  11.2 us (21%)
  Pallas kernels  7.35 us (14%)
  local copies, waits for them, and re-layouts  3.93 us (7%)
  between operations  0.75 us (1%)
    all_to_all x1, blocking collectives, on_device(): gathered = lax.all_to_all(sums, ('gx', 'gy'), 0, 0, tiled=True)  14.5 us
    ppermute x3, starting transfers between devices, exchange(): lax.ppermute(to_next, axis, ups)  11 us
    ppermute x3, waiting for transfers between devices, exchange(): lax.ppermute(to_last, axis, downs)  8.95 us
    pallas_call x1, Pallas kernels, on_device(): call(functools.partial(steps_kernel, sizes), (shape_of(Q, ROWS, 2 * LANES...  5.69 us
    ppermute x3, starting transfers between devices, exchange(): lax.ppermute(to_last, axis, downs)  4.01 us
    unnamed x12, local copies, waits for them, and re-layouts  3.93 us
    ppermute x3, waiting for transfers between devices, exchange(): lax.ppermute(to_next, axis, ups)  2.25 us
  transfers between devices with their start and end apart: 6, of which 3 were waited for; matrix products, arithmetic and copies ran while one was open for 0% of the time, Pallas kernels for 0%

profile of v3, /device:TPU:0, one launch (start us, length us, event | category | flops | bytes accessed | tf_op | source)
XLA Modules:
  0.0 52.7 jit_solution(5851247948269308901)
XLA Ops:
  0.6 0.0 copy-start
  0.6 0.9 %copy-done = f32[19,8,256]{2,1,0:T(8,128)S(1)} copy-done((f32[19,8,256]{2,1,0:T(8,128)S(1)}, f32[19,8,256]{2,1,0:T(8,128)}, u32[]{:S(2)}) %copy-start) | copy-done | bytes 155672
  1.5 0.0 copy-start.2
  1.5 0.9 %copy-done.2 = f32[19,8,256]{2,1,0:T(8,128)S(1)} copy-done((f32[19,8,256]{2,1,0:T(8,128)S(1)}, f32[19,8,256]{2,1,0:T(8,128)}, u32[]{:S(2)}) %copy-start.2) | copy-done | bytes 155672
  2.5 0.0 copy-start.3
  2.5 0.7 %copy-done.3 = s32[8,256]{1,0:T(8,128)S(1)} copy-done((s32[8,256]{1,0:T(8,128)S(1)}, s32[8,256]{1,0:T(8,128)}, u32[]{:S(2)}) %copy-start.3) | copy-done | bytes 8216
  3.2 0.0 copy-start.4
  3.2 0.8 %copy-done.4 = s32[4,8,256]{2,1,0:T(8,128)S(1)} copy-done((s32[4,8,256]{2,1,0:T(8,128)S(1)}, s32[4,8,256]{2,1,0:T(8,128)}, u32[]{:S(2)}) %copy-start.4) | copy-done | bytes 32792
  3.9 0.0 copy-start.5
  3.9 0.7 %copy-done.5 = f32[64]{0:T(128)S(1)} copy-done((f32[64]{0:T(128)S(1)}, f32[64]{0:T(128)}, u32[]{:S(2)}) %copy-start.5) | copy-done | bytes 280
  4.6 0.9 %pack_y.1 = (f32[43,8,128]{2,1,0:T(8,128)S(1)}, f32[43,8,128]{2,1,0:T(8,128)S(1)}, f32[38,8,128]{2,1,0:T(8,128)S(1)}, f32[10,8,128]{2,1,0:T(8,128)S(1)}) custom-call(f32[19,8,256]{2,1,0:T(8,128)S(1)} %copy-done.2, f32[19,8,256]{2,1,0:T(8,128)S(1)} %copy-done, s32[4,8,256]{2,1,0:T(8,128)S(1)} %copy-done.4, s32[8,256]{1,0:T(8,128)S(1)} %copy-done.3, ...), custom_call_target="tpu_custom_call" | custom-call | tf_op jit(solution)/shard_map/pack_y/pallas_call | solution.py:677
  5.5 4.9 %collective-permute-start = (f32[43,8,128]{2,1,0:T(8,128)S(1)}, f32[43,8,128]{2,1,0:T(8,128)S(1)}, u32[]{:S(2)}, u32[]{:S(2)}) collective-permute-start(f32[43,8,128]{2,1,0:T(8,128)S(1)} %get-tuple-element.14), channel_id=1, source_target_pairs={{0,1},{1,2},{2,3},{4,5},{5,6},{6,7},{8,9},{9,10},{10,11},{12,13},{... | collective-permute-start | bytes 528392 | tf_op jit(solution)/shard_map/ppermute | solution.py:675
  10.3 0.0 copy-start.1
  10.4 1.4 %collective-permute-start.1 = (f32[43,8,128]{2,1,0:T(8,128)S(1)}, f32[43,8,128]{2,1,0:T(8,128)S(1)}, u32[]{:S(2)}, u32[]{:S(2)}) collective-permute-start(f32[43,8,128]{2,1,0:T(8,128)S(1)} %get-tuple-element.15), channel_id=1, source_target_pairs={{1,0},{2,1},{3,2},{5,4},{6,5},{7,6},{9,8},{10,9},{11,10},{13,12},{... | collective-permute-start | bytes 528392 | tf_op jit(solution)/shard_map/ppermute | solution.py:675
  11.8 2.2 %collective-permute-done.left_ref = f32[43,8,128]{2,1,0:T(8,128)S(1)} collective-permute-done((f32[43,8,128]{2,1,0:T(8,128)S(1)}, f32[43,8,128]{2,1,0:T(8,128)S(1)}, u32[]{:S(2)}, u32[]{:S(2)}) %collective-permute-start) | collective-permute-done | bytes 176160 | tf_op jit(solution)/shard_map/ppermute | solution.py:675
  14.0 5.7 %collective-permute-done.1.right_ref = f32[43,8,128]{2,1,0:T(8,128)S(1)} collective-permute-done((f32[43,8,128]{2,1,0:T(8,128)S(1)}, f32[43,8,128]{2,1,0:T(8,128)S(1)}, u32[]{:S(2)}, u32[]{:S(2)}) %collective-permute-start.1) | collective-permute-done | bytes 176160 | tf_op jit(solution)/shard_map/ppermute | solution.py:675
  19.8 0.2 pack_corner.1
  19.9 1.3 %collective-permute-start.4 = (f32[64,8,128]{2,1,0:T(8,128)S(1)}, f32[64,8,128]{2,1,0:T(8,128)S(1)}, u32[]{:S(2)}, u32[]{:S(2)}) collective-permute-start(f32[64,8,128]{2,1,0:T(8,128)S(1)} %get-tuple-element.18), channel_id=1, source_target_pairs={{0,4},{4,8},{8,12},{12,16},{16,20},{20,24},{24,28},{1,5},{5,9},{9,... | collective-permute-start | bytes 786440 | tf_op jit(solution)/shard_map/ppermute | solution.py:675
  21.2 1.3 %collective-permute-start.5 = (f32[64,8,128]{2,1,0:T(8,128)S(1)}, f32[64,8,128]{2,1,0:T(8,128)S(1)}, u32[]{:S(2)}, u32[]{:S(2)}) collective-permute-start(f32[64,8,128]{2,1,0:T(8,128)S(1)} %get-tuple-element.19), channel_id=1, source_target_pairs={{4,0},{8,4},{12,8},{16,12},{20,16},{24,20},{28,24},{5,1},{9,5},{13... | collective-permute-start | bytes 786440 | tf_op jit(solution)/shard_map/ppermute | solution.py:675
  22.5 0.0 copy-done.1
  22.6 4.8 %collective-permute-start.2 = (f32[44,8,128]{2,1,0:T(8,128)S(1)}, f32[44,8,128]{2,1,0:T(8,128)S(1)}, u32[]{:S(2)}, u32[]{:S(2)}) collective-permute-start(f32[44,8,128]{2,1,0:T(8,128)S(1)} %get-tuple-element.16), channel_id=1, source_target_pairs={{0,4},{4,8},{8,12},{12,16},{16,20},{20,24},{24,28},{1,5},{5,9},{9,... | collective-permute-start | bytes 540680 | tf_op jit(solution)/shard_map/ppermute | solution.py:675
  27.4 1.3 %collective-permute-start.3 = (f32[44,8,128]{2,1,0:T(8,128)S(1)}, f32[44,8,128]{2,1,0:T(8,128)S(1)}, u32[]{:S(2)}, u32[]{:S(2)}) collective-permute-start(f32[44,8,128]{2,1,0:T(8,128)S(1)} %get-tuple-element.17), channel_id=1, source_target_pairs={{4,0},{8,4},{12,8},{16,12},{20,16},{24,20},{28,24},{5,1},{9,5},{13... | collective-permute-start | bytes 540680 | tf_op jit(solution)/shard_map/ppermute | solution.py:675
  28.7 0.0 collective-permute-done.2.below_ref
  28.8 3.2 %collective-permute-done.3.above_ref = f32[44,8,128]{2,1,0:T(8,128)S(1)} collective-permute-done((f32[44,8,128]{2,1,0:T(8,128)S(1)}, f32[44,8,128]{2,1,0:T(8,128)S(1)}, u32[]{:S(2)}, u32[]{:S(2)}) %collective-permute-start.3) | collective-permute-done | bytes 180256 | tf_op jit(solution)/shard_map/ppermute | solution.py:675
  32.0 0.0 collective-permute-done.4.below_corner_ref
  32.0 0.0 collective-permute-done.5.above_corner_ref
  32.0 5.7 %steps.1 = (f32[19,8,256]{2,1,0:T(8,128)}, f32[32,64]{1,0:T(8,128)S(1)}) custom-call(s32[8,256]{1,0:T(8,128)S(1)} %copy-done.3, f32[19,8,256]{2,1,0:T(8,128)S(1)} %copy-done.2, f32[19,8,256]{2,1,0:T(8,128)S(1)} %copy-done.1, f32[38,8,128]{2,1,0:T(8,128)S(1)} %get-tuple-element.12.own_ref, f32[10,8,128]{2,1,0:T(8,128)S(1)} %get-tuple-element.13.field_ref.own_field_ref, ...), custom_call_target="tpu_custom_call" | custom-call | tf_op jit(solution)/shard_map/steps/pallas_call | solution.py:701
  37.7 14.5 %all_to_all.9.parts_ref = f32[32,1,64]{2,1,0:T(1,128)S(1)} all-to-all(f32[32,1,64]{2,1,0:T(1,128)S(1)} %bitcast.2), channel_id=1, replica_groups=mesh['gx'=8,'gy'=4] {'gx','gy'}, dimensions={0} | all-to-all | bytes 16384 | tf_op jit(solution)/shard_map/all_to_all | solution.py:730
  52.2 0.5 %add_panels.1 = f32[1,64]{1,0:T(1,128)} custom-call(f32[32,1,64]{2,1,0:T(1,128)S(1)} %all_to_all.9.parts_ref), custom_call_target="tpu_custom_call" | custom-call | tf_op jit(solution)/shard_map/add_panels/pallas_call | solution.py:731
  (1 shorter events, 0.0 us)
Async XLA Ops:
  0.6 0.9 %copy-start = (f32[19,8,256]{2,1,0:T(8,128)S(1)}, f32[19,8,256]{2,1,0:T(8,128)}, u32[]{:S(2)}) copy-start(f32[19,8,256]{2,1,0:T(8,128)} %cot_ref.3) | copy-start | bytes 466948
  1.5 0.9 %copy-start.2 = (f32[19,8,256]{2,1,0:T(8,128)S(1)}, f32[19,8,256]{2,1,0:T(8,128)}, u32[]{:S(2)}) copy-start(f32[19,8,256]{2,1,0:T(8,128)} %f_ref.1) | copy-start | bytes 466948
  2.5 0.7 %copy-start.3 = (s32[8,256]{1,0:T(8,128)S(1)}, s32[8,256]{1,0:T(8,128)}, u32[]{:S(2)}) copy-start(s32[8,256]{1,0:T(8,128)} %panels_hbm.3) | copy-start | bytes 24580
  3.2 0.8 %copy-start.4 = (s32[4,8,256]{2,1,0:T(8,128)S(1)}, s32[4,8,256]{2,1,0:T(8,128)}, u32[]{:S(2)}) copy-start(s32[4,8,256]{2,1,0:T(8,128)} %codes_hbm.1) | copy-start | bytes 98308
  3.9 0.7 %copy-start.5 = (f32[64]{0:T(128)S(1)}, f32[64]{0:T(128)}, u32[]{:S(2)}) copy-start(f32[64]{0:T(128)} %porosity_hbm.1) | copy-start | bytes 772
  5.5 8.6 %collective-permute-start = (f32[43,8,128]{2,1,0:T(8,128)S(1)}, f32[43,8,128]{2,1,0:T(8,128)S(1)}, u32[]{:S(2)}, u32[]{:S(2)}) collective-permute-start(f32[43,8,128]{2,1,0:T(8,128)S(1)} %get-tuple-element.14), channel_id=1, source_target_pairs={{0,1},{1,2},{2,3},{4,5},{5,6},{6,7},{8,9},{9,10},{10,11},{12,13},{... | collective-permute-start | bytes 528392 | tf_op jit(solution)/shard_map/ppermute | solution.py:675
  10.3 12.2 %copy-start.1 = (f32[19,8,256]{2,1,0:T(8,128)S(1)}, f32[19,8,256]{2,1,0:T(8,128)}, u32[]{:S(2)}) copy-start(f32[19,8,256]{2,1,0:T(8,128)} %cot_ref.3) | copy-start | bytes 466948
  10.4 9.4 %collective-permute-start.1 = (f32[43,8,128]{2,1,0:T(8,128)S(1)}, f32[43,8,128]{2,1,0:T(8,128)S(1)}, u32[]{:S(2)}, u32[]{:S(2)}) collective-permute-start(f32[43,8,128]{2,1,0:T(8,128)S(1)} %get-tuple-element.15), channel_id=1, source_target_pairs={{1,0},{2,1},{3,2},{5,4},{6,5},{7,6},{9,8},{10,9},{11,10},{13,12},{... | collective-permute-start | bytes 528392 | tf_op jit(solution)/shard_map/ppermute | solution.py:675
  19.9 12.1 %collective-permute-start.4 = (f32[64,8,128]{2,1,0:T(8,128)S(1)}, f32[64,8,128]{2,1,0:T(8,128)S(1)}, u32[]{:S(2)}, u32[]{:S(2)}) collective-permute-start(f32[64,8,128]{2,1,0:T(8,128)S(1)} %get-tuple-element.18), channel_id=1, source_target_pairs={{0,4},{4,8},{8,12},{12,16},{16,20},{20,24},{24,28},{1,5},{5,9},{9,... | collective-permute-start | bytes 786440 | tf_op jit(solution)/shard_map/ppermute | solution.py:675
  21.2 10.7 %collective-permute-start.5 = (f32[64,8,128]{2,1,0:T(8,128)S(1)}, f32[64,8,128]{2,1,0:T(8,128)S(1)}, u32[]{:S(2)}, u32[]{:S(2)}) collective-permute-start(f32[64,8,128]{2,1,0:T(8,128)S(1)} %get-tuple-element.19), channel_id=1, source_target_pairs={{4,0},{8,4},{12,8},{16,12},{20,16},{24,20},{28,24},{5,1},{9,5},{13... | collective-permute-start | bytes 786440 | tf_op jit(solution)/shard_map/ppermute | solution.py:675
  22.6 6.1 %collective-permute-start.2 = (f32[44,8,128]{2,1,0:T(8,128)S(1)}, f32[44,8,128]{2,1,0:T(8,128)S(1)}, u32[]{:S(2)}, u32[]{:S(2)}) collective-permute-start(f32[44,8,128]{2,1,0:T(8,128)S(1)} %get-tuple-element.16), channel_id=1, source_target_pairs={{0,4},{4,8},{8,12},{12,16},{16,20},{20,24},{24,28},{1,5},{5,9},{9,... | collective-permute-start | bytes 540680 | tf_op jit(solution)/shard_map/ppermute | solution.py:675
  27.4 4.5 %collective-permute-start.3 = (f32[44,8,128]{2,1,0:T(8,128)S(1)}, f32[44,8,128]{2,1,0:T(8,128)S(1)}, u32[]{:S(2)}, u32[]{:S(2)}) collective-permute-start(f32[44,8,128]{2,1,0:T(8,128)S(1)} %get-tuple-element.17), channel_id=1, source_target_pairs={{4,0},{8,4},{12,8},{16,12},{20,16},{24,20},{28,24},{5,1},{9,5},{13... | collective-permute-start | bytes 540680 | tf_op jit(solution)/shard_map/ppermute | solution.py:675

commit v4 on v3

--- a/solution.py
+++ b/solution.py
@@ -47,7 +47,9 @@
 X_EXTRA, X_CODE13, X_CODE2 = 19, 20, 21
 X_LANE = 22
 X_RING = 2 * X_LANE
-X_CORNER = X_RING + Q + 1
+X_OWN2 = X_RING + Q + 1
+X_CORNER = X_OWN2 + 1
+X_SIDE = X_LANE - 1
 F_CODE1, F_CODE2, F_CODE3, F_PHI = 0, 5, 9, 13
 FIELDS = 18
 OWN_PHI = 4
@@ -238,7 +240,7 @@
     return pltpu.roll(value, amount, 0) if amount else value
 
 
-def pack_y(
+def pack_own(
     f_hbm,
     cot_hbm,
     codes_hbm,
@@ -246,6 +248,8 @@
     porosity_hbm,
     up_ref,
     down_ref,
+    side_up_ref,
+    side_down_ref,
     own_ref,
     field_ref,
     f_ref,
@@ -319,6 +323,16 @@
             value = columns(tile_of(cot_ref, i, near), k - (1 if way == 1 else 2))
             extra = value if extra is None else jnp.where(column == k, value, extra)
         out_ref[Y_COT] = extra
+    for t in range(2):
+        for out_ref, way in ((side_up_ref, 1), (side_down_ref, -1)):
+            pack_lines(
+                out_ref,
+                X_SIDE * t,
+                way,
+                lambda i: own_ref[2 * i + t],
+                lambda i: tile_of(cot_ref, i, t),
+                lambda s: codes[t][s - 1],
+            )
 
 
 def from_y(left_ref, right_ref):
@@ -375,10 +389,9 @@
         extra = jnp.where(row == 4 + k, value, extra)
     out_ref[first + X_EXTRA] = extra
     out_ref[first + X_CODE13] = mixed(codes(1), codes(3), 3)
-    out_ref[first + X_CODE2] = codes(2)
-
-
-def from_x(ref, first, way):
+
+
+def from_x(ref, first, way, second):
     row, lane, column, depth = iotas()
 
     def population(i):
@@ -399,33 +412,15 @@
 
     def codes(s):
         if s == 2:
-            return ref[first + X_CODE2]
+            return second
         value = ref[first + X_CODE13]
         return value if s == 1 else lines(value, -3 * way)
 
     return population, cotangent, codes
 
 
-def pack_x(own_ref, cot_ref, field_ref, up_ref, down_ref):
+def pack_corner(left_ref, right_ref, field_ref, below_ref, above_ref, up_ref, down_ref):
     row, lane, column, depth = iotas()
-    for t in range(2):
-
-        def codes(s):
-            value = field_ref[2 * s + t]
-            return jnp.where(depth == NZ - 1, field_ref[2 * OWN_PHI + t], value) if s == 1 else value
-
-        for out_ref, way in ((up_ref, 1), (down_ref, -1)):
-            pack_lines(
-                out_ref,
-                X_LANE * t,
-                way,
-                lambda i: own_ref[2 * i + t],
-                lambda i: cot_ref[i, :, pl.ds(t * LANES, LANES)],
-                codes,
-            )
-
-
-def pack_corner(left_ref, right_ref, up_ref, down_ref):
     population, cotangent, codes = from_y(left_ref, right_ref)
     for n, c in enumerate((1, 4)):
         for out_ref, way in ((up_ref, 1), (down_ref, -1)):
@@ -437,10 +432,14 @@
                 lambda i: cotangent(i, c),
                 lambda s: codes(s, c),
             )
+            out_ref[X_LANE * n + X_CODE2] = codes(2, c)
     for n in range(Q + 1):
         value = population(n, 0) if n < Q else codes(1, 0)
         up_ref[X_RING + n] = value
         down_ref[X_RING + n] = value
+    first, second = field_ref[4], lines(field_ref[5], 4)
+    up_ref[X_OWN2] = jnp.where(row >= 4, first, second)
+    down_ref[X_OWN2] = jnp.where(row < 4, first, second)
 
 
 def add_panels(parts_ref, out_ref):
@@ -486,9 +485,12 @@
         (-1, 2, own_x[1], corner_x[1]),
     ):
         for t in range(2):
-            put(2 + t, r, *from_x(side_ref, X_LANE * t, way))
+            second = corner_ref[X_OWN2]
+            second = lines(second, 4) if t else second
+            put(2 + t, r, *from_x(side_ref, X_SIDE * t, way, second))
         for n, c in enumerate((1, 4)):
-            put(c, r, *from_x(corner_ref, X_LANE * n, way))
+            second = corner_ref[X_LANE * n + X_CODE2]
+            put(c, r, *from_x(corner_ref, X_LANE * n, way, second))
         put(
             0,
             r,
@@ -643,6 +645,7 @@
 
 VMEM = pl.BlockSpec(memory_space=pltpu.VMEM)
 HBM = pl.BlockSpec(memory_space=pltpu.HBM)
+ANY = pl.BlockSpec(memory_space=pl.ANY)
 
 
 def shape_of(*dims):
@@ -674,9 +677,15 @@
         downs = [(i + 1, i) for i in range(size - 1)]
         return lax.ppermute(to_next, axis, ups), lax.ppermute(to_last, axis, downs)
 
-    up, down, own, field = call(
-        pack_y,
-        (tiles_of(Y_TILES), tiles_of(Y_TILES), tiles_of(2 * Q), tiles_of(2 * OWN_PHI + 2)),
+    arguments = [
+        pltpu.with_memory_space_constraint(value, pltpu.HBM)
+        for value in (checkpoint, cotangent, cell_codes, baffle_index, porosity)
+    ]
+    up, down, side_up, side_down, own, field = call(
+        pack_own,
+        (tiles_of(Y_TILES),) * 2
+        + (tiles_of(2 * X_SIDE),) * 2
+        + (tiles_of(2 * Q), tiles_of(2 * OWN_PHI + 2)),
         [HBM] * 5,
         [
             pltpu.VMEM((Q, ROWS, 2 * LANES), jnp.float32),
@@ -686,16 +695,13 @@
             pltpu.SMEM(porosity.shape, jnp.float32),
             pltpu.SemaphoreType.DMA((5,)),
         ],
-        name="pack_y",
-    )(checkpoint, cotangent, cell_codes, baffle_index, porosity)
+        name="pack_own",
+    )(*arguments)
     left, right = exchange(up, down, "gy", size_y)
-    side_up, side_down = call(
-        pack_x, (tiles_of(2 * X_LANE), tiles_of(2 * X_LANE)), [VMEM] * 3, name="pack_x"
-    )(own, cotangent, field)
     below, above = exchange(side_up, side_down, "gx", size_x)
     corner_up, corner_down = call(
-        pack_corner, (tiles_of(X_CORNER), tiles_of(X_CORNER)), [VMEM] * 2, name="pack_corner"
-    )(left, right)
+        pack_corner, (tiles_of(X_CORNER),) * 2, [VMEM] * 3 + [ANY] * 2, name="pack_corner"
+    )(left, right, field, below, above)
     below_corner, above_corner = exchange(corner_up, corner_down, "gx", size_x)
 
     adjoint, sums = call(

time: 53.1 us -> 47.4 us (0.89)
  local copies, waits for them, and re-layouts: 3.93 us -> 0.01 us
  waiting for transfers between devices: 11.2 us -> 7.45 us
  blocking collectives: 14.5 us -> 16.9 us
  starting transfers between devices: 15 us -> 14.4 us
    unnamed x12 -> x6, local copies, waits for them, and re-layouts: 3.93 us -> 0.01 us
    all_to_all x1, blocking collectives: 14.5 us -> 16.9 us  [on_device(): gathered = lax.all_to_all(sums, ('gx', 'gy'), 0, 0, tiled=True)]
    ppermute x3, waiting for transfers between devices: 2.25 us -> 0.01 us  [exchange(): lax.ppermute(to_next, axis, ups)]
    ppermute x3, waiting for transfers between devices: 8.95 us -> 7.45 us  [exchange(): lax.ppermute(to_last, axis, downs)]
    pallas_call x3 -> x2, Pallas kernels: 1.11 us -> 1.35 us  [the longest x1 1.19 us: on_device(): call(pack_own, (tiles_of(Y_TILES),) * 2 + (tiles_of(2 * X_SIDE),) * 2 + (...]
where the time goes in v4:
time: 47.4 us; the launch traced here: 47 us
  blocking collectives  16.9 us (36%)
  starting transfers between devices  14.4 us (30%)
  Pallas kernels  7.6 us (16%)
  waiting for transfers between devices  7.45 us (16%)
  between operations  0.72 us (2%)
    all_to_all x1, blocking collectives, on_device(): gathered = lax.all_to_all(sums, ('gx', 'gy'), 0, 0, tiled=True)  16.9 us
    ppermute x3, starting transfers between devices, exchange(): lax.ppermute(to_next, axis, ups)  10.5 us
    ppermute x3, waiting for transfers between devices, exchange(): lax.ppermute(to_last, axis, downs)  7.45 us
    pallas_call x1, Pallas kernels, on_device(): call(functools.partial(steps_kernel, sizes), (shape_of(Q, ROWS, 2 * LANES...  5.7 us
    ppermute x3, starting transfers between devices, exchange(): lax.ppermute(to_last, axis, downs)  3.88 us
    pallas_call x1, Pallas kernels, on_device(): call(pack_own, (tiles_of(Y_TILES),) * 2 + (tiles_of(2 * X_SIDE),) * 2 + (...  1.19 us
  transfers between devices with their start and end apart: 6, of which 3 were waited for; matrix products, arithmetic and copies ran while one was open for 0% of the time, Pallas kernels for 0%

profile of v4, /device:TPU:0, one launch (start us, length us, event | category | flops | bytes accessed | tf_op | source)
XLA Modules:
  0.0 47.0 jit_solution(4145848655207375733)
XLA Ops:
  0.6 1.2 %pack_own.1 = (f32[43,8,128]{2,1,0:T(8,128)S(1)}, f32[43,8,128]{2,1,0:T(8,128)S(1)}, f32[42,8,128]{2,1,0:T(8,128)S(1)}, f32[42,8,128]{2,1,0:T(8,128)S(1)}, f32[3...) custom-call(f32[19,8,256]{2,1,0:T(8,128)} %f_ref.1, f32[19,8,256]{2,1,0:T(8,128)} %cot_ref.1, s32[4,8,256]{2,1,0:T(8,128)} %codes_hbm.1, ...), custom_call_target="tpu_custom_call" | custom-call | tf_op jit(solution)/shard_map/pack_own/pallas_call | solution.py:684
  1.8 4.9 %collective-permute-start = (f32[43,8,128]{2,1,0:T(8,128)S(1)}, f32[43,8,128]{2,1,0:T(8,128)S(1)}, u32[]{:S(2)}, u32[]{:S(2)}) collective-permute-start(f32[43,8,128]{2,1,0:T(8,128)S(1)} %get-tuple-element.14), channel_id=1, source_target_pairs={{0,1},{1,2},{2,3},{4,5},{5,6},{6,7},{8,9},{9,10},{10,11},{12,13},{... | collective-permute-start | bytes 528392 | tf_op jit(solution)/shard_map/ppermute | solution.py:678
  6.7 1.3 %collective-permute-start.1 = (f32[43,8,128]{2,1,0:T(8,128)S(1)}, f32[43,8,128]{2,1,0:T(8,128)S(1)}, u32[]{:S(2)}, u32[]{:S(2)}) collective-permute-start(f32[43,8,128]{2,1,0:T(8,128)S(1)} %get-tuple-element.15), channel_id=1, source_target_pairs={{1,0},{2,1},{3,2},{5,4},{6,5},{7,6},{9,8},{10,9},{11,10},{13,12},{... | collective-permute-start | bytes 528392 | tf_op jit(solution)/shard_map/ppermute | solution.py:678
  8.0 1.5 %collective-permute-start.2 = (f32[42,8,128]{2,1,0:T(8,128)S(1)}, f32[42,8,128]{2,1,0:T(8,128)S(1)}, u32[]{:S(2)}, u32[]{:S(2)}) collective-permute-start(f32[42,8,128]{2,1,0:T(8,128)S(1)} %get-tuple-element.16), channel_id=1, source_target_pairs={{0,4},{4,8},{8,12},{12,16},{16,20},{20,24},{24,28},{1,5},{5,9},{9,... | collective-permute-start | bytes 516104 | tf_op jit(solution)/shard_map/ppermute | solution.py:678
  9.5 1.3 %collective-permute-start.3 = (f32[42,8,128]{2,1,0:T(8,128)S(1)}, f32[42,8,128]{2,1,0:T(8,128)S(1)}, u32[]{:S(2)}, u32[]{:S(2)}) collective-permute-start(f32[42,8,128]{2,1,0:T(8,128)S(1)} %get-tuple-element.17), channel_id=1, source_target_pairs={{4,0},{8,4},{12,8},{16,12},{20,16},{24,20},{28,24},{5,1},{9,5},{13... | collective-permute-start | bytes 516104 | tf_op jit(solution)/shard_map/ppermute | solution.py:678
  10.8 0.0 collective-permute-done.2.below_ref
  10.8 3.6 %collective-permute-done.3.above_ref = f32[42,8,128]{2,1,0:T(8,128)S(1)} collective-permute-done((f32[42,8,128]{2,1,0:T(8,128)S(1)}, f32[42,8,128]{2,1,0:T(8,128)S(1)}, u32[]{:S(2)}, u32[]{:S(2)}) %collective-permute-start.3) | collective-permute-done | bytes 172064 | tf_op jit(solution)/shard_map/ppermute | solution.py:678
  14.4 0.0 collective-permute-done.left_ref
  14.4 1.7 %collective-permute-done.1.right_ref = f32[43,8,128]{2,1,0:T(8,128)S(1)} collective-permute-done((f32[43,8,128]{2,1,0:T(8,128)S(1)}, f32[43,8,128]{2,1,0:T(8,128)S(1)}, u32[]{:S(2)}, u32[]{:S(2)}) %collective-permute-start.1) | collective-permute-done | bytes 176160 | tf_op jit(solution)/shard_map/ppermute | solution.py:678
  16.1 0.0 copy-start
  16.1 0.0 copy-start.1
  16.1 0.0 copy-start.2
  16.1 0.2 pack_corner.1
  16.3 4.2 %collective-permute-start.4 = (f32[65,8,128]{2,1,0:T(8,128)S(1)}, f32[65,8,128]{2,1,0:T(8,128)S(1)}, u32[]{:S(2)}, u32[]{:S(2)}) collective-permute-start(f32[65,8,128]{2,1,0:T(8,128)S(1)} %get-tuple-element.18), channel_id=1, source_target_pairs={{0,4},{4,8},{8,12},{12,16},{16,20},{20,24},{24,28},{1,5},{5,9},{9,... | collective-permute-start | bytes 798728 | tf_op jit(solution)/shard_map/ppermute | solution.py:678
  20.5 1.3 %collective-permute-start.5 = (f32[65,8,128]{2,1,0:T(8,128)S(1)}, f32[65,8,128]{2,1,0:T(8,128)S(1)}, u32[]{:S(2)}, u32[]{:S(2)}) collective-permute-start(f32[65,8,128]{2,1,0:T(8,128)S(1)} %get-tuple-element.19), channel_id=1, source_target_pairs={{4,0},{8,4},{12,8},{16,12},{20,16},{24,20},{28,24},{5,1},{9,5},{13... | collective-permute-start | bytes 798728 | tf_op jit(solution)/shard_map/ppermute | solution.py:678
  21.8 0.0 collective-permute-done.4.below_corner_ref
  21.8 2.1 %collective-permute-done.5.above_corner_ref = f32[65,8,128]{2,1,0:T(8,128)S(1)} collective-permute-done((f32[65,8,128]{2,1,0:T(8,128)S(1)}, f32[65,8,128]{2,1,0:T(8,128)S(1)}, u32[]{:S(2)}, u32[]{:S(2)}) %collective-permute-start.5) | collective-permute-done | bytes 266272 | tf_op jit(solution)/shard_map/ppermute | solution.py:678
  23.9 0.0 copy-done
  23.9 0.0 copy-done.1
  23.9 0.0 copy-done.2
  23.9 5.7 %steps.1 = (f32[19,8,256]{2,1,0:T(8,128)}, f32[32,64]{1,0:T(8,128)S(1)}) custom-call(s32[8,256]{1,0:T(8,128)S(1)} %copy-done.2, f32[19,8,256]{2,1,0:T(8,128)S(1)} %copy-done, f32[19,8,256]{2,1,0:T(8,128)S(1)} %copy-done.1, f32[38,8,128]{2,1,0:T(8,128)S(1)} %get-tuple-element.12.own_ref, f32[10,8,128]{2,1,0:T(8,128)S(1)} %get-tuple-element.13.field_ref.own_field_ref, ...), custom_call_target="tpu_custom_call" | custom-call | tf_op jit(solution)/shard_map/steps/pallas_call | solution.py:707
  29.6 16.9 %all_to_all.9.parts_ref = f32[32,1,64]{2,1,0:T(1,128)S(1)} all-to-all(f32[32,1,64]{2,1,0:T(1,128)S(1)} %bitcast.2), channel_id=1, replica_groups=mesh['gx'=8,'gy'=4] {'gx','gy'}, dimensions={0} | all-to-all | bytes 16384 | tf_op jit(solution)/shard_map/all_to_all | solution.py:736
  46.5 0.5 %add_panels.1 = f32[1,64]{1,0:T(1,128)} custom-call(f32[32,1,64]{2,1,0:T(1,128)S(1)} %all_to_all.9.parts_ref), custom_call_target="tpu_custom_call" | custom-call | tf_op jit(solution)/shard_map/add_panels/pallas_call | solution.py:737
Async XLA Ops:
  1.8 12.6 %collective-permute-start = (f32[43,8,128]{2,1,0:T(8,128)S(1)}, f32[43,8,128]{2,1,0:T(8,128)S(1)}, u32[]{:S(2)}, u32[]{:S(2)}) collective-permute-start(f32[43,8,128]{2,1,0:T(8,128)S(1)} %get-tuple-element.14), channel_id=1, source_target_pairs={{0,1},{1,2},{2,3},{4,5},{5,6},{6,7},{8,9},{9,10},{10,11},{12,13},{... | collective-permute-start | bytes 528392 | tf_op jit(solution)/shard_map/ppermute | solution.py:678
  6.7 9.4 %collective-permute-start.1 = (f32[43,8,128]{2,1,0:T(8,128)S(1)}, f32[43,8,128]{2,1,0:T(8,128)S(1)}, u32[]{:S(2)}, u32[]{:S(2)}) collective-permute-start(f32[43,8,128]{2,1,0:T(8,128)S(1)} %get-tuple-element.15), channel_id=1, source_target_pairs={{1,0},{2,1},{3,2},{5,4},{6,5},{7,6},{9,8},{10,9},{11,10},{13,12},{... | collective-permute-start | bytes 528392 | tf_op jit(solution)/shard_map/ppermute | solution.py:678
  8.0 2.8 %collective-permute-start.2 = (f32[42,8,128]{2,1,0:T(8,128)S(1)}, f32[42,8,128]{2,1,0:T(8,128)S(1)}, u32[]{:S(2)}, u32[]{:S(2)}) collective-permute-start(f32[42,8,128]{2,1,0:T(8,128)S(1)} %get-tuple-element.16), channel_id=1, source_target_pairs={{0,4},{4,8},{8,12},{12,16},{16,20},{20,24},{24,28},{1,5},{5,9},{9,... | collective-permute-start | bytes 516104 | tf_op jit(solution)/shard_map/ppermute | solution.py:678
  9.5 4.9 %collective-permute-start.3 = (f32[42,8,128]{2,1,0:T(8,128)S(1)}, f32[42,8,128]{2,1,0:T(8,128)S(1)}, u32[]{:S(2)}, u32[]{:S(2)}) collective-permute-start(f32[42,8,128]{2,1,0:T(8,128)S(1)} %get-tuple-element.17), channel_id=1, source_target_pairs={{4,0},{8,4},{12,8},{16,12},{20,16},{24,20},{28,24},{5,1},{9,5},{13... | collective-permute-start | bytes 516104 | tf_op jit(solution)/shard_map/ppermute | solution.py:678
  16.1 7.8 %copy-start = (f32[19,8,256]{2,1,0:T(8,128)S(1)}, f32[19,8,256]{2,1,0:T(8,128)}, u32[]{:S(2)}) copy-start(f32[19,8,256]{2,1,0:T(8,128)} %f_ref.1) | copy-start | bytes 466948
  16.1 7.8 %copy-start.1 = (f32[19,8,256]{2,1,0:T(8,128)S(1)}, f32[19,8,256]{2,1,0:T(8,128)}, u32[]{:S(2)}) copy-start(f32[19,8,256]{2,1,0:T(8,128)} %cot_ref.1) | copy-start | bytes 466948
  16.1 7.8 %copy-start.2 = (s32[8,256]{1,0:T(8,128)S(1)}, s32[8,256]{1,0:T(8,128)}, u32[]{:S(2)}) copy-start(s32[8,256]{1,0:T(8,128)} %panels_hbm.3) | copy-start | bytes 24580
  16.3 5.5 %collective-permute-start.4 = (f32[65,8,128]{2,1,0:T(8,128)S(1)}, f32[65,8,128]{2,1,0:T(8,128)S(1)}, u32[]{:S(2)}, u32[]{:S(2)}) collective-permute-start(f32[65,8,128]{2,1,0:T(8,128)S(1)} %get-tuple-element.18), channel_id=1, source_target_pairs={{0,4},{4,8},{8,12},{12,16},{16,20},{20,24},{24,28},{1,5},{5,9},{9,... | collective-permute-start | bytes 798728 | tf_op jit(solution)/shard_map/ppermute | solution.py:678
  20.5 3.4 %collective-permute-start.5 = (f32[65,8,128]{2,1,0:T(8,128)S(1)}, f32[65,8,128]{2,1,0:T(8,128)S(1)}, u32[]{:S(2)}, u32[]{:S(2)}) collective-permute-start(f32[65,8,128]{2,1,0:T(8,128)S(1)} %get-tuple-element.19), channel_id=1, source_target_pairs={{4,0},{8,4},{12,8},{16,12},{20,16},{24,20},{28,24},{5,1},{9,5},{13... | collective-permute-start | bytes 798728 | tf_op jit(solution)/shard_map/ppermute | solution.py:678

commit v5 on v4

--- a/solution.py
+++ b/solution.py
@@ -44,12 +44,11 @@
 
 Y_CODE1, Y_CODE2, Y_CODE3, Y_POP, Y_COT = 38, 39, 40, 41, 42
 Y_TILES = 43
-X_EXTRA, X_CODE13, X_CODE2 = 19, 20, 21
-X_LANE = 22
-X_RING = 2 * X_LANE
-X_OWN2 = X_RING + Q + 1
-X_CORNER = X_OWN2 + 1
-X_SIDE = X_LANE - 1
+X_EXTRA, X_CODE13 = 19, 20
+X_LANE = 21
+X_RING = 4 * X_LANE
+X_CODE2 = X_RING + Q + 1
+X_TILES = X_CODE2 + 2
 F_CODE1, F_CODE2, F_CODE3, F_PHI = 0, 5, 9, 13
 FIELDS = 18
 OWN_PHI = 4
@@ -240,18 +239,45 @@
     return pltpu.roll(value, amount, 0) if amount else value
 
 
+class Pick:
+    def __init__(self, flag, first, second):
+        self.flag, self.first, self.second = flag, first, second
+
+    def __getitem__(self, at):
+        return jnp.where(self.flag, self.first[at], self.second[at])
+
+
+class Deal:
+    def __init__(self, even, first, second):
+        self.even, self.refs, self.held = even, (first, second), {}
+
+    def put(self, way, at, value):
+        if (-way, at) not in self.held:
+            self.held[way, at] = value
+            return
+        other = self.held.pop((-way, at))
+        up, down = (value, other) if way == 1 else (other, value)
+        self.refs[0][at] = jnp.where(self.even, up, down)
+        self.refs[1][at] = jnp.where(self.even, down, up)
+
+
+def is_even(axis):
+    return lax.rem(lax.axis_index(axis), 2) == 0
+
+
 def pack_own(
     f_hbm,
     cot_hbm,
     codes_hbm,
     panels_hbm,
     porosity_hbm,
-    up_ref,
-    down_ref,
-    side_up_ref,
-    side_down_ref,
+    first_ref,
+    second_ref,
     own_ref,
+    state_ref,
+    own_cot_ref,
     field_ref,
+    names_ref,
     f_ref,
     cot_ref,
     codes_ref,
@@ -274,6 +300,7 @@
         copy.start()
     for copy in copies[:4]:
         copy.wait()
+    deal = Deal(is_even("gy"), first_ref, second_ref)
     row, lane, column, depth = iotas()
     top = depth == NZ - 1
 
@@ -282,22 +309,23 @@
 
     codes, phis = [], []
     for t in range(2):
-        upper = porosity_ref[panels_ref[0, t * LANES]]
-        lower = porosity_ref[panels_ref[4, t * LANES]]
-        phi = jnp.where(row < 4, upper, lower)
+        names = panels_ref[0, t * LANES], panels_ref[4, t * LANES]
+        phi = jnp.where(row < 4, porosity_ref[names[0]], porosity_ref[names[1]])
+        names_ref[t] = jnp.where(row < 4, names[0], names[1])
         kinds = [tile_of(codes_ref, s, t).astype(jnp.float32) for s in range(STEPS)]
         f = [tile_of(f_ref, i, t) for i in range(Q)]
         g = collide(f, kinds[0], phi, moments(f))
         for i in range(Q):
             own_ref[2 * i + t] = g[i]
+            state_ref[2 * i + t] = f[i]
         for s in range(STEPS):
             field_ref[2 * s + t] = kinds[s]
         field_ref[2 * OWN_PHI + t] = phi
         codes.append([jnp.where(top, phi, kinds[1]), kinds[2], kinds[3]])
     copies[4].wait()
-    for out_ref, way in ((up_ref, 1), (down_ref, -1)):
-        near, far = (1, 0) if way == 1 else (0, 1)
-        for i in range(Q):
+    for i in range(Q):
+        for way in (1, -1):
+            near, far = (1, 0) if way == 1 else (0, 1)
             deep = 3 - way * VELOCITIES[i][1]
             cot = tile_of(cot_ref, i, near)
             g_far = own_ref[2 * i + far]
@@ -305,34 +333,28 @@
                 mixed = jnp.where(column >= deep, g_far, columns(cot, deep - 4))
             else:
                 mixed = jnp.where(column < 4 - deep, g_far, columns(cot, 4 - deep))
-            out_ref[2 * i + near] = own_ref[2 * i + near]
-            out_ref[2 * i + far] = mixed
+            deal.put(way, 2 * i, mixed if far == 0 else own_ref[2 * i])
+            deal.put(way, 2 * i + 1, mixed if far == 1 else own_ref[2 * i + 1])
+    for way in (1, -1):
+        near, far = (1, 0) if way == 1 else (0, 1)
         outer = 3 if way == 1 else 0
-        out_ref[Y_CODE1] = codes[near][0]
-        out_ref[Y_CODE2] = codes[near][1]
-        out_ref[Y_CODE3] = jnp.where(
-            column == 3 - outer, columns(codes[far][0], 3 - 2 * outer), codes[near][2]
-        )
+        deal.put(way, Y_CODE1, codes[near][0])
+        deal.put(way, Y_CODE2, codes[near][1])
+        outside = columns(codes[far][0], 3 - 2 * outer)
+        deal.put(way, Y_CODE3, jnp.where(column == 3 - outer, outside, codes[near][2]))
         extra = None
         for k, i in enumerate(turned(1, -way)):
             value = columns(own_ref[2 * i + far], k - outer)
             extra = value if extra is None else jnp.where(column == k, value, extra)
-        out_ref[Y_POP] = extra
+        deal.put(way, Y_POP, extra)
         extra = None
         for k, i in enumerate(turned(1, way)):
             value = columns(tile_of(cot_ref, i, near), k - (1 if way == 1 else 2))
             extra = value if extra is None else jnp.where(column == k, value, extra)
-        out_ref[Y_COT] = extra
+        deal.put(way, Y_COT, extra)
     for t in range(2):
-        for out_ref, way in ((side_up_ref, 1), (side_down_ref, -1)):
-            pack_lines(
-                out_ref,
-                X_SIDE * t,
-                way,
-                lambda i: own_ref[2 * i + t],
-                lambda i: tile_of(cot_ref, i, t),
-                lambda s: codes[t][s - 1],
-            )
+        for i in range(Q):
+            own_cot_ref[2 * i + t] = tile_of(cot_ref, i, t)
 
 
 def from_y(left_ref, right_ref):
@@ -370,29 +392,35 @@
     return population, cotangent, codes
 
 
-def pack_lines(out_ref, first, way, population, cotangent, codes):
+def pack_lines(deal, first, population, cotangent, codes):
     row, lane, column, depth = iotas()
 
-    def mixed(pop, cot, deep):
+    def put(at, pop, cot, deep, way):
         if way == 1:
-            return jnp.where(row >= deep, pop, lines(cot, deep))
-        return jnp.where(row < ROWS - deep, pop, lines(cot, -deep))
+            mixed = jnp.where(row >= deep, pop, lines(cot, deep))
+        else:
+            mixed = jnp.where(row < ROWS - deep, pop, lines(cot, -deep))
+        deal.put(way, first + at, mixed)
 
     for i in range(Q):
-        out_ref[first + i] = mixed(population(i), cotangent(i), 3 - way * VELOCITIES[i][0])
-    extra = None
-    for k, i in enumerate(turned(0, -way)):
-        value = lines(population(i), k - (3 if way == 1 else 4))
-        extra = value if extra is None else jnp.where(row == k, value, extra)
-    for k, i in enumerate(turned(0, way)):
-        value = lines(cotangent(i), 4 + k - (5 if way == 1 else 2))
-        extra = jnp.where(row == 4 + k, value, extra)
-    out_ref[first + X_EXTRA] = extra
-    out_ref[first + X_CODE13] = mixed(codes(1), codes(3), 3)
-
-
-def from_x(ref, first, way, second):
+        pop, cot = population(i), cotangent(i)
+        for way in (1, -1):
+            put(i, pop, cot, 3 - way * VELOCITIES[i][0], way)
+    for way in (1, -1):
+        extra = None
+        for k, i in enumerate(turned(0, -way)):
+            value = lines(population(i), k - (3 if way == 1 else 4))
+            extra = value if extra is None else jnp.where(row == k, value, extra)
+        for k, i in enumerate(turned(0, way)):
+            value = lines(cotangent(i), 4 + k - (5 if way == 1 else 2))
+            extra = jnp.where(row == 4 + k, value, extra)
+        deal.put(way, first + X_EXTRA, extra)
+        put(X_CODE13, codes(1), codes(3), 3, way)
+
+
+def from_x(ref, n, way):
     row, lane, column, depth = iotas()
+    first = X_LANE * n
 
     def population(i):
         value = ref[first + i]
@@ -412,46 +440,63 @@
 
     def codes(s):
         if s == 2:
-            return second
+            return lines(ref[X_CODE2 + n // 2], 4 * (n % 2))
         value = ref[first + X_CODE13]
         return value if s == 1 else lines(value, -3 * way)
 
     return population, cotangent, codes
 
 
-def pack_corner(left_ref, right_ref, field_ref, below_ref, above_ref, up_ref, down_ref):
+def pack_x(own_ref, cot_ref, field_ref, first_y_ref, second_y_ref, first_ref, second_ref):
     row, lane, column, depth = iotas()
-    population, cotangent, codes = from_y(left_ref, right_ref)
-    for n, c in enumerate((1, 4)):
-        for out_ref, way in ((up_ref, 1), (down_ref, -1)):
-            pack_lines(
-                out_ref,
-                X_LANE * n,
-                way,
-                lambda i: population(i, c),
-                lambda i: cotangent(i, c),
-                lambda s: codes(s, c),
-            )
-            out_ref[X_LANE * n + X_CODE2] = codes(2, c)
+    deal = Deal(is_even("gx"), first_ref, second_ref)
+    population, cotangent, codes = from_y(*sides(first_y_ref, second_y_ref, "gy"))
+
+    def own_codes(s, t):
+        value = field_ref[2 * s + t]
+        return jnp.where(depth == NZ - 1, field_ref[2 * OWN_PHI + t], value) if s == 1 else value
+
+    def both_codes(at, first, second):
+        second = lines(second, 4)
+        deal.put(1, at, jnp.where(row >= 4, first, second))
+        deal.put(-1, at, jnp.where(row < 4, first, second))
+
+    for t in range(2):
+        pack_lines(
+            deal,
+            X_LANE * t,
+            lambda i: own_ref[2 * i + t],
+            lambda i: cot_ref[2 * i + t],
+            lambda s: own_codes(s, t),
+        )
+    for n, c in ((2, 1), (3, 4)):
+        pack_lines(
+            deal,
+            X_LANE * n,
+            lambda i: population(i, c),
+            lambda i: cotangent(i, c),
+            lambda s: codes(s, c),
+        )
     for n in range(Q + 1):
         value = population(n, 0) if n < Q else codes(1, 0)
-        up_ref[X_RING + n] = value
-        down_ref[X_RING + n] = value
-    first, second = field_ref[4], lines(field_ref[5], 4)
-    up_ref[X_OWN2] = jnp.where(row >= 4, first, second)
-    down_ref[X_OWN2] = jnp.where(row < 4, first, second)
+        first_ref[X_RING + n] = value
+        second_ref[X_RING + n] = value
+    both_codes(X_CODE2, own_codes(2, 0), own_codes(2, 1))
+    both_codes(X_CODE2 + 1, codes(2, 1), codes(2, 4))
+
+
+def sides(first_ref, second_ref, axis):
+    even = is_even(axis)
+    return Pick(even, second_ref, first_ref), Pick(even, first_ref, second_ref)
 
 
 def add_panels(parts_ref, out_ref):
     out_ref[...] = jnp.sum(parts_ref[...], axis=0)
 
 
-def fill(
-    left_ref, right_ref, own_ref, field_ref, cot_ref, own_x, corner_x, pop, cot, field
-):
+def fill(from_left, own_ref, field_ref, cot_ref, from_below, pop, cot, field):
     row, lane, column, depth = iotas()
     top = depth == NZ - 1
-    from_left = from_y(left_ref, right_ref)
 
     def put(c, r, population, cotangent, codes):
         rows = pl.ds(ROWS * (r + 1), ROWS)
@@ -475,44 +520,28 @@
         rows = pl.ds(2 * ROWS, ROWS)
         for i in range(Q):
             pop[5 * i + 2 + t, rows, :] = own_ref[2 * i + t]
-            cot[4 * i + 1 + t, rows, :] = cot_ref[i, :, pl.ds(t * LANES, LANES)]
+            cot[4 * i + 1 + t, rows, :] = cot_ref[2 * i + t]
         field[F_CODE1 + 2 + t, rows, :] = field_ref[2 + t]
         field[F_CODE2 + 1 + t, rows, :] = field_ref[4 + t]
         field[F_CODE3 + 1 + t, rows, :] = field_ref[6 + t]
         field[F_PHI + 2 + t, rows, :] = field_ref[2 * OWN_PHI + t]
-    for way, r, side_ref, corner_ref in (
-        (1, 0, own_x[0], corner_x[0]),
-        (-1, 2, own_x[1], corner_x[1]),
-    ):
-        for t in range(2):
-            second = corner_ref[X_OWN2]
-            second = lines(second, 4) if t else second
-            put(2 + t, r, *from_x(side_ref, X_SIDE * t, way, second))
-        for n, c in enumerate((1, 4)):
-            second = corner_ref[X_LANE * n + X_CODE2]
-            put(c, r, *from_x(corner_ref, X_LANE * n, way, second))
-        put(
-            0,
-            r,
-            lambda i: corner_ref[X_RING + i],
-            None,
-            lambda s: corner_ref[X_RING + Q],
-        )
+    for way, r, ref in ((1, 0, from_below[0]), (-1, 2, from_below[1])):
+        for n, c in enumerate((2, 3, 1, 4)):
+            put(c, r, *from_x(ref, n, way))
+        put(0, r, lambda i: ref[X_RING + i], None, lambda s: ref[X_RING + Q])
 
 
 def steps_kernel(
     sizes,
-    panels_hbm,
-    f_ref,
+    state_ref,
     cot_ref,
     own_ref,
     own_field_ref,
-    left_ref,
-    right_ref,
-    below_ref,
-    above_ref,
-    below_corner_ref,
-    above_corner_ref,
+    names_ref,
+    first_y_ref,
+    second_y_ref,
+    first_x_ref,
+    second_x_ref,
     adjoint_ref,
     panel_ref,
     pop_a,
@@ -522,20 +551,14 @@
     saved,
     mom,
     grad,
-    panels_ref,
-    sem,
 ):
     size_x, size_y = sizes
-    names = pltpu.make_async_copy(panels_hbm, panels_ref, sem)
-    names.start()
     fill(
-        left_ref,
-        right_ref,
+        from_y(*sides(first_y_ref, second_y_ref, "gy")),
         own_ref,
         own_field_ref,
         cot_ref,
-        (below_ref, above_ref),
-        (below_corner_ref, above_corner_ref),
+        sides(first_x_ref, second_x_ref, "gx"),
         pop_a,
         cot,
         field,
@@ -620,14 +643,13 @@
     backward(pop_a, 2, pop_b)
     backward(pop_b, 1, pop_a)
 
-    names.wait()
     row = lax.broadcasted_iota(jnp.int32, (ROWS, LANES), 0)
     panel = lax.broadcasted_iota(jnp.int32, panel_ref.shape, 1)
     sums = jnp.zeros(panel_ref.shape, jnp.float32)
     for tile in range(2):
         lanes = pl.ds(tile * LANES, LANES)
         b = streamed(pop_a, tile + 1, 4, 1, -1, masks_of(tile, 0, 1), None)
-        f = [f_ref[i, :, lanes] for i in range(Q)]
+        f = [state_ref[2 * i + tile] for i in range(Q)]
         kind = own_field_ref[tile]
         phi = own_field_ref[2 * OWN_PHI + tile]
         _, _, rho, rinv, u = moments(f)
@@ -638,14 +660,13 @@
         for part in range(2):
             inside = (row < 4) if part == 0 else (row >= 4)
             amount = jnp.sum(jnp.where(inside, term, 0.0))
-            name = panels_ref[4 * part, tile * LANES]
+            name = names_ref[tile, 4 * part : 4 * part + 1, 0:1]
             sums = sums + jnp.where(panel == name, amount, 0.0)
     panel_ref[...] = sums
 
 
 VMEM = pl.BlockSpec(memory_space=pltpu.VMEM)
 HBM = pl.BlockSpec(memory_space=pltpu.HBM)
-ANY = pl.BlockSpec(memory_space=pl.ANY)
 
 
 def shape_of(*dims):
@@ -672,20 +693,21 @@
             name=name,
         )
 
-    def exchange(to_next, to_last, axis, size):
-        ups = [(i, i + 1) for i in range(size - 1)]
-        downs = [(i + 1, i) for i in range(size - 1)]
-        return lax.ppermute(to_next, axis, ups), lax.ppermute(to_last, axis, downs)
+    def exchange(first, second, axis, size):
+        pairs = [(i, i ^ 1) for i in range(size) if i ^ 1 < size]
+        between = [(i, i + 1) for i in range(1, size - 1, 2)]
+        between += [(j, i) for i, j in between]
+        return lax.ppermute(first, axis, pairs), lax.ppermute(second, axis, between)
 
     arguments = [
         pltpu.with_memory_space_constraint(value, pltpu.HBM)
         for value in (checkpoint, cotangent, cell_codes, baffle_index, porosity)
     ]
-    up, down, side_up, side_down, own, field = call(
+    first_y, second_y, own, state, cot, field, names = call(
         pack_own,
         (tiles_of(Y_TILES),) * 2
-        + (tiles_of(2 * X_SIDE),) * 2
-        + (tiles_of(2 * Q), tiles_of(2 * OWN_PHI + 2)),
+        + (tiles_of(2 * Q),) * 3
+        + (tiles_of(2 * OWN_PHI + 2), jax.ShapeDtypeStruct((2, ROWS, LANES), jnp.int32)),
         [HBM] * 5,
         [
             pltpu.VMEM((Q, ROWS, 2 * LANES), jnp.float32),
@@ -697,17 +719,16 @@
         ],
         name="pack_own",
     )(*arguments)
-    left, right = exchange(up, down, "gy", size_y)
-    below, above = exchange(side_up, side_down, "gx", size_x)
-    corner_up, corner_down = call(
-        pack_corner, (tiles_of(X_CORNER),) * 2, [VMEM] * 3 + [ANY] * 2, name="pack_corner"
-    )(left, right, field, below, above)
-    below_corner, above_corner = exchange(corner_up, corner_down, "gx", size_x)
+    first_y, second_y = exchange(first_y, second_y, "gy", size_y)
+    first_x, second_x = call(pack_x, (tiles_of(X_TILES),) * 2, [VMEM] * 5, name="pack_x")(
+        own, cot, field, first_y, second_y
+    )
+    first_x, second_x = exchange(first_x, second_x, "gx", size_x)
 
     adjoint, sums = call(
         functools.partial(steps_kernel, sizes),
         (shape_of(Q, ROWS, 2 * LANES), shape_of(devices, panels)),
-        [HBM] + [VMEM] * 10,
+        [VMEM] * 9,
         [
             pltpu.VMEM((5 * Q, 5 * ROWS, LANES), jnp.float32),
             pltpu.VMEM((5 * Q, 5 * ROWS, LANES), jnp.float32),
@@ -716,23 +737,9 @@
             pltpu.VMEM((3, Q, 5, ROWS, LANES), jnp.float32),
             pltpu.VMEM((3, 5, 5, 3 * ROWS, LANES), jnp.float32),
             pltpu.VMEM((4, ROWS, LANES), jnp.float32),
-            pltpu.SMEM(baffle_index.shape, jnp.int32),
-            pltpu.SemaphoreType.DMA,
         ],
         name="steps",
-    )(
-        baffle_index,
-        checkpoint,
-        cotangent,
-        own,
-        field,
-        left,
-        right,
-        below,
-        above,
-        below_corner,
-        above_corner,
-    )
+    )(state, cot, own, field, names, first_y, second_y, first_x, second_x)
     gathered = lax.all_to_all(sums, ("gx", "gy"), 0, 0, tiled=True)
     totals = call(add_panels, shape_of(1, panels), [VMEM], name="add_panels")(
         gathered.reshape(devices, 1, panels)

time: 47.4 us -> 42.5 us (0.90)
  starting transfers between devices: 14.4 us -> 4.42 us
  blocking collectives: 16.9 us -> 24.6 us
  waiting for transfers between devices: 7.45 us -> 4.87 us
    ppermute x6 -> x4, starting transfers between devices: 14.4 us -> 4.42 us  [the longest x2 3.07 us: exchange(): lax.ppermute(first, axis, pairs)]
    all_to_all x1, blocking collectives: 16.9 us -> 24.6 us  [on_device(): gathered = lax.all_to_all(sums, ('gx', 'gy'), 0, 0, tiled=True)]
    ppermute x6 -> x4, waiting for transfers between devices: 7.45 us -> 4.87 us  [the longest x2 4.87 us: exchange(): lax.ppermute(first, axis, pairs)]
  transfers between devices with their start and end apart: 6 -> 4, of which waited for: 3 -> 2; matrix products, arithmetic and copies ran while one was open for 0% -> 0% of each run, Pallas kernels for 0% -> 0%
where the time goes in v5:
time: 42.5 us; the launch traced here: 42.2 us
  blocking collectives  24.6 us (58%)
  Pallas kernels  7.63 us (18%)
  waiting for transfers between devices  4.87 us (11%)
  starting transfers between devices  4.42 us (10%)
  between operations  0.67 us (2%)
    all_to_all x1, blocking collectives, on_device(): gathered = lax.all_to_all(sums, ('gx', 'gy'), 0, 0, tiled=True)  24.6 us
    pallas_call x1, Pallas kernels, on_device(): call(functools.partial(steps_kernel, sizes), (shape_of(Q, ROWS, 2 * LANES...  5.75 us
    ppermute x2, waiting for transfers between devices, exchange(): lax.ppermute(first, axis, pairs)  4.87 us
    ppermute x2, starting transfers between devices, exchange(): lax.ppermute(first, axis, pairs)  3.07 us
    ppermute x2, starting transfers between devices, exchange(): lax.ppermute(second, axis, between)  1.35 us
    pallas_call x1, Pallas kernels, on_device(): call(pack_own, (tiles_of(Y_TILES),) * 2 + (tiles_of(2 * Q),) * 3 + (tiles...  1.18 us
  transfers between devices with their start and end apart: 4, of which 2 were waited for; matrix products, arithmetic and copies ran while one was open for 0% of the time, Pallas kernels for 0%

profile of v5, /device:TPU:0, one launch (start us, length us, event | category | flops | bytes accessed | tf_op | source)
XLA Modules:
  0.0 42.2 jit_solution(3447304690212101923)
XLA Ops:
  0.6 1.2 %pack_own.1 = (f32[43,8,128]{2,1,0:T(8,128)S(1)}, f32[43,8,128]{2,1,0:T(8,128)S(1)}, f32[38,8,128]{2,1,0:T(8,128)S(1)}, f32[38,8,128]{2,1,0:T(8,128)S(1)}, f32[3...) custom-call(f32[19,8,256]{2,1,0:T(8,128)} %f_hbm.1, f32[19,8,256]{2,1,0:T(8,128)} %cot_hbm.1, ...), custom_call_target="tpu_custom_call" | custom-call | tf_op jit(solution)/shard_map/pack_own/pallas_call | solution.py:706
  1.8 3.0 %collective-permute-start = (f32[43,8,128]{2,1,0:T(8,128)S(1)}, f32[43,8,128]{2,1,0:T(8,128)S(1)}, u32[]{:S(2)}, u32[]{:S(2)}) collective-permute-start(f32[43,8,128]{2,1,0:T(8,128)S(1)} %get-tuple-element.18), channel_id=1, source_target_pairs={{0,1},{1,0},{2,3},{3,2},{4,5},{5,4},{6,7},{7,6},{8,9},{9,8},{10,11... | collective-permute-start | bytes 528392 | tf_op jit(solution)/shard_map/ppermute | solution.py:700
  4.8 0.7 %collective-permute-start.1 = (f32[43,8,128]{2,1,0:T(8,128)S(1)}, f32[43,8,128]{2,1,0:T(8,128)S(1)}, u32[]{:S(2)}, u32[]{:S(2)}) collective-permute-start(f32[43,8,128]{2,1,0:T(8,128)S(1)} %get-tuple-element.19), channel_id=1, source_target_pairs={{1,2},{2,1},{5,6},{6,5},{9,10},{10,9},{13,14},{14,13},{17,18},{18,... | collective-permute-start | bytes 528392 | tf_op jit(solution)/shard_map/ppermute | solution.py:700
  5.5 3.8 %collective-permute-done.first_y_ref = f32[43,8,128]{2,1,0:T(8,128)S(1)} collective-permute-done((f32[43,8,128]{2,1,0:T(8,128)S(1)}, f32[43,8,128]{2,1,0:T(8,128)S(1)}, u32[]{:S(2)}, u32[]{:S(2)}) %collective-permute-start) | collective-permute-done | bytes 176160 | tf_op jit(solution)/shard_map/ppermute | solution.py:700
  9.3 0.0 collective-permute-done.1.second_y_ref
  9.3 0.2 pack_x.1
  9.5 0.1 collective-permute-start.2
  9.5 0.7 %collective-permute-start.3 = (f32[106,8,128]{2,1,0:T(8,128)S(1)}, f32[106,8,128]{2,1,0:T(8,128)S(1)}, u32[]{:S(2)}, u32[]{:S(2)}) collective-permute-start(f32[106,8,128]{2,1,0:T(8,128)S(1)} %get-tuple-element.21), channel_id=1, source_target_pairs={{4,8},{12,16},{20,24},{8,4},{16,12},{24,20},{5,9},{13,17},{21,25},... | collective-permute-start | bytes 1302536 | tf_op jit(solution)/shard_map/ppermute | solution.py:700
  10.2 1.1 %collective-permute-done.2.first_x_ref = f32[106,8,128]{2,1,0:T(8,128)S(1)} collective-permute-done((f32[106,8,128]{2,1,0:T(8,128)S(1)}, f32[106,8,128]{2,1,0:T(8,128)S(1)}, u32[]{:S(2)}, u32[]{:S(2)}) %collective-permute-start.2) | collective-permute-done | bytes 434208 | tf_op jit(solution)/shard_map/ppermute | solution.py:700
  11.3 0.0 collective-permute-done.3.second_x_ref
  11.3 5.7 %steps.1 = (f32[19,8,256]{2,1,0:T(8,128)}, f32[32,64]{1,0:T(8,128)S(1)}) custom-call(f32[38,8,128]{2,1,0:T(8,128)S(1)} %get-tuple-element.13.state_ref, f32[38,8,128]{2,1,0:T(8,128)S(1)} %get-tuple-element.14.cot_ref, f32[38,8,128]{2,1,0:T(8,128)S(1)} %get-tuple-element.15.own_ref, f32[10,8,128]{2,1,0:T(8,128)S(1)} %get-tuple-element.16.field_ref.own_field_ref, ...), custom_call_target="tpu_custom_call" | custom-call | tf_op jit(solution)/shard_map/steps/pallas_call | solution.py:728
  17.1 24.6 %all_to_all.9.parts_ref = f32[32,1,64]{2,1,0:T(1,128)S(1)} all-to-all(f32[32,1,64]{2,1,0:T(1,128)S(1)} %bitcast.2), channel_id=1, replica_groups=mesh['gx'=8,'gy'=4] {'gx','gy'}, dimensions={0} | all-to-all | bytes 16384 | tf_op jit(solution)/shard_map/all_to_all | solution.py:743
  41.7 0.5 %add_panels.1 = f32[1,64]{1,0:T(1,128)} custom-call(f32[32,1,64]{2,1,0:T(1,128)S(1)} %all_to_all.9.parts_ref), custom_call_target="tpu_custom_call" | custom-call | tf_op jit(solution)/shard_map/add_panels/pallas_call | solution.py:744
Async XLA Ops:
  1.8 7.5 %collective-permute-start = (f32[43,8,128]{2,1,0:T(8,128)S(1)}, f32[43,8,128]{2,1,0:T(8,128)S(1)}, u32[]{:S(2)}, u32[]{:S(2)}) collective-permute-start(f32[43,8,128]{2,1,0:T(8,128)S(1)} %get-tuple-element.18), channel_id=1, source_target_pairs={{0,1},{1,0},{2,3},{3,2},{4,5},{5,4},{6,7},{7,6},{8,9},{9,8},{10,11... | collective-permute-start | bytes 528392 | tf_op jit(solution)/shard_map/ppermute | solution.py:700
  4.8 4.5 %collective-permute-start.1 = (f32[43,8,128]{2,1,0:T(8,128)S(1)}, f32[43,8,128]{2,1,0:T(8,128)S(1)}, u32[]{:S(2)}, u32[]{:S(2)}) collective-permute-start(f32[43,8,128]{2,1,0:T(8,128)S(1)} %get-tuple-element.19), channel_id=1, source_target_pairs={{1,2},{2,1},{5,6},{6,5},{9,10},{10,9},{13,14},{14,13},{17,18},{18,... | collective-permute-start | bytes 528392 | tf_op jit(solution)/shard_map/ppermute | solution.py:700
  9.5 1.8 %collective-permute-start.2 = (f32[106,8,128]{2,1,0:T(8,128)S(1)}, f32[106,8,128]{2,1,0:T(8,128)S(1)}, u32[]{:S(2)}, u32[]{:S(2)}) collective-permute-start(f32[106,8,128]{2,1,0:T(8,128)S(1)} %get-tuple-element.20), channel_id=1, source_target_pairs={{0,4},{4,0},{8,12},{12,8},{16,20},{20,16},{24,28},{28,24},{1,5},{5... | collective-permute-start | bytes 1302536 | tf_op jit(solution)/shard_map/ppermute | solution.py:700
  9.5 1.8 %collective-permute-start.3 = (f32[106,8,128]{2,1,0:T(8,128)S(1)}, f32[106,8,128]{2,1,0:T(8,128)S(1)}, u32[]{:S(2)}, u32[]{:S(2)}) collective-permute-start(f32[106,8,128]{2,1,0:T(8,128)S(1)} %get-tuple-element.21), channel_id=1, source_target_pairs={{4,8},{12,16},{20,24},{8,4},{16,12},{24,20},{5,9},{13,17},{21,25},... | collective-permute-start | bytes 1302536 | tf_op jit(solution)/shard_map/ppermute | solution.py:700

commit v6 on v5

--- a/solution.py
+++ b/solution.py
@@ -44,11 +44,13 @@
 
 Y_CODE1, Y_CODE2, Y_CODE3, Y_POP, Y_COT = 38, 39, 40, 41, 42
 Y_TILES = 43
+SPARE = 1
 X_EXTRA, X_CODE13 = 19, 20
 X_LANE = 21
 X_RING = 4 * X_LANE
 X_CODE2 = X_RING + Q + 1
 X_TILES = X_CODE2 + 2
+X_SIDE = 2 * X_LANE
 F_CODE1, F_CODE2, F_CODE3, F_PHI = 0, 5, 9, 13
 FIELDS = 18
 OWN_PHI = 4
@@ -248,8 +250,8 @@
 
 
 class Deal:
-    def __init__(self, even, first, second):
-        self.even, self.refs, self.held = even, (first, second), {}
+    def __init__(self, even, first, second, skip=0):
+        self.even, self.first, self.second, self.skip, self.held = even, first, second, skip, {}
 
     def put(self, way, at, value):
         if (-way, at) not in self.held:
@@ -257,8 +259,16 @@
             return
         other = self.held.pop((-way, at))
         up, down = (value, other) if way == 1 else (other, value)
-        self.refs[0][at] = jnp.where(self.even, up, down)
-        self.refs[1][at] = jnp.where(self.even, down, up)
+        self.first[at - self.skip] = jnp.where(self.even, up, down)
+        self.second[at - self.skip] = jnp.where(self.even, down, up)
+
+
+class Joined:
+    def __init__(self, first, second, cut):
+        self.first, self.second, self.cut = first, second, cut
+
+    def __getitem__(self, at):
+        return self.first[at] if at < self.cut else self.second[at - self.cut]
 
 
 def is_even(axis):
@@ -273,6 +283,8 @@
     porosity_hbm,
     first_ref,
     second_ref,
+    first_side_ref,
+    second_side_ref,
     own_ref,
     state_ref,
     own_cot_ref,
@@ -352,9 +364,17 @@
             value = columns(tile_of(cot_ref, i, near), k - (1 if way == 1 else 2))
             extra = value if extra is None else jnp.where(column == k, value, extra)
         deal.put(way, Y_COT, extra)
+    second_ref[Y_TILES] = jnp.zeros((ROWS, LANES), jnp.float32)
     for t in range(2):
         for i in range(Q):
             own_cot_ref[2 * i + t] = tile_of(cot_ref, i, t)
+        pack_lines(
+            Deal(is_even("gx"), first_side_ref, second_side_ref),
+            X_LANE * t,
+            lambda i: own_ref[2 * i + t],
+            lambda i: tile_of(cot_ref, i, t),
+            lambda s: codes[t][s - 1],
+        )
 
 
 def from_y(left_ref, right_ref):
@@ -447,28 +467,16 @@
     return population, cotangent, codes
 
 
-def pack_x(own_ref, cot_ref, field_ref, first_y_ref, second_y_ref, first_ref, second_ref):
+def pack_x(field_ref, first_y_ref, second_y_ref, early_a, early_b, first_ref, second_ref):
     row, lane, column, depth = iotas()
-    deal = Deal(is_even("gx"), first_ref, second_ref)
+    deal = Deal(is_even("gx"), first_ref, second_ref, X_SIDE)
     population, cotangent, codes = from_y(*sides(first_y_ref, second_y_ref, "gy"))
-
-    def own_codes(s, t):
-        value = field_ref[2 * s + t]
-        return jnp.where(depth == NZ - 1, field_ref[2 * OWN_PHI + t], value) if s == 1 else value
 
     def both_codes(at, first, second):
         second = lines(second, 4)
         deal.put(1, at, jnp.where(row >= 4, first, second))
         deal.put(-1, at, jnp.where(row < 4, first, second))
 
-    for t in range(2):
-        pack_lines(
-            deal,
-            X_LANE * t,
-            lambda i: own_ref[2 * i + t],
-            lambda i: cot_ref[2 * i + t],
-            lambda s: own_codes(s, t),
-        )
     for n, c in ((2, 1), (3, 4)):
         pack_lines(
             deal,
@@ -479,10 +487,11 @@
         )
     for n in range(Q + 1):
         value = population(n, 0) if n < Q else codes(1, 0)
-        first_ref[X_RING + n] = value
-        second_ref[X_RING + n] = value
-    both_codes(X_CODE2, own_codes(2, 0), own_codes(2, 1))
+        first_ref[X_RING + n - X_SIDE] = value
+        second_ref[X_RING + n - X_SIDE] = value
+    both_codes(X_CODE2, field_ref[4], field_ref[5])
     both_codes(X_CODE2 + 1, codes(2, 1), codes(2, 4))
+    second_ref[X_TILES - X_SIDE] = jnp.zeros((ROWS, LANES), jnp.float32)
 
 
 def sides(first_ref, second_ref, axis):
@@ -540,6 +549,8 @@
     names_ref,
     first_y_ref,
     second_y_ref,
+    first_side_ref,
+    second_side_ref,
     first_x_ref,
     second_x_ref,
     adjoint_ref,
@@ -558,7 +569,11 @@
         own_ref,
         own_field_ref,
         cot_ref,
-        sides(first_x_ref, second_x_ref, "gx"),
+        sides(
+            Joined(first_side_ref, first_x_ref, X_SIDE),
+            Joined(second_side_ref, second_x_ref, X_SIDE),
+            "gx",
+        ),
         pop_a,
         cot,
         field,
@@ -667,6 +682,7 @@
 
 VMEM = pl.BlockSpec(memory_space=pltpu.VMEM)
 HBM = pl.BlockSpec(memory_space=pltpu.HBM)
+ANY = pl.BlockSpec(memory_space=pl.ANY)
 
 
 def shape_of(*dims):
@@ -693,19 +709,21 @@
             name=name,
         )
 
-    def exchange(first, second, axis, size):
-        pairs = [(i, i ^ 1) for i in range(size) if i ^ 1 < size]
-        between = [(i, i + 1) for i in range(1, size - 1, 2)]
-        between += [(j, i) for i, j in between]
-        return lax.ppermute(first, axis, pairs), lax.ppermute(second, axis, between)
+    def swap(value, axis, size):
+        return lax.ppermute(value, axis, [(i, i ^ 1) for i in range(size) if i ^ 1 < size])
+
+    def swap_between(value, axis, size):
+        pairs = [(i, i + 1) for i in range(1, size - 1, 2)]
+        return lax.ppermute(value, axis, pairs + [(j, i) for i, j in pairs])
 
     arguments = [
         pltpu.with_memory_space_constraint(value, pltpu.HBM)
         for value in (checkpoint, cotangent, cell_codes, baffle_index, porosity)
     ]
-    first_y, second_y, own, state, cot, field, names = call(
+    first_y, second_y, first_side, second_side, own, state, cot, field, names = call(
         pack_own,
-        (tiles_of(Y_TILES),) * 2
+        (tiles_of(Y_TILES), tiles_of(Y_TILES + SPARE))
+        + (tiles_of(X_SIDE),) * 2
         + (tiles_of(2 * Q),) * 3
         + (tiles_of(2 * OWN_PHI + 2), jax.ShapeDtypeStruct((2, ROWS, LANES), jnp.int32)),
         [HBM] * 5,
@@ -719,16 +737,24 @@
         ],
         name="pack_own",
     )(*arguments)
-    first_y, second_y = exchange(first_y, second_y, "gy", size_y)
-    first_x, second_x = call(pack_x, (tiles_of(X_TILES),) * 2, [VMEM] * 5, name="pack_x")(
-        own, cot, field, first_y, second_y
-    )
-    first_x, second_x = exchange(first_x, second_x, "gx", size_x)
+    second_y = swap_between(second_y, "gy", size_y)
+    first_y = swap(first_y, "gy", size_y)
+    second_side = swap_between(second_side, "gx", size_x)
+    first_side = swap(first_side, "gx", size_x)
+    rest = X_TILES - X_SIDE
+    first_x, second_x = call(
+        pack_x,
+        (tiles_of(rest), tiles_of(rest + SPARE)),
+        [VMEM] * 3 + [ANY] * 2,
+        name="pack_x",
+    )(field, first_y, second_y, first_side, second_side)
+    second_x = swap_between(second_x, "gx", size_x)
+    first_x = swap(first_x, "gx", size_x)
 
     adjoint, sums = call(
         functools.partial(steps_kernel, sizes),
         (shape_of(Q, ROWS, 2 * LANES), shape_of(devices, panels)),
-        [VMEM] * 9,
+        [VMEM] * 11,
         [
             pltpu.VMEM((5 * Q, 5 * ROWS, LANES), jnp.float32),
             pltpu.VMEM((5 * Q, 5 * ROWS, LANES), jnp.float32),
@@ -739,7 +765,7 @@
             pltpu.VMEM((4, ROWS, LANES), jnp.float32),
         ],
         name="steps",
-    )(state, cot, own, field, names, first_y, second_y, first_x, second_x)
+    )(state, cot, own, field, names, first_y, second_y, first_side, second_side, first_x, second_x)
     gathered = lax.all_to_all(sums, ("gx", "gy"), 0, 0, tiled=True)
     totals = call(add_panels, shape_of(1, panels), [VMEM], name="add_panels")(
         gathered.reshape(devices, 1, panels)

time: 42.5 us -> 42.5 us (level)
  blocking collectives: 24.6 us -> 14.7 us
  starting transfers between devices: 4.42 us -> 10.7 us
  waiting for transfers between devices: 4.87 us -> 8.45 us
    all_to_all x1, blocking collectives: 24.6 us -> 14.7 us  [on_device(): gathered = lax.all_to_all(sums, ('gx', 'gy'), 0, 0, tiled=True)]
    ppermute x4 -> x6, starting transfers between devices: 4.42 us -> 10.7 us  [the longest x3 8.72 us: swap(): lax.ppermute(value, axis, [(i, i ^ 1) for i in range(size) if i ^ 1 < size])]
    ppermute x4 -> x6, waiting for transfers between devices: 4.87 us -> 8.45 us  [the longest x3 8.44 us: swap(): lax.ppermute(value, axis, [(i, i ^ 1) for i in range(size) if i ^ 1 < size])]
  transfers between devices with their start and end apart: 4 -> 6, of which waited for: 2 -> 3; matrix products, arithmetic and copies ran while one was open for 0% -> 0% of each run, Pallas kernels for 0% -> 0%
where the time goes in v6:
time: 42.5 us; the launch traced here: 42.2 us
  blocking collectives  14.7 us (35%)
  starting transfers between devices  10.7 us (25%)
  waiting for transfers between devices  8.45 us (20%)
  Pallas kernels  7.63 us (18%)
  between operations  0.68 us (2%)
    all_to_all x1, blocking collectives, on_device(): gathered = lax.all_to_all(sums, ('gx', 'gy'), 0, 0, tiled=True)  14.7 us
    ppermute x3, starting transfers between devices, swap(): lax.ppermute(value, axis, [(i, i ^ 1) for i in range(size) if i ^ 1 < size])  8.72 us
    ppermute x3, waiting for transfers between devices, swap(): lax.ppermute(value, axis, [(i, i ^ 1) for i in range(size) if i ^ 1 < size])  8.44 us
    pallas_call x1, Pallas kernels, on_device(): call(functools.partial(steps_kernel, sizes), (shape_of(Q, ROWS, 2 * LANES...  5.76 us
    ppermute x3, starting transfers between devices, swap_between(): return lax.ppermute(value, axis, pairs + [(j, i) for i, j in pairs])  2.01 us
    pallas_call x1, Pallas kernels, on_device(): call(pack_own, (tiles_of(Y_TILES), tiles_of(Y_TILES + SPARE)) + (tiles_of...  1.19 us
  transfers between devices with their start and end apart: 6, of which 3 were waited for; matrix products, arithmetic and copies ran while one was open for 0% of the time, Pallas kernels for 0%

profile of v6, /device:TPU:0, one launch (start us, length us, event | category | flops | bytes accessed | tf_op | source)
XLA Modules:
  0.0 42.2 jit_solution(14567936058301833346)
XLA Ops:
  0.6 1.2 %pack_own.1 = (f32[43,8,128]{2,1,0:T(8,128)S(1)}, f32[44,8,128]{2,1,0:T(8,128)S(1)}, f32[42,8,128]{2,1,0:T(8,128)S(1)}, f32[42,8,128]{2,1,0:T(8,128)S(1)}, f32[3...) custom-call(f32[19,8,256]{2,1,0:T(8,128)} %f_hbm.1, ...), custom_call_target="tpu_custom_call" | custom-call | tf_op jit(solution)/shard_map/pack_own/pallas_call | solution.py:723
  1.8 0.7 %collective-permute-start.1 = (f32[44,8,128]{2,1,0:T(8,128)S(1)}, f32[44,8,128]{2,1,0:T(8,128)S(1)}, u32[]{:S(2)}, u32[]{:S(2)}) collective-permute-start(f32[44,8,128]{2,1,0:T(8,128)S(1)} %get-tuple-element.21), channel_id=1, source_target_pairs={{1,2},{2,1},{5,6},{6,5},{9,10},{10,9},{13,14},{14,13},{17,18},{18,... | collective-permute-start | bytes 540680 | tf_op jit(solution)/shard_map/ppermute | solution.py:717
  2.5 5.7 %collective-permute-start = (f32[43,8,128]{2,1,0:T(8,128)S(1)}, f32[43,8,128]{2,1,0:T(8,128)S(1)}, u32[]{:S(2)}, u32[]{:S(2)}) collective-permute-start(f32[43,8,128]{2,1,0:T(8,128)S(1)} %get-tuple-element.20), channel_id=1, source_target_pairs={{0,1},{1,0},{2,3},{3,2},{4,5},{5,4},{6,7},{7,6},{8,9},{9,8},{10,11... | collective-permute-start | bytes 528392 | tf_op jit(solution)/shard_map/ppermute | solution.py:713
  8.2 0.0 collective-permute-start.2
  8.2 0.7 %collective-permute-start.3 = (f32[42,8,128]{2,1,0:T(8,128)S(1)}, f32[42,8,128]{2,1,0:T(8,128)S(1)}, u32[]{:S(2)}, u32[]{:S(2)}) collective-permute-start(f32[42,8,128]{2,1,0:T(8,128)S(1)} %get-tuple-element.23), channel_id=1, source_target_pairs={{4,8},{12,16},{20,24},{8,4},{16,12},{24,20},{5,9},{13,17},{21,25},... | collective-permute-start | bytes 516104 | tf_op jit(solution)/shard_map/ppermute | solution.py:717
  8.9 0.7 %collective-permute-done.2.early_a.first_side_ref = f32[42,8,128]{2,1,0:T(8,128)S(1)} collective-permute-done((f32[42,8,128]{2,1,0:T(8,128)S(1)}, f32[42,8,128]{2,1,0:T(8,128)S(1)}, u32[]{:S(2)}, u32[]{:S(2)}) %collective-permute-start.2) | collective-permute-done | bytes 172064 | tf_op jit(solution)/shard_map/ppermute | solution.py:713
  9.6 0.0 collective-permute-done.3.early_b.second_side_ref
  9.7 6.5 %collective-permute-done.first_y_ref = f32[43,8,128]{2,1,0:T(8,128)S(1)} collective-permute-done((f32[43,8,128]{2,1,0:T(8,128)S(1)}, f32[43,8,128]{2,1,0:T(8,128)S(1)}, u32[]{:S(2)}, u32[]{:S(2)}) %collective-permute-start) | collective-permute-done | bytes 176160 | tf_op jit(solution)/shard_map/ppermute | solution.py:713
  16.2 0.0 collective-permute-done.1.second_y_ref
  16.2 0.1 pack_x.1
  16.3 0.7 %collective-permute-start.5 = (f32[65,8,128]{2,1,0:T(8,128)S(1)}, f32[65,8,128]{2,1,0:T(8,128)S(1)}, u32[]{:S(2)}, u32[]{:S(2)}) collective-permute-start(f32[65,8,128]{2,1,0:T(8,128)S(1)} %get-tuple-element.25), channel_id=1, source_target_pairs={{4,8},{12,16},{20,24},{8,4},{16,12},{24,20},{5,9},{13,17},{21,25},... | collective-permute-start | bytes 798728 | tf_op jit(solution)/shard_map/ppermute | solution.py:717
  17.0 3.0 %collective-permute-start.4 = (f32[64,8,128]{2,1,0:T(8,128)S(1)}, f32[64,8,128]{2,1,0:T(8,128)S(1)}, u32[]{:S(2)}, u32[]{:S(2)}) collective-permute-start(f32[64,8,128]{2,1,0:T(8,128)S(1)} %get-tuple-element.24), channel_id=1, source_target_pairs={{0,4},{4,0},{8,12},{12,8},{16,20},{20,16},{24,28},{28,24},{1,5},{5... | collective-permute-start | bytes 786440 | tf_op jit(solution)/shard_map/ppermute | solution.py:713
  20.0 1.2 %collective-permute-done.4.first_x_ref = f32[64,8,128]{2,1,0:T(8,128)S(1)} collective-permute-done((f32[64,8,128]{2,1,0:T(8,128)S(1)}, f32[64,8,128]{2,1,0:T(8,128)S(1)}, u32[]{:S(2)}, u32[]{:S(2)}) %collective-permute-start.4) | collective-permute-done | bytes 262176 | tf_op jit(solution)/shard_map/ppermute | solution.py:713
  21.2 0.0 collective-permute-done.5.second_x_ref
  21.2 5.8 %steps.1 = (f32[19,8,256]{2,1,0:T(8,128)}, f32[32,64]{1,0:T(8,128)S(1)}) custom-call(f32[38,8,128]{2,1,0:T(8,128)S(1)} %get-tuple-element.15.state_ref, f32[38,8,128]{2,1,0:T(8,128)S(1)} %get-tuple-element.16.cot_ref, f32[38,8,128]{2,1,0:T(8,128)S(1)} %get-tuple-element.17.own_ref, f32[10,8,128]{2,1,0:T(8,128)S(1)} %get-tuple-element.18.field_ref.own_field_ref, ...), custom_call_target="tpu_custom_call" | custom-call | tf_op jit(solution)/shard_map/steps/pallas_call | solution.py:754
  26.9 14.7 %all_to_all.9.parts_ref = f32[32,1,64]{2,1,0:T(1,128)S(1)} all-to-all(f32[32,1,64]{2,1,0:T(1,128)S(1)} %bitcast.2), channel_id=1, replica_groups=mesh['gx'=8,'gy'=4] {'gx','gy'}, dimensions={0} | all-to-all | bytes 16384 | tf_op jit(solution)/shard_map/all_to_all | solution.py:769
  41.6 0.5 %add_panels.1 = f32[1,64]{1,0:T(1,128)} custom-call(f32[32,1,64]{2,1,0:T(1,128)S(1)} %all_to_all.9.parts_ref), custom_call_target="tpu_custom_call" | custom-call | tf_op jit(solution)/shard_map/add_panels/pallas_call | solution.py:770
Async XLA Ops:
  1.8 14.4 %collective-permute-start.1 = (f32[44,8,128]{2,1,0:T(8,128)S(1)}, f32[44,8,128]{2,1,0:T(8,128)S(1)}, u32[]{:S(2)}, u32[]{:S(2)}) collective-permute-start(f32[44,8,128]{2,1,0:T(8,128)S(1)} %get-tuple-element.21), channel_id=1, source_target_pairs={{1,2},{2,1},{5,6},{6,5},{9,10},{10,9},{13,14},{14,13},{17,18},{18,... | collective-permute-start | bytes 540680 | tf_op jit(solution)/shard_map/ppermute | solution.py:717
  2.5 13.7 %collective-permute-start = (f32[43,8,128]{2,1,0:T(8,128)S(1)}, f32[43,8,128]{2,1,0:T(8,128)S(1)}, u32[]{:S(2)}, u32[]{:S(2)}) collective-permute-start(f32[43,8,128]{2,1,0:T(8,128)S(1)} %get-tuple-element.20), channel_id=1, source_target_pairs={{0,1},{1,0},{2,3},{3,2},{4,5},{5,4},{6,7},{7,6},{8,9},{9,8},{10,11... | collective-permute-start | bytes 528392 | tf_op jit(solution)/shard_map/ppermute | solution.py:713
  8.2 1.4 %collective-permute-start.2 = (f32[42,8,128]{2,1,0:T(8,128)S(1)}, f32[42,8,128]{2,1,0:T(8,128)S(1)}, u32[]{:S(2)}, u32[]{:S(2)}) collective-permute-start(f32[42,8,128]{2,1,0:T(8,128)S(1)} %get-tuple-element.22), channel_id=1, source_target_pairs={{0,4},{4,0},{8,12},{12,8},{16,20},{20,16},{24,28},{28,24},{1,5},{5... | collective-permute-start | bytes 516104 | tf_op jit(solution)/shard_map/ppermute | solution.py:713
  8.2 1.4 %collective-permute-start.3 = (f32[42,8,128]{2,1,0:T(8,128)S(1)}, f32[42,8,128]{2,1,0:T(8,128)S(1)}, u32[]{:S(2)}, u32[]{:S(2)}) collective-permute-start(f32[42,8,128]{2,1,0:T(8,128)S(1)} %get-tuple-element.23), channel_id=1, source_target_pairs={{4,8},{12,16},{20,24},{8,4},{16,12},{24,20},{5,9},{13,17},{21,25},... | collective-permute-start | bytes 516104 | tf_op jit(solution)/shard_map/ppermute | solution.py:717
  16.3 4.8 %collective-permute-start.5 = (f32[65,8,128]{2,1,0:T(8,128)S(1)}, f32[65,8,128]{2,1,0:T(8,128)S(1)}, u32[]{:S(2)}, u32[]{:S(2)}) collective-permute-start(f32[65,8,128]{2,1,0:T(8,128)S(1)} %get-tuple-element.25), channel_id=1, source_target_pairs={{4,8},{12,16},{20,24},{8,4},{16,12},{24,20},{5,9},{13,17},{21,25},... | collective-permute-start | bytes 798728 | tf_op jit(solution)/shard_map/ppermute | solution.py:717
  17.0 4.2 %collective-permute-start.4 = (f32[64,8,128]{2,1,0:T(8,128)S(1)}, f32[64,8,128]{2,1,0:T(8,128)S(1)}, u32[]{:S(2)}, u32[]{:S(2)}) collective-permute-start(f32[64,8,128]{2,1,0:T(8,128)S(1)} %get-tuple-element.24), channel_id=1, source_target_pairs={{0,4},{4,0},{8,12},{12,8},{16,20},{20,16},{24,28},{28,24},{1,5},{5... | collective-permute-start | bytes 786440 | tf_op jit(solution)/shard_map/ppermute | solution.py:713

commit v7 on v6

--- a/solution.py
+++ b/solution.py
@@ -364,7 +364,6 @@
             value = columns(tile_of(cot_ref, i, near), k - (1 if way == 1 else 2))
             extra = value if extra is None else jnp.where(column == k, value, extra)
         deal.put(way, Y_COT, extra)
-    second_ref[Y_TILES] = jnp.zeros((ROWS, LANES), jnp.float32)
     for t in range(2):
         for i in range(Q):
             own_cot_ref[2 * i + t] = tile_of(cot_ref, i, t)
@@ -722,7 +721,7 @@
     ]
     first_y, second_y, first_side, second_side, own, state, cot, field, names = call(
         pack_own,
-        (tiles_of(Y_TILES), tiles_of(Y_TILES + SPARE))
+        (tiles_of(Y_TILES),) * 2
         + (tiles_of(X_SIDE),) * 2
         + (tiles_of(2 * Q),) * 3
         + (tiles_of(2 * OWN_PHI + 2), jax.ShapeDtypeStruct((2, ROWS, LANES), jnp.int32)),

time: 42.5 us -> 41.4 us (0.974)
  waiting for transfers between devices: 8.45 us -> 4.2 us
  blocking collectives: 14.7 us -> 17.5 us
    ppermute x3, waiting for transfers between devices: 8.44 us -> 4.19 us  [swap(): lax.ppermute(value, axis, [(i, i ^ 1) for i in range(size) if i ^ 1 < size])]
    all_to_all x1, blocking collectives: 14.7 us -> 17.5 us  [on_device(): gathered = lax.all_to_all(sums, ('gx', 'gy'), 0, 0, tiled=True)]
where the time goes in v7:
time: 41.4 us; the launch traced here: 41.1 us
  blocking collectives  17.5 us (42%)
  starting transfers between devices  11.1 us (27%)
  Pallas kernels  7.64 us (18%)
  waiting for transfers between devices  4.2 us (10%)
  between operations  0.68 us (2%)
    all_to_all x1, blocking collectives, on_device(): gathered = lax.all_to_all(sums, ('gx', 'gy'), 0, 0, tiled=True)  17.5 us
    ppermute x3, starting transfers between devices, swap(): lax.ppermute(value, axis, [(i, i ^ 1) for i in range(size) if i ^ 1 < size])  9.08 us
    pallas_call x1, Pallas kernels, on_device(): call(functools.partial(steps_kernel, sizes), (shape_of(Q, ROWS, 2 * LANES...  5.76 us
    ppermute x3, waiting for transfers between devices, swap(): lax.ppermute(value, axis, [(i, i ^ 1) for i in range(size) if i ^ 1 < size])  4.19 us
    ppermute x3, starting transfers between devices, swap_between(): return lax.ppermute(value, axis, pairs + [(j, i) for i, j in pairs])  2.01 us
    pallas_call x1, Pallas kernels, on_device(): call(pack_own, (tiles_of(Y_TILES),) * 2 + (tiles_of(X_SIDE),) * 2 + (tile...  1.19 us
  transfers between devices with their start and end apart: 6, of which 3 were waited for; matrix products, arithmetic and copies ran while one was open for 0% of the time, Pallas kernels for 0%

profile of v7, /device:TPU:0, one launch (start us, length us, event | category | flops | bytes accessed | tf_op | source)
XLA Modules:
  0.0 41.1 jit_solution(10159663862279001537)
XLA Ops:
  0.6 1.2 %pack_own.1 = (f32[43,8,128]{2,1,0:T(8,128)S(1)}, f32[43,8,128]{2,1,0:T(8,128)S(1)}, f32[42,8,128]{2,1,0:T(8,128)S(1)}, f32[42,8,128]{2,1,0:T(8,128)S(1)}, f32[3...) custom-call(f32[19,8,256]{2,1,0:T(8,128)} %f_hbm.1, ...), custom_call_target="tpu_custom_call" | custom-call | tf_op jit(solution)/shard_map/pack_own/pallas_call | solution.py:722
  1.8 3.0 %collective-permute-start = (f32[43,8,128]{2,1,0:T(8,128)S(1)}, f32[43,8,128]{2,1,0:T(8,128)S(1)}, u32[]{:S(2)}, u32[]{:S(2)}) collective-permute-start(f32[43,8,128]{2,1,0:T(8,128)S(1)} %get-tuple-element.20), channel_id=1, source_target_pairs={{0,1},{1,0},{2,3},{3,2},{4,5},{5,4},{6,7},{7,6},{8,9},{9,8},{10,11... | collective-permute-start | bytes 528392 | tf_op jit(solution)/shard_map/ppermute | solution.py:712
  4.8 0.7 %collective-permute-start.1 = (f32[43,8,128]{2,1,0:T(8,128)S(1)}, f32[43,8,128]{2,1,0:T(8,128)S(1)}, u32[]{:S(2)}, u32[]{:S(2)}) collective-permute-start(f32[43,8,128]{2,1,0:T(8,128)S(1)} %get-tuple-element.21), channel_id=1, source_target_pairs={{1,2},{2,1},{5,6},{6,5},{9,10},{10,9},{13,14},{14,13},{17,18},{18,... | collective-permute-start | bytes 528392 | tf_op jit(solution)/shard_map/ppermute | solution.py:716
  5.5 0.1 collective-permute-start.2
  5.6 0.7 %collective-permute-start.3 = (f32[42,8,128]{2,1,0:T(8,128)S(1)}, f32[42,8,128]{2,1,0:T(8,128)S(1)}, u32[]{:S(2)}, u32[]{:S(2)}) collective-permute-start(f32[42,8,128]{2,1,0:T(8,128)S(1)} %get-tuple-element.23), channel_id=1, source_target_pairs={{4,8},{12,16},{20,24},{8,4},{16,12},{24,20},{5,9},{13,17},{21,25},... | collective-permute-start | bytes 516104 | tf_op jit(solution)/shard_map/ppermute | solution.py:716
  6.3 0.7 %collective-permute-done.2.early_a.first_side_ref = f32[42,8,128]{2,1,0:T(8,128)S(1)} collective-permute-done((f32[42,8,128]{2,1,0:T(8,128)S(1)}, f32[42,8,128]{2,1,0:T(8,128)S(1)}, u32[]{:S(2)}, u32[]{:S(2)}) %collective-permute-start.2) | collective-permute-done | bytes 172064 | tf_op jit(solution)/shard_map/ppermute | solution.py:712
  7.0 0.0 collective-permute-done.3.early_b.second_side_ref
  7.0 2.3 %collective-permute-done.first_y_ref = f32[43,8,128]{2,1,0:T(8,128)S(1)} collective-permute-done((f32[43,8,128]{2,1,0:T(8,128)S(1)}, f32[43,8,128]{2,1,0:T(8,128)S(1)}, u32[]{:S(2)}, u32[]{:S(2)}) %collective-permute-start) | collective-permute-done | bytes 176160 | tf_op jit(solution)/shard_map/ppermute | solution.py:712
  9.3 0.0 collective-permute-done.1.second_y_ref
  9.3 0.1 pack_x.1
  9.5 0.7 %collective-permute-start.5 = (f32[65,8,128]{2,1,0:T(8,128)S(1)}, f32[65,8,128]{2,1,0:T(8,128)S(1)}, u32[]{:S(2)}, u32[]{:S(2)}) collective-permute-start(f32[65,8,128]{2,1,0:T(8,128)S(1)} %get-tuple-element.25), channel_id=1, source_target_pairs={{4,8},{12,16},{20,24},{8,4},{16,12},{24,20},{5,9},{13,17},{21,25},... | collective-permute-start | bytes 798728 | tf_op jit(solution)/shard_map/ppermute | solution.py:716
  10.1 6.0 %collective-permute-start.4 = (f32[64,8,128]{2,1,0:T(8,128)S(1)}, f32[64,8,128]{2,1,0:T(8,128)S(1)}, u32[]{:S(2)}, u32[]{:S(2)}) collective-permute-start(f32[64,8,128]{2,1,0:T(8,128)S(1)} %get-tuple-element.24), channel_id=1, source_target_pairs={{0,4},{4,0},{8,12},{12,8},{16,20},{20,16},{24,28},{28,24},{1,5},{5... | collective-permute-start | bytes 786440 | tf_op jit(solution)/shard_map/ppermute | solution.py:712
  16.1 1.2 %collective-permute-done.4.first_x_ref = f32[64,8,128]{2,1,0:T(8,128)S(1)} collective-permute-done((f32[64,8,128]{2,1,0:T(8,128)S(1)}, f32[64,8,128]{2,1,0:T(8,128)S(1)}, u32[]{:S(2)}, u32[]{:S(2)}) %collective-permute-start.4) | collective-permute-done | bytes 262176 | tf_op jit(solution)/shard_map/ppermute | solution.py:712
  17.3 0.0 collective-permute-done.5.second_x_ref
  17.3 5.8 %steps.1 = (f32[19,8,256]{2,1,0:T(8,128)}, f32[32,64]{1,0:T(8,128)S(1)}) custom-call(f32[38,8,128]{2,1,0:T(8,128)S(1)} %get-tuple-element.15.state_ref, f32[38,8,128]{2,1,0:T(8,128)S(1)} %get-tuple-element.16.cot_ref, f32[38,8,128]{2,1,0:T(8,128)S(1)} %get-tuple-element.17.own_ref, f32[10,8,128]{2,1,0:T(8,128)S(1)} %get-tuple-element.18.field_ref.own_field_ref, ...), custom_call_target="tpu_custom_call" | custom-call | tf_op jit(solution)/shard_map/steps/pallas_call | solution.py:753
  23.1 17.5 %all_to_all.9.parts_ref = f32[32,1,64]{2,1,0:T(1,128)S(1)} all-to-all(f32[32,1,64]{2,1,0:T(1,128)S(1)} %bitcast.2), channel_id=1, replica_groups=mesh['gx'=8,'gy'=4] {'gx','gy'}, dimensions={0} | all-to-all | bytes 16384 | tf_op jit(solution)/shard_map/all_to_all | solution.py:768
  40.6 0.5 %add_panels.1 = f32[1,64]{1,0:T(1,128)} custom-call(f32[32,1,64]{2,1,0:T(1,128)S(1)} %all_to_all.9.parts_ref), custom_call_target="tpu_custom_call" | custom-call | tf_op jit(solution)/shard_map/add_panels/pallas_call | solution.py:769
Async XLA Ops:
  1.8 7.5 %collective-permute-start = (f32[43,8,128]{2,1,0:T(8,128)S(1)}, f32[43,8,128]{2,1,0:T(8,128)S(1)}, u32[]{:S(2)}, u32[]{:S(2)}) collective-permute-start(f32[43,8,128]{2,1,0:T(8,128)S(1)} %get-tuple-element.20), channel_id=1, source_target_pairs={{0,1},{1,0},{2,3},{3,2},{4,5},{5,4},{6,7},{7,6},{8,9},{9,8},{10,11... | collective-permute-start | bytes 528392 | tf_op jit(solution)/shard_map/ppermute | solution.py:712
  4.8 4.5 %collective-permute-start.1 = (f32[43,8,128]{2,1,0:T(8,128)S(1)}, f32[43,8,128]{2,1,0:T(8,128)S(1)}, u32[]{:S(2)}, u32[]{:S(2)}) collective-permute-start(f32[43,8,128]{2,1,0:T(8,128)S(1)} %get-tuple-element.21), channel_id=1, source_target_pairs={{1,2},{2,1},{5,6},{6,5},{9,10},{10,9},{13,14},{14,13},{17,18},{18,... | collective-permute-start | bytes 528392 | tf_op jit(solution)/shard_map/ppermute | solution.py:716
  5.5 1.5 %collective-permute-start.2 = (f32[42,8,128]{2,1,0:T(8,128)S(1)}, f32[42,8,128]{2,1,0:T(8,128)S(1)}, u32[]{:S(2)}, u32[]{:S(2)}) collective-permute-start(f32[42,8,128]{2,1,0:T(8,128)S(1)} %get-tuple-element.22), channel_id=1, source_target_pairs={{0,4},{4,0},{8,12},{12,8},{16,20},{20,16},{24,28},{28,24},{1,5},{5... | collective-permute-start | bytes 516104 | tf_op jit(solution)/shard_map/ppermute | solution.py:712
  5.6 1.4 %collective-permute-start.3 = (f32[42,8,128]{2,1,0:T(8,128)S(1)}, f32[42,8,128]{2,1,0:T(8,128)S(1)}, u32[]{:S(2)}, u32[]{:S(2)}) collective-permute-start(f32[42,8,128]{2,1,0:T(8,128)S(1)} %get-tuple-element.23), channel_id=1, source_target_pairs={{4,8},{12,16},{20,24},{8,4},{16,12},{24,20},{5,9},{13,17},{21,25},... | collective-permute-start | bytes 516104 | tf_op jit(solution)/shard_map/ppermute | solution.py:716
  9.5 7.9 %collective-permute-start.5 = (f32[65,8,128]{2,1,0:T(8,128)S(1)}, f32[65,8,128]{2,1,0:T(8,128)S(1)}, u32[]{:S(2)}, u32[]{:S(2)}) collective-permute-start(f32[65,8,128]{2,1,0:T(8,128)S(1)} %get-tuple-element.25), channel_id=1, source_target_pairs={{4,8},{12,16},{20,24},{8,4},{16,12},{24,20},{5,9},{13,17},{21,25},... | collective-permute-start | bytes 798728 | tf_op jit(solution)/shard_map/ppermute | solution.py:716
  10.1 7.2 %collective-permute-start.4 = (f32[64,8,128]{2,1,0:T(8,128)S(1)}, f32[64,8,128]{2,1,0:T(8,128)S(1)}, u32[]{:S(2)}, u32[]{:S(2)}) collective-permute-start(f32[64,8,128]{2,1,0:T(8,128)S(1)} %get-tuple-element.24), channel_id=1, source_target_pairs={{0,4},{4,0},{8,12},{12,8},{16,20},{20,16},{24,28},{28,24},{1,5},{5... | collective-permute-start | bytes 786440 | tf_op jit(solution)/shard_map/ppermute | solution.py:712

commit v8 on v7

--- a/solution.py
+++ b/solution.py
@@ -752,7 +752,7 @@
 
     adjoint, sums = call(
         functools.partial(steps_kernel, sizes),
-        (shape_of(Q, ROWS, 2 * LANES), shape_of(devices, panels)),
+        (shape_of(Q, ROWS, 2 * LANES), shape_of(1, panels)),
         [VMEM] * 11,
         [
             pltpu.VMEM((5 * Q, 5 * ROWS, LANES), jnp.float32),
@@ -765,7 +765,7 @@
         ],
         name="steps",
     )(state, cot, own, field, names, first_y, second_y, first_side, second_side, first_x, second_x)
-    gathered = lax.all_to_all(sums, ("gx", "gy"), 0, 0, tiled=True)
+    gathered = lax.all_gather(sums, ("gx", "gy"), tiled=True)
     totals = call(add_panels, shape_of(1, panels), [VMEM], name="add_panels")(
         gathered.reshape(devices, 1, panels)
     )

time: 41.4 us -> 91 us (2.20)
  blocking collectives: 17.5 us -> 67.1 us
    all_gather x0 -> x1, blocking collectives: none -> 67.1 us  [on_device(): gathered = lax.all_gather(sums, ('gx', 'gy'), tiled=True)]
    all_to_all x1 -> x0, blocking collectives: 17.5 us -> none  [on_device(): gathered = lax.all_to_all(sums, ('gx', 'gy'), 0, 0, tiled=True)]
where the time goes in v8:
time: 91 us; the launch traced here: 90.7 us
  blocking collectives  67.1 us (74%)
  starting transfers between devices  11.1 us (12%)
  Pallas kernels  7.64 us (8%)
  waiting for transfers between devices  4.2 us (5%)
    all_gather x1, blocking collectives, on_device(): gathered = lax.all_gather(sums, ('gx', 'gy'), tiled=True)  67.1 us
    ppermute x3, starting transfers between devices, swap(): lax.ppermute(value, axis, [(i, i ^ 1) for i in range(size) if i ^ 1 < size])  9.08 us
    pallas_call x1, Pallas kernels, on_device(): call(functools.partial(steps_kernel, sizes), (shape_of(Q, ROWS, 2 * LANES...  5.75 us
    ppermute x3, waiting for transfers between devices, swap(): lax.ppermute(value, axis, [(i, i ^ 1) for i in range(size) if i ^ 1 < size])  4.19 us
    ppermute x3, starting transfers between devices, swap_between(): return lax.ppermute(value, axis, pairs + [(j, i) for i, j in pairs])  2.01 us
  transfers between devices with their start and end apart: 6, of which 3 were waited for; matrix products, arithmetic and copies ran while one was open for 0% of the time, Pallas kernels for 0%

profile of v8, /device:TPU:0, one launch (start us, length us, event | category | flops | bytes accessed | tf_op | source)
XLA Modules:
  0.0 90.7 jit_solution(14645490718276064325)
XLA Ops:
  0.6 1.2 %pack_own.1 = (f32[43,8,128]{2,1,0:T(8,128)S(1)}, f32[43,8,128]{2,1,0:T(8,128)S(1)}, f32[42,8,128]{2,1,0:T(8,128)S(1)}, f32[42,8,128]{2,1,0:T(8,128)S(1)}, f32[3...) custom-call(f32[19,8,256]{2,1,0:T(8,128)} %f_hbm.1, ...), custom_call_target="tpu_custom_call" | custom-call | tf_op jit(solution)/shard_map/pack_own/pallas_call | solution.py:722
  1.8 3.0 %collective-permute-start = (f32[43,8,128]{2,1,0:T(8,128)S(1)}, f32[43,8,128]{2,1,0:T(8,128)S(1)}, u32[]{:S(2)}, u32[]{:S(2)}) collective-permute-start(f32[43,8,128]{2,1,0:T(8,128)S(1)} %get-tuple-element.20), channel_id=1, source_target_pairs={{0,1},{1,0},{2,3},{3,2},{4,5},{5,4},{6,7},{7,6},{8,9},{9,8},{10,11... | collective-permute-start | bytes 528392 | tf_op jit(solution)/shard_map/ppermute | solution.py:712
  4.8 0.7 collective-permute-start.1
  5.5 0.1 collective-permute-start.2
  5.6 0.7 collective-permute-start.3
  6.3 0.7 collective-permute-done.2.early_a.first_side_ref
  7.0 0.0 collective-permute-done.3.early_b.second_side_ref
  7.0 2.3 %collective-permute-done.first_y_ref = f32[43,8,128]{2,1,0:T(8,128)S(1)} collective-permute-done((f32[43,8,128]{2,1,0:T(8,128)S(1)}, f32[43,8,128]{2,1,0:T(8,128)S(1)}, u32[]{:S(2)}, u32[]{:S(2)}) %collective-permute-start) | collective-permute-done | bytes 176160 | tf_op jit(solution)/shard_map/ppermute | solution.py:712
  9.3 0.0 collective-permute-done.1.second_y_ref
  9.3 0.1 pack_x.1
  9.5 0.7 collective-permute-start.5
  10.1 6.0 %collective-permute-start.4 = (f32[64,8,128]{2,1,0:T(8,128)S(1)}, f32[64,8,128]{2,1,0:T(8,128)S(1)}, u32[]{:S(2)}, u32[]{:S(2)}) collective-permute-start(f32[64,8,128]{2,1,0:T(8,128)S(1)} %get-tuple-element.24), channel_id=1, source_target_pairs={{0,4},{4,0},{8,12},{12,8},{16,20},{20,16},{24,28},{28,24},{1,5},{5... | collective-permute-start | bytes 786440 | tf_op jit(solution)/shard_map/ppermute | solution.py:712
  16.1 1.2 %collective-permute-done.4.first_x_ref = f32[64,8,128]{2,1,0:T(8,128)S(1)} collective-permute-done((f32[64,8,128]{2,1,0:T(8,128)S(1)}, f32[64,8,128]{2,1,0:T(8,128)S(1)}, u32[]{:S(2)}, u32[]{:S(2)}) %collective-permute-start.4) | collective-permute-done | bytes 262176 | tf_op jit(solution)/shard_map/ppermute | solution.py:712
  17.3 0.0 collective-permute-done.5.second_x_ref
  17.3 5.8 %steps.1 = (f32[19,8,256]{2,1,0:T(8,128)}, f32[1,64]{1,0:T(1,128)S(1)}) custom-call(f32[38,8,128]{2,1,0:T(8,128)S(1)} %get-tuple-element.15.state_ref, f32[38,8,128]{2,1,0:T(8,128)S(1)} %get-tuple-element.16.cot_ref, f32[38,8,128]{2,1,0:T(8,128)S(1)} %get-tuple-element.17.own_ref, f32[10,8,128]{2,1,0:T(8,128)S(1)} %get-tuple-element.18.field_ref.own_field_ref, ...), custom_call_target="tpu_custom_call" | custom-call | tf_op jit(solution)/shard_map/steps/pallas_call | solution.py:753
  23.1 67.1 %all-gather.parts_ref = f32[32,1,64]{2,1,0:T(1,128)S(1)} all-gather(f32[1,1,64]{2,1,0:T(1,128)S(1)} %bitcast.2), channel_id=1, replica_groups=mesh['gx'=8,'gy'=4] {'gx','gy'}, dimensions={0}, use_global_device_ids=true | all-gather | bytes 8448 | tf_op jit(solution)/shard_map/all_gather | solution.py:768
  90.2 0.5 add_panels.1
Async XLA Ops:
  1.8 7.5 %collective-permute-start = (f32[43,8,128]{2,1,0:T(8,128)S(1)}, f32[43,8,128]{2,1,0:T(8,128)S(1)}, u32[]{:S(2)}, u32[]{:S(2)}) collective-permute-start(f32[43,8,128]{2,1,0:T(8,128)S(1)} %get-tuple-element.20), channel_id=1, source_target_pairs={{0,1},{1,0},{2,3},{3,2},{4,5},{5,4},{6,7},{7,6},{8,9},{9,8},{10,11... | collective-permute-start | bytes 528392 | tf_op jit(solution)/shard_map/ppermute | solution.py:712
  4.8 4.5 %collective-permute-start.1 = (f32[43,8,128]{2,1,0:T(8,128)S(1)}, f32[43,8,128]{2,1,0:T(8,128)S(1)}, u32[]{:S(2)}, u32[]{:S(2)}) collective-permute-start(f32[43,8,128]{2,1,0:T(8,128)S(1)} %get-tuple-element.21), channel_id=1, source_target_pairs={{1,2},{2,1},{5,6},{6,5},{9,10},{10,9},{13,14},{14,13},{17,18},{18,... | collective-permute-start | bytes 528392 | tf_op jit(solution)/shard_map/ppermute | solution.py:716
  5.5 1.5 %collective-permute-start.2 = (f32[42,8,128]{2,1,0:T(8,128)S(1)}, f32[42,8,128]{2,1,0:T(8,128)S(1)}, u32[]{:S(2)}, u32[]{:S(2)}) collective-permute-start(f32[42,8,128]{2,1,0:T(8,128)S(1)} %get-tuple-element.22), channel_id=1, source_target_pairs={{0,4},{4,0},{8,12},{12,8},{16,20},{20,16},{24,28},{28,24},{1,5},{5... | collective-permute-start | bytes 516104 | tf_op jit(solution)/shard_map/ppermute | solution.py:712
  5.6 1.4 %collective-permute-start.3 = (f32[42,8,128]{2,1,0:T(8,128)S(1)}, f32[42,8,128]{2,1,0:T(8,128)S(1)}, u32[]{:S(2)}, u32[]{:S(2)}) collective-permute-start(f32[42,8,128]{2,1,0:T(8,128)S(1)} %get-tuple-element.23), channel_id=1, source_target_pairs={{4,8},{12,16},{20,24},{8,4},{16,12},{24,20},{5,9},{13,17},{21,25},... | collective-permute-start | bytes 516104 | tf_op jit(solution)/shard_map/ppermute | solution.py:716
  9.5 7.9 %collective-permute-start.5 = (f32[65,8,128]{2,1,0:T(8,128)S(1)}, f32[65,8,128]{2,1,0:T(8,128)S(1)}, u32[]{:S(2)}, u32[]{:S(2)}) collective-permute-start(f32[65,8,128]{2,1,0:T(8,128)S(1)} %get-tuple-element.25), channel_id=1, source_target_pairs={{4,8},{12,16},{20,24},{8,4},{16,12},{24,20},{5,9},{13,17},{21,25},... | collective-permute-start | bytes 798728 | tf_op jit(solution)/shard_map/ppermute | solution.py:716
  10.1 7.2 %collective-permute-start.4 = (f32[64,8,128]{2,1,0:T(8,128)S(1)}, f32[64,8,128]{2,1,0:T(8,128)S(1)}, u32[]{:S(2)}, u32[]{:S(2)}) collective-permute-start(f32[64,8,128]{2,1,0:T(8,128)S(1)} %get-tuple-element.24), channel_id=1, source_target_pairs={{0,4},{4,0},{8,12},{12,8},{16,20},{20,16},{24,28},{28,24},{1,5},{5... | collective-permute-start | bytes 786440 | tf_op jit(solution)/shard_map/ppermute | solution.py:712

commit v9 on v7

--- a/solution.py
+++ b/solution.py
@@ -51,8 +51,6 @@
 X_CODE2 = X_RING + Q + 1
 X_TILES = X_CODE2 + 2
 X_SIDE = 2 * X_LANE
-F_CODE1, F_CODE2, F_CODE3, F_PHI = 0, 5, 9, 13
-FIELDS = 18
 OWN_PHI = 4
 
 
@@ -203,11 +201,11 @@
     out = []
     for i, vector in enumerate(VELOCITIES):
         v = tuple(sign * c for c in vector)
-        value = load(i, 0, -v[0])
+        value = load(i, 0, -v[0], v[1])
         if v[1] == 1:
-            value = jnp.where(cross_low, load(i, -1, -v[0]), value)
+            value = jnp.where(cross_low, load(i, -1, -v[0], 1), value)
         elif v[1] == -1:
-            value = jnp.where(cross_high, load(i, 1, -v[0]), value)
+            value = jnp.where(cross_high, load(i, 1, -v[0], -1), value)
         amount = (v[1] * NZ + v[2]) % LANES
         if amount:
             value = pltpu.roll(value, amount, 1)
@@ -220,7 +218,7 @@
             combined[v] = outside
         outside = combined[v]
         if outside is not None:
-            value = jnp.where(outside, load(OPPOSITE[i], 0, 0), value)
+            value = jnp.where(outside, load(OPPOSITE[i], 0, 0, 0), value)
         out.append(value)
     return out
 
@@ -498,45 +496,68 @@
     return Pick(even, second_ref, first_ref), Pick(even, first_ref, second_ref)
 
 
-def add_panels(parts_ref, out_ref):
-    out_ref[...] = jnp.sum(parts_ref[...], axis=0)
-
-
-def fill(from_left, own_ref, field_ref, cot_ref, from_below, pop, cot, field):
+def own_rows(step=0):
+    return pl.ds(ROWS + step, ROWS)
+
+
+def halo_rows(step=0):
+    return pl.ds({0: 2 * ROWS, -1: 2 * ROWS - 1, 1: 1}[step], ROWS)
+
+
+def put_ring(ref, at, own, halo):
+    ref[at, own_rows(), :] = own
+    ref[at, pl.ds(0, ROWS), :] = halo
+    ref[at, halo_rows(), :] = halo
+
+
+def fill(from_left, own_ref, field_ref, cot_ref, from_below, pop, cot, wide, field):
     row, lane, column, depth = iotas()
     top = depth == NZ - 1
-
-    def put(c, r, population, cotangent, codes):
-        rows = pl.ds(ROWS * (r + 1), ROWS)
-        for i in range(Q):
-            pop[5 * i + c, rows, :] = population(i)
-            if c:
-                cot[4 * i + c - 1, rows, :] = cotangent(i)
-        code = codes(1)
+    after = row < 4
+
+    def expand(code):
         phi = jnp.where(top, code, 0.0)
         for step in (1, 2, 4, 8, 16):
             phi = phi + pltpu.roll(phi, LANES - step, 1)
-        field[F_CODE1 + c, rows, :] = jnp.where(top, 0.0, code)
-        field[F_PHI + c, rows, :] = phi
+        return jnp.where(top, 0.0, code), phi
+
+    for c in range(5):
+        t = c - 2
+        if t in (0, 1):
+            own = (
+                lambda i: own_ref[2 * i + t],
+                lambda i: cot_ref[2 * i + t],
+                lambda s: field_ref[2 * s + t],
+            )
+            code_phi = field_ref[2 + t], field_ref[2 * OWN_PHI + t]
+        else:
+            own = tuple(functools.partial(lambda g, n: g(n, c), get) for get in from_left)
+            code_phi = expand(own[2](1))
         if c:
-            field[F_CODE2 + c - 1, rows, :] = codes(2)
-            field[F_CODE3 + c - 1, rows, :] = codes(3)
-
-    for c in (0, 1, 4):
-        put(c, 1, *(functools.partial(lambda g, n: g(n, c), get) for get in from_left))
-    for t in range(2):
-        rows = pl.ds(2 * ROWS, ROWS)
+            n = (None, 2, 0, 1, 3)[c]
+            below, above = from_x(from_below[0], n, 1), from_x(from_below[1], n, -1)
+        else:
+            below, above = (
+                (lambda i, ref=ref: ref[X_RING + i], None, lambda s, ref=ref: ref[X_RING + Q])
+                for ref in from_below
+            )
+        parts = (expand(below[2](1)), code_phi, expand(above[2](1)))
         for i in range(Q):
-            pop[5 * i + 2 + t, rows, :] = own_ref[2 * i + t]
-            cot[4 * i + 1 + t, rows, :] = cot_ref[2 * i + t]
-        field[F_CODE1 + 2 + t, rows, :] = field_ref[2 + t]
-        field[F_CODE2 + 1 + t, rows, :] = field_ref[4 + t]
-        field[F_CODE3 + 1 + t, rows, :] = field_ref[6 + t]
-        field[F_PHI + 2 + t, rows, :] = field_ref[2 * OWN_PHI + t]
-    for way, r, ref in ((1, 0, from_below[0]), (-1, 2, from_below[1])):
-        for n, c in enumerate((2, 3, 1, 4)):
-            put(c, r, *from_x(ref, n, way))
-        put(0, r, lambda i: ref[X_RING + i], None, lambda s: ref[X_RING + Q])
+            for r, side in enumerate((below, own, above)):
+                pop[5 * i + c, pl.ds(ROWS * (r + 1), ROWS), :] = side[0](i)
+        for n in range(2):
+            for r in range(3):
+                wide[n, c, r] = parts[r][n]
+        if c:
+            for i in range(Q):
+                halo = jnp.where(after, above[1](i), below[1](i))
+                put_ring(cot, 4 * i + c - 1, own[1](i), halo)
+            for n, place in ((0, 1), (1, 0)):
+                field[place, c - 1, 0] = parts[1][n]
+                field[place, c - 1, 1] = jnp.where(after, parts[2][n], parts[0][n])
+            for s in (2, 3):
+                field[s, c - 1, 0] = own[2](s)
+                field[s, c - 1, 1] = jnp.where(after, above[2](s), below[2](s))
 
 
 def steps_kernel(
@@ -556,7 +577,9 @@
     panel_ref,
     pop_a,
     pop_b,
-    cot,
+    ring_a,
+    ring_b,
+    wide,
     field,
     saved,
     mom,
@@ -574,7 +597,8 @@
             "gx",
         ),
         pop_a,
-        cot,
+        ring_a,
+        wide,
         field,
     )
 
@@ -585,98 +609,157 @@
         jnp.where(at_y == 0, 1, 0),
         jnp.where(at_y == size_y - 1, 1, 0),
     )
-    lane = lax.broadcasted_iota(jnp.int32, (ROWS, LANES), 1)
-
-    def streamed(ref, tile, tiles, r, sign, masks, four):
-        step = {0: tile, -1: lax.rem(tile + tiles - 1, tiles), 1: lax.rem(tile + 1, tiles)}
-
-        def load(i, tile_step, row_step):
-            return ref[tiles * i + step[tile_step], pl.ds(ROWS * (r + 1) + row_step, ROWS), :]
-
-        return stream_tile(load, sign, masks, lane)
+    row, lane, column, depth = iotas()
+    after = row < 4
 
     def masks_of(tile, first, r):
-        return wall_masks(r == 1, tile == first, tile == first + 1, edges)
-
-    def rows_of(r):
-        return pl.ds(ROWS * (r + 1), ROWS)
-
-    def forward(source, tiles, own, s, target, target_tiles, offset):
-        def body(tile, carry):
-            ring = tile - offset if target_tiles != tiles else tile
-            for r in range(3):
-                f = streamed(source, tile, tiles, r, 1, masks_of(tile, own, r), None)
-                parts = moments(f)
-                _, _, rho, rinv, u = parts
-                place = tile if tiles == 4 else lax.rem(tile + 4, 5)
-                for n, value in enumerate((rho, rinv, *u)):
-                    mom[s - 1, n, place, pl.ds(ROWS * r, ROWS), :] = value
-                if r == 1:
-                    for i in range(Q):
-                        saved[s - 1, i, place] = f[i]
-                if target is not None:
-                    at = tile if tiles == 5 else tile + 1
-                    first = F_CODE1 if s == 1 else F_CODE2 - 1
-                    kind = field[first + at, rows_of(r), :]
-                    phi = field[F_PHI + at, rows_of(r), :]
-                    g = collide(f, kind, phi, parts)
-                    for i in range(Q):
-                        target[target_tiles * i + ring, rows_of(r), :] = g[i]
-            return carry
-
-        start, stop = (0, 5) if target_tiles == 5 else (1, 5)
-        if tiles == 4:
-            start, stop = 0, 4
-        lax.fori_loop(start, stop, body, 0)
-
-    forward(pop_a, 5, 2, 1, pop_b, 5, 0)
-    forward(pop_b, 5, 2, 2, pop_a, 4, 1)
-    forward(pop_a, 4, 1, 3, None, 4, 0)
-
-    def backward(source, s, target):
-        def body(tile, carry):
-            for r in range(3):
-                b = streamed(source, tile, 4, r, -1, masks_of(tile, 1, r), None)
-                rho, rinv, *u = [
-                    mom[s - 1, n, tile, pl.ds(ROWS * r, ROWS), :] for n in range(5)
-                ]
-                first = (F_CODE1 + 1, F_CODE2, F_CODE3)[s - 1]
-                kind = field[first + tile, rows_of(r), :]
-                phi = field[F_PHI + 1 + tile, rows_of(r), :]
-                state = [saved[s - 1, i, tile] for i in range(Q)] if r == 1 else None
-                back, term = collide_back(b, kind, phi, rho, rinv, u, state)
+        return wall_masks(r == 0, tile == first, tile == first + 1, edges)
+
+    def neighbours(tile, tiles):
+        if isinstance(tile, int):
+            return {0: tile, -1: (tile - 1) % tiles, 1: (tile + 1) % tiles}
+        return {0: tile, -1: lax.rem(tile + tiles - 1, tiles), 1: lax.rem(tile + 1, tiles)}
+
+    def from_wide(ref, tile, r):
+        step = neighbours(tile, 5)
+
+        def load(i, tile_step, row_step, move):
+            at = 5 * i + step[tile_step]
+            before, own, behind = (ref[at, pl.ds(ROWS * n + row_step, ROWS), :] for n in (1, 2, 3))
+            return (own, jnp.where(after, behind, before), before, behind)[r]
+
+        return load
+
+    def from_ring(ref, tile, tiles, r):
+        step = neighbours(tile, tiles)
+
+        def load(i, tile_step, row_step, move):
+            rows = own_rows(row_step) if r == 0 else halo_rows(row_step)
+            return ref[tiles * i + step[tile_step], rows, :]
+
+        return load
+
+    def from_outer(ref, r):
+        def load(i, tile_step, row_step, move):
+            rows = own_rows(row_step) if r == 0 else halo_rows(row_step)
+            if tile_step:
+                return ref[4 * i + (2 if tile_step < 0 else 1), rows, :]
+            cut = {0: 2, 1: 1, -1: 3}[move]
+            return jnp.where(column < cut, ref[4 * i + 3, rows, :], ref[4 * i, rows, :])
+
+        return load
+
+    def note(s, tile, r, parts):
+        for n, value in enumerate(parts[2:4] + tuple(parts[4])):
+            mom[s - 1, n, tile, r] = value
+
+    def first_step(tile, carry):
+        place = lax.rem(tile + 4, 5)
+        halo = []
+        for r in (2, 0, 3):
+            f = stream_tile(from_wide(pop_a, tile, r), 1, masks_of(tile, 2, r), lane)
+            parts = moments(f)
+            if r == 0:
+                note(1, place, 0, parts)
                 for i in range(Q):
-                    target[4 * i + tile, rows_of(r), :] = back[i]
-                if r == 1:
-                    grad[tile] = term if s == 3 else grad[tile] + term
-            return carry
-
-        lax.fori_loop(0, 4, body, 0)
-
-    backward(cot, 3, pop_a)
-    backward(pop_a, 2, pop_b)
-    backward(pop_b, 1, pop_a)
-
-    row = lax.broadcasted_iota(jnp.int32, (ROWS, LANES), 0)
+                    saved[0, i, place] = f[i]
+            else:
+                halo.append(parts[2:4] + tuple(parts[4]))
+            at = {2: 0, 0: 1, 3: 2}[r]
+            g = collide(f, wide[0, tile, at], wide[1, tile, at], parts)
+            for i in range(Q):
+                pop_b[5 * i + tile, pl.ds(ROWS * (at + 1), ROWS), :] = g[i]
+        for n in range(5):
+            mom[0, n, place, 1] = jnp.where(after, halo[1][n], halo[0][n])
+        return carry
+
+    lax.fori_loop(0, 5, first_step, 0)
+
+    def second_step(tile, carry):
+        out = []
+        for r in range(2):
+            f = stream_tile(from_wide(pop_b, tile + 1, r), 1, masks_of(tile, 1, r), lane)
+            parts = moments(f)
+            note(2, tile, r, parts)
+            if r == 0:
+                for i in range(Q):
+                    saved[1, i, tile] = f[i]
+            out.append(collide(f, field[2, tile, r], field[0, tile, r], parts))
+        for i in range(Q):
+            put_ring(ring_b, 4 * i + tile, out[0][i], out[1][i])
+        return carry
+
+    lax.fori_loop(0, 4, second_step, 0)
+
+    def third_step(tile, carry):
+        for r in range(2):
+            f = stream_tile(from_ring(ring_b, tile, 4, r), 1, masks_of(tile, 1, r), lane)
+            note(3, tile, r, moments(f))
+            if r == 0:
+                for i in range(Q):
+                    saved[2, i, tile] = f[i]
+        return carry
+
+    lax.fori_loop(0, 4, third_step, 0)
+
+    def back_tile(load, s, tile, r, own):
+        b = stream_tile(load, -1, masks_of(4 if tile is None else tile, 1, r), lane)
+
+        def read(get):
+            return jnp.where(column < 2, get(3), get(0)) if tile is None else get(tile)
+
+        rho, rinv, *u = [read(lambda at: mom[s - 1, n, at, r]) for n in range(5)]
+        kind, phi = read(lambda at: field[s, at, r]), read(lambda at: field[0, at, r])
+        state = [saved[s - 1, i, tile] for i in range(Q)] if own else None
+        back, term = collide_back(b, kind, phi, rho, rinv, u, state)
+        if own:
+            grad[tile] = term if s == 3 else grad[tile] + term
+        return back
+
+    def last_step(tile, carry):
+        out = [back_tile(from_ring(ring_a, tile, 4, r), 3, tile, r, r == 0) for r in range(2)]
+        for i in range(Q):
+            put_ring(ring_b, 4 * i + tile, out[0][i], out[1][i])
+        return carry
+
+    lax.fori_loop(0, 4, last_step, 0)
+
+    for k, tile in enumerate((1, 2, None)):
+        out = []
+        for r in range(2):
+            load = from_outer(ring_b, r) if tile is None else from_ring(ring_b, tile, 4, r)
+            out.append(back_tile(load, 2, tile, r, r == 0 and tile is not None))
+        for i in range(Q):
+            put_ring(ring_a, 3 * i + k, out[0][i], out[1][i])
+
+    for k, tile in enumerate((1, 2, None)):
+        out = []
+        for r in range(2):
+            load = from_ring(ring_a, k, 3, r)
+            out.append(back_tile(load, 1, tile, r, r == 0 and tile is not None))
+        for i in range(Q):
+            put_ring(ring_b, 3 * i + k, out[0][i], out[1][i])
+
     panel = lax.broadcasted_iota(jnp.int32, panel_ref.shape, 1)
     sums = jnp.zeros(panel_ref.shape, jnp.float32)
-    for tile in range(2):
-        lanes = pl.ds(tile * LANES, LANES)
-        b = streamed(pop_a, tile + 1, 4, 1, -1, masks_of(tile, 0, 1), None)
-        f = [state_ref[2 * i + tile] for i in range(Q)]
-        kind = own_field_ref[tile]
-        phi = own_field_ref[2 * OWN_PHI + tile]
+    for t in range(2):
+        b = stream_tile(from_ring(ring_b, t, 3, 0), -1, masks_of(t, 0, 0), lane)
+        f = [state_ref[2 * i + t] for i in range(Q)]
+        kind, phi = own_field_ref[t], own_field_ref[2 * OWN_PHI + t]
         _, _, rho, rinv, u = moments(f)
         back, term = collide_back(b, kind, phi, rho, rinv, u, f)
         for i in range(Q):
-            adjoint_ref[i, :, lanes] = back[i]
-        term = term + grad[tile + 1]
+            adjoint_ref[i, :, pl.ds(t * LANES, LANES)] = back[i]
+        term = term + grad[t + 1]
         for part in range(2):
-            inside = (row < 4) if part == 0 else (row >= 4)
-            amount = jnp.sum(jnp.where(inside, term, 0.0))
-            name = names_ref[tile, 4 * part : 4 * part + 1, 0:1]
+            amount = jnp.sum(jnp.where((row < 4) == (part == 0), term, 0.0))
+            name = names_ref[t, 4 * part : 4 * part + 1, 0:1]
             sums = sums + jnp.where(panel == name, amount, 0.0)
     panel_ref[...] = sums
+
+
+def add_panels(parts_ref, out_ref):
+    out_ref[...] = jnp.sum(parts_ref[...], axis=0)
 
 
 VMEM = pl.BlockSpec(memory_space=pltpu.VMEM)
@@ -757,10 +840,12 @@
         [
             pltpu.VMEM((5 * Q, 5 * ROWS, LANES), jnp.float32),
             pltpu.VMEM((5 * Q, 5 * ROWS, LANES), jnp.float32),
-            pltpu.VMEM((4 * Q, 5 * ROWS, LANES), jnp.float32),
-            pltpu.VMEM((FIELDS, 5 * ROWS, LANES), jnp.float32),
+            pltpu.VMEM((4 * Q, 3 * ROWS, LANES), jnp.float32),
+            pltpu.VMEM((4 * Q, 3 * ROWS, LANES), jnp.float32),
+            pltpu.VMEM((2, 5, 3, ROWS, LANES), jnp.float32),
+            pltpu.VMEM((4, 4, 2, ROWS, LANES), jnp.float32),
             pltpu.VMEM((3, Q, 5, ROWS, LANES), jnp.float32),
-            pltpu.VMEM((3, 5, 5, 3 * ROWS, LANES), jnp.float32),
+            pltpu.VMEM((3, 5, 5, 2, ROWS, LANES), jnp.float32),
             pltpu.VMEM((4, ROWS, LANES), jnp.float32),
         ],
         name="steps",

time: 41.4 us -> 40.1 us (0.969)
  Pallas kernels: 7.64 us -> 6.37 us
    pallas_call x1, Pallas kernels: 5.76 us -> 4.49 us  [on_device(): call(functools.partial(steps_kernel, sizes), (shape_of(Q, ROWS, 2 * LANES...]
where the time goes in v9:
time: 40.1 us; the launch traced here: 39.8 us
  blocking collectives  17.5 us (44%)
  starting transfers between devices  11.1 us (28%)
  Pallas kernels  6.37 us (16%)
  waiting for transfers between devices  4.2 us (10%)
  between operations  0.68 us (2%)
    all_to_all x1, blocking collectives, on_device(): gathered = lax.all_to_all(sums, ('gx', 'gy'), 0, 0, tiled=True)  17.5 us
    ppermute x3, starting transfers between devices, swap(): lax.ppermute(value, axis, [(i, i ^ 1) for i in range(size) if i ^ 1 < size])  9.08 us
    pallas_call x1, Pallas kernels, on_device(): call(functools.partial(steps_kernel, sizes), (shape_of(Q, ROWS, 2 * LANES...  4.49 us
    ppermute x3, waiting for transfers between devices, swap(): lax.ppermute(value, axis, [(i, i ^ 1) for i in range(size) if i ^ 1 < size])  4.19 us
    ppermute x3, starting transfers between devices, swap_between(): return lax.ppermute(value, axis, pairs + [(j, i) for i, j in pairs])  2.01 us
    pallas_call x1, Pallas kernels, on_device(): call(pack_own, (tiles_of(Y_TILES),) * 2 + (tiles_of(X_SIDE),) * 2 + (tile...  1.19 us
  transfers between devices with their start and end apart: 6, of which 3 were waited for; matrix products, arithmetic and copies ran while one was open for 0% of the time, Pallas kernels for 0%

profile of v9, /device:TPU:0, one launch (start us, length us, event | category | flops | bytes accessed | tf_op | source)
XLA Modules:
  0.0 39.8 jit_solution(3538239016717248820)
XLA Ops:
  0.6 1.2 %pack_own.1 = (f32[43,8,128]{2,1,0:T(8,128)S(1)}, f32[43,8,128]{2,1,0:T(8,128)S(1)}, f32[42,8,128]{2,1,0:T(8,128)S(1)}, f32[42,8,128]{2,1,0:T(8,128)S(1)}, f32[3...) custom-call(f32[19,8,256]{2,1,0:T(8,128)} %f_hbm.1, ...), custom_call_target="tpu_custom_call" | custom-call | tf_op jit(solution)/shard_map/pack_own/pallas_call | solution.py:805
  1.8 3.0 %collective-permute-start = (f32[43,8,128]{2,1,0:T(8,128)S(1)}, f32[43,8,128]{2,1,0:T(8,128)S(1)}, u32[]{:S(2)}, u32[]{:S(2)}) collective-permute-start(f32[43,8,128]{2,1,0:T(8,128)S(1)} %get-tuple-element.20), channel_id=1, source_target_pairs={{0,1},{1,0},{2,3},{3,2},{4,5},{5,4},{6,7},{7,6},{8,9},{9,8},{10,11... | collective-permute-start | bytes 528392 | tf_op jit(solution)/shard_map/ppermute | solution.py:795
  4.8 0.7 %collective-permute-start.1 = (f32[43,8,128]{2,1,0:T(8,128)S(1)}, f32[43,8,128]{2,1,0:T(8,128)S(1)}, u32[]{:S(2)}, u32[]{:S(2)}) collective-permute-start(f32[43,8,128]{2,1,0:T(8,128)S(1)} %get-tuple-element.21), channel_id=1, source_target_pairs={{1,2},{2,1},{5,6},{6,5},{9,10},{10,9},{13,14},{14,13},{17,18},{18,... | collective-permute-start | bytes 528392 | tf_op jit(solution)/shard_map/ppermute | solution.py:799
  5.5 0.1 collective-permute-start.2
  5.6 0.7 %collective-permute-start.3 = (f32[42,8,128]{2,1,0:T(8,128)S(1)}, f32[42,8,128]{2,1,0:T(8,128)S(1)}, u32[]{:S(2)}, u32[]{:S(2)}) collective-permute-start(f32[42,8,128]{2,1,0:T(8,128)S(1)} %get-tuple-element.23), channel_id=1, source_target_pairs={{4,8},{12,16},{20,24},{8,4},{16,12},{24,20},{5,9},{13,17},{21,25},... | collective-permute-start | bytes 516104 | tf_op jit(solution)/shard_map/ppermute | solution.py:799
  6.3 0.7 %collective-permute-done.2.early_a.first_side_ref = f32[42,8,128]{2,1,0:T(8,128)S(1)} collective-permute-done((f32[42,8,128]{2,1,0:T(8,128)S(1)}, f32[42,8,128]{2,1,0:T(8,128)S(1)}, u32[]{:S(2)}, u32[]{:S(2)}) %collective-permute-start.2) | collective-permute-done | bytes 172064 | tf_op jit(solution)/shard_map/ppermute | solution.py:795
  7.0 0.0 collective-permute-done.3.early_b.second_side_ref
  7.0 2.3 %collective-permute-done.first_y_ref = f32[43,8,128]{2,1,0:T(8,128)S(1)} collective-permute-done((f32[43,8,128]{2,1,0:T(8,128)S(1)}, f32[43,8,128]{2,1,0:T(8,128)S(1)}, u32[]{:S(2)}, u32[]{:S(2)}) %collective-permute-start) | collective-permute-done | bytes 176160 | tf_op jit(solution)/shard_map/ppermute | solution.py:795
  9.3 0.0 collective-permute-done.1.second_y_ref
  9.3 0.1 pack_x.1
  9.5 0.7 %collective-permute-start.5 = (f32[65,8,128]{2,1,0:T(8,128)S(1)}, f32[65,8,128]{2,1,0:T(8,128)S(1)}, u32[]{:S(2)}, u32[]{:S(2)}) collective-permute-start(f32[65,8,128]{2,1,0:T(8,128)S(1)} %get-tuple-element.25), channel_id=1, source_target_pairs={{4,8},{12,16},{20,24},{8,4},{16,12},{24,20},{5,9},{13,17},{21,25},... | collective-permute-start | bytes 798728 | tf_op jit(solution)/shard_map/ppermute | solution.py:799
  10.1 6.0 %collective-permute-start.4 = (f32[64,8,128]{2,1,0:T(8,128)S(1)}, f32[64,8,128]{2,1,0:T(8,128)S(1)}, u32[]{:S(2)}, u32[]{:S(2)}) collective-permute-start(f32[64,8,128]{2,1,0:T(8,128)S(1)} %get-tuple-element.24), channel_id=1, source_target_pairs={{0,4},{4,0},{8,12},{12,8},{16,20},{20,16},{24,28},{28,24},{1,5},{5... | collective-permute-start | bytes 786440 | tf_op jit(solution)/shard_map/ppermute | solution.py:795
  16.1 1.2 %collective-permute-done.4.first_x_ref = f32[64,8,128]{2,1,0:T(8,128)S(1)} collective-permute-done((f32[64,8,128]{2,1,0:T(8,128)S(1)}, f32[64,8,128]{2,1,0:T(8,128)S(1)}, u32[]{:S(2)}, u32[]{:S(2)}) %collective-permute-start.4) | collective-permute-done | bytes 262176 | tf_op jit(solution)/shard_map/ppermute | solution.py:795
  17.3 0.0 collective-permute-done.5.second_x_ref
  17.3 4.5 %steps.1 = (f32[19,8,256]{2,1,0:T(8,128)}, f32[32,64]{1,0:T(8,128)S(1)}) custom-call(f32[38,8,128]{2,1,0:T(8,128)S(1)} %get-tuple-element.15.state_ref, f32[38,8,128]{2,1,0:T(8,128)S(1)} %get-tuple-element.16.cot_ref, f32[38,8,128]{2,1,0:T(8,128)S(1)} %get-tuple-element.17.own_ref, f32[10,8,128]{2,1,0:T(8,128)S(1)} %get-tuple-element.18.field_ref.own_field_ref, ...), custom_call_target="tpu_custom_call" | custom-call | tf_op jit(solution)/shard_map/steps/pallas_call | solution.py:836
  21.8 17.5 %all_to_all.9.parts_ref = f32[32,1,64]{2,1,0:T(1,128)S(1)} all-to-all(f32[32,1,64]{2,1,0:T(1,128)S(1)} %bitcast.2), channel_id=1, replica_groups=mesh['gx'=8,'gy'=4] {'gx','gy'}, dimensions={0} | all-to-all | bytes 16384 | tf_op jit(solution)/shard_map/all_to_all | solution.py:853
  39.3 0.5 %add_panels.1 = f32[1,64]{1,0:T(1,128)} custom-call(f32[32,1,64]{2,1,0:T(1,128)S(1)} %all_to_all.9.parts_ref), custom_call_target="tpu_custom_call" | custom-call | tf_op jit(solution)/shard_map/add_panels/pallas_call | solution.py:854
Async XLA Ops:
  1.8 7.5 %collective-permute-start = (f32[43,8,128]{2,1,0:T(8,128)S(1)}, f32[43,8,128]{2,1,0:T(8,128)S(1)}, u32[]{:S(2)}, u32[]{:S(2)}) collective-permute-start(f32[43,8,128]{2,1,0:T(8,128)S(1)} %get-tuple-element.20), channel_id=1, source_target_pairs={{0,1},{1,0},{2,3},{3,2},{4,5},{5,4},{6,7},{7,6},{8,9},{9,8},{10,11... | collective-permute-start | bytes 528392 | tf_op jit(solution)/shard_map/ppermute | solution.py:795
  4.8 4.5 %collective-permute-start.1 = (f32[43,8,128]{2,1,0:T(8,128)S(1)}, f32[43,8,128]{2,1,0:T(8,128)S(1)}, u32[]{:S(2)}, u32[]{:S(2)}) collective-permute-start(f32[43,8,128]{2,1,0:T(8,128)S(1)} %get-tuple-element.21), channel_id=1, source_target_pairs={{1,2},{2,1},{5,6},{6,5},{9,10},{10,9},{13,14},{14,13},{17,18},{18,... | collective-permute-start | bytes 528392 | tf_op jit(solution)/shard_map/ppermute | solution.py:799
  5.5 1.5 %collective-permute-start.2 = (f32[42,8,128]{2,1,0:T(8,128)S(1)}, f32[42,8,128]{2,1,0:T(8,128)S(1)}, u32[]{:S(2)}, u32[]{:S(2)}) collective-permute-start(f32[42,8,128]{2,1,0:T(8,128)S(1)} %get-tuple-element.22), channel_id=1, source_target_pairs={{0,4},{4,0},{8,12},{12,8},{16,20},{20,16},{24,28},{28,24},{1,5},{5... | collective-permute-start | bytes 516104 | tf_op jit(solution)/shard_map/ppermute | solution.py:795
  5.6 1.4 %collective-permute-start.3 = (f32[42,8,128]{2,1,0:T(8,128)S(1)}, f32[42,8,128]{2,1,0:T(8,128)S(1)}, u32[]{:S(2)}, u32[]{:S(2)}) collective-permute-start(f32[42,8,128]{2,1,0:T(8,128)S(1)} %get-tuple-element.23), channel_id=1, source_target_pairs={{4,8},{12,16},{20,24},{8,4},{16,12},{24,20},{5,9},{13,17},{21,25},... | collective-permute-start | bytes 516104 | tf_op jit(solution)/shard_map/ppermute | solution.py:799
  9.5 7.9 %collective-permute-start.5 = (f32[65,8,128]{2,1,0:T(8,128)S(1)}, f32[65,8,128]{2,1,0:T(8,128)S(1)}, u32[]{:S(2)}, u32[]{:S(2)}) collective-permute-start(f32[65,8,128]{2,1,0:T(8,128)S(1)} %get-tuple-element.25), channel_id=1, source_target_pairs={{4,8},{12,16},{20,24},{8,4},{16,12},{24,20},{5,9},{13,17},{21,25},... | collective-permute-start | bytes 798728 | tf_op jit(solution)/shard_map/ppermute | solution.py:799
  10.1 7.2 %collective-permute-start.4 = (f32[64,8,128]{2,1,0:T(8,128)S(1)}, f32[64,8,128]{2,1,0:T(8,128)S(1)}, u32[]{:S(2)}, u32[]{:S(2)}) collective-permute-start(f32[64,8,128]{2,1,0:T(8,128)S(1)} %get-tuple-element.24), channel_id=1, source_target_pairs={{0,4},{4,0},{8,12},{12,8},{16,20},{20,16},{24,28},{28,24},{1,5},{5... | collective-permute-start | bytes 786440 | tf_op jit(solution)/shard_map/ppermute | solution.py:795

commit v10 on v9

--- a/solution.py
+++ b/solution.py
@@ -44,13 +44,16 @@
 
 Y_CODE1, Y_CODE2, Y_CODE3, Y_POP, Y_COT = 38, 39, 40, 41, 42
 Y_TILES = 43
-SPARE = 1
 X_EXTRA, X_CODE13 = 19, 20
 X_LANE = 21
 X_RING = 4 * X_LANE
 X_CODE2 = X_RING + Q + 1
 X_TILES = X_CODE2 + 2
 X_SIDE = 2 * X_LANE
+EMPTY = 25
+FREE = NZ - EMPTY
+WEIGHTS = [W_REST] + [W_AXIS] * 6 + [W_DIAG] * 12
+LEVEL = [i for i, v in enumerate(VELOCITIES) if v[2] < 1]
 OWN_PHI = 4
 
 
@@ -239,6 +242,77 @@
     return pltpu.roll(value, amount, 0) if amount else value
 
 
+class Layout:
+    def __init__(self, count, guests, fills):
+        self.fills = fills
+        hosts = [at for at in fills if at not in guests]
+        self.hosts = {at: hosts[4 * n : 4 * n + 4] for n, at in enumerate(guests)}
+        self.guests = guests
+        kept = [at for at in range(count) if at not in guests]
+        self.place = {at: n for n, at in enumerate(kept)}
+        self.size = len(kept)
+
+
+class Packing:
+    def __init__(self, ref, layout):
+        self.ref, self.layout, self.held = ref, layout, {}
+
+    def __setitem__(self, at, value):
+        if at in self.layout.guests:
+            self.held[at] = value
+        else:
+            self.ref[self.layout.place[at]] = value
+
+    def finish(self):
+        row, lane, column, depth = iotas()
+        spare = depth >= EMPTY
+        for at, value in self.held.items():
+            for k, host in enumerate(self.layout.hosts[at]):
+                place = self.layout.place[host]
+                source = jnp.where(spare, NZ * k + FREE * column + depth - EMPTY, 0)
+                moved = jnp.take_along_axis(value, source, axis=1, mode="promise_in_bounds")
+                self.ref[place] = jnp.where(spare, moved, self.ref[place])
+        for place in range(self.layout.size, self.ref.shape[0]):
+            self.ref[place] = jnp.zeros((ROWS, LANES), jnp.float32)
+
+
+class Unpacking:
+    def __init__(self, source, layout):
+        self.source, self.layout = source, layout
+
+    def __getitem__(self, at):
+        row, lane, column, depth = iotas()
+        layout = self.layout
+        if at in layout.guests:
+            value = None
+            lanes = jnp.where(depth < EMPTY, NZ * (depth // FREE) + EMPTY + depth % FREE, 0)
+            for k, host in enumerate(layout.hosts[at]):
+                tile = self.source[layout.place[host]]
+                moved = jnp.take_along_axis(tile, lanes, axis=1, mode="promise_in_bounds")
+                value = moved if value is None else jnp.where(column == k, moved, value)
+        else:
+            value = self.source[layout.place[at]]
+        if at in layout.fills:
+            value = jnp.where(depth >= EMPTY, layout.fills[at], value)
+        return value
+
+
+def layouts():
+    y_fills = {2 * i + t: WEIGHTS[i] for i in LEVEL for t in range(2)}
+    y_fills.update({Y_POP: W_DIAG, Y_CODE2: 0.0})
+    x_fills = {X_LANE * n + i: WEIGHTS[i] for n in range(4) for i in LEVEL}
+    side = {at: fill for at, fill in x_fills.items() if at < X_SIDE}
+    rest = {at - X_SIDE: fill for at, fill in x_fills.items() if at >= X_SIDE}
+    rest.update({X_CODE2 - X_SIDE: 0.0, X_CODE2 + 1 - X_SIDE: 0.0})
+    rest.update({X_RING - X_SIDE + i: WEIGHTS[i] for i in range(Q)})
+    ring = [X_RING - X_SIDE + i for i in range(9)]
+    return (
+        Layout(Y_TILES, [2 * i for i in LEVEL[:6]], y_fills),
+        Layout(X_SIDE, LEVEL[:5], side),
+        Layout(X_TILES - X_SIDE, ring, rest),
+    )
+
+
 class Pick:
     def __init__(self, flag, first, second):
         self.flag, self.first, self.second = flag, first, second
@@ -248,8 +322,9 @@
 
 
 class Deal:
-    def __init__(self, even, first, second, skip=0):
-        self.even, self.first, self.second, self.skip, self.held = even, first, second, skip, {}
+    def __init__(self, even, first, second, layout, skip=0):
+        self.even, self.skip, self.held = even, skip, {}
+        self.first, self.second = Packing(first, layout), Packing(second, layout)
 
     def put(self, way, at, value):
         if (-way, at) not in self.held:
@@ -259,6 +334,14 @@
         up, down = (value, other) if way == 1 else (other, value)
         self.first[at - self.skip] = jnp.where(self.even, up, down)
         self.second[at - self.skip] = jnp.where(self.even, down, up)
+
+    def put_both(self, at, value):
+        self.first[at - self.skip] = value
+        self.second[at - self.skip] = value
+
+    def finish(self):
+        self.first.finish()
+        self.second.finish()
 
 
 class Joined:
@@ -310,7 +393,9 @@
         copy.start()
     for copy in copies[:4]:
         copy.wait()
-    deal = Deal(is_even("gy"), first_ref, second_ref)
+    y_layout, side_layout, _ = layouts()
+    deal = Deal(is_even("gy"), first_ref, second_ref, y_layout)
+    side = Deal(is_even("gx"), first_side_ref, second_side_ref, side_layout)
     row, lane, column, depth = iotas()
     top = depth == NZ - 1
 
@@ -362,16 +447,18 @@
             value = columns(tile_of(cot_ref, i, near), k - (1 if way == 1 else 2))
             extra = value if extra is None else jnp.where(column == k, value, extra)
         deal.put(way, Y_COT, extra)
+    deal.finish()
     for t in range(2):
         for i in range(Q):
             own_cot_ref[2 * i + t] = tile_of(cot_ref, i, t)
         pack_lines(
-            Deal(is_even("gx"), first_side_ref, second_side_ref),
+            side,
             X_LANE * t,
             lambda i: own_ref[2 * i + t],
             lambda i: tile_of(cot_ref, i, t),
             lambda s: codes[t][s - 1],
         )
+    side.finish()
 
 
 def from_y(left_ref, right_ref):
@@ -466,8 +553,9 @@
 
 def pack_x(field_ref, first_y_ref, second_y_ref, early_a, early_b, first_ref, second_ref):
     row, lane, column, depth = iotas()
-    deal = Deal(is_even("gx"), first_ref, second_ref, X_SIDE)
-    population, cotangent, codes = from_y(*sides(first_y_ref, second_y_ref, "gy"))
+    y_layout, _, layout = layouts()
+    deal = Deal(is_even("gx"), first_ref, second_ref, layout, X_SIDE)
+    population, cotangent, codes = from_y(*sides(first_y_ref, second_y_ref, "gy", y_layout))
 
     def both_codes(at, first, second):
         second = lines(second, 4)
@@ -484,16 +572,16 @@
         )
     for n in range(Q + 1):
         value = population(n, 0) if n < Q else codes(1, 0)
-        first_ref[X_RING + n - X_SIDE] = value
-        second_ref[X_RING + n - X_SIDE] = value
+        deal.put_both(X_RING + n, value)
     both_codes(X_CODE2, field_ref[4], field_ref[5])
     both_codes(X_CODE2 + 1, codes(2, 1), codes(2, 4))
-    second_ref[X_TILES - X_SIDE] = jnp.zeros((ROWS, LANES), jnp.float32)
-
-
-def sides(first_ref, second_ref, axis):
+    deal.finish()
+
+
+def sides(first_ref, second_ref, axis, layout):
     even = is_even(axis)
-    return Pick(even, second_ref, first_ref), Pick(even, first_ref, second_ref)
+    picks = Pick(even, second_ref, first_ref), Pick(even, first_ref, second_ref)
+    return [Unpacking(pick, layout) for pick in picks]
 
 
 def own_rows(step=0):
@@ -586,16 +674,19 @@
     grad,
 ):
     size_x, size_y = sizes
+    y_layout, side_layout, rest_layout = layouts()
     fill(
-        from_y(*sides(first_y_ref, second_y_ref, "gy")),
+        from_y(*sides(first_y_ref, second_y_ref, "gy", y_layout)),
         own_ref,
         own_field_ref,
         cot_ref,
-        sides(
-            Joined(first_side_ref, first_x_ref, X_SIDE),
-            Joined(second_side_ref, second_x_ref, X_SIDE),
-            "gx",
-        ),
+        [
+            Joined(side, rest, X_SIDE)
+            for side, rest in zip(
+                sides(first_side_ref, second_side_ref, "gx", side_layout),
+                sides(first_x_ref, second_x_ref, "gx", rest_layout),
+            )
+        ],
         pop_a,
         ring_a,
         wide,
@@ -779,6 +870,7 @@
     size_x, size_y = sizes
     panels = porosity.shape[0]
     devices = size_x * size_y
+    y_layout, side_layout, rest_layout = layouts()
 
     def call(kernel, out_shape, in_specs, scratch=(), name=None):
         return pl.pallas_call(
@@ -804,8 +896,8 @@
     ]
     first_y, second_y, first_side, second_side, own, state, cot, field, names = call(
         pack_own,
-        (tiles_of(Y_TILES),) * 2
-        + (tiles_of(X_SIDE),) * 2
+        (tiles_of(y_layout.size + 2), tiles_of(y_layout.size))
+        + (tiles_of(side_layout.size), tiles_of(y_layout.size + 1))
         + (tiles_of(2 * Q),) * 3
         + (tiles_of(2 * OWN_PHI + 2), jax.ShapeDtypeStruct((2, ROWS, LANES), jnp.int32)),
         [HBM] * 5,
@@ -823,10 +915,9 @@
     first_y = swap(first_y, "gy", size_y)
     second_side = swap_between(second_side, "gx", size_x)
     first_side = swap(first_side, "gx", size_x)
-    rest = X_TILES - X_SIDE
     first_x, second_x = call(
         pack_x,
-        (tiles_of(rest), tiles_of(rest + SPARE)),
+        (tiles_of(rest_layout.size), tiles_of(rest_layout.size + 1)),
         [VMEM] * 3 + [ANY] * 2,
         name="pack_x",
     )(field, first_y, second_y, first_side, second_side)

time: 40.1 us -> 40.9 us (1.020)
  waiting for transfers between devices: 4.2 us -> 2.13 us
  Pallas kernels: 6.37 us -> 7.85 us
  starting transfers between devices: 11.1 us -> 12.2 us
    ppermute x3, waiting for transfers between devices: 4.19 us -> 2.12 us  [swap(): lax.ppermute(value, axis, [(i, i ^ 1) for i in range(size) if i ^ 1 < size])]
    ppermute x3, starting transfers between devices: 9.08 us -> 10.2 us  [swap(): lax.ppermute(value, axis, [(i, i ^ 1) for i in range(size) if i ^ 1 < size])]
    pallas_call x1, Pallas kernels: 4.49 us -> 5.51 us  [on_device(): call(functools.partial(steps_kernel, sizes), (shape_of(Q, ROWS, 2 * LANES...]
    pallas_call x2, Pallas kernels: 1.34 us -> 1.8 us  [the longest x1 1.43 us: on_device(): call(pack_own, (tiles_of(y_layout.size + 2), tiles_of(y_layout.size)) + (...]
  transfers between devices with their start and end apart: 6 -> 6, of which waited for: 3 -> 2; matrix products, arithmetic and copies ran while one was open for 0% -> 0% of each run, Pallas kernels for 0% -> 0%
where the time goes in v10:
time: 40.9 us; the launch traced here: 40.7 us
  blocking collectives  17.9 us (44%)
  starting transfers between devices  12.2 us (30%)
  Pallas kernels  7.85 us (19%)
  waiting for transfers between devices  2.13 us (5%)
  between operations  0.67 us (2%)
    all_to_all x1, blocking collectives, on_device(): gathered = lax.all_to_all(sums, ('gx', 'gy'), 0, 0, tiled=True)  17.9 us
    ppermute x3, starting transfers between devices, swap(): lax.ppermute(value, axis, [(i, i ^ 1) for i in range(size) if i ^ 1 < size])  10.2 us
    pallas_call x1, Pallas kernels, on_device(): call(functools.partial(steps_kernel, sizes), (shape_of(Q, ROWS, 2 * LANES...  5.51 us
    ppermute x3, waiting for transfers between devices, swap(): lax.ppermute(value, axis, [(i, i ^ 1) for i in range(size) if i ^ 1 < size])  2.12 us
    ppermute x3, starting transfers between devices, swap_between(): return lax.ppermute(value, axis, pairs + [(j, i) for i, j in pairs])  2 us
    pallas_call x1, Pallas kernels, on_device(): call(pack_own, (tiles_of(y_layout.size + 2), tiles_of(y_layout.size)) + (...  1.43 us
  transfers between devices with their start and end apart: 6, of which 2 were waited for; matrix products, arithmetic and copies ran while one was open for 0% of the time, Pallas kernels for 0%

profile of v10, /device:TPU:0, one launch (start us, length us, event | category | flops | bytes accessed | tf_op | source)
XLA Modules:
  0.0 40.7 jit_solution(328071070988365823)
XLA Ops:
  0.6 1.4 %pack_own.1 = (f32[39,8,128]{2,1,0:T(8,128)S(1)}, f32[37,8,128]{2,1,0:T(8,128)S(1)}, f32[37,8,128]{2,1,0:T(8,128)S(1)}, f32[38,8,128]{2,1,0:T(8,128)S(1)}, f32[3...) custom-call(f32[19,8,256]{2,1,0:T(8,128)} %f_hbm.1, ...), custom_call_target="tpu_custom_call" | custom-call | tf_op jit(solution)/shard_map/pack_own/pallas_call | solution.py:897
  2.1 3.0 %collective-permute-start = (f32[39,8,128]{2,1,0:T(8,128)S(1)}, f32[39,8,128]{2,1,0:T(8,128)S(1)}, u32[]{:S(2)}, u32[]{:S(2)}) collective-permute-start(f32[39,8,128]{2,1,0:T(8,128)S(1)} %get-tuple-element.20), channel_id=1, source_target_pairs={{0,1},{1,0},{2,3},{3,2},{4,5},{5,4},{6,7},{7,6},{8,9},{9,8},{10,11... | collective-permute-start | bytes 479240 | tf_op jit(solution)/shard_map/ppermute | solution.py:887
  5.1 0.7 %collective-permute-start.3 = (f32[38,8,128]{2,1,0:T(8,128)S(1)}, f32[38,8,128]{2,1,0:T(8,128)S(1)}, u32[]{:S(2)}, u32[]{:S(2)}) collective-permute-start(f32[38,8,128]{2,1,0:T(8,128)S(1)} %get-tuple-element.23), channel_id=1, source_target_pairs={{4,8},{12,16},{20,24},{8,4},{16,12},{24,20},{5,9},{13,17},{21,25},... | collective-permute-start | bytes 466952 | tf_op jit(solution)/shard_map/ppermute | solution.py:891
  5.7 0.7 %collective-permute-start.1 = (f32[37,8,128]{2,1,0:T(8,128)S(1)}, f32[37,8,128]{2,1,0:T(8,128)S(1)}, u32[]{:S(2)}, u32[]{:S(2)}) collective-permute-start(f32[37,8,128]{2,1,0:T(8,128)S(1)} %get-tuple-element.21), channel_id=1, source_target_pairs={{1,2},{2,1},{5,6},{6,5},{9,10},{10,9},{13,14},{14,13},{17,18},{18,... | collective-permute-start | bytes 454664 | tf_op jit(solution)/shard_map/ppermute | solution.py:891
  6.4 3.0 %collective-permute-start.2 = (f32[37,8,128]{2,1,0:T(8,128)S(1)}, f32[37,8,128]{2,1,0:T(8,128)S(1)}, u32[]{:S(2)}, u32[]{:S(2)}) collective-permute-start(f32[37,8,128]{2,1,0:T(8,128)S(1)} %get-tuple-element.22), channel_id=1, source_target_pairs={{0,4},{4,0},{8,12},{12,8},{16,20},{20,16},{24,28},{28,24},{1,5},{5... | collective-permute-start | bytes 454664 | tf_op jit(solution)/shard_map/ppermute | solution.py:887
  9.4 0.0 collective-permute-done.1.second_y_ref
  9.4 1.0 %collective-permute-done.2.early_a.first_side_ref = f32[37,8,128]{2,1,0:T(8,128)S(1)} collective-permute-done((f32[37,8,128]{2,1,0:T(8,128)S(1)}, f32[37,8,128]{2,1,0:T(8,128)S(1)}, u32[]{:S(2)}, u32[]{:S(2)}) %collective-permute-start.2) | collective-permute-done | bytes 151584 | tf_op jit(solution)/shard_map/ppermute | solution.py:887
  10.4 0.0 collective-permute-done.3.early_b.second_side_ref
  10.4 0.0 collective-permute-done.first_y_ref
  10.4 0.4 pack_x.1
  10.8 0.7 %collective-permute-start.5 = (f32[56,8,128]{2,1,0:T(8,128)S(1)}, f32[56,8,128]{2,1,0:T(8,128)S(1)}, u32[]{:S(2)}, u32[]{:S(2)}) collective-permute-start(f32[56,8,128]{2,1,0:T(8,128)S(1)} %get-tuple-element.25), channel_id=1, source_target_pairs={{4,8},{12,16},{20,24},{8,4},{16,12},{24,20},{5,9},{13,17},{21,25},... | collective-permute-start | bytes 688136 | tf_op jit(solution)/shard_map/ppermute | solution.py:891
  11.5 4.2 %collective-permute-start.4 = (f32[55,8,128]{2,1,0:T(8,128)S(1)}, f32[55,8,128]{2,1,0:T(8,128)S(1)}, u32[]{:S(2)}, u32[]{:S(2)}) collective-permute-start(f32[55,8,128]{2,1,0:T(8,128)S(1)} %get-tuple-element.24), channel_id=1, source_target_pairs={{0,4},{4,0},{8,12},{12,8},{16,20},{20,16},{24,28},{28,24},{1,5},{5... | collective-permute-start | bytes 675848 | tf_op jit(solution)/shard_map/ppermute | solution.py:887
  15.6 1.1 %collective-permute-done.4.first_x_ref = f32[55,8,128]{2,1,0:T(8,128)S(1)} collective-permute-done((f32[55,8,128]{2,1,0:T(8,128)S(1)}, f32[55,8,128]{2,1,0:T(8,128)S(1)}, u32[]{:S(2)}, u32[]{:S(2)}) %collective-permute-start.4) | collective-permute-done | bytes 225312 | tf_op jit(solution)/shard_map/ppermute | solution.py:887
  16.8 0.0 collective-permute-done.5.second_x_ref
  16.8 5.5 %steps.1 = (f32[19,8,256]{2,1,0:T(8,128)}, f32[32,64]{1,0:T(8,128)S(1)}) custom-call(f32[38,8,128]{2,1,0:T(8,128)S(1)} %get-tuple-element.15.state_ref, f32[38,8,128]{2,1,0:T(8,128)S(1)} %get-tuple-element.16.cot_ref, f32[38,8,128]{2,1,0:T(8,128)S(1)} %get-tuple-element.17.own_ref, f32[10,8,128]{2,1,0:T(8,128)S(1)} %get-tuple-element.18.field_ref.own_field_ref, ...), custom_call_target="tpu_custom_call" | custom-call | tf_op jit(solution)/shard_map/steps/pallas_call | solution.py:927
  22.3 17.9 %all_to_all.9.parts_ref = f32[32,1,64]{2,1,0:T(1,128)S(1)} all-to-all(f32[32,1,64]{2,1,0:T(1,128)S(1)} %bitcast.2), channel_id=1, replica_groups=mesh['gx'=8,'gy'=4] {'gx','gy'}, dimensions={0} | all-to-all | bytes 16384 | tf_op jit(solution)/shard_map/all_to_all | solution.py:944
  40.1 0.5 %add_panels.1 = f32[1,64]{1,0:T(1,128)} custom-call(f32[32,1,64]{2,1,0:T(1,128)S(1)} %all_to_all.9.parts_ref), custom_call_target="tpu_custom_call" | custom-call | tf_op jit(solution)/shard_map/add_panels/pallas_call | solution.py:945
Async XLA Ops:
  2.1 8.4 %collective-permute-start = (f32[39,8,128]{2,1,0:T(8,128)S(1)}, f32[39,8,128]{2,1,0:T(8,128)S(1)}, u32[]{:S(2)}, u32[]{:S(2)}) collective-permute-start(f32[39,8,128]{2,1,0:T(8,128)S(1)} %get-tuple-element.20), channel_id=1, source_target_pairs={{0,1},{1,0},{2,3},{3,2},{4,5},{5,4},{6,7},{7,6},{8,9},{9,8},{10,11... | collective-permute-start | bytes 479240 | tf_op jit(solution)/shard_map/ppermute | solution.py:887
  5.1 5.4 %collective-permute-start.3 = (f32[38,8,128]{2,1,0:T(8,128)S(1)}, f32[38,8,128]{2,1,0:T(8,128)S(1)}, u32[]{:S(2)}, u32[]{:S(2)}) collective-permute-start(f32[38,8,128]{2,1,0:T(8,128)S(1)} %get-tuple-element.23), channel_id=1, source_target_pairs={{4,8},{12,16},{20,24},{8,4},{16,12},{24,20},{5,9},{13,17},{21,25},... | collective-permute-start | bytes 466952 | tf_op jit(solution)/shard_map/ppermute | solution.py:891
  5.7 3.7 %collective-permute-start.1 = (f32[37,8,128]{2,1,0:T(8,128)S(1)}, f32[37,8,128]{2,1,0:T(8,128)S(1)}, u32[]{:S(2)}, u32[]{:S(2)}) collective-permute-start(f32[37,8,128]{2,1,0:T(8,128)S(1)} %get-tuple-element.21), channel_id=1, source_target_pairs={{1,2},{2,1},{5,6},{6,5},{9,10},{10,9},{13,14},{14,13},{17,18},{18,... | collective-permute-start | bytes 454664 | tf_op jit(solution)/shard_map/ppermute | solution.py:891
  6.4 4.0 %collective-permute-start.2 = (f32[37,8,128]{2,1,0:T(8,128)S(1)}, f32[37,8,128]{2,1,0:T(8,128)S(1)}, u32[]{:S(2)}, u32[]{:S(2)}) collective-permute-start(f32[37,8,128]{2,1,0:T(8,128)S(1)} %get-tuple-element.22), channel_id=1, source_target_pairs={{0,4},{4,0},{8,12},{12,8},{16,20},{20,16},{24,28},{28,24},{1,5},{5... | collective-permute-start | bytes 454664 | tf_op jit(solution)/shard_map/ppermute | solution.py:887
  10.8 6.0 %collective-permute-start.5 = (f32[56,8,128]{2,1,0:T(8,128)S(1)}, f32[56,8,128]{2,1,0:T(8,128)S(1)}, u32[]{:S(2)}, u32[]{:S(2)}) collective-permute-start(f32[56,8,128]{2,1,0:T(8,128)S(1)} %get-tuple-element.25), channel_id=1, source_target_pairs={{4,8},{12,16},{20,24},{8,4},{16,12},{24,20},{5,9},{13,17},{21,25},... | collective-permute-start | bytes 688136 | tf_op jit(solution)/shard_map/ppermute | solution.py:891
  11.5 5.3 %collective-permute-start.4 = (f32[55,8,128]{2,1,0:T(8,128)S(1)}, f32[55,8,128]{2,1,0:T(8,128)S(1)}, u32[]{:S(2)}, u32[]{:S(2)}) collective-permute-start(f32[55,8,128]{2,1,0:T(8,128)S(1)} %get-tuple-element.24), channel_id=1, source_target_pairs={{0,4},{4,0},{8,12},{12,8},{16,20},{20,16},{24,28},{28,24},{1,5},{5... | collective-permute-start | bytes 675848 | tf_op jit(solution)/shard_map/ppermute | solution.py:887

commit v11 on v10

--- a/solution.py
+++ b/solution.py
@@ -44,12 +44,13 @@
 
 Y_CODE1, Y_CODE2, Y_CODE3, Y_POP, Y_COT = 38, 39, 40, 41, 42
 Y_TILES = 43
-X_EXTRA, X_CODE13 = 19, 20
-X_LANE = 21
+X_EXTRA = 19
+X_LANE = 20
+X_SIDE = 2 * X_LANE
 X_RING = 4 * X_LANE
-X_CODE2 = X_RING + Q + 1
+X_CODE13 = X_RING + Q + 1
+X_CODE2 = X_CODE13 + 4
 X_TILES = X_CODE2 + 2
-X_SIDE = 2 * X_LANE
 EMPTY = 25
 FREE = NZ - EMPTY
 WEIGHTS = [W_REST] + [W_AXIS] * 6 + [W_DIAG] * 12
@@ -269,8 +270,7 @@
         for at, value in self.held.items():
             for k, host in enumerate(self.layout.hosts[at]):
                 place = self.layout.place[host]
-                source = jnp.where(spare, NZ * k + FREE * column + depth - EMPTY, 0)
-                moved = jnp.take_along_axis(value, source, axis=1, mode="promise_in_bounds")
+                moved = pltpu.roll(value, EMPTY - FREE * k, 1)
                 self.ref[place] = jnp.where(spare, moved, self.ref[place])
         for place in range(self.layout.size, self.ref.shape[0]):
             self.ref[place] = jnp.zeros((ROWS, LANES), jnp.float32)
@@ -278,21 +278,26 @@
 
 class Unpacking:
     def __init__(self, source, layout):
-        self.source, self.layout = source, layout
+        self.source, self.layout, self.cache = source, layout, {}
+        self.changed = set(layout.guests).union(*layout.hosts.values())
 
     def __getitem__(self, at):
+        if at not in self.cache:
+            self.cache[at] = self.read(at)
+        return self.cache[at]
+
+    def read(self, at):
         row, lane, column, depth = iotas()
         layout = self.layout
         if at in layout.guests:
             value = None
-            lanes = jnp.where(depth < EMPTY, NZ * (depth // FREE) + EMPTY + depth % FREE, 0)
             for k, host in enumerate(layout.hosts[at]):
                 tile = self.source[layout.place[host]]
-                moved = jnp.take_along_axis(tile, lanes, axis=1, mode="promise_in_bounds")
-                value = moved if value is None else jnp.where(column == k, moved, value)
+                moved = pltpu.roll(tile, LANES - (EMPTY - FREE * k), 1)
+                value = moved if value is None else jnp.where(depth >= FREE * k, moved, value)
         else:
             value = self.source[layout.place[at]]
-        if at in layout.fills:
+        if at in self.changed:
             value = jnp.where(depth >= EMPTY, layout.fills[at], value)
         return value
 
@@ -456,7 +461,6 @@
             X_LANE * t,
             lambda i: own_ref[2 * i + t],
             lambda i: tile_of(cot_ref, i, t),
-            lambda s: codes[t][s - 1],
         )
     side.finish()
 
@@ -496,20 +500,22 @@
     return population, cotangent, codes
 
 
-def pack_lines(deal, first, population, cotangent, codes):
+def mix_lines(deal, at, pop, cot, deep, way):
     row, lane, column, depth = iotas()
-
-    def put(at, pop, cot, deep, way):
-        if way == 1:
-            mixed = jnp.where(row >= deep, pop, lines(cot, deep))
-        else:
-            mixed = jnp.where(row < ROWS - deep, pop, lines(cot, -deep))
-        deal.put(way, first + at, mixed)
+    if way == 1:
+        mixed = jnp.where(row >= deep, pop, lines(cot, deep))
+    else:
+        mixed = jnp.where(row < ROWS - deep, pop, lines(cot, -deep))
+    deal.put(way, at, mixed)
+
+
+def pack_lines(deal, first, population, cotangent):
+    row, lane, column, depth = iotas()
 
     for i in range(Q):
         pop, cot = population(i), cotangent(i)
         for way in (1, -1):
-            put(i, pop, cot, 3 - way * VELOCITIES[i][0], way)
+            mix_lines(deal, first + i, pop, cot, 3 - way * VELOCITIES[i][0], way)
     for way in (1, -1):
         extra = None
         for k, i in enumerate(turned(0, -way)):
@@ -519,7 +525,6 @@
             value = lines(cotangent(i), 4 + k - (5 if way == 1 else 2))
             extra = jnp.where(row == 4 + k, value, extra)
         deal.put(way, first + X_EXTRA, extra)
-        put(X_CODE13, codes(1), codes(3), 3, way)
 
 
 def from_x(ref, n, way):
@@ -545,7 +550,7 @@
     def codes(s):
         if s == 2:
             return lines(ref[X_CODE2 + n // 2], 4 * (n % 2))
-        value = ref[first + X_CODE13]
+        value = ref[X_CODE13 + n]
         return value if s == 1 else lines(value, -3 * way)
 
     return population, cotangent, codes
@@ -568,11 +573,19 @@
             X_LANE * n,
             lambda i: population(i, c),
             lambda i: cotangent(i, c),
-            lambda s: codes(s, c),
         )
     for n in range(Q + 1):
         value = population(n, 0) if n < Q else codes(1, 0)
         deal.put_both(X_RING + n, value)
+    for n in range(4):
+        if n < 2:
+            first = jnp.where(depth == NZ - 1, field_ref[2 * OWN_PHI + n], field_ref[2 + n])
+            third = field_ref[6 + n]
+        else:
+            c = (1, 4)[n - 2]
+            first, third = codes(1, c), codes(3, c)
+        for way in (1, -1):
+            mix_lines(deal, X_CODE13 + n, first, third, 3, way)
     both_codes(X_CODE2, field_ref[4], field_ref[5])
     both_codes(X_CODE2 + 1, codes(2, 1), codes(2, 4))
     deal.finish()
@@ -592,106 +605,124 @@
     return pl.ds({0: 2 * ROWS, -1: 2 * ROWS - 1, 1: 1}[step], ROWS)
 
 
+def put_halo(ref, at, halo):
+    ref[at, pl.ds(0, ROWS), :] = halo
+    ref[at, halo_rows(), :] = halo
+
+
 def put_ring(ref, at, own, halo):
     ref[at, own_rows(), :] = own
-    ref[at, pl.ds(0, ROWS), :] = halo
-    ref[at, halo_rows(), :] = halo
-
-
-def fill(from_left, own_ref, field_ref, cot_ref, from_below, pop, cot, wide, field):
+    put_halo(ref, at, halo)
+
+
+def expand(code):
     row, lane, column, depth = iotas()
     top = depth == NZ - 1
-    after = row < 4
-
-    def expand(code):
-        phi = jnp.where(top, code, 0.0)
-        for step in (1, 2, 4, 8, 16):
-            phi = phi + pltpu.roll(phi, LANES - step, 1)
-        return jnp.where(top, 0.0, code), phi
-
-    for c in range(5):
-        t = c - 2
-        if t in (0, 1):
-            own = (
-                lambda i: own_ref[2 * i + t],
-                lambda i: cot_ref[2 * i + t],
-                lambda s: field_ref[2 * s + t],
-            )
-            code_phi = field_ref[2 + t], field_ref[2 * OWN_PHI + t]
-        else:
-            own = tuple(functools.partial(lambda g, n: g(n, c), get) for get in from_left)
-            code_phi = expand(own[2](1))
+    phi = jnp.where(top, code, 0.0)
+    for step in (1, 2, 4, 8, 16):
+        phi = phi + pltpu.roll(phi, LANES - step, 1)
+    return jnp.where(top, 0.0, code), phi
+
+
+def lay_own(c, population, cotangent, codes, code_phi, pop, cot, wide, field):
+    for i in range(Q):
+        pop[5 * i + c, pl.ds(2 * ROWS, ROWS), :] = population(i)
         if c:
-            n = (None, 2, 0, 1, 3)[c]
-            below, above = from_x(from_below[0], n, 1), from_x(from_below[1], n, -1)
-        else:
-            below, above = (
-                (lambda i, ref=ref: ref[X_RING + i], None, lambda s, ref=ref: ref[X_RING + Q])
-                for ref in from_below
-            )
-        parts = (expand(below[2](1)), code_phi, expand(above[2](1)))
-        for i in range(Q):
-            for r, side in enumerate((below, own, above)):
-                pop[5 * i + c, pl.ds(ROWS * (r + 1), ROWS), :] = side[0](i)
-        for n in range(2):
-            for r in range(3):
-                wide[n, c, r] = parts[r][n]
+            cot[4 * i + c - 1, own_rows(), :] = cotangent(i)
+    for n in range(2):
+        wide[n, c, 1] = code_phi[n]
+    if c:
+        field[0, c - 1, 0], field[1, c - 1, 0] = code_phi[1], code_phi[0]
+        for s in (2, 3):
+            field[s, c - 1, 0] = codes(s)
+
+
+def lay_halo(c, below, above, pop, cot):
+    row, lane, column, depth = iotas()
+    for i in range(Q):
+        pop[5 * i + c, pl.ds(ROWS, ROWS), :] = below[0](i)
+        pop[5 * i + c, pl.ds(3 * ROWS, ROWS), :] = above[0](i)
         if c:
-            for i in range(Q):
-                halo = jnp.where(after, above[1](i), below[1](i))
-                put_ring(cot, 4 * i + c - 1, own[1](i), halo)
-            for n, place in ((0, 1), (1, 0)):
-                field[place, c - 1, 0] = parts[1][n]
-                field[place, c - 1, 1] = jnp.where(after, parts[2][n], parts[0][n])
-            for s in (2, 3):
-                field[s, c - 1, 0] = own[2](s)
-                field[s, c - 1, 1] = jnp.where(after, above[2](s), below[2](s))
-
-
-def steps_kernel(
-    sizes,
-    state_ref,
-    cot_ref,
-    own_ref,
-    own_field_ref,
-    names_ref,
+            put_halo(cot, 4 * i + c - 1, jnp.where(row < 4, above[1](i), below[1](i)))
+
+
+def lay_codes(c, below, above, wide, field):
+    row, lane, column, depth = iotas()
+    before, after = expand(below[2](1)), expand(above[2](1))
+    for n in range(2):
+        wide[n, c, 0], wide[n, c, 2] = before[n], after[n]
+    if c:
+        for n, place in ((0, 1), (1, 0)):
+            field[place, c - 1, 1] = jnp.where(row < 4, after[n], before[n])
+        for s in (2, 3):
+            field[s, c - 1, 1] = jnp.where(row < 4, above[2](s), below[2](s))
+
+
+def lay_out(
     first_y_ref,
     second_y_ref,
     first_side_ref,
     second_side_ref,
+    own_ref,
+    field_ref,
+    cot_ref,
+    pop,
+    cot,
+    wide,
+    field,
+):
+    y_layout, side_layout, _ = layouts()
+    from_left = from_y(*sides(first_y_ref, second_y_ref, "gy", y_layout))
+    below, above = sides(first_side_ref, second_side_ref, "gx", side_layout)
+    for c in range(5):
+        t = c - 2
+        if t in (0, 1):
+            lay_own(
+                c,
+                lambda i: own_ref[2 * i + t],
+                lambda i: cot_ref[2 * i + t],
+                lambda s: field_ref[2 * s + t],
+                (field_ref[2 + t], field_ref[2 * OWN_PHI + t]),
+                pop,
+                cot,
+                wide,
+                field,
+            )
+            lay_halo(c, from_x(below, t, 1), from_x(above, t, -1), pop, cot)
+        else:
+            own = [functools.partial(lambda g, n: g(n, c), get) for get in from_left]
+            lay_own(c, *own, expand(own[2](1)), pop, cot, wide, field)
+
+
+def lay_corners(first_x_ref, second_x_ref, pop, cot, wide, field):
+    _, _, layout = layouts()
+    below, above = (
+        Joined(None, side, X_SIDE) for side in sides(first_x_ref, second_x_ref, "gx", layout)
+    )
+    lay_halo(
+        0, (lambda i: below[X_RING + i],), (lambda i: above[X_RING + i],), pop, cot
+    )
+    ring = [(None, None, lambda s, ref=ref: ref[X_RING + Q]) for ref in (below, above)]
+    lay_codes(0, *ring, wide, field)
+    for n, c in enumerate((2, 3, 1, 4)):
+        halves = from_x(below, n, 1), from_x(above, n, -1)
+        if n > 1:
+            lay_halo(c, *halves, pop, cot)
+        lay_codes(c, *halves, wide, field)
+
+
+def steps_kernel(
+    sizes,
+    state_ref,
+    own_field_ref,
+    names_ref,
     first_x_ref,
     second_x_ref,
-    adjoint_ref,
-    panel_ref,
-    pop_a,
-    pop_b,
-    ring_a,
-    ring_b,
-    wide,
-    field,
-    saved,
-    mom,
-    grad,
+    *refs,
 ):
+    adjoint_ref, panel_ref, pop_a, ring_a, wide, field, pop_b, ring_b, saved, mom, grad = refs[4:]
     size_x, size_y = sizes
-    y_layout, side_layout, rest_layout = layouts()
-    fill(
-        from_y(*sides(first_y_ref, second_y_ref, "gy", y_layout)),
-        own_ref,
-        own_field_ref,
-        cot_ref,
-        [
-            Joined(side, rest, X_SIDE)
-            for side, rest in zip(
-                sides(first_side_ref, second_side_ref, "gx", side_layout),
-                sides(first_x_ref, second_x_ref, "gx", rest_layout),
-            )
-        ],
-        pop_a,
-        ring_a,
-        wide,
-        field,
-    )
+    lay_corners(first_x_ref, second_x_ref, pop_a, ring_a, wide, field)
 
     at_x, at_y = lax.axis_index("gx"), lax.axis_index("gy")
     edges = (
@@ -872,13 +903,14 @@
     devices = size_x * size_y
     y_layout, side_layout, rest_layout = layouts()
 
-    def call(kernel, out_shape, in_specs, scratch=(), name=None):
+    def call(kernel, out_shape, in_specs, scratch=(), name=None, aliases={}):
         return pl.pallas_call(
             kernel,
             out_shape=out_shape,
             in_specs=in_specs,
             out_specs=jax.tree.map(lambda _: VMEM, out_shape),
             scratch_shapes=scratch,
+            input_output_aliases=aliases,
             compiler_params=pltpu.CompilerParams(vmem_limit_bytes=32 * 1024 * 1024),
             name=name,
         )
@@ -896,8 +928,8 @@
     ]
     first_y, second_y, first_side, second_side, own, state, cot, field, names = call(
         pack_own,
-        (tiles_of(y_layout.size + 2), tiles_of(y_layout.size))
-        + (tiles_of(side_layout.size), tiles_of(y_layout.size + 1))
+        (tiles_of(y_layout.size),) * 2
+        + (tiles_of(side_layout.size), tiles_of(side_layout.size + 1))
         + (tiles_of(2 * Q),) * 3
         + (tiles_of(2 * OWN_PHI + 2), jax.ShapeDtypeStruct((2, ROWS, LANES), jnp.int32)),
         [HBM] * 5,
@@ -924,23 +956,29 @@
     second_x = swap_between(second_x, "gx", size_x)
     first_x = swap(first_x, "gx", size_x)
 
-    adjoint, sums = call(
+    spaces = (
+        shape_of(5 * Q, 5 * ROWS, LANES),
+        shape_of(4 * Q, 3 * ROWS, LANES),
+        shape_of(2, 5, 3, ROWS, LANES),
+        shape_of(4, 4, 2, ROWS, LANES),
+    )
+    laid = call(lay_out, spaces, [VMEM] * 7, name="lay_out")(
+        first_y, second_y, first_side, second_side, own, field, cot
+    )
+    adjoint, sums, *_ = call(
         functools.partial(steps_kernel, sizes),
-        (shape_of(Q, ROWS, 2 * LANES), shape_of(devices, panels)),
-        [VMEM] * 11,
+        (shape_of(Q, ROWS, 2 * LANES), shape_of(devices, panels)) + spaces,
+        [VMEM] * 9,
         [
             pltpu.VMEM((5 * Q, 5 * ROWS, LANES), jnp.float32),
-            pltpu.VMEM((5 * Q, 5 * ROWS, LANES), jnp.float32),
             pltpu.VMEM((4 * Q, 3 * ROWS, LANES), jnp.float32),
-            pltpu.VMEM((4 * Q, 3 * ROWS, LANES), jnp.float32),
-            pltpu.VMEM((2, 5, 3, ROWS, LANES), jnp.float32),
-            pltpu.VMEM((4, 4, 2, ROWS, LANES), jnp.float32),
             pltpu.VMEM((3, Q, 5, ROWS, LANES), jnp.float32),
             pltpu.VMEM((3, 5, 5, 2, ROWS, LANES), jnp.float32),
             pltpu.VMEM((4, ROWS, LANES), jnp.float32),
         ],
         name="steps",
-    )(state, cot, own, field, names, first_y, second_y, first_side, second_side, first_x, second_x)
+        aliases={5 + n: 2 + n for n in range(4)},
+    )(state, field, names, first_x, second_x, *laid)
     gathered = lax.all_to_all(sums, ("gx", "gy"), 0, 0, tiled=True)
     totals = call(add_panels, shape_of(1, panels), [VMEM], name="add_panels")(
         gathered.reshape(devices, 1, panels)

time: 40.9 us -> 39.5 us (0.966)
  Pallas kernels: 7.85 us -> 6.89 us
  blocking collectives: 17.9 us -> 17.2 us
  starting transfers between devices: 12.2 us -> 12.8 us
  waiting for transfers between devices: 2.13 us -> 1.7 us
    pallas_call x1, Pallas kernels: 5.51 us -> 4.4 us  [on_device(): call(functools.partial(steps_kernel, sizes), (shape_of(Q, ROWS, 2 * LANES...]
    all_to_all x1, blocking collectives: 17.9 us -> 17.2 us  [on_device(): gathered = lax.all_to_all(sums, ('gx', 'gy'), 0, 0, tiled=True)]
    ppermute x3, starting transfers between devices: 10.2 us -> 10.8 us  [swap(): lax.ppermute(value, axis, [(i, i ^ 1) for i in range(size) if i ^ 1 < size])]
    ppermute x3, waiting for transfers between devices: 2.12 us -> 1.69 us  [swap(): lax.ppermute(value, axis, [(i, i ^ 1) for i in range(size) if i ^ 1 < size])]
    pallas_call x1 -> x2, Pallas kernels: 1.43 us -> 1.72 us  [the longest x1 1.29 us: on_device(): call(pack_own, (tiles_of(y_layout.size),) * 2 + (tiles_of(side_layout.siz...]
  transfers between devices with their start and end apart: 6 -> 6, of which waited for: 2 -> 2; matrix products, arithmetic and copies ran while one was open for 0% -> 0% of each run, Pallas kernels for 0% -> 1%
where the time goes in v11:
time: 39.5 us; the launch traced here: 39.3 us
  blocking collectives  17.2 us (44%)
  starting transfers between devices  12.8 us (32%)
  Pallas kernels  6.89 us (17%)
  waiting for transfers between devices  1.7 us (4%)
  between operations  0.68 us (2%)
    all_to_all x1, blocking collectives, on_device(): gathered = lax.all_to_all(sums, ('gx', 'gy'), 0, 0, tiled=True)  17.2 us
    ppermute x3, starting transfers between devices, swap(): lax.ppermute(value, axis, [(i, i ^ 1) for i in range(size) if i ^ 1 < size])  10.8 us
    pallas_call x1, Pallas kernels, on_device(): call(functools.partial(steps_kernel, sizes), (shape_of(Q, ROWS, 2 * LANES...  4.4 us
    ppermute x3, starting transfers between devices, swap_between(): return lax.ppermute(value, axis, pairs + [(j, i) for i, j in pairs])  2 us
    ppermute x3, waiting for transfers between devices, swap(): lax.ppermute(value, axis, [(i, i ^ 1) for i in range(size) if i ^ 1 < size])  1.69 us
    pallas_call x1, Pallas kernels, on_device(): call(pack_own, (tiles_of(y_layout.size),) * 2 + (tiles_of(side_layout.siz...  1.29 us
  transfers between devices with their start and end apart: 6, of which 2 were waited for; matrix products, arithmetic and copies ran while one was open for 0% of the time, Pallas kernels for 1%

profile of v11, /device:TPU:0, one launch (start us, length us, event | category | flops | bytes accessed | tf_op | source)
XLA Modules:
  0.0 39.3 jit_solution(1246798892150297405)
XLA Ops:
  0.6 1.3 %pack_own.1 = (f32[37,8,128]{2,1,0:T(8,128)S(1)}, f32[37,8,128]{2,1,0:T(8,128)S(1)}, f32[35,8,128]{2,1,0:T(8,128)S(1)}, f32[36,8,128]{2,1,0:T(8,128)S(1)}, f32[3...) custom-call(f32[19,8,256]{2,1,0:T(8,128)} %f_hbm.1, ...), custom_call_target="tpu_custom_call" | custom-call | tf_op jit(solution)/shard_map/pack_own/pallas_call | solution.py:929
  1.9 3.0 %collective-permute-start = (f32[37,8,128]{2,1,0:T(8,128)S(1)}, f32[37,8,128]{2,1,0:T(8,128)S(1)}, u32[]{:S(2)}, u32[]{:S(2)}) collective-permute-start(f32[37,8,128]{2,1,0:T(8,128)S(1)} %get-tuple-element.22), channel_id=1, source_target_pairs={{0,1},{1,0},{2,3},{3,2},{4,5},{5,4},{6,7},{7,6},{8,9},{9,8},{10,11... | collective-permute-start | bytes 454664 | tf_op jit(solution)/shard_map/ppermute | solution.py:919
  4.9 0.7 %collective-permute-start.1 = (f32[37,8,128]{2,1,0:T(8,128)S(1)}, f32[37,8,128]{2,1,0:T(8,128)S(1)}, u32[]{:S(2)}, u32[]{:S(2)}) collective-permute-start(f32[37,8,128]{2,1,0:T(8,128)S(1)} %get-tuple-element.23), channel_id=1, source_target_pairs={{1,2},{2,1},{5,6},{6,5},{9,10},{10,9},{13,14},{14,13},{17,18},{18,... | collective-permute-start | bytes 454664 | tf_op jit(solution)/shard_map/ppermute | solution.py:923
  5.6 0.7 %collective-permute-start.3 = (f32[36,8,128]{2,1,0:T(8,128)S(1)}, f32[36,8,128]{2,1,0:T(8,128)S(1)}, u32[]{:S(2)}, u32[]{:S(2)}) collective-permute-start(f32[36,8,128]{2,1,0:T(8,128)S(1)} %get-tuple-element.25), channel_id=1, source_target_pairs={{4,8},{12,16},{20,24},{8,4},{16,12},{24,20},{5,9},{13,17},{21,25},... | collective-permute-start | bytes 442376 | tf_op jit(solution)/shard_map/ppermute | solution.py:923
  6.3 3.0 %collective-permute-start.2 = (f32[35,8,128]{2,1,0:T(8,128)S(1)}, f32[35,8,128]{2,1,0:T(8,128)S(1)}, u32[]{:S(2)}, u32[]{:S(2)}) collective-permute-start(f32[35,8,128]{2,1,0:T(8,128)S(1)} %get-tuple-element.24), channel_id=1, source_target_pairs={{0,4},{4,0},{8,12},{12,8},{16,20},{20,16},{24,28},{28,24},{1,5},{5... | collective-permute-start | bytes 430088 | tf_op jit(solution)/shard_map/ppermute | solution.py:919
  9.3 1.0 %collective-permute-done.2.early_a.first_side_ref = f32[35,8,128]{2,1,0:T(8,128)S(1)} collective-permute-done((f32[35,8,128]{2,1,0:T(8,128)S(1)}, f32[35,8,128]{2,1,0:T(8,128)S(1)}, u32[]{:S(2)}, u32[]{:S(2)}) %collective-permute-start.2) | collective-permute-done | bytes 143392 | tf_op jit(solution)/shard_map/ppermute | solution.py:919
  10.3 0.0 collective-permute-done.3.early_b.second_side_ref
  10.3 0.0 collective-permute-done.first_y_ref
  10.3 0.0 collective-permute-done.1.second_y_ref
  10.3 0.2 pack_x.1
  10.5 0.7 %collective-permute-start.5 = (f32[58,8,128]{2,1,0:T(8,128)S(1)}, f32[58,8,128]{2,1,0:T(8,128)S(1)}, u32[]{:S(2)}, u32[]{:S(2)}) collective-permute-start(f32[58,8,128]{2,1,0:T(8,128)S(1)} %get-tuple-element.27), channel_id=1, source_target_pairs={{4,8},{12,16},{20,24},{8,4},{16,12},{24,20},{5,9},{13,17},{21,25},... | collective-permute-start | bytes 712712 | tf_op jit(solution)/shard_map/ppermute | solution.py:923
  11.2 4.8 %collective-permute-start.4 = (f32[57,8,128]{2,1,0:T(8,128)S(1)}, f32[57,8,128]{2,1,0:T(8,128)S(1)}, u32[]{:S(2)}, u32[]{:S(2)}) collective-permute-start(f32[57,8,128]{2,1,0:T(8,128)S(1)} %get-tuple-element.26), channel_id=1, source_target_pairs={{0,4},{4,0},{8,12},{12,8},{16,20},{20,16},{24,28},{28,24},{1,5},{5... | collective-permute-start | bytes 700424 | tf_op jit(solution)/shard_map/ppermute | solution.py:919
  16.0 0.4 %lay_out.1 = (f32[95,40,128]{2,1,0:T(8,128)S(1)}, f32[76,24,128]{2,1,0:T(8,128)S(1)}, f32[2,5,3,8,128]{4,3,2,1,0:T(8,128)S(1)}, f32[4,4,2,8,128]{4,3,2,1,0:T(8,128)S(1)}) custom-call(f32[37,8,128]{2,1,0:T(8,128)S(1)} %collective-permute-done.first_y_ref, f32[37,8,128]{2,1,0:T(8,128)S(1)} %collective-permute-done.1.second_y_ref, ...), custom_call_target="tpu_custom_call" | custom-call | tf_op jit(solution)/shard_map/lay_out/pallas_call | solution.py:965
  16.4 0.7 %collective-permute-done.4.first_x_ref = f32[57,8,128]{2,1,0:T(8,128)S(1)} collective-permute-done((f32[57,8,128]{2,1,0:T(8,128)S(1)}, f32[57,8,128]{2,1,0:T(8,128)S(1)}, u32[]{:S(2)}, u32[]{:S(2)}) %collective-permute-start.4) | collective-permute-done | bytes 233504 | tf_op jit(solution)/shard_map/ppermute | solution.py:919
  17.1 0.0 collective-permute-done.5.second_x_ref
  17.1 4.4 %steps.1 = (f32[19,8,256]{2,1,0:T(8,128)}, f32[32,64]{1,0:T(8,128)S(1)}, f32[95,40,128]{2,1,0:T(8,128)S(1)}, f32[76,24,128]{2,1,0:T(8,128)S(1)}, f32[2,5,3,8,128...) custom-call(f32[38,8,128]{2,1,0:T(8,128)S(1)} %get-tuple-element.19., ...), custom_call_target="tpu_custom_call", output_to_operand_aliasing={{2}: (5, {}), {3}: (6, {}), {4}: (7, {}), {5}: (8, {})} | custom-call | tf_op jit(solution)/shard_map/steps/pallas_call | solution.py:968
  21.5 17.2 %all_to_all.9.parts_ref = f32[32,1,64]{2,1,0:T(1,128)S(1)} all-to-all(f32[32,1,64]{2,1,0:T(1,128)S(1)} %bitcast.2), channel_id=1, replica_groups=mesh['gx'=8,'gy'=4] {'gx','gy'}, dimensions={0} | all-to-all | bytes 16384 | tf_op jit(solution)/shard_map/all_to_all | solution.py:982
  38.7 0.5 %add_panels.1 = f32[1,64]{1,0:T(1,128)} custom-call(f32[32,1,64]{2,1,0:T(1,128)S(1)} %all_to_all.9.parts_ref), custom_call_target="tpu_custom_call" | custom-call | tf_op jit(solution)/shard_map/add_panels/pallas_call | solution.py:983
Async XLA Ops:
  1.9 8.4 %collective-permute-start = (f32[37,8,128]{2,1,0:T(8,128)S(1)}, f32[37,8,128]{2,1,0:T(8,128)S(1)}, u32[]{:S(2)}, u32[]{:S(2)}) collective-permute-start(f32[37,8,128]{2,1,0:T(8,128)S(1)} %get-tuple-element.22), channel_id=1, source_target_pairs={{0,1},{1,0},{2,3},{3,2},{4,5},{5,4},{6,7},{7,6},{8,9},{9,8},{10,11... | collective-permute-start | bytes 454664 | tf_op jit(solution)/shard_map/ppermute | solution.py:919
  4.9 5.4 %collective-permute-start.1 = (f32[37,8,128]{2,1,0:T(8,128)S(1)}, f32[37,8,128]{2,1,0:T(8,128)S(1)}, u32[]{:S(2)}, u32[]{:S(2)}) collective-permute-start(f32[37,8,128]{2,1,0:T(8,128)S(1)} %get-tuple-element.23), channel_id=1, source_target_pairs={{1,2},{2,1},{5,6},{6,5},{9,10},{10,9},{13,14},{14,13},{17,18},{18,... | collective-permute-start | bytes 454664 | tf_op jit(solution)/shard_map/ppermute | solution.py:923
  5.6 4.7 %collective-permute-start.3 = (f32[36,8,128]{2,1,0:T(8,128)S(1)}, f32[36,8,128]{2,1,0:T(8,128)S(1)}, u32[]{:S(2)}, u32[]{:S(2)}) collective-permute-start(f32[36,8,128]{2,1,0:T(8,128)S(1)} %get-tuple-element.25), channel_id=1, source_target_pairs={{4,8},{12,16},{20,24},{8,4},{16,12},{24,20},{5,9},{13,17},{21,25},... | collective-permute-start | bytes 442376 | tf_op jit(solution)/shard_map/ppermute | solution.py:923
  6.3 4.0 %collective-permute-start.2 = (f32[35,8,128]{2,1,0:T(8,128)S(1)}, f32[35,8,128]{2,1,0:T(8,128)S(1)}, u32[]{:S(2)}, u32[]{:S(2)}) collective-permute-start(f32[35,8,128]{2,1,0:T(8,128)S(1)} %get-tuple-element.24), channel_id=1, source_target_pairs={{0,4},{4,0},{8,12},{12,8},{16,20},{20,16},{24,28},{28,24},{1,5},{5... | collective-permute-start | bytes 430088 | tf_op jit(solution)/shard_map/ppermute | solution.py:919
  10.5 6.6 %collective-permute-start.5 = (f32[58,8,128]{2,1,0:T(8,128)S(1)}, f32[58,8,128]{2,1,0:T(8,128)S(1)}, u32[]{:S(2)}, u32[]{:S(2)}) collective-permute-start(f32[58,8,128]{2,1,0:T(8,128)S(1)} %get-tuple-element.27), channel_id=1, source_target_pairs={{4,8},{12,16},{20,24},{8,4},{16,12},{24,20},{5,9},{13,17},{21,25},... | collective-permute-start | bytes 712712 | tf_op jit(solution)/shard_map/ppermute | solution.py:923
  11.2 5.9 %collective-permute-start.4 = (f32[57,8,128]{2,1,0:T(8,128)S(1)}, f32[57,8,128]{2,1,0:T(8,128)S(1)}, u32[]{:S(2)}, u32[]{:S(2)}) collective-permute-start(f32[57,8,128]{2,1,0:T(8,128)S(1)} %get-tuple-element.26), channel_id=1, source_target_pairs={{0,4},{4,0},{8,12},{12,8},{16,20},{20,16},{24,28},{28,24},{1,5},{5... | collective-permute-start | bytes 700424 | tf_op jit(solution)/shard_map/ppermute | solution.py:919

commit v12 on v11

--- a/solution.py
+++ b/solution.py
@@ -46,7 +46,6 @@
 Y_TILES = 43
 X_EXTRA = 19
 X_LANE = 20
-X_SIDE = 2 * X_LANE
 X_RING = 4 * X_LANE
 X_CODE13 = X_RING + Q + 1
 X_CODE2 = X_CODE13 + 4
@@ -306,15 +305,11 @@
     y_fills = {2 * i + t: WEIGHTS[i] for i in LEVEL for t in range(2)}
     y_fills.update({Y_POP: W_DIAG, Y_CODE2: 0.0})
     x_fills = {X_LANE * n + i: WEIGHTS[i] for n in range(4) for i in LEVEL}
-    side = {at: fill for at, fill in x_fills.items() if at < X_SIDE}
-    rest = {at - X_SIDE: fill for at, fill in x_fills.items() if at >= X_SIDE}
-    rest.update({X_CODE2 - X_SIDE: 0.0, X_CODE2 + 1 - X_SIDE: 0.0})
-    rest.update({X_RING - X_SIDE + i: WEIGHTS[i] for i in range(Q)})
-    ring = [X_RING - X_SIDE + i for i in range(9)]
+    x_fills.update({X_CODE2: 0.0, X_CODE2 + 1: 0.0})
+    x_fills.update({X_RING + i: WEIGHTS[i] for i in range(Q)})
     return (
         Layout(Y_TILES, [2 * i for i in LEVEL[:6]], y_fills),
-        Layout(X_SIDE, LEVEL[:5], side),
-        Layout(X_TILES - X_SIDE, ring, rest),
+        Layout(X_TILES, [X_RING + i for i in range(15)], x_fills),
     )
 
 
@@ -327,8 +322,8 @@
 
 
 class Deal:
-    def __init__(self, even, first, second, layout, skip=0):
-        self.even, self.skip, self.held = even, skip, {}
+    def __init__(self, even, first, second, layout):
+        self.even, self.held = even, {}
         self.first, self.second = Packing(first, layout), Packing(second, layout)
 
     def put(self, way, at, value):
@@ -337,24 +332,16 @@
             return
         other = self.held.pop((-way, at))
         up, down = (value, other) if way == 1 else (other, value)
-        self.first[at - self.skip] = jnp.where(self.even, up, down)
-        self.second[at - self.skip] = jnp.where(self.even, down, up)
+        self.first[at] = jnp.where(self.even, up, down)
+        self.second[at] = jnp.where(self.even, down, up)
 
     def put_both(self, at, value):
-        self.first[at - self.skip] = value
-        self.second[at - self.skip] = value
+        self.first[at] = value
+        self.second[at] = value
 
     def finish(self):
         self.first.finish()
         self.second.finish()
-
-
-class Joined:
-    def __init__(self, first, second, cut):
-        self.first, self.second, self.cut = first, second, cut
-
-    def __getitem__(self, at):
-        return self.first[at] if at < self.cut else self.second[at - self.cut]
 
 
 def is_even(axis):
@@ -369,8 +356,6 @@
     porosity_hbm,
     first_ref,
     second_ref,
-    first_side_ref,
-    second_side_ref,
     own_ref,
     state_ref,
     own_cot_ref,
@@ -398,9 +383,7 @@
         copy.start()
     for copy in copies[:4]:
         copy.wait()
-    y_layout, side_layout, _ = layouts()
-    deal = Deal(is_even("gy"), first_ref, second_ref, y_layout)
-    side = Deal(is_even("gx"), first_side_ref, second_side_ref, side_layout)
+    deal = Deal(is_even("gy"), first_ref, second_ref, layouts()[0])
     row, lane, column, depth = iotas()
     top = depth == NZ - 1
 
@@ -456,13 +439,6 @@
     for t in range(2):
         for i in range(Q):
             own_cot_ref[2 * i + t] = tile_of(cot_ref, i, t)
-        pack_lines(
-            side,
-            X_LANE * t,
-            lambda i: own_ref[2 * i + t],
-            lambda i: tile_of(cot_ref, i, t),
-        )
-    side.finish()
 
 
 def from_y(left_ref, right_ref):
@@ -556,10 +532,10 @@
     return population, cotangent, codes
 
 
-def pack_x(field_ref, first_y_ref, second_y_ref, early_a, early_b, first_ref, second_ref):
+def pack_x(own_ref, cot_ref, field_ref, first_y_ref, second_y_ref, first_ref, second_ref):
     row, lane, column, depth = iotas()
-    y_layout, _, layout = layouts()
-    deal = Deal(is_even("gx"), first_ref, second_ref, layout, X_SIDE)
+    y_layout, x_layout = layouts()
+    deal = Deal(is_even("gx"), first_ref, second_ref, x_layout)
     population, cotangent, codes = from_y(*sides(first_y_ref, second_y_ref, "gy", y_layout))
 
     def both_codes(at, first, second):
@@ -567,6 +543,13 @@
         deal.put(1, at, jnp.where(row >= 4, first, second))
         deal.put(-1, at, jnp.where(row < 4, first, second))
 
+    for t in range(2):
+        pack_lines(
+            deal,
+            X_LANE * t,
+            lambda i: own_ref[2 * i + t],
+            lambda i: cot_ref[2 * i + t],
+        )
     for n, c in ((2, 1), (3, 4)):
         pack_lines(
             deal,
@@ -658,22 +641,8 @@
             field[s, c - 1, 1] = jnp.where(row < 4, above[2](s), below[2](s))
 
 
-def lay_out(
-    first_y_ref,
-    second_y_ref,
-    first_side_ref,
-    second_side_ref,
-    own_ref,
-    field_ref,
-    cot_ref,
-    pop,
-    cot,
-    wide,
-    field,
-):
-    y_layout, side_layout, _ = layouts()
-    from_left = from_y(*sides(first_y_ref, second_y_ref, "gy", y_layout))
-    below, above = sides(first_side_ref, second_side_ref, "gx", side_layout)
+def lay_out(first_y_ref, second_y_ref, own_ref, field_ref, cot_ref, pop, cot, wide, field):
+    from_left = from_y(*sides(first_y_ref, second_y_ref, "gy", layouts()[0]))
     for c in range(5):
         t = c - 2
         if t in (0, 1):
@@ -688,26 +657,22 @@
                 wide,
                 field,
             )
-            lay_halo(c, from_x(below, t, 1), from_x(above, t, -1), pop, cot)
         else:
             own = [functools.partial(lambda g, n: g(n, c), get) for get in from_left]
             lay_own(c, *own, expand(own[2](1)), pop, cot, wide, field)
 
 
-def lay_corners(first_x_ref, second_x_ref, pop, cot, wide, field):
-    _, _, layout = layouts()
-    below, above = (
-        Joined(None, side, X_SIDE) for side in sides(first_x_ref, second_x_ref, "gx", layout)
-    )
-    lay_halo(
-        0, (lambda i: below[X_RING + i],), (lambda i: above[X_RING + i],), pop, cot
-    )
-    ring = [(None, None, lambda s, ref=ref: ref[X_RING + Q]) for ref in (below, above)]
+def lay_halos(first_x_ref, second_x_ref, pop, cot, wide, field):
+    below, above = sides(first_x_ref, second_x_ref, "gx", layouts()[1])
+    ring = [
+        (lambda i, ref=ref: ref[X_RING + i], None, lambda s, ref=ref: ref[X_RING + Q])
+        for ref in (below, above)
+    ]
+    lay_halo(0, *ring, pop, cot)
     lay_codes(0, *ring, wide, field)
     for n, c in enumerate((2, 3, 1, 4)):
         halves = from_x(below, n, 1), from_x(above, n, -1)
-        if n > 1:
-            lay_halo(c, *halves, pop, cot)
+        lay_halo(c, *halves, pop, cot)
         lay_codes(c, *halves, wide, field)
 
 
@@ -722,7 +687,7 @@
 ):
     adjoint_ref, panel_ref, pop_a, ring_a, wide, field, pop_b, ring_b, saved, mom, grad = refs[4:]
     size_x, size_y = sizes
-    lay_corners(first_x_ref, second_x_ref, pop_a, ring_a, wide, field)
+    lay_halos(first_x_ref, second_x_ref, pop_a, ring_a, wide, field)
 
     at_x, at_y = lax.axis_index("gx"), lax.axis_index("gy")
     edges = (
@@ -886,7 +851,6 @@
 
 VMEM = pl.BlockSpec(memory_space=pltpu.VMEM)
 HBM = pl.BlockSpec(memory_space=pltpu.HBM)
-ANY = pl.BlockSpec(memory_space=pl.ANY)
 
 
 def shape_of(*dims):
@@ -901,7 +865,7 @@
     size_x, size_y = sizes
     panels = porosity.shape[0]
     devices = size_x * size_y
-    y_layout, side_layout, rest_layout = layouts()
+    y_layout, x_layout = layouts()
 
     def call(kernel, out_shape, in_specs, scratch=(), name=None, aliases={}):
         return pl.pallas_call(
@@ -926,10 +890,9 @@
         pltpu.with_memory_space_constraint(value, pltpu.HBM)
         for value in (checkpoint, cotangent, cell_codes, baffle_index, porosity)
     ]
-    first_y, second_y, first_side, second_side, own, state, cot, field, names = call(
+    first_y, second_y, own, state, cot, field, names = call(
         pack_own,
         (tiles_of(y_layout.size),) * 2
-        + (tiles_of(side_layout.size), tiles_of(side_layout.size + 1))
         + (tiles_of(2 * Q),) * 3
         + (tiles_of(2 * OWN_PHI + 2), jax.ShapeDtypeStruct((2, ROWS, LANES), jnp.int32)),
         [HBM] * 5,
@@ -943,28 +906,23 @@
         ],
         name="pack_own",
     )(*arguments)
+    first_y = swap(first_y, "gy", size_y)
     second_y = swap_between(second_y, "gy", size_y)
-    first_y = swap(first_y, "gy", size_y)
-    second_side = swap_between(second_side, "gx", size_x)
-    first_side = swap(first_side, "gx", size_x)
     first_x, second_x = call(
         pack_x,
-        (tiles_of(rest_layout.size), tiles_of(rest_layout.size + 1)),
-        [VMEM] * 3 + [ANY] * 2,
+        (tiles_of(x_layout.size), tiles_of(x_layout.size + 1)),
+        [VMEM] * 5,
         name="pack_x",
-    )(field, first_y, second_y, first_side, second_side)
+    )(own, cot, field, first_y, second_y)
     second_x = swap_between(second_x, "gx", size_x)
     first_x = swap(first_x, "gx", size_x)
-
     spaces = (
         shape_of(5 * Q, 5 * ROWS, LANES),
         shape_of(4 * Q, 3 * ROWS, LANES),
         shape_of(2, 5, 3, ROWS, LANES),
         shape_of(4, 4, 2, ROWS, LANES),
     )
-    laid = call(lay_out, spaces, [VMEM] * 7, name="lay_out")(
-        first_y, second_y, first_side, second_side, own, field, cot
-    )
+    laid = call(lay_out, spaces, [VMEM] * 5, name="lay_out")(first_y, second_y, own, field, cot)
     adjoint, sums, *_ = call(
         functools.partial(steps_kernel, sizes),
         (shape_of(Q, ROWS, 2 * LANES), shape_of(devices, panels)) + spaces,

time: 39.5 us -> 39.6 us (level)
  starting transfers between devices: 12.8 us -> 7.58 us
  blocking collectives: 17.2 us -> 20 us
  waiting for transfers between devices: 1.7 us -> 4.17 us
    ppermute x3 -> x2, starting transfers between devices: 10.8 us -> 6.23 us  [swap(): lax.ppermute(value, axis, [(i, i ^ 1) for i in range(size) if i ^ 1 < size])]
    all_to_all x1, blocking collectives: 17.2 us -> 20 us  [on_device(): gathered = lax.all_to_all(sums, ('gx', 'gy'), 0, 0, tiled=True)]
    ppermute x3 -> x2, waiting for transfers between devices: 1.69 us -> 4.17 us  [swap(): lax.ppermute(value, axis, [(i, i ^ 1) for i in range(size) if i ^ 1 < size])]
    ppermute x3 -> x2, starting transfers between devices: 2 us -> 1.34 us  [swap_between(): return lax.ppermute(value, axis, pairs + [(j, i) for i, j in pairs])]
  transfers between devices with their start and end apart: 6 -> 4, of which waited for: 2 -> 2; matrix products, arithmetic and copies ran while one was open for 0% -> 0% of each run, Pallas kernels for 1% -> 1%
where the time goes in v12:
time: 39.6 us; the launch traced here: 39.3 us
  blocking collectives  20 us (51%)
  starting transfers between devices  7.58 us (19%)
  Pallas kernels  6.9 us (17%)
  waiting for transfers between devices  4.17 us (11%)
  between operations  0.67 us (2%)
    all_to_all x1, blocking collectives, on_device(): gathered = lax.all_to_all(sums, ('gx', 'gy'), 0, 0, tiled=True)  20 us
    ppermute x2, starting transfers between devices, swap(): lax.ppermute(value, axis, [(i, i ^ 1) for i in range(size) if i ^ 1 < size])  6.23 us
    pallas_call x1, Pallas kernels, on_device(): call(functools.partial(steps_kernel, sizes), (shape_of(Q, ROWS, 2 * LANES...  4.42 us
    ppermute x2, waiting for transfers between devices, swap(): lax.ppermute(value, axis, [(i, i ^ 1) for i in range(size) if i ^ 1 < size])  4.17 us
    ppermute x2, starting transfers between devices, swap_between(): return lax.ppermute(value, axis, pairs + [(j, i) for i, j in pairs])  1.34 us
    pallas_call x1, Pallas kernels, on_device(): call(pack_own, (tiles_of(y_layout.size),) * 2 + (tiles_of(2 * Q),) * 3 +...  1.24 us
  transfers between devices with their start and end apart: 4, of which 2 were waited for; matrix products, arithmetic and copies ran while one was open for 0% of the time, Pallas kernels for 1%

profile of v12, /device:TPU:0, one launch (start us, length us, event | category | flops | bytes accessed | tf_op | source)
XLA Modules:
  0.0 39.3 jit_solution(10823427078047817129)
XLA Ops:
  0.6 1.2 %pack_own.1 = (f32[37,8,128]{2,1,0:T(8,128)S(1)}, f32[37,8,128]{2,1,0:T(8,128)S(1)}, f32[38,8,128]{2,1,0:T(8,128)S(1)}, f32[38,8,128]{2,1,0:T(8,128)S(1)}, f32[3...) custom-call(f32[19,8,256]{2,1,0:T(8,128)} %f_hbm.1, f32[19,8,256]{2,1,0:T(8,128)} %cot_hbm.1, ...), custom_call_target="tpu_custom_call" | custom-call | tf_op jit(solution)/shard_map/pack_own/pallas_call | solution.py:893
  1.9 3.0 %collective-permute-start = (f32[37,8,128]{2,1,0:T(8,128)S(1)}, f32[37,8,128]{2,1,0:T(8,128)S(1)}, u32[]{:S(2)}, u32[]{:S(2)}) collective-permute-start(f32[37,8,128]{2,1,0:T(8,128)S(1)} %get-tuple-element.22), channel_id=1, source_target_pairs={{0,1},{1,0},{2,3},{3,2},{4,5},{5,4},{6,7},{7,6},{8,9},{9,8},{10,11... | collective-permute-start | bytes 454664 | tf_op jit(solution)/shard_map/ppermute | solution.py:883
  4.9 0.7 %collective-permute-start.1 = (f32[37,8,128]{2,1,0:T(8,128)S(1)}, f32[37,8,128]{2,1,0:T(8,128)S(1)}, u32[]{:S(2)}, u32[]{:S(2)}) collective-permute-start(f32[37,8,128]{2,1,0:T(8,128)S(1)} %get-tuple-element.23), channel_id=1, source_target_pairs={{1,2},{2,1},{5,6},{6,5},{9,10},{10,9},{13,14},{14,13},{17,18},{18,... | collective-permute-start | bytes 454664 | tf_op jit(solution)/shard_map/ppermute | solution.py:887
  5.5 3.3 %collective-permute-done.first_y_ref = f32[37,8,128]{2,1,0:T(8,128)S(1)} collective-permute-done((f32[37,8,128]{2,1,0:T(8,128)S(1)}, f32[37,8,128]{2,1,0:T(8,128)S(1)}, u32[]{:S(2)}, u32[]{:S(2)}) %collective-permute-start) | collective-permute-done | bytes 151584 | tf_op jit(solution)/shard_map/ppermute | solution.py:883
  8.8 0.0 collective-permute-done.1.second_y_ref
  8.8 0.3 pack_x.1
  9.1 0.7 %collective-permute-start.3 = (f32[92,8,128]{2,1,0:T(8,128)S(1)}, f32[92,8,128]{2,1,0:T(8,128)S(1)}, u32[]{:S(2)}, u32[]{:S(2)}) collective-permute-start(f32[92,8,128]{2,1,0:T(8,128)S(1)} %get-tuple-element.25), channel_id=1, source_target_pairs={{4,8},{12,16},{20,24},{8,4},{16,12},{24,20},{5,9},{13,17},{21,25},... | collective-permute-start | bytes 1130504 | tf_op jit(solution)/shard_map/ppermute | solution.py:887
  9.8 3.2 %collective-permute-start.2 = (f32[91,8,128]{2,1,0:T(8,128)S(1)}, f32[91,8,128]{2,1,0:T(8,128)S(1)}, u32[]{:S(2)}, u32[]{:S(2)}) collective-permute-start(f32[91,8,128]{2,1,0:T(8,128)S(1)} %get-tuple-element.24), channel_id=1, source_target_pairs={{0,4},{4,0},{8,12},{12,8},{16,20},{20,16},{24,28},{28,24},{1,5},{5... | collective-permute-start | bytes 1118216 | tf_op jit(solution)/shard_map/ppermute | solution.py:883
  13.0 0.4 %lay_out.1 = (f32[95,40,128]{2,1,0:T(8,128)S(1)}, f32[76,24,128]{2,1,0:T(8,128)S(1)}, f32[2,5,3,8,128]{4,3,2,1,0:T(8,128)S(1)}, f32[4,4,2,8,128]{4,3,2,1,0:T(8,128)S(1)}) custom-call(f32[37,8,128]{2,1,0:T(8,128)S(1)} %collective-permute-done.first_y_ref, f32[37,8,128]{2,1,0:T(8,128)S(1)} %collective-permute-done.1.second_y_ref, ...), custom_call_target="tpu_custom_call" | custom-call | tf_op jit(solution)/shard_map/lay_out/pallas_call | solution.py:925
  13.4 0.9 %collective-permute-done.2.first_x_ref = f32[91,8,128]{2,1,0:T(8,128)S(1)} collective-permute-done((f32[91,8,128]{2,1,0:T(8,128)S(1)}, f32[91,8,128]{2,1,0:T(8,128)S(1)}, u32[]{:S(2)}, u32[]{:S(2)}) %collective-permute-start.2) | collective-permute-done | bytes 372768 | tf_op jit(solution)/shard_map/ppermute | solution.py:883
  14.3 0.0 collective-permute-done.3.second_x_ref
  14.3 4.4 %steps.1 = (f32[19,8,256]{2,1,0:T(8,128)}, f32[32,64]{1,0:T(8,128)S(1)}, f32[95,40,128]{2,1,0:T(8,128)S(1)}, f32[76,24,128]{2,1,0:T(8,128)S(1)}, f32[2,5,3,8,128...) custom-call(f32[38,8,128]{2,1,0:T(8,128)S(1)} %get-tuple-element.17., ...), custom_call_target="tpu_custom_call", output_to_operand_aliasing={{2}: (5, {}), {3}: (6, {}), {4}: (7, {}), {5}: (8, {})} | custom-call | tf_op jit(solution)/shard_map/steps/pallas_call | solution.py:926
  18.8 20.0 %all_to_all.9.parts_ref = f32[32,1,64]{2,1,0:T(1,128)S(1)} all-to-all(f32[32,1,64]{2,1,0:T(1,128)S(1)} %bitcast.2), channel_id=1, replica_groups=mesh['gx'=8,'gy'=4] {'gx','gy'}, dimensions={0} | all-to-all | bytes 16384 | tf_op jit(solution)/shard_map/all_to_all | solution.py:940
  38.8 0.5 %add_panels.1 = f32[1,64]{1,0:T(1,128)} custom-call(f32[32,1,64]{2,1,0:T(1,128)S(1)} %all_to_all.9.parts_ref), custom_call_target="tpu_custom_call" | custom-call | tf_op jit(solution)/shard_map/add_panels/pallas_call | solution.py:941
Async XLA Ops:
  1.9 6.9 %collective-permute-start = (f32[37,8,128]{2,1,0:T(8,128)S(1)}, f32[37,8,128]{2,1,0:T(8,128)S(1)}, u32[]{:S(2)}, u32[]{:S(2)}) collective-permute-start(f32[37,8,128]{2,1,0:T(8,128)S(1)} %get-tuple-element.22), channel_id=1, source_target_pairs={{0,1},{1,0},{2,3},{3,2},{4,5},{5,4},{6,7},{7,6},{8,9},{9,8},{10,11... | collective-permute-start | bytes 454664 | tf_op jit(solution)/shard_map/ppermute | solution.py:883
  4.9 3.9 %collective-permute-start.1 = (f32[37,8,128]{2,1,0:T(8,128)S(1)}, f32[37,8,128]{2,1,0:T(8,128)S(1)}, u32[]{:S(2)}, u32[]{:S(2)}) collective-permute-start(f32[37,8,128]{2,1,0:T(8,128)S(1)} %get-tuple-element.23), channel_id=1, source_target_pairs={{1,2},{2,1},{5,6},{6,5},{9,10},{10,9},{13,14},{14,13},{17,18},{18,... | collective-permute-start | bytes 454664 | tf_op jit(solution)/shard_map/ppermute | solution.py:887
  9.1 5.2 %collective-permute-start.3 = (f32[92,8,128]{2,1,0:T(8,128)S(1)}, f32[92,8,128]{2,1,0:T(8,128)S(1)}, u32[]{:S(2)}, u32[]{:S(2)}) collective-permute-start(f32[92,8,128]{2,1,0:T(8,128)S(1)} %get-tuple-element.25), channel_id=1, source_target_pairs={{4,8},{12,16},{20,24},{8,4},{16,12},{24,20},{5,9},{13,17},{21,25},... | collective-permute-start | bytes 1130504 | tf_op jit(solution)/shard_map/ppermute | solution.py:887
  9.8 4.5 %collective-permute-start.2 = (f32[91,8,128]{2,1,0:T(8,128)S(1)}, f32[91,8,128]{2,1,0:T(8,128)S(1)}, u32[]{:S(2)}, u32[]{:S(2)}) collective-permute-start(f32[91,8,128]{2,1,0:T(8,128)S(1)} %get-tuple-element.24), channel_id=1, source_target_pairs={{0,4},{4,0},{8,12},{12,8},{16,20},{20,16},{24,28},{28,24},{1,5},{5... | collective-permute-start | bytes 1118216 | tf_op jit(solution)/shard_map/ppermute | solution.py:883

commit v13 on v11

--- a/solution.py
+++ b/solution.py
@@ -556,7 +556,7 @@
     return population, cotangent, codes
 
 
-def pack_x(field_ref, first_y_ref, second_y_ref, early_a, early_b, first_ref, second_ref):
+def pack_x(field_ref, first_y_ref, second_y_ref, first_ref, second_ref):
     row, lane, column, depth = iotas()
     y_layout, _, layout = layouts()
     deal = Deal(is_even("gx"), first_ref, second_ref, layout, X_SIDE)
@@ -658,22 +658,8 @@
             field[s, c - 1, 1] = jnp.where(row < 4, above[2](s), below[2](s))
 
 
-def lay_out(
-    first_y_ref,
-    second_y_ref,
-    first_side_ref,
-    second_side_ref,
-    own_ref,
-    field_ref,
-    cot_ref,
-    pop,
-    cot,
-    wide,
-    field,
-):
-    y_layout, side_layout, _ = layouts()
-    from_left = from_y(*sides(first_y_ref, second_y_ref, "gy", y_layout))
-    below, above = sides(first_side_ref, second_side_ref, "gx", side_layout)
+def lay_out(first_y_ref, second_y_ref, own_ref, field_ref, cot_ref, pop, cot, wide, field):
+    from_left = from_y(*sides(first_y_ref, second_y_ref, "gy", layouts()[0]))
     for c in range(5):
         t = c - 2
         if t in (0, 1):
@@ -688,26 +674,21 @@
                 wide,
                 field,
             )
-            lay_halo(c, from_x(below, t, 1), from_x(above, t, -1), pop, cot)
         else:
             own = [functools.partial(lambda g, n: g(n, c), get) for get in from_left]
             lay_own(c, *own, expand(own[2](1)), pop, cot, wide, field)
 
 
-def lay_corners(first_x_ref, second_x_ref, pop, cot, wide, field):
-    _, _, layout = layouts()
-    below, above = (
-        Joined(None, side, X_SIDE) for side in sides(first_x_ref, second_x_ref, "gx", layout)
-    )
-    lay_halo(
-        0, (lambda i: below[X_RING + i],), (lambda i: above[X_RING + i],), pop, cot
-    )
-    ring = [(None, None, lambda s, ref=ref: ref[X_RING + Q]) for ref in (below, above)]
+def lay_halos(below, above, pop, cot, wide, field):
+    ring = [
+        (lambda i, ref=ref: ref[X_RING + i], None, lambda s, ref=ref: ref[X_RING + Q])
+        for ref in (below, above)
+    ]
+    lay_halo(0, *ring, pop, cot)
     lay_codes(0, *ring, wide, field)
     for n, c in enumerate((2, 3, 1, 4)):
         halves = from_x(below, n, 1), from_x(above, n, -1)
-        if n > 1:
-            lay_halo(c, *halves, pop, cot)
+        lay_halo(c, *halves, pop, cot)
         lay_codes(c, *halves, wide, field)
 
 
@@ -716,13 +697,23 @@
     state_ref,
     own_field_ref,
     names_ref,
+    first_side_ref,
+    second_side_ref,
     first_x_ref,
     second_x_ref,
     *refs,
 ):
     adjoint_ref, panel_ref, pop_a, ring_a, wide, field, pop_b, ring_b, saved, mom, grad = refs[4:]
     size_x, size_y = sizes
-    lay_corners(first_x_ref, second_x_ref, pop_a, ring_a, wide, field)
+    _, side_layout, rest_layout = layouts()
+    below, above = (
+        Joined(side, rest, X_SIDE)
+        for side, rest in zip(
+            sides(first_side_ref, second_side_ref, "gx", side_layout),
+            sides(first_x_ref, second_x_ref, "gx", rest_layout),
+        )
+    )
+    lay_halos(below, above, pop_a, ring_a, wide, field)
 
     at_x, at_y = lax.axis_index("gx"), lax.axis_index("gy")
     edges = (
@@ -886,7 +877,6 @@
 
 VMEM = pl.BlockSpec(memory_space=pltpu.VMEM)
 HBM = pl.BlockSpec(memory_space=pltpu.HBM)
-ANY = pl.BlockSpec(memory_space=pl.ANY)
 
 
 def shape_of(*dims):
@@ -929,7 +919,7 @@
     first_y, second_y, first_side, second_side, own, state, cot, field, names = call(
         pack_own,
         (tiles_of(y_layout.size),) * 2
-        + (tiles_of(side_layout.size), tiles_of(side_layout.size + 1))
+        + (tiles_of(side_layout.size), tiles_of(rest_layout.size + 8))
         + (tiles_of(2 * Q),) * 3
         + (tiles_of(2 * OWN_PHI + 2), jax.ShapeDtypeStruct((2, ROWS, LANES), jnp.int32)),
         [HBM] * 5,
@@ -950,9 +940,9 @@
     first_x, second_x = call(
         pack_x,
         (tiles_of(rest_layout.size), tiles_of(rest_layout.size + 1)),
-        [VMEM] * 3 + [ANY] * 2,
+        [VMEM] * 3,
         name="pack_x",
-    )(field, first_y, second_y, first_side, second_side)
+    )(field, first_y, second_y)
     second_x = swap_between(second_x, "gx", size_x)
     first_x = swap(first_x, "gx", size_x)
 
@@ -962,13 +952,11 @@
         shape_of(2, 5, 3, ROWS, LANES),
         shape_of(4, 4, 2, ROWS, LANES),
     )
-    laid = call(lay_out, spaces, [VMEM] * 7, name="lay_out")(
-        first_y, second_y, first_side, second_side, own, field, cot
-    )
+    laid = call(lay_out, spaces, [VMEM] * 5, name="lay_out")(first_y, second_y, own, field, cot)
     adjoint, sums, *_ = call(
         functools.partial(steps_kernel, sizes),
         (shape_of(Q, ROWS, 2 * LANES), shape_of(devices, panels)) + spaces,
-        [VMEM] * 9,
+        [VMEM] * 11,
         [
             pltpu.VMEM((5 * Q, 5 * ROWS, LANES), jnp.float32),
             pltpu.VMEM((4 * Q, 3 * ROWS, LANES), jnp.float32),
@@ -977,8 +965,8 @@
             pltpu.VMEM((4, ROWS, LANES), jnp.float32),
         ],
         name="steps",
-        aliases={5 + n: 2 + n for n in range(4)},
-    )(state, field, names, first_x, second_x, *laid)
+        aliases={7 + n: 2 + n for n in range(4)},
+    )(state, field, names, first_side, second_side, first_x, second_x, *laid)
     gathered = lax.all_to_all(sums, ("gx", "gy"), 0, 0, tiled=True)
     totals = call(add_panels, shape_of(1, panels), [VMEM], name="add_panels")(
         gathered.reshape(devices, 1, panels)

time: 39.5 us -> 38.1 us (0.965)
  starting transfers between devices: 12.8 us -> 8.33 us
  waiting for transfers between devices: 1.7 us -> 3.46 us
  blocking collectives: 17.2 us -> 18.4 us
    ppermute x3, starting transfers between devices: 10.8 us -> 6.32 us  [swap(): lax.ppermute(value, axis, [(i, i ^ 1) for i in range(size) if i ^ 1 < size])]
    ppermute x3, waiting for transfers between devices: 1.69 us -> 3.45 us  [swap(): lax.ppermute(value, axis, [(i, i ^ 1) for i in range(size) if i ^ 1 < size])]
    all_to_all x1, blocking collectives: 17.2 us -> 18.4 us  [on_device(): gathered = lax.all_to_all(sums, ('gx', 'gy'), 0, 0, tiled=True)]
  transfers between devices with their start and end apart: 6 -> 6, of which waited for: 2 -> 2; matrix products, arithmetic and copies ran while one was open for 0% -> 0% of each run, Pallas kernels for 1% -> 2%
where the time goes in v13:
time: 38.1 us; the launch traced here: 37.8 us
  blocking collectives  18.4 us (48%)
  starting transfers between devices  8.33 us (22%)
  Pallas kernels  6.91 us (18%)
  waiting for transfers between devices  3.46 us (9%)
  between operations  0.68 us (2%)
    all_to_all x1, blocking collectives, on_device(): gathered = lax.all_to_all(sums, ('gx', 'gy'), 0, 0, tiled=True)  18.4 us
    ppermute x3, starting transfers between devices, swap(): lax.ppermute(value, axis, [(i, i ^ 1) for i in range(size) if i ^ 1 < size])  6.32 us
    pallas_call x1, Pallas kernels, on_device(): call(functools.partial(steps_kernel, sizes), (shape_of(Q, ROWS, 2 * LANES...  4.44 us
    ppermute x3, waiting for transfers between devices, swap(): lax.ppermute(value, axis, [(i, i ^ 1) for i in range(size) if i ^ 1 < size])  3.45 us
    ppermute x3, starting transfers between devices, swap_between(): return lax.ppermute(value, axis, pairs + [(j, i) for i, j in pairs])  2.01 us
    pallas_call x1, Pallas kernels, on_device(): call(pack_own, (tiles_of(y_layout.size),) * 2 + (tiles_of(side_layout.siz...  1.29 us
  transfers between devices with their start and end apart: 6, of which 2 were waited for; matrix products, arithmetic and copies ran while one was open for 0% of the time, Pallas kernels for 2%

profile of v13, /device:TPU:0, one launch (start us, length us, event | category | flops | bytes accessed | tf_op | source)
XLA Modules:
  0.0 37.8 jit_solution(7366860505843789363)
XLA Ops:
  0.6 1.3 %pack_own.1 = (f32[37,8,128]{2,1,0:T(8,128)S(1)}, f32[37,8,128]{2,1,0:T(8,128)S(1)}, f32[35,8,128]{2,1,0:T(8,128)S(1)}, f32[65,8,128]{2,1,0:T(8,128)S(1)}, f32[3...) custom-call(f32[19,8,256]{2,1,0:T(8,128)} %f_hbm.1, ...), custom_call_target="tpu_custom_call" | custom-call | tf_op jit(solution)/shard_map/pack_own/pallas_call | solution.py:919
  1.9 3.0 %collective-permute-start.2 = (f32[37,8,128]{2,1,0:T(8,128)S(1)}, f32[37,8,128]{2,1,0:T(8,128)S(1)}, u32[]{:S(2)}, u32[]{:S(2)}) collective-permute-start(f32[37,8,128]{2,1,0:T(8,128)S(1)} %get-tuple-element.24), channel_id=1, source_target_pairs={{0,1},{1,0},{2,3},{3,2},{4,5},{5,4},{6,7},{7,6},{8,9},{9,8},{10,11... | collective-permute-start | bytes 454664 | tf_op jit(solution)/shard_map/ppermute | solution.py:909
  4.9 0.7 %collective-permute-start.3 = (f32[37,8,128]{2,1,0:T(8,128)S(1)}, f32[37,8,128]{2,1,0:T(8,128)S(1)}, u32[]{:S(2)}, u32[]{:S(2)}) collective-permute-start(f32[37,8,128]{2,1,0:T(8,128)S(1)} %get-tuple-element.25), channel_id=1, source_target_pairs={{1,2},{2,1},{5,6},{6,5},{9,10},{10,9},{13,14},{14,13},{17,18},{18,... | collective-permute-start | bytes 454664 | tf_op jit(solution)/shard_map/ppermute | solution.py:913
  5.6 0.7 %collective-permute-start.1 = (f32[65,8,128]{2,1,0:T(8,128)S(1)}, f32[65,8,128]{2,1,0:T(8,128)S(1)}, u32[]{:S(2)}, u32[]{:S(2)}) collective-permute-start(f32[65,8,128]{2,1,0:T(8,128)S(1)} %get-tuple-element.23), channel_id=1, source_target_pairs={{4,8},{12,16},{20,24},{8,4},{16,12},{24,20},{5,9},{13,17},{21,25},... | collective-permute-start | bytes 798728 | tf_op jit(solution)/shard_map/ppermute | solution.py:913
  6.3 2.6 %collective-permute-done.2.first_y_ref = f32[37,8,128]{2,1,0:T(8,128)S(1)} collective-permute-done((f32[37,8,128]{2,1,0:T(8,128)S(1)}, f32[37,8,128]{2,1,0:T(8,128)S(1)}, u32[]{:S(2)}, u32[]{:S(2)}) %collective-permute-start.2) | collective-permute-done | bytes 151584 | tf_op jit(solution)/shard_map/ppermute | solution.py:909
  8.9 0.0 collective-permute-done.3.second_y_ref
  8.9 0.2 pack_x.1
  9.1 0.7 %collective-permute-start.5 = (f32[58,8,128]{2,1,0:T(8,128)S(1)}, f32[58,8,128]{2,1,0:T(8,128)S(1)}, u32[]{:S(2)}, u32[]{:S(2)}) collective-permute-start(f32[58,8,128]{2,1,0:T(8,128)S(1)} %get-tuple-element.27), channel_id=1, source_target_pairs={{4,8},{12,16},{20,24},{8,4},{16,12},{24,20},{5,9},{13,17},{21,25},... | collective-permute-start | bytes 712712 | tf_op jit(solution)/shard_map/ppermute | solution.py:913
  9.8 3.2 %collective-permute-start.4 = (f32[57,8,128]{2,1,0:T(8,128)S(1)}, f32[57,8,128]{2,1,0:T(8,128)S(1)}, u32[]{:S(2)}, u32[]{:S(2)}) collective-permute-start(f32[57,8,128]{2,1,0:T(8,128)S(1)} %get-tuple-element.26), channel_id=1, source_target_pairs={{0,4},{4,0},{8,12},{12,8},{16,20},{20,16},{24,28},{28,24},{1,5},{5... | collective-permute-start | bytes 700424 | tf_op jit(solution)/shard_map/ppermute | solution.py:909
  13.0 0.1 collective-permute-start
  13.1 0.4 %lay_out.1 = (f32[95,40,128]{2,1,0:T(8,128)S(1)}, f32[76,24,128]{2,1,0:T(8,128)S(1)}, f32[2,5,3,8,128]{4,3,2,1,0:T(8,128)S(1)}, f32[4,4,2,8,128]{4,3,2,1,0:T(8,128)S(1)}) custom-call(f32[37,8,128]{2,1,0:T(8,128)S(1)} %collective-permute-done.2.first_y_ref, f32[37,8,128]{2,1,0:T(8,128)S(1)} %collective-permute-done.3.second_y_ref, ...), custom_call_target="tpu_custom_call" | custom-call | tf_op jit(solution)/shard_map/lay_out/pallas_call | solution.py:955
  13.5 0.9 %collective-permute-done.first_side_ref = f32[35,8,128]{2,1,0:T(8,128)S(1)} collective-permute-done((f32[35,8,128]{2,1,0:T(8,128)S(1)}, f32[35,8,128]{2,1,0:T(8,128)S(1)}, u32[]{:S(2)}, u32[]{:S(2)}) %collective-permute-start) | collective-permute-done | bytes 143392 | tf_op jit(solution)/shard_map/ppermute | solution.py:909
  14.4 0.0 collective-permute-done.1.second_side_ref
  14.4 0.0 collective-permute-done.4.first_x_ref
  14.4 0.0 collective-permute-done.5.second_x_ref
  14.4 4.4 %steps.1 = (f32[19,8,256]{2,1,0:T(8,128)}, f32[32,64]{1,0:T(8,128)S(1)}, f32[95,40,128]{2,1,0:T(8,128)S(1)}, f32[76,24,128]{2,1,0:T(8,128)S(1)}, f32[2,5,3,8,128...) custom-call(f32[38,8,128]{2,1,0:T(8,128)S(1)} %get-tuple-element.19., ...), custom_call_target="tpu_custom_call", output_to_operand_aliasing={{2}: (7, {}), {3}: (8, {}), {4}: (9, {}), {5}: (10, {})} | custom-call | tf_op jit(solution)/shard_map/steps/pallas_call | solution.py:956
  18.8 18.4 %all_to_all.9.parts_ref = f32[32,1,64]{2,1,0:T(1,128)S(1)} all-to-all(f32[32,1,64]{2,1,0:T(1,128)S(1)} %bitcast.2), channel_id=1, replica_groups=mesh['gx'=8,'gy'=4] {'gx','gy'}, dimensions={0} | all-to-all | bytes 16384 | tf_op jit(solution)/shard_map/all_to_all | solution.py:970
  37.3 0.5 %add_panels.1 = f32[1,64]{1,0:T(1,128)} custom-call(f32[32,1,64]{2,1,0:T(1,128)S(1)} %all_to_all.9.parts_ref), custom_call_target="tpu_custom_call" | custom-call | tf_op jit(solution)/shard_map/add_panels/pallas_call | solution.py:971
Async XLA Ops:
  1.9 6.9 %collective-permute-start.2 = (f32[37,8,128]{2,1,0:T(8,128)S(1)}, f32[37,8,128]{2,1,0:T(8,128)S(1)}, u32[]{:S(2)}, u32[]{:S(2)}) collective-permute-start(f32[37,8,128]{2,1,0:T(8,128)S(1)} %get-tuple-element.24), channel_id=1, source_target_pairs={{0,1},{1,0},{2,3},{3,2},{4,5},{5,4},{6,7},{7,6},{8,9},{9,8},{10,11... | collective-permute-start | bytes 454664 | tf_op jit(solution)/shard_map/ppermute | solution.py:909
  4.9 3.9 %collective-permute-start.3 = (f32[37,8,128]{2,1,0:T(8,128)S(1)}, f32[37,8,128]{2,1,0:T(8,128)S(1)}, u32[]{:S(2)}, u32[]{:S(2)}) collective-permute-start(f32[37,8,128]{2,1,0:T(8,128)S(1)} %get-tuple-element.25), channel_id=1, source_target_pairs={{1,2},{2,1},{5,6},{6,5},{9,10},{10,9},{13,14},{14,13},{17,18},{18,... | collective-permute-start | bytes 454664 | tf_op jit(solution)/shard_map/ppermute | solution.py:913
  5.6 8.8 %collective-permute-start.1 = (f32[65,8,128]{2,1,0:T(8,128)S(1)}, f32[65,8,128]{2,1,0:T(8,128)S(1)}, u32[]{:S(2)}, u32[]{:S(2)}) collective-permute-start(f32[65,8,128]{2,1,0:T(8,128)S(1)} %get-tuple-element.23), channel_id=1, source_target_pairs={{4,8},{12,16},{20,24},{8,4},{16,12},{24,20},{5,9},{13,17},{21,25},... | collective-permute-start | bytes 798728 | tf_op jit(solution)/shard_map/ppermute | solution.py:913
  9.1 5.3 %collective-permute-start.5 = (f32[58,8,128]{2,1,0:T(8,128)S(1)}, f32[58,8,128]{2,1,0:T(8,128)S(1)}, u32[]{:S(2)}, u32[]{:S(2)}) collective-permute-start(f32[58,8,128]{2,1,0:T(8,128)S(1)} %get-tuple-element.27), channel_id=1, source_target_pairs={{4,8},{12,16},{20,24},{8,4},{16,12},{24,20},{5,9},{13,17},{21,25},... | collective-permute-start | bytes 712712 | tf_op jit(solution)/shard_map/ppermute | solution.py:913
  9.8 4.6 %collective-permute-start.4 = (f32[57,8,128]{2,1,0:T(8,128)S(1)}, f32[57,8,128]{2,1,0:T(8,128)S(1)}, u32[]{:S(2)}, u32[]{:S(2)}) collective-permute-start(f32[57,8,128]{2,1,0:T(8,128)S(1)} %get-tuple-element.26), channel_id=1, source_target_pairs={{0,4},{4,0},{8,12},{12,8},{16,20},{20,16},{24,28},{28,24},{1,5},{5... | collective-permute-start | bytes 700424 | tf_op jit(solution)/shard_map/ppermute | solution.py:909
  13.0 1.4 %collective-permute-start = (f32[35,8,128]{2,1,0:T(8,128)S(1)}, f32[35,8,128]{2,1,0:T(8,128)S(1)}, u32[]{:S(2)}, u32[]{:S(2)}) collective-permute-start(f32[35,8,128]{2,1,0:T(8,128)S(1)} %get-tuple-element.22), channel_id=1, source_target_pairs={{0,4},{4,0},{8,12},{12,8},{16,20},{20,16},{24,28},{28,24},{1,5},{5... | collective-permute-start | bytes 430088 | tf_op jit(solution)/shard_map/ppermute | solution.py:909

commit v14 on v11

--- a/solution.py
+++ b/solution.py
@@ -349,12 +349,12 @@
         self.second.finish()
 
 
-class Joined:
-    def __init__(self, first, second, cut):
-        self.first, self.second, self.cut = first, second, cut
+class Shifted:
+    def __init__(self, ref, start):
+        self.ref, self.start = ref, start
 
     def __getitem__(self, at):
-        return self.first[at] if at < self.cut else self.second[at - self.cut]
+        return self.ref[at - self.start]
 
 
 def is_even(axis):
@@ -556,7 +556,7 @@
     return population, cotangent, codes
 
 
-def pack_x(field_ref, first_y_ref, second_y_ref, early_a, early_b, first_ref, second_ref):
+def pack_x(field_ref, first_y_ref, second_y_ref, first_ref, second_ref):
     row, lane, column, depth = iotas()
     y_layout, _, layout = layouts()
     deal = Deal(is_even("gx"), first_ref, second_ref, layout, X_SIDE)
@@ -694,15 +694,12 @@
             lay_own(c, *own, expand(own[2](1)), pop, cot, wide, field)
 
 
-def lay_corners(first_x_ref, second_x_ref, pop, cot, wide, field):
-    _, _, layout = layouts()
-    below, above = (
-        Joined(None, side, X_SIDE) for side in sides(first_x_ref, second_x_ref, "gx", layout)
-    )
-    lay_halo(
-        0, (lambda i: below[X_RING + i],), (lambda i: above[X_RING + i],), pop, cot
-    )
-    ring = [(None, None, lambda s, ref=ref: ref[X_RING + Q]) for ref in (below, above)]
+def lay_halos(below, above, pop, cot, wide, field):
+    ring = [
+        (lambda i, ref=ref: ref[X_RING + i], None, lambda s, ref=ref: ref[X_RING + Q])
+        for ref in (below, above)
+    ]
+    lay_halo(0, *ring, pop, cot)
     lay_codes(0, *ring, wide, field)
     for n, c in enumerate((2, 3, 1, 4)):
         halves = from_x(below, n, 1), from_x(above, n, -1)
@@ -722,7 +719,9 @@
 ):
     adjoint_ref, panel_ref, pop_a, ring_a, wide, field, pop_b, ring_b, saved, mom, grad = refs[4:]
     size_x, size_y = sizes
-    lay_corners(first_x_ref, second_x_ref, pop_a, ring_a, wide, field)
+    halves = sides(first_x_ref, second_x_ref, "gx", layouts()[2])
+    below, above = (Shifted(ref, X_SIDE) for ref in halves)
+    lay_halos(below, above, pop_a, ring_a, wide, field)
 
     at_x, at_y = lax.axis_index("gx"), lax.axis_index("gy")
     edges = (
@@ -880,13 +879,15 @@
     panel_ref[...] = sums
 
 
-def add_panels(parts_ref, out_ref):
-    out_ref[...] = jnp.sum(parts_ref[...], axis=0)
+def finish(parts_ref, adjoint_ref, sums_ref, adjoint_hbm, sem):
+    copy = pltpu.make_async_copy(adjoint_ref, adjoint_hbm, sem)
+    copy.start()
+    sums_ref[...] = jnp.sum(parts_ref[...], axis=0)
+    copy.wait()
 
 
 VMEM = pl.BlockSpec(memory_space=pltpu.VMEM)
 HBM = pl.BlockSpec(memory_space=pltpu.HBM)
-ANY = pl.BlockSpec(memory_space=pl.ANY)
 
 
 def shape_of(*dims):
@@ -929,7 +930,7 @@
     first_y, second_y, first_side, second_side, own, state, cot, field, names = call(
         pack_own,
         (tiles_of(y_layout.size),) * 2
-        + (tiles_of(side_layout.size), tiles_of(side_layout.size + 1))
+        + (tiles_of(side_layout.size), tiles_of(rest_layout.size + 8))
         + (tiles_of(2 * Q),) * 3
         + (tiles_of(2 * OWN_PHI + 2), jax.ShapeDtypeStruct((2, ROWS, LANES), jnp.int32)),
         [HBM] * 5,
@@ -950,9 +951,9 @@
     first_x, second_x = call(
         pack_x,
         (tiles_of(rest_layout.size), tiles_of(rest_layout.size + 1)),
-        [VMEM] * 3 + [ANY] * 2,
+        [VMEM] * 3,
         name="pack_x",
-    )(field, first_y, second_y, first_side, second_side)
+    )(field, first_y, second_y)
     second_x = swap_between(second_x, "gx", size_x)
     first_x = swap(first_x, "gx", size_x)
 
@@ -967,7 +968,7 @@
     )
     adjoint, sums, *_ = call(
         functools.partial(steps_kernel, sizes),
-        (shape_of(Q, ROWS, 2 * LANES), shape_of(devices, panels)) + spaces,
+        (pltpu.VMEM((Q, ROWS, 2 * LANES), jnp.float32), shape_of(devices, panels)) + spaces,
         [VMEM] * 9,
         [
             pltpu.VMEM((5 * Q, 5 * ROWS, LANES), jnp.float32),
@@ -980,9 +981,14 @@
         aliases={5 + n: 2 + n for n in range(4)},
     )(state, field, names, first_x, second_x, *laid)
     gathered = lax.all_to_all(sums, ("gx", "gy"), 0, 0, tiled=True)
-    totals = call(add_panels, shape_of(1, panels), [VMEM], name="add_panels")(
-        gathered.reshape(devices, 1, panels)
-    )
+    totals, adjoint = pl.pallas_call(
+        finish,
+        out_shape=(shape_of(1, panels), shape_of(Q, ROWS, 2 * LANES)),
+        in_specs=[VMEM, VMEM],
+        out_specs=(VMEM, HBM),
+        scratch_shapes=[pltpu.SemaphoreType.DMA],
+        name="finish",
+    )(gathered.reshape(devices, 1, panels), adjoint)
     return adjoint, totals.reshape(panels)
 
 

time: 39.5 us -> 39.9 us (1.010)
  starting transfers between devices: 12.8 us -> 8.33 us
  waiting for transfers between devices: 1.7 us -> 3.88 us
  Pallas kernels: 6.89 us -> 7.91 us
  blocking collectives: 17.2 us -> 18.1 us
  local copies, waits for them, and re-layouts: 0 us -> 0.65 us
    ppermute x3, starting transfers between devices: 10.8 us -> 6.32 us  [swap(): lax.ppermute(value, axis, [(i, i ^ 1) for i in range(size) if i ^ 1 < size])]
    ppermute x3, waiting for transfers between devices: 1.69 us -> 3.87 us  [swap(): lax.ppermute(value, axis, [(i, i ^ 1) for i in range(size) if i ^ 1 < size])]
    pallas_call x2, Pallas kernels: 4.94 us -> 5.97 us  [the longest x1 3.86 us: on_device(): call(functools.partial(steps_kernel, sizes), (pltpu.VMEM((Q, ROWS, 2 * LA...]
    all_to_all x1, blocking collectives: 17.2 us -> 18.1 us  [on_device(): gathered = lax.all_to_all(sums, ('gx', 'gy'), 0, 0, tiled=True)]
    unnamed x0 -> x2, local copies, waits for them, and re-layouts: none -> 0.65 us
  transfers between devices with their start and end apart: 6 -> 6, of which waited for: 2 -> 2; matrix products, arithmetic and copies ran while one was open for 0% -> 0% of each run, Pallas kernels for 1% -> 2%
where the time goes in v14:
time: 39.9 us; the launch traced here: 39.6 us
  blocking collectives  18.1 us (45%)
  starting transfers between devices  8.33 us (21%)
  Pallas kernels  7.91 us (20%)
  waiting for transfers between devices  3.88 us (10%)
  between operations  0.69 us (2%)
  local copies, waits for them, and re-layouts  0.65 us (2%)
    all_to_all x1, blocking collectives, on_device(): gathered = lax.all_to_all(sums, ('gx', 'gy'), 0, 0, tiled=True)  18.1 us
    ppermute x3, starting transfers between devices, swap(): lax.ppermute(value, axis, [(i, i ^ 1) for i in range(size) if i ^ 1 < size])  6.32 us
    ppermute x3, waiting for transfers between devices, swap(): lax.ppermute(value, axis, [(i, i ^ 1) for i in range(size) if i ^ 1 < size])  3.87 us
    pallas_call x1, Pallas kernels, on_device(): call(functools.partial(steps_kernel, sizes), (pltpu.VMEM((Q, ROWS, 2 * LA...  3.86 us
    pallas_call x1, Pallas kernels, on_device(): pl.pallas_call(finish, out_shape=(shape_of(1, panels), shape_of(Q, ROWS,...  2.11 us
    ppermute x3, starting transfers between devices, swap_between(): return lax.ppermute(value, axis, pairs + [(j, i) for i, j in pairs])  2.01 us
    pallas_call x1, Pallas kernels, on_device(): call(pack_own, (tiles_of(y_layout.size),) * 2 + (tiles_of(side_layout.siz...  1.29 us
  transfers between devices with their start and end apart: 6, of which 2 were waited for; matrix products, arithmetic and copies ran while one was open for 0% of the time, Pallas kernels for 2%

profile of v14, /device:TPU:0, one launch (start us, length us, event | category | flops | bytes accessed | tf_op | source)
XLA Modules:
  0.0 39.6 jit_solution(13576975880907476738)
XLA Ops:
  0.6 1.3 %pack_own.1 = (f32[37,8,128]{2,1,0:T(8,128)S(1)}, f32[37,8,128]{2,1,0:T(8,128)S(1)}, f32[35,8,128]{2,1,0:T(8,128)S(1)}, f32[65,8,128]{2,1,0:T(8,128)S(1)}, f32[3...) custom-call(f32[19,8,256]{2,1,0:T(8,128)} %f_hbm.1, ...), custom_call_target="tpu_custom_call" | custom-call | tf_op jit(solution)/shard_map/pack_own/pallas_call | solution.py:930
  1.9 3.0 %collective-permute-start = (f32[37,8,128]{2,1,0:T(8,128)S(1)}, f32[37,8,128]{2,1,0:T(8,128)S(1)}, u32[]{:S(2)}, u32[]{:S(2)}) collective-permute-start(f32[37,8,128]{2,1,0:T(8,128)S(1)} %get-tuple-element.24), channel_id=1, source_target_pairs={{0,1},{1,0},{2,3},{3,2},{4,5},{5,4},{6,7},{7,6},{8,9},{9,8},{10,11... | collective-permute-start | bytes 454664 | tf_op jit(solution)/shard_map/ppermute | solution.py:920
  4.9 0.7 %collective-permute-start.1 = (f32[37,8,128]{2,1,0:T(8,128)S(1)}, f32[37,8,128]{2,1,0:T(8,128)S(1)}, u32[]{:S(2)}, u32[]{:S(2)}) collective-permute-start(f32[37,8,128]{2,1,0:T(8,128)S(1)} %get-tuple-element.25), channel_id=1, source_target_pairs={{1,2},{2,1},{5,6},{6,5},{9,10},{10,9},{13,14},{14,13},{17,18},{18,... | collective-permute-start | bytes 454664 | tf_op jit(solution)/shard_map/ppermute | solution.py:924
  5.6 0.7 %collective-permute-start.5 = (f32[65,8,128]{2,1,0:T(8,128)S(1)}, f32[65,8,128]{2,1,0:T(8,128)S(1)}, u32[]{:S(2)}, u32[]{:S(2)}) collective-permute-start(f32[65,8,128]{2,1,0:T(8,128)S(1)} %get-tuple-element.29), channel_id=1, source_target_pairs={{4,8},{12,16},{20,24},{8,4},{16,12},{24,20},{5,9},{13,17},{21,25},... | collective-permute-start | bytes 798728 | tf_op jit(solution)/shard_map/ppermute | solution.py:924
  6.3 2.6 %collective-permute-done.first_y_ref = f32[37,8,128]{2,1,0:T(8,128)S(1)} collective-permute-done((f32[37,8,128]{2,1,0:T(8,128)S(1)}, f32[37,8,128]{2,1,0:T(8,128)S(1)}, u32[]{:S(2)}, u32[]{:S(2)}) %collective-permute-start) | collective-permute-done | bytes 151584 | tf_op jit(solution)/shard_map/ppermute | solution.py:920
  8.9 0.0 collective-permute-done.1.second_y_ref
  8.9 0.2 pack_x.1
  9.1 0.7 %collective-permute-start.3 = (f32[58,8,128]{2,1,0:T(8,128)S(1)}, f32[58,8,128]{2,1,0:T(8,128)S(1)}, u32[]{:S(2)}, u32[]{:S(2)}) collective-permute-start(f32[58,8,128]{2,1,0:T(8,128)S(1)} %get-tuple-element.27), channel_id=1, source_target_pairs={{4,8},{12,16},{20,24},{8,4},{16,12},{24,20},{5,9},{13,17},{21,25},... | collective-permute-start | bytes 712712 | tf_op jit(solution)/shard_map/ppermute | solution.py:924
  9.8 3.2 %collective-permute-start.2 = (f32[57,8,128]{2,1,0:T(8,128)S(1)}, f32[57,8,128]{2,1,0:T(8,128)S(1)}, u32[]{:S(2)}, u32[]{:S(2)}) collective-permute-start(f32[57,8,128]{2,1,0:T(8,128)S(1)} %get-tuple-element.26), channel_id=1, source_target_pairs={{0,4},{4,0},{8,12},{12,8},{16,20},{20,16},{24,28},{28,24},{1,5},{5... | collective-permute-start | bytes 700424 | tf_op jit(solution)/shard_map/ppermute | solution.py:920
  13.0 0.1 collective-permute-start.4
  13.1 1.3 %collective-permute-done.4.first_side_ref = f32[35,8,128]{2,1,0:T(8,128)S(1)} collective-permute-done((f32[35,8,128]{2,1,0:T(8,128)S(1)}, f32[35,8,128]{2,1,0:T(8,128)S(1)}, u32[]{:S(2)}, u32[]{:S(2)}) %collective-permute-start.4) | collective-permute-done | bytes 143392 | tf_op jit(solution)/shard_map/ppermute | solution.py:920
  14.4 0.0 collective-permute-done.5.second_side_ref
  14.4 0.4 %lay_out.1 = (f32[95,40,128]{2,1,0:T(8,128)S(1)}, f32[76,24,128]{2,1,0:T(8,128)S(1)}, f32[2,5,3,8,128]{4,3,2,1,0:T(8,128)S(1)}, f32[4,4,2,8,128]{4,3,2,1,0:T(8,128)S(1)}) custom-call(f32[37,8,128]{2,1,0:T(8,128)S(1)} %collective-permute-done.first_y_ref, f32[37,8,128]{2,1,0:T(8,128)S(1)} %collective-permute-done.1.second_y_ref, ...), custom_call_target="tpu_custom_call" | custom-call | tf_op jit(solution)/shard_map/lay_out/pallas_call | solution.py:966
  14.8 0.0 collective-permute-done.2.first_x_ref
  14.8 0.0 collective-permute-done.3.second_x_ref
  14.8 3.9 %steps.1 = (f32[19,8,256]{2,1,0:T(8,128)S(1)}, f32[32,64]{1,0:T(8,128)S(1)}, f32[95,40,128]{2,1,0:T(8,128)S(1)}, f32[76,24,128]{2,1,0:T(8,128)S(1)}, f32[2,5,3,8...) custom-call(f32[38,8,128]{2,1,0:T(8,128)S(1)} %get-tuple-element.21., ...), custom_call_target="tpu_custom_call", output_to_operand_aliasing={{2}: (5, {}), {3}: (6, {}), {4}: (7, {}), {5}: (8, {})} | custom-call | tf_op jit(solution)/shard_map/steps/pallas_call | solution.py:969
  18.7 0.0 copy-start
  18.7 0.7 %copy-done = f32[19,8,256]{2,1,0:T(8,128)} copy-done((f32[19,8,256]{2,1,0:T(8,128)}, f32[19,8,256]{2,1,0:T(8,128)S(1)}, u32[]{:S(2)}) %copy-start) | copy-done | bytes 155672
  19.4 18.1 %all_to_all.9.parts_ref = f32[32,1,64]{2,1,0:T(1,128)} all-to-all(f32[32,1,64]{2,1,0:T(1,128)S(1)} %bitcast.2), channel_id=1, replica_groups=mesh['gx'=8,'gy'=4] {'gx','gy'}, dimensions={0} | all-to-all | bytes 16384 | tf_op jit(solution)/shard_map/all_to_all | solution.py:983
  37.5 2.1 %finish.1 = (f32[1,64]{1,0:T(1,128)}, f32[19,8,256]{2,1,0:T(8,128)}) custom-call(f32[32,1,64]{2,1,0:T(1,128)} %all_to_all.9.parts_ref, f32[19,8,256]{2,1,0:T(8,128)} %copy-done), custom_call_target="tpu_custom_call" | custom-call | tf_op jit(solution)/shard_map/finish/pallas_call | solution.py:984
Async XLA Ops:
  1.9 6.9 %collective-permute-start = (f32[37,8,128]{2,1,0:T(8,128)S(1)}, f32[37,8,128]{2,1,0:T(8,128)S(1)}, u32[]{:S(2)}, u32[]{:S(2)}) collective-permute-start(f32[37,8,128]{2,1,0:T(8,128)S(1)} %get-tuple-element.24), channel_id=1, source_target_pairs={{0,1},{1,0},{2,3},{3,2},{4,5},{5,4},{6,7},{7,6},{8,9},{9,8},{10,11... | collective-permute-start | bytes 454664 | tf_op jit(solution)/shard_map/ppermute | solution.py:920
  4.9 3.9 %collective-permute-start.1 = (f32[37,8,128]{2,1,0:T(8,128)S(1)}, f32[37,8,128]{2,1,0:T(8,128)S(1)}, u32[]{:S(2)}, u32[]{:S(2)}) collective-permute-start(f32[37,8,128]{2,1,0:T(8,128)S(1)} %get-tuple-element.25), channel_id=1, source_target_pairs={{1,2},{2,1},{5,6},{6,5},{9,10},{10,9},{13,14},{14,13},{17,18},{18,... | collective-permute-start | bytes 454664 | tf_op jit(solution)/shard_map/ppermute | solution.py:924
  5.6 8.8 %collective-permute-start.5 = (f32[65,8,128]{2,1,0:T(8,128)S(1)}, f32[65,8,128]{2,1,0:T(8,128)S(1)}, u32[]{:S(2)}, u32[]{:S(2)}) collective-permute-start(f32[65,8,128]{2,1,0:T(8,128)S(1)} %get-tuple-element.29), channel_id=1, source_target_pairs={{4,8},{12,16},{20,24},{8,4},{16,12},{24,20},{5,9},{13,17},{21,25},... | collective-permute-start | bytes 798728 | tf_op jit(solution)/shard_map/ppermute | solution.py:924
  9.1 5.7 %collective-permute-start.3 = (f32[58,8,128]{2,1,0:T(8,128)S(1)}, f32[58,8,128]{2,1,0:T(8,128)S(1)}, u32[]{:S(2)}, u32[]{:S(2)}) collective-permute-start(f32[58,8,128]{2,1,0:T(8,128)S(1)} %get-tuple-element.27), channel_id=1, source_target_pairs={{4,8},{12,16},{20,24},{8,4},{16,12},{24,20},{5,9},{13,17},{21,25},... | collective-permute-start | bytes 712712 | tf_op jit(solution)/shard_map/ppermute | solution.py:924
  9.8 5.0 %collective-permute-start.2 = (f32[57,8,128]{2,1,0:T(8,128)S(1)}, f32[57,8,128]{2,1,0:T(8,128)S(1)}, u32[]{:S(2)}, u32[]{:S(2)}) collective-permute-start(f32[57,8,128]{2,1,0:T(8,128)S(1)} %get-tuple-element.26), channel_id=1, source_target_pairs={{0,4},{4,0},{8,12},{12,8},{16,20},{20,16},{24,28},{28,24},{1,5},{5... | collective-permute-start | bytes 700424 | tf_op jit(solution)/shard_map/ppermute | solution.py:920
  13.0 1.4 %collective-permute-start.4 = (f32[35,8,128]{2,1,0:T(8,128)S(1)}, f32[35,8,128]{2,1,0:T(8,128)S(1)}, u32[]{:S(2)}, u32[]{:S(2)}) collective-permute-start(f32[35,8,128]{2,1,0:T(8,128)S(1)} %get-tuple-element.28), channel_id=1, source_target_pairs={{0,4},{4,0},{8,12},{12,8},{16,20},{20,16},{24,28},{28,24},{1,5},{5... | collective-permute-start | bytes 430088 | tf_op jit(solution)/shard_map/ppermute | solution.py:920
  18.7 0.7 %copy-start = (f32[19,8,256]{2,1,0:T(8,128)}, f32[19,8,256]{2,1,0:T(8,128)S(1)}, u32[]{:S(2)}) copy-start(f32[19,8,256]{2,1,0:T(8,128)S(1)} %get-tuple-element.37.adjoint_ref) | copy-start | bytes 466948

commit v15 on v14

--- a/solution.py
+++ b/solution.py
@@ -904,6 +904,8 @@
     devices = size_x * size_y
     y_layout, side_layout, rest_layout = layouts()
 
+    params = pltpu.CompilerParams(vmem_limit_bytes=32 * 1024 * 1024)
+
     def call(kernel, out_shape, in_specs, scratch=(), name=None, aliases={}):
         return pl.pallas_call(
             kernel,
@@ -912,7 +914,7 @@
             out_specs=jax.tree.map(lambda _: VMEM, out_shape),
             scratch_shapes=scratch,
             input_output_aliases=aliases,
-            compiler_params=pltpu.CompilerParams(vmem_limit_bytes=32 * 1024 * 1024),
+            compiler_params=params,
             name=name,
         )
 
@@ -987,6 +989,7 @@
         in_specs=[VMEM, VMEM],
         out_specs=(VMEM, HBM),
         scratch_shapes=[pltpu.SemaphoreType.DMA],
+        compiler_params=params,
         name="finish",
     )(gathered.reshape(devices, 1, panels), adjoint)
     return adjoint, totals.reshape(panels)

time: 39.9 us -> 38.2 us (0.957)
  Pallas kernels: 7.91 us -> 6.98 us
  local copies, waits for them, and re-layouts: 0.65 us -> 0 us
    pallas_call x1, Pallas kernels: 2.11 us -> 1.18 us  [on_device(): pl.pallas_call(finish, out_shape=(shape_of(1, panels), shape_of(Q, ROWS,...]
    unnamed x2 -> x0, local copies, waits for them, and re-layouts: 0.65 us -> none
where the time goes in v15:
time: 38.2 us; the launch traced here: 37.9 us
  blocking collectives  18 us (47%)
  starting transfers between devices  8.33 us (22%)
  Pallas kernels  6.98 us (18%)
  waiting for transfers between devices  3.88 us (10%)
  between operations  0.68 us (2%)
    all_to_all x1, blocking collectives, on_device(): gathered = lax.all_to_all(sums, ('gx', 'gy'), 0, 0, tiled=True)  18 us
    ppermute x3, starting transfers between devices, swap(): lax.ppermute(value, axis, [(i, i ^ 1) for i in range(size) if i ^ 1 < size])  6.32 us
    ppermute x3, waiting for transfers between devices, swap(): lax.ppermute(value, axis, [(i, i ^ 1) for i in range(size) if i ^ 1 < size])  3.87 us
    pallas_call x1, Pallas kernels, on_device(): call(functools.partial(steps_kernel, sizes), (pltpu.VMEM((Q, ROWS, 2 * LA...  3.86 us
    ppermute x3, starting transfers between devices, swap_between(): return lax.ppermute(value, axis, pairs + [(j, i) for i, j in pairs])  2.01 us
    pallas_call x1, Pallas kernels, on_device(): call(pack_own, (tiles_of(y_layout.size),) * 2 + (tiles_of(side_layout.siz...  1.29 us
    pallas_call x1, Pallas kernels, on_device(): pl.pallas_call(finish, out_shape=(shape_of(1, panels), shape_of(Q, ROWS,...  1.18 us
  transfers between devices with their start and end apart: 6, of which 2 were waited for; matrix products, arithmetic and copies ran while one was open for 0% of the time, Pallas kernels for 2%

profile of v15, /device:TPU:0, one launch (start us, length us, event | category | flops | bytes accessed | tf_op | source)
XLA Modules:
  0.0 37.9 jit_solution(14790536762830731210)
XLA Ops:
  0.6 1.3 %pack_own.1 = (f32[37,8,128]{2,1,0:T(8,128)S(1)}, f32[37,8,128]{2,1,0:T(8,128)S(1)}, f32[35,8,128]{2,1,0:T(8,128)S(1)}, f32[65,8,128]{2,1,0:T(8,128)S(1)}, f32[3...) custom-call(f32[19,8,256]{2,1,0:T(8,128)} %f_hbm.1, ...), custom_call_target="tpu_custom_call" | custom-call | tf_op jit(solution)/shard_map/pack_own/pallas_call | solution.py:932
  1.9 3.0 %collective-permute-start = (f32[37,8,128]{2,1,0:T(8,128)S(1)}, f32[37,8,128]{2,1,0:T(8,128)S(1)}, u32[]{:S(2)}, u32[]{:S(2)}) collective-permute-start(f32[37,8,128]{2,1,0:T(8,128)S(1)} %get-tuple-element.24), channel_id=1, source_target_pairs={{0,1},{1,0},{2,3},{3,2},{4,5},{5,4},{6,7},{7,6},{8,9},{9,8},{10,11... | collective-permute-start | bytes 454664 | tf_op jit(solution)/shard_map/ppermute | solution.py:922
  4.9 0.7 %collective-permute-start.1 = (f32[37,8,128]{2,1,0:T(8,128)S(1)}, f32[37,8,128]{2,1,0:T(8,128)S(1)}, u32[]{:S(2)}, u32[]{:S(2)}) collective-permute-start(f32[37,8,128]{2,1,0:T(8,128)S(1)} %get-tuple-element.25), channel_id=1, source_target_pairs={{1,2},{2,1},{5,6},{6,5},{9,10},{10,9},{13,14},{14,13},{17,18},{18,... | collective-permute-start | bytes 454664 | tf_op jit(solution)/shard_map/ppermute | solution.py:926
  5.6 0.7 %collective-permute-start.5 = (f32[65,8,128]{2,1,0:T(8,128)S(1)}, f32[65,8,128]{2,1,0:T(8,128)S(1)}, u32[]{:S(2)}, u32[]{:S(2)}) collective-permute-start(f32[65,8,128]{2,1,0:T(8,128)S(1)} %get-tuple-element.29), channel_id=1, source_target_pairs={{4,8},{12,16},{20,24},{8,4},{16,12},{24,20},{5,9},{13,17},{21,25},... | collective-permute-start | bytes 798728 | tf_op jit(solution)/shard_map/ppermute | solution.py:926
  6.3 2.6 %collective-permute-done.first_y_ref = f32[37,8,128]{2,1,0:T(8,128)S(1)} collective-permute-done((f32[37,8,128]{2,1,0:T(8,128)S(1)}, f32[37,8,128]{2,1,0:T(8,128)S(1)}, u32[]{:S(2)}, u32[]{:S(2)}) %collective-permute-start) | collective-permute-done | bytes 151584 | tf_op jit(solution)/shard_map/ppermute | solution.py:922
  8.9 0.0 collective-permute-done.1.second_y_ref
  8.9 0.2 pack_x.1
  9.1 0.7 %collective-permute-start.3 = (f32[58,8,128]{2,1,0:T(8,128)S(1)}, f32[58,8,128]{2,1,0:T(8,128)S(1)}, u32[]{:S(2)}, u32[]{:S(2)}) collective-permute-start(f32[58,8,128]{2,1,0:T(8,128)S(1)} %get-tuple-element.27), channel_id=1, source_target_pairs={{4,8},{12,16},{20,24},{8,4},{16,12},{24,20},{5,9},{13,17},{21,25},... | collective-permute-start | bytes 712712 | tf_op jit(solution)/shard_map/ppermute | solution.py:926
  9.8 3.2 %collective-permute-start.2 = (f32[57,8,128]{2,1,0:T(8,128)S(1)}, f32[57,8,128]{2,1,0:T(8,128)S(1)}, u32[]{:S(2)}, u32[]{:S(2)}) collective-permute-start(f32[57,8,128]{2,1,0:T(8,128)S(1)} %get-tuple-element.26), channel_id=1, source_target_pairs={{0,4},{4,0},{8,12},{12,8},{16,20},{20,16},{24,28},{28,24},{1,5},{5... | collective-permute-start | bytes 700424 | tf_op jit(solution)/shard_map/ppermute | solution.py:922
  13.0 0.1 collective-permute-start.4
  13.1 1.3 %collective-permute-done.4.first_side_ref = f32[35,8,128]{2,1,0:T(8,128)S(1)} collective-permute-done((f32[35,8,128]{2,1,0:T(8,128)S(1)}, f32[35,8,128]{2,1,0:T(8,128)S(1)}, u32[]{:S(2)}, u32[]{:S(2)}) %collective-permute-start.4) | collective-permute-done | bytes 143392 | tf_op jit(solution)/shard_map/ppermute | solution.py:922
  14.4 0.0 collective-permute-done.5.second_side_ref
  14.4 0.4 %lay_out.1 = (f32[95,40,128]{2,1,0:T(8,128)S(1)}, f32[76,24,128]{2,1,0:T(8,128)S(1)}, f32[2,5,3,8,128]{4,3,2,1,0:T(8,128)S(1)}, f32[4,4,2,8,128]{4,3,2,1,0:T(8,128)S(1)}) custom-call(f32[37,8,128]{2,1,0:T(8,128)S(1)} %collective-permute-done.first_y_ref, f32[37,8,128]{2,1,0:T(8,128)S(1)} %collective-permute-done.1.second_y_ref, ...), custom_call_target="tpu_custom_call" | custom-call | tf_op jit(solution)/shard_map/lay_out/pallas_call | solution.py:968
  14.8 0.0 collective-permute-done.2.first_x_ref
  14.8 0.0 collective-permute-done.3.second_x_ref
  14.8 3.9 %steps.1 = (f32[19,8,256]{2,1,0:T(8,128)S(1)}, f32[32,64]{1,0:T(8,128)S(1)}, f32[95,40,128]{2,1,0:T(8,128)S(1)}, f32[76,24,128]{2,1,0:T(8,128)S(1)}, f32[2,5,3,8...) custom-call(f32[38,8,128]{2,1,0:T(8,128)S(1)} %get-tuple-element.21., ...), custom_call_target="tpu_custom_call", output_to_operand_aliasing={{2}: (5, {}), {3}: (6, {}), {4}: (7, {}), {5}: (8, {})} | custom-call | tf_op jit(solution)/shard_map/steps/pallas_call | solution.py:971
  18.7 18.0 %all_to_all.9.parts_ref = f32[32,1,64]{2,1,0:T(1,128)S(1)} all-to-all(f32[32,1,64]{2,1,0:T(1,128)S(1)} %bitcast.2), channel_id=1, replica_groups=mesh['gx'=8,'gy'=4] {'gx','gy'}, dimensions={0} | all-to-all | bytes 16384 | tf_op jit(solution)/shard_map/all_to_all | solution.py:985
  36.7 1.2 %finish.1 = (f32[1,64]{1,0:T(1,128)}, f32[19,8,256]{2,1,0:T(8,128)}) custom-call(f32[32,1,64]{2,1,0:T(1,128)S(1)} %all_to_all.9.parts_ref, f32[19,8,256]{2,1,0:T(8,128)S(1)} %get-tuple-element.37.adjoint_ref), custom_call_target="tpu_custom_call" | custom-call | tf_op jit(solution)/shard_map/finish/pallas_call | solution.py:986
Async XLA Ops:
  1.9 6.9 %collective-permute-start = (f32[37,8,128]{2,1,0:T(8,128)S(1)}, f32[37,8,128]{2,1,0:T(8,128)S(1)}, u32[]{:S(2)}, u32[]{:S(2)}) collective-permute-start(f32[37,8,128]{2,1,0:T(8,128)S(1)} %get-tuple-element.24), channel_id=1, source_target_pairs={{0,1},{1,0},{2,3},{3,2},{4,5},{5,4},{6,7},{7,6},{8,9},{9,8},{10,11... | collective-permute-start | bytes 454664 | tf_op jit(solution)/shard_map/ppermute | solution.py:922
  4.9 3.9 %collective-permute-start.1 = (f32[37,8,128]{2,1,0:T(8,128)S(1)}, f32[37,8,128]{2,1,0:T(8,128)S(1)}, u32[]{:S(2)}, u32[]{:S(2)}) collective-permute-start(f32[37,8,128]{2,1,0:T(8,128)S(1)} %get-tuple-element.25), channel_id=1, source_target_pairs={{1,2},{2,1},{5,6},{6,5},{9,10},{10,9},{13,14},{14,13},{17,18},{18,... | collective-permute-start | bytes 454664 | tf_op jit(solution)/shard_map/ppermute | solution.py:926
  5.6 8.8 %collective-permute-start.5 = (f32[65,8,128]{2,1,0:T(8,128)S(1)}, f32[65,8,128]{2,1,0:T(8,128)S(1)}, u32[]{:S(2)}, u32[]{:S(2)}) collective-permute-start(f32[65,8,128]{2,1,0:T(8,128)S(1)} %get-tuple-element.29), channel_id=1, source_target_pairs={{4,8},{12,16},{20,24},{8,4},{16,12},{24,20},{5,9},{13,17},{21,25},... | collective-permute-start | bytes 798728 | tf_op jit(solution)/shard_map/ppermute | solution.py:926
  9.1 5.7 %collective-permute-start.3 = (f32[58,8,128]{2,1,0:T(8,128)S(1)}, f32[58,8,128]{2,1,0:T(8,128)S(1)}, u32[]{:S(2)}, u32[]{:S(2)}) collective-permute-start(f32[58,8,128]{2,1,0:T(8,128)S(1)} %get-tuple-element.27), channel_id=1, source_target_pairs={{4,8},{12,16},{20,24},{8,4},{16,12},{24,20},{5,9},{13,17},{21,25},... | collective-permute-start | bytes 712712 | tf_op jit(solution)/shard_map/ppermute | solution.py:926
  9.8 5.0 %collective-permute-start.2 = (f32[57,8,128]{2,1,0:T(8,128)S(1)}, f32[57,8,128]{2,1,0:T(8,128)S(1)}, u32[]{:S(2)}, u32[]{:S(2)}) collective-permute-start(f32[57,8,128]{2,1,0:T(8,128)S(1)} %get-tuple-element.26), channel_id=1, source_target_pairs={{0,4},{4,0},{8,12},{12,8},{16,20},{20,16},{24,28},{28,24},{1,5},{5... | collective-permute-start | bytes 700424 | tf_op jit(solution)/shard_map/ppermute | solution.py:922
  13.0 1.4 %collective-permute-start.4 = (f32[35,8,128]{2,1,0:T(8,128)S(1)}, f32[35,8,128]{2,1,0:T(8,128)S(1)}, u32[]{:S(2)}, u32[]{:S(2)}) collective-permute-start(f32[35,8,128]{2,1,0:T(8,128)S(1)} %get-tuple-element.28), channel_id=1, source_target_pairs={{0,4},{4,0},{8,12},{12,8},{16,20},{20,16},{24,28},{28,24},{1,5},{5... | collective-permute-start | bytes 430088 | tf_op jit(solution)/shard_map/ppermute | solution.py:922

commit v16 on v15

--- a/solution.py
+++ b/solution.py
@@ -879,11 +879,14 @@
     panel_ref[...] = sums
 
 
-def finish(parts_ref, adjoint_ref, sums_ref, adjoint_hbm, sem):
-    copy = pltpu.make_async_copy(adjoint_ref, adjoint_hbm, sem)
-    copy.start()
+def finish(parts_ref, adjoint_ref, sums_hbm, adjoint_hbm, sums_ref, sems):
+    adjoint_copy = pltpu.make_async_copy(adjoint_ref, adjoint_hbm, sems.at[0])
+    adjoint_copy.start()
     sums_ref[...] = jnp.sum(parts_ref[...], axis=0)
-    copy.wait()
+    sums_copy = pltpu.make_async_copy(sums_ref, sums_hbm, sems.at[1])
+    sums_copy.start()
+    sums_copy.wait()
+    adjoint_copy.wait()
 
 
 VMEM = pl.BlockSpec(memory_space=pltpu.VMEM)
@@ -987,8 +990,8 @@
         finish,
         out_shape=(shape_of(1, panels), shape_of(Q, ROWS, 2 * LANES)),
         in_specs=[VMEM, VMEM],
-        out_specs=(VMEM, HBM),
-        scratch_shapes=[pltpu.SemaphoreType.DMA],
+        out_specs=(HBM, HBM),
+        scratch_shapes=[pltpu.VMEM((1, panels), jnp.float32), pltpu.SemaphoreType.DMA((2,))],
         compiler_params=params,
         name="finish",
     )(gathered.reshape(devices, 1, panels), adjoint)

time: 38.2 us -> 37.7 us (0.987)
  Pallas kernels: 6.98 us -> 6.48 us
    pallas_call x1, Pallas kernels: 1.18 us -> 0.68 us  [on_device(): pl.pallas_call(finish, out_shape=(shape_of(1, panels), shape_of(Q, ROWS,...]
where the time goes in v16:
time: 37.7 us; the launch traced here: 37.4 us
  blocking collectives  18 us (48%)
  starting transfers between devices  8.33 us (22%)
  Pallas kernels  6.48 us (17%)
  waiting for transfers between devices  3.88 us (10%)
  between operations  0.68 us (2%)
    all_to_all x1, blocking collectives, on_device(): gathered = lax.all_to_all(sums, ('gx', 'gy'), 0, 0, tiled=True)  18 us
    ppermute x3, starting transfers between devices, swap(): lax.ppermute(value, axis, [(i, i ^ 1) for i in range(size) if i ^ 1 < size])  6.32 us
    ppermute x3, waiting for transfers between devices, swap(): lax.ppermute(value, axis, [(i, i ^ 1) for i in range(size) if i ^ 1 < size])  3.87 us
    pallas_call x1, Pallas kernels, on_device(): call(functools.partial(steps_kernel, sizes), (pltpu.VMEM((Q, ROWS, 2 * LA...  3.86 us
    ppermute x3, starting transfers between devices, swap_between(): return lax.ppermute(value, axis, pairs + [(j, i) for i, j in pairs])  2.01 us
    pallas_call x1, Pallas kernels, on_device(): call(pack_own, (tiles_of(y_layout.size),) * 2 + (tiles_of(side_layout.siz...  1.29 us
  transfers between devices with their start and end apart: 6, of which 2 were waited for; matrix products, arithmetic and copies ran while one was open for 0% of the time, Pallas kernels for 2%

profile of v16, /device:TPU:0, one launch (start us, length us, event | category | flops | bytes accessed | tf_op | source)
XLA Modules:
  0.0 37.4 jit_solution(4678854013835769148)
XLA Ops:
  0.6 1.3 %pack_own.1 = (f32[37,8,128]{2,1,0:T(8,128)S(1)}, f32[37,8,128]{2,1,0:T(8,128)S(1)}, f32[35,8,128]{2,1,0:T(8,128)S(1)}, f32[65,8,128]{2,1,0:T(8,128)S(1)}, f32[3...) custom-call(f32[19,8,256]{2,1,0:T(8,128)} %f_hbm.1, ...), custom_call_target="tpu_custom_call" | custom-call | tf_op jit(solution)/shard_map/pack_own/pallas_call | solution.py:935
  1.9 3.0 %collective-permute-start = (f32[37,8,128]{2,1,0:T(8,128)S(1)}, f32[37,8,128]{2,1,0:T(8,128)S(1)}, u32[]{:S(2)}, u32[]{:S(2)}) collective-permute-start(f32[37,8,128]{2,1,0:T(8,128)S(1)} %get-tuple-element.24), channel_id=1, source_target_pairs={{0,1},{1,0},{2,3},{3,2},{4,5},{5,4},{6,7},{7,6},{8,9},{9,8},{10,11... | collective-permute-start | bytes 454664 | tf_op jit(solution)/shard_map/ppermute | solution.py:925
  4.9 0.7 %collective-permute-start.1 = (f32[37,8,128]{2,1,0:T(8,128)S(1)}, f32[37,8,128]{2,1,0:T(8,128)S(1)}, u32[]{:S(2)}, u32[]{:S(2)}) collective-permute-start(f32[37,8,128]{2,1,0:T(8,128)S(1)} %get-tuple-element.25), channel_id=1, source_target_pairs={{1,2},{2,1},{5,6},{6,5},{9,10},{10,9},{13,14},{14,13},{17,18},{18,... | collective-permute-start | bytes 454664 | tf_op jit(solution)/shard_map/ppermute | solution.py:929
  5.6 0.7 %collective-permute-start.5 = (f32[65,8,128]{2,1,0:T(8,128)S(1)}, f32[65,8,128]{2,1,0:T(8,128)S(1)}, u32[]{:S(2)}, u32[]{:S(2)}) collective-permute-start(f32[65,8,128]{2,1,0:T(8,128)S(1)} %get-tuple-element.29), channel_id=1, source_target_pairs={{4,8},{12,16},{20,24},{8,4},{16,12},{24,20},{5,9},{13,17},{21,25},... | collective-permute-start | bytes 798728 | tf_op jit(solution)/shard_map/ppermute | solution.py:929
  6.3 2.6 %collective-permute-done.first_y_ref = f32[37,8,128]{2,1,0:T(8,128)S(1)} collective-permute-done((f32[37,8,128]{2,1,0:T(8,128)S(1)}, f32[37,8,128]{2,1,0:T(8,128)S(1)}, u32[]{:S(2)}, u32[]{:S(2)}) %collective-permute-start) | collective-permute-done | bytes 151584 | tf_op jit(solution)/shard_map/ppermute | solution.py:925
  8.9 0.0 collective-permute-done.1.second_y_ref
  8.9 0.2 pack_x.1
  9.1 0.7 %collective-permute-start.3 = (f32[58,8,128]{2,1,0:T(8,128)S(1)}, f32[58,8,128]{2,1,0:T(8,128)S(1)}, u32[]{:S(2)}, u32[]{:S(2)}) collective-permute-start(f32[58,8,128]{2,1,0:T(8,128)S(1)} %get-tuple-element.27), channel_id=1, source_target_pairs={{4,8},{12,16},{20,24},{8,4},{16,12},{24,20},{5,9},{13,17},{21,25},... | collective-permute-start | bytes 712712 | tf_op jit(solution)/shard_map/ppermute | solution.py:929
  9.8 3.2 %collective-permute-start.2 = (f32[57,8,128]{2,1,0:T(8,128)S(1)}, f32[57,8,128]{2,1,0:T(8,128)S(1)}, u32[]{:S(2)}, u32[]{:S(2)}) collective-permute-start(f32[57,8,128]{2,1,0:T(8,128)S(1)} %get-tuple-element.26), channel_id=1, source_target_pairs={{0,4},{4,0},{8,12},{12,8},{16,20},{20,16},{24,28},{28,24},{1,5},{5... | collective-permute-start | bytes 700424 | tf_op jit(solution)/shard_map/ppermute | solution.py:925
  13.0 0.1 collective-permute-start.4
  13.1 1.3 %collective-permute-done.4.first_side_ref = f32[35,8,128]{2,1,0:T(8,128)S(1)} collective-permute-done((f32[35,8,128]{2,1,0:T(8,128)S(1)}, f32[35,8,128]{2,1,0:T(8,128)S(1)}, u32[]{:S(2)}, u32[]{:S(2)}) %collective-permute-start.4) | collective-permute-done | bytes 143392 | tf_op jit(solution)/shard_map/ppermute | solution.py:925
  14.4 0.0 collective-permute-done.5.second_side_ref
  14.4 0.4 %lay_out.1 = (f32[95,40,128]{2,1,0:T(8,128)S(1)}, f32[76,24,128]{2,1,0:T(8,128)S(1)}, f32[2,5,3,8,128]{4,3,2,1,0:T(8,128)S(1)}, f32[4,4,2,8,128]{4,3,2,1,0:T(8,128)S(1)}) custom-call(f32[37,8,128]{2,1,0:T(8,128)S(1)} %collective-permute-done.first_y_ref, f32[37,8,128]{2,1,0:T(8,128)S(1)} %collective-permute-done.1.second_y_ref, ...), custom_call_target="tpu_custom_call" | custom-call | tf_op jit(solution)/shard_map/lay_out/pallas_call | solution.py:971
  14.8 0.0 collective-permute-done.2.first_x_ref
  14.8 0.0 collective-permute-done.3.second_x_ref
  14.8 3.9 %steps.1 = (f32[19,8,256]{2,1,0:T(8,128)S(1)}, f32[32,64]{1,0:T(8,128)S(1)}, f32[95,40,128]{2,1,0:T(8,128)S(1)}, f32[76,24,128]{2,1,0:T(8,128)S(1)}, f32[2,5,3,8...) custom-call(f32[38,8,128]{2,1,0:T(8,128)S(1)} %get-tuple-element.21., ...), custom_call_target="tpu_custom_call", output_to_operand_aliasing={{2}: (5, {}), {3}: (6, {}), {4}: (7, {}), {5}: (8, {})} | custom-call | tf_op jit(solution)/shard_map/steps/pallas_call | solution.py:974
  18.7 18.0 %all_to_all.9.parts_ref = f32[32,1,64]{2,1,0:T(1,128)S(1)} all-to-all(f32[32,1,64]{2,1,0:T(1,128)S(1)} %bitcast.2), channel_id=1, replica_groups=mesh['gx'=8,'gy'=4] {'gx','gy'}, dimensions={0} | all-to-all | bytes 16384 | tf_op jit(solution)/shard_map/all_to_all | solution.py:988
  36.7 0.7 %finish.1 = (f32[1,64]{1,0:T(1,128)}, f32[19,8,256]{2,1,0:T(8,128)}) custom-call(f32[32,1,64]{2,1,0:T(1,128)S(1)} %all_to_all.9.parts_ref, f32[19,8,256]{2,1,0:T(8,128)S(1)} %get-tuple-element.37.adjoint_ref), custom_call_target="tpu_custom_call" | custom-call | tf_op jit(solution)/shard_map/finish/pallas_call | solution.py:989
Async XLA Ops:
  1.9 6.9 %collective-permute-start = (f32[37,8,128]{2,1,0:T(8,128)S(1)}, f32[37,8,128]{2,1,0:T(8,128)S(1)}, u32[]{:S(2)}, u32[]{:S(2)}) collective-permute-start(f32[37,8,128]{2,1,0:T(8,128)S(1)} %get-tuple-element.24), channel_id=1, source_target_pairs={{0,1},{1,0},{2,3},{3,2},{4,5},{5,4},{6,7},{7,6},{8,9},{9,8},{10,11... | collective-permute-start | bytes 454664 | tf_op jit(solution)/shard_map/ppermute | solution.py:925
  4.9 3.9 %collective-permute-start.1 = (f32[37,8,128]{2,1,0:T(8,128)S(1)}, f32[37,8,128]{2,1,0:T(8,128)S(1)}, u32[]{:S(2)}, u32[]{:S(2)}) collective-permute-start(f32[37,8,128]{2,1,0:T(8,128)S(1)} %get-tuple-element.25), channel_id=1, source_target_pairs={{1,2},{2,1},{5,6},{6,5},{9,10},{10,9},{13,14},{14,13},{17,18},{18,... | collective-permute-start | bytes 454664 | tf_op jit(solution)/shard_map/ppermute | solution.py:929
  5.6 8.8 %collective-permute-start.5 = (f32[65,8,128]{2,1,0:T(8,128)S(1)}, f32[65,8,128]{2,1,0:T(8,128)S(1)}, u32[]{:S(2)}, u32[]{:S(2)}) collective-permute-start(f32[65,8,128]{2,1,0:T(8,128)S(1)} %get-tuple-element.29), channel_id=1, source_target_pairs={{4,8},{12,16},{20,24},{8,4},{16,12},{24,20},{5,9},{13,17},{21,25},... | collective-permute-start | bytes 798728 | tf_op jit(solution)/shard_map/ppermute | solution.py:929
  9.1 5.7 %collective-permute-start.3 = (f32[58,8,128]{2,1,0:T(8,128)S(1)}, f32[58,8,128]{2,1,0:T(8,128)S(1)}, u32[]{:S(2)}, u32[]{:S(2)}) collective-permute-start(f32[58,8,128]{2,1,0:T(8,128)S(1)} %get-tuple-element.27), channel_id=1, source_target_pairs={{4,8},{12,16},{20,24},{8,4},{16,12},{24,20},{5,9},{13,17},{21,25},... | collective-permute-start | bytes 712712 | tf_op jit(solution)/shard_map/ppermute | solution.py:929
  9.8 5.0 %collective-permute-start.2 = (f32[57,8,128]{2,1,0:T(8,128)S(1)}, f32[57,8,128]{2,1,0:T(8,128)S(1)}, u32[]{:S(2)}, u32[]{:S(2)}) collective-permute-start(f32[57,8,128]{2,1,0:T(8,128)S(1)} %get-tuple-element.26), channel_id=1, source_target_pairs={{0,4},{4,0},{8,12},{12,8},{16,20},{20,16},{24,28},{28,24},{1,5},{5... | collective-permute-start | bytes 700424 | tf_op jit(solution)/shard_map/ppermute | solution.py:925
  13.0 1.4 %collective-permute-start.4 = (f32[35,8,128]{2,1,0:T(8,128)S(1)}, f32[35,8,128]{2,1,0:T(8,128)S(1)}, u32[]{:S(2)}, u32[]{:S(2)}) collective-permute-start(f32[35,8,128]{2,1,0:T(8,128)S(1)} %get-tuple-element.28), channel_id=1, source_target_pairs={{0,4},{4,0},{8,12},{12,8},{16,20},{20,16},{24,28},{28,24},{1,5},{5... | collective-permute-start | bytes 430088 | tf_op jit(solution)/shard_map/ppermute | solution.py:925

commit v17 on v16

--- a/solution.py
+++ b/solution.py
@@ -556,11 +556,11 @@
     return population, cotangent, codes
 
 
-def pack_x(field_ref, first_y_ref, second_y_ref, first_ref, second_ref):
+def pack_x(field_ref, first_y_ref, up_y_ref, down_y_ref, first_ref, second_ref):
     row, lane, column, depth = iotas()
     y_layout, _, layout = layouts()
     deal = Deal(is_even("gx"), first_ref, second_ref, layout, X_SIDE)
-    population, cotangent, codes = from_y(*sides(first_y_ref, second_y_ref, "gy", y_layout))
+    population, cotangent, codes = from_y(*sides(first_y_ref, (up_y_ref, down_y_ref), "gy", y_layout))
 
     def both_codes(at, first, second):
         second = lines(second, 4)
@@ -593,6 +593,8 @@
 
 def sides(first_ref, second_ref, axis, layout):
     even = is_even(axis)
+    if isinstance(second_ref, tuple):
+        second_ref = Pick(even, *second_ref)
     picks = Pick(even, second_ref, first_ref), Pick(even, first_ref, second_ref)
     return [Unpacking(pick, layout) for pick in picks]
 
@@ -660,7 +662,8 @@
 
 def lay_out(
     first_y_ref,
-    second_y_ref,
+    up_y_ref,
+    down_y_ref,
     first_side_ref,
     second_side_ref,
     own_ref,
@@ -672,7 +675,7 @@
     field,
 ):
     y_layout, side_layout, _ = layouts()
-    from_left = from_y(*sides(first_y_ref, second_y_ref, "gy", y_layout))
+    from_left = from_y(*sides(first_y_ref, (up_y_ref, down_y_ref), "gy", y_layout))
     below, above = sides(first_side_ref, second_side_ref, "gx", side_layout)
     for c in range(5):
         t = c - 2
@@ -714,12 +717,13 @@
     own_field_ref,
     names_ref,
     first_x_ref,
-    second_x_ref,
+    up_x_ref,
+    down_x_ref,
     *refs,
 ):
     adjoint_ref, panel_ref, pop_a, ring_a, wide, field, pop_b, ring_b, saved, mom, grad = refs[4:]
     size_x, size_y = sizes
-    halves = sides(first_x_ref, second_x_ref, "gx", layouts()[2])
+    halves = sides(first_x_ref, (up_x_ref, down_x_ref), "gx", layouts()[2])
     below, above = (Shifted(ref, X_SIDE) for ref in halves)
     lay_halos(below, above, pop_a, ring_a, wide, field)
 
@@ -927,6 +931,12 @@
     def swap_between(value, axis, size):
         pairs = [(i, i + 1) for i in range(1, size - 1, 2)]
         return lax.ppermute(value, axis, pairs + [(j, i) for i, j in pairs])
+
+    def pass_between(value, axis, size):
+        pairs = [(i, i + 1) for i in range(1, size - 1, 2)]
+        return tuple(
+            lax.ppermute(value, axis, way) for way in (pairs, [(j, i) for i, j in pairs])
+        )
 
     arguments = [
         pltpu.with_memory_space_constraint(value, pltpu.HBM)
@@ -949,17 +959,17 @@
         ],
         name="pack_own",
     )(*arguments)
-    second_y = swap_between(second_y, "gy", size_y)
+    second_y = pass_between(second_y, "gy", size_y)
     first_y = swap(first_y, "gy", size_y)
     second_side = swap_between(second_side, "gx", size_x)
     first_side = swap(first_side, "gx", size_x)
     first_x, second_x = call(
         pack_x,
         (tiles_of(rest_layout.size), tiles_of(rest_layout.size + 1)),
-        [VMEM] * 3,
+        [VMEM] * 4,
         name="pack_x",
-    )(field, first_y, second_y)
-    second_x = swap_between(second_x, "gx", size_x)
+    )(field, first_y, *second_y)
+    second_x = pass_between(second_x, "gx", size_x)
     first_x = swap(first_x, "gx", size_x)
 
     spaces = (
@@ -968,13 +978,13 @@
         shape_of(2, 5, 3, ROWS, LANES),
         shape_of(4, 4, 2, ROWS, LANES),
     )
-    laid = call(lay_out, spaces, [VMEM] * 7, name="lay_out")(
-        first_y, second_y, first_side, second_side, own, field, cot
+    laid = call(lay_out, spaces, [VMEM] * 8, name="lay_out")(
+        first_y, *second_y, first_side, second_side, own, field, cot
     )
     adjoint, sums, *_ = call(
         functools.partial(steps_kernel, sizes),
         (pltpu.VMEM((Q, ROWS, 2 * LANES), jnp.float32), shape_of(devices, panels)) + spaces,
-        [VMEM] * 9,
+        [VMEM] * 10,
         [
             pltpu.VMEM((5 * Q, 5 * ROWS, LANES), jnp.float32),
             pltpu.VMEM((4 * Q, 3 * ROWS, LANES), jnp.float32),
@@ -983,8 +993,8 @@
             pltpu.VMEM((4, ROWS, LANES), jnp.float32),
         ],
         name="steps",
-        aliases={5 + n: 2 + n for n in range(4)},
-    )(state, field, names, first_x, second_x, *laid)
+        aliases={6 + n: 2 + n for n in range(4)},
+    )(state, field, names, first_x, *second_x, *laid)
     gathered = lax.all_to_all(sums, ("gx", "gy"), 0, 0, tiled=True)
     totals, adjoint = pl.pallas_call(
         finish,

time: 37.7 us -> 41 us (1.088)
  starting transfers between devices: 8.33 us -> 11.8 us
  waiting for transfers between devices: 3.88 us -> 3.21 us
  blocking collectives: 18 us -> 18.5 us
    ppermute x0 -> x4, starting transfers between devices: none -> 2.68 us  [pass_between(): lax.ppermute(value, axis, way)]
    ppermute x3, starting transfers between devices: 6.32 us -> 8.42 us  [swap(): lax.ppermute(value, axis, [(i, i ^ 1) for i in range(size) if i ^ 1 < size])]
    ppermute x3 -> x1, starting transfers between devices: 2.01 us -> 0.68 us  [swap_between(): return lax.ppermute(value, axis, pairs + [(j, i) for i, j in pairs])]
    ppermute x3, waiting for transfers between devices: 3.87 us -> 3.19 us  [swap(): lax.ppermute(value, axis, [(i, i ^ 1) for i in range(size) if i ^ 1 < size])]
    all_to_all x1, blocking collectives: 18 us -> 18.5 us  [on_device(): gathered = lax.all_to_all(sums, ('gx', 'gy'), 0, 0, tiled=True)]
  transfers between devices with their start and end apart: 6 -> 8, of which waited for: 2 -> 2; matrix products, arithmetic and copies ran while one was open for 0% -> 0% of each run, Pallas kernels for 2% -> 2%
where the time goes in v17:
time: 41 us; the launch traced here: 40.7 us
  blocking collectives  18.5 us (45%)
  starting transfers between devices  11.8 us (29%)
  Pallas kernels  6.5 us (16%)
  waiting for transfers between devices  3.21 us (8%)
  between operations  0.72 us (2%)
    all_to_all x1, blocking collectives, on_device(): gathered = lax.all_to_all(sums, ('gx', 'gy'), 0, 0, tiled=True)  18.5 us
    ppermute x3, starting transfers between devices, swap(): lax.ppermute(value, axis, [(i, i ^ 1) for i in range(size) if i ^ 1 < size])  8.42 us
    pallas_call x1, Pallas kernels, on_device(): call(functools.partial(steps_kernel, sizes), (pltpu.VMEM((Q, ROWS, 2 * LA...  3.87 us
    ppermute x3, waiting for transfers between devices, swap(): lax.ppermute(value, axis, [(i, i ^ 1) for i in range(size) if i ^ 1 < size])  3.19 us
    ppermute x4, starting transfers between devices, pass_between(): lax.ppermute(value, axis, way)  2.68 us
    pallas_call x1, Pallas kernels, on_device(): call(pack_own, (tiles_of(y_layout.size),) * 2 + (tiles_of(side_layout.siz...  1.29 us
  transfers between devices with their start and end apart: 8, of which 2 were waited for; matrix products, arithmetic and copies ran while one was open for 0% of the time, Pallas kernels for 2%

profile of v17, /device:TPU:0, one launch (start us, length us, event | category | flops | bytes accessed | tf_op | source)
XLA Modules:
  0.0 40.7 jit_solution(4833223847322712655)
XLA Ops:
  0.6 1.3 %pack_own.1 = (f32[37,8,128]{2,1,0:T(8,128)S(1)}, f32[37,8,128]{2,1,0:T(8,128)S(1)}, f32[35,8,128]{2,1,0:T(8,128)S(1)}, f32[65,8,128]{2,1,0:T(8,128)S(1)}, f32[3...) custom-call(f32[19,8,256]{2,1,0:T(8,128)} %f_hbm.1, ...), custom_call_target="tpu_custom_call" | custom-call | tf_op jit(solution)/shard_map/pack_own/pallas_call | solution.py:945
  1.9 3.0 %collective-permute-start = (f32[37,8,128]{2,1,0:T(8,128)S(1)}, f32[37,8,128]{2,1,0:T(8,128)S(1)}, u32[]{:S(2)}, u32[]{:S(2)}) collective-permute-start(f32[37,8,128]{2,1,0:T(8,128)S(1)} %get-tuple-element.24), channel_id=1, source_target_pairs={{0,1},{1,0},{2,3},{3,2},{4,5},{5,4},{6,7},{7,6},{8,9},{9,8},{10,11... | collective-permute-start | bytes 454664 | tf_op jit(solution)/shard_map/ppermute | solution.py:929
  4.9 0.7 %collective-permute-start.2 = (f32[37,8,128]{2,1,0:T(8,128)S(1)}, f32[37,8,128]{2,1,0:T(8,128)S(1)}, u32[]{:S(2)}, u32[]{:S(2)}) collective-permute-start(f32[37,8,128]{2,1,0:T(8,128)S(1)} %get-tuple-element.25), channel_id=1, source_target_pairs={{2,1},{6,5},{10,9},{14,13},{18,17},{22,21},{26,25},{30,29}} | collective-permute-start | bytes 454664 | tf_op jit(solution)/shard_map/ppermute | solution.py:938
  5.6 0.7 %collective-permute-start.1 = (f32[37,8,128]{2,1,0:T(8,128)S(1)}, f32[37,8,128]{2,1,0:T(8,128)S(1)}, u32[]{:S(2)}, u32[]{:S(2)}) collective-permute-start(f32[37,8,128]{2,1,0:T(8,128)S(1)} %get-tuple-element.25), channel_id=1, source_target_pairs={{1,2},{5,6},{9,10},{13,14},{17,18},{21,22},{25,26},{29,30}} | collective-permute-start | bytes 454664 | tf_op jit(solution)/shard_map/ppermute | solution.py:938
  6.3 0.7 %collective-permute-start.7 = (f32[65,8,128]{2,1,0:T(8,128)S(1)}, f32[65,8,128]{2,1,0:T(8,128)S(1)}, u32[]{:S(2)}, u32[]{:S(2)}) collective-permute-start(f32[65,8,128]{2,1,0:T(8,128)S(1)} %get-tuple-element.29), channel_id=1, source_target_pairs={{4,8},{12,16},{20,24},{8,4},{16,12},{24,20},{5,9},{13,17},{21,25},... | collective-permute-start | bytes 798728 | tf_op jit(solution)/shard_map/ppermute | solution.py:933
  7.0 1.9 %collective-permute-done.first_y_ref = f32[37,8,128]{2,1,0:T(8,128)S(1)} collective-permute-done((f32[37,8,128]{2,1,0:T(8,128)S(1)}, f32[37,8,128]{2,1,0:T(8,128)S(1)}, u32[]{:S(2)}, u32[]{:S(2)}) %collective-permute-start) | collective-permute-done | bytes 151584 | tf_op jit(solution)/shard_map/ppermute | solution.py:929
  8.9 0.0 collective-permute-done.2.down_y_ref
  8.9 0.0 collective-permute-done.1.up_y_ref
  8.9 0.2 pack_x.1
  9.1 0.7 %collective-permute-start.5 = (f32[58,8,128]{2,1,0:T(8,128)S(1)}, f32[58,8,128]{2,1,0:T(8,128)S(1)}, u32[]{:S(2)}, u32[]{:S(2)}) collective-permute-start(f32[58,8,128]{2,1,0:T(8,128)S(1)} %get-tuple-element.27), channel_id=1, source_target_pairs={{8,4},{16,12},{24,20},{9,5},{17,13},{25,21},{10,6},{18,14},{26,22}... | collective-permute-start | bytes 712712 | tf_op jit(solution)/shard_map/ppermute | solution.py:938
  9.8 0.7 %collective-permute-start.4 = (f32[58,8,128]{2,1,0:T(8,128)S(1)}, f32[58,8,128]{2,1,0:T(8,128)S(1)}, u32[]{:S(2)}, u32[]{:S(2)}) collective-permute-start(f32[58,8,128]{2,1,0:T(8,128)S(1)} %get-tuple-element.27), channel_id=1, source_target_pairs={{4,8},{12,16},{20,24},{5,9},{13,17},{21,25},{6,10},{14,18},{22,26}... | collective-permute-start | bytes 712712 | tf_op jit(solution)/shard_map/ppermute | solution.py:938
  10.5 5.3 %collective-permute-start.3 = (f32[57,8,128]{2,1,0:T(8,128)S(1)}, f32[57,8,128]{2,1,0:T(8,128)S(1)}, u32[]{:S(2)}, u32[]{:S(2)}) collective-permute-start(f32[57,8,128]{2,1,0:T(8,128)S(1)} %get-tuple-element.26), channel_id=1, source_target_pairs={{0,4},{4,0},{8,12},{12,8},{16,20},{20,16},{24,28},{28,24},{1,5},{5... | collective-permute-start | bytes 700424 | tf_op jit(solution)/shard_map/ppermute | solution.py:929
  15.8 0.1 collective-permute-start.6
  15.9 1.3 %collective-permute-done.6.first_side_ref = f32[35,8,128]{2,1,0:T(8,128)S(1)} collective-permute-done((f32[35,8,128]{2,1,0:T(8,128)S(1)}, f32[35,8,128]{2,1,0:T(8,128)S(1)}, u32[]{:S(2)}, u32[]{:S(2)}) %collective-permute-start.6) | collective-permute-done | bytes 143392 | tf_op jit(solution)/shard_map/ppermute | solution.py:929
  17.2 0.0 collective-permute-done.7.second_side_ref
  17.2 0.4 %lay_out.1 = (f32[95,40,128]{2,1,0:T(8,128)S(1)}, f32[76,24,128]{2,1,0:T(8,128)S(1)}, f32[2,5,3,8,128]{4,3,2,1,0:T(8,128)S(1)}, f32[4,4,2,8,128]{4,3,2,1,0:T(8,128)S(1)}) custom-call(f32[37,8,128]{2,1,0:T(8,128)S(1)} %collective-permute-done.first_y_ref, f32[37,8,128]{2,1,0:T(8,128)S(1)} %collective-permute-done.1.up_y_ref, ...), custom_call_target="tpu_custom_call" | custom-call | tf_op jit(solution)/shard_map/lay_out/pallas_call | solution.py:981
  17.6 0.0 collective-permute-done.3.first_x_ref
  17.6 0.0 collective-permute-done.5.down_x_ref
  17.6 0.0 collective-permute-done.4.up_x_ref
  17.6 3.9 %steps.1 = (f32[19,8,256]{2,1,0:T(8,128)S(1)}, f32[32,64]{1,0:T(8,128)S(1)}, f32[95,40,128]{2,1,0:T(8,128)S(1)}, f32[76,24,128]{2,1,0:T(8,128)S(1)}, f32[2,5,3,8...) custom-call(f32[38,8,128]{2,1,0:T(8,128)S(1)} %get-tuple-element.21., ...), custom_call_target="tpu_custom_call", output_to_operand_aliasing={{2}: (6, {}), {3}: (7, {}), {4}: (8, {}), {5}: (9, {})} | custom-call | tf_op jit(solution)/shard_map/steps/pallas_call | solution.py:984
  21.5 18.5 %all_to_all.9.parts_ref = f32[32,1,64]{2,1,0:T(1,128)S(1)} all-to-all(f32[32,1,64]{2,1,0:T(1,128)S(1)} %bitcast.2), channel_id=1, replica_groups=mesh['gx'=8,'gy'=4] {'gx','gy'}, dimensions={0} | all-to-all | bytes 16384 | tf_op jit(solution)/shard_map/all_to_all | solution.py:998
  40.0 0.7 %finish.1 = (f32[1,64]{1,0:T(1,128)}, f32[19,8,256]{2,1,0:T(8,128)}) custom-call(f32[32,1,64]{2,1,0:T(1,128)S(1)} %all_to_all.9.parts_ref, f32[19,8,256]{2,1,0:T(8,128)S(1)} %get-tuple-element.37.adjoint_ref), custom_call_target="tpu_custom_call" | custom-call | tf_op jit(solution)/shard_map/finish/pallas_call | solution.py:999
Async XLA Ops:
  1.9 6.9 %collective-permute-start = (f32[37,8,128]{2,1,0:T(8,128)S(1)}, f32[37,8,128]{2,1,0:T(8,128)S(1)}, u32[]{:S(2)}, u32[]{:S(2)}) collective-permute-start(f32[37,8,128]{2,1,0:T(8,128)S(1)} %get-tuple-element.24), channel_id=1, source_target_pairs={{0,1},{1,0},{2,3},{3,2},{4,5},{5,4},{6,7},{7,6},{8,9},{9,8},{10,11... | collective-permute-start | bytes 454664 | tf_op jit(solution)/shard_map/ppermute | solution.py:929
  4.9 3.9 %collective-permute-start.2 = (f32[37,8,128]{2,1,0:T(8,128)S(1)}, f32[37,8,128]{2,1,0:T(8,128)S(1)}, u32[]{:S(2)}, u32[]{:S(2)}) collective-permute-start(f32[37,8,128]{2,1,0:T(8,128)S(1)} %get-tuple-element.25), channel_id=1, source_target_pairs={{2,1},{6,5},{10,9},{14,13},{18,17},{22,21},{26,25},{30,29}} | collective-permute-start | bytes 454664 | tf_op jit(solution)/shard_map/ppermute | solution.py:938
  5.6 3.3 %collective-permute-start.1 = (f32[37,8,128]{2,1,0:T(8,128)S(1)}, f32[37,8,128]{2,1,0:T(8,128)S(1)}, u32[]{:S(2)}, u32[]{:S(2)}) collective-permute-start(f32[37,8,128]{2,1,0:T(8,128)S(1)} %get-tuple-element.25), channel_id=1, source_target_pairs={{1,2},{5,6},{9,10},{13,14},{17,18},{21,22},{25,26},{29,30}} | collective-permute-start | bytes 454664 | tf_op jit(solution)/shard_map/ppermute | solution.py:938
  6.3 10.9 %collective-permute-start.7 = (f32[65,8,128]{2,1,0:T(8,128)S(1)}, f32[65,8,128]{2,1,0:T(8,128)S(1)}, u32[]{:S(2)}, u32[]{:S(2)}) collective-permute-start(f32[65,8,128]{2,1,0:T(8,128)S(1)} %get-tuple-element.29), channel_id=1, source_target_pairs={{4,8},{12,16},{20,24},{8,4},{16,12},{24,20},{5,9},{13,17},{21,25},... | collective-permute-start | bytes 798728 | tf_op jit(solution)/shard_map/ppermute | solution.py:933
  9.1 8.5 %collective-permute-start.5 = (f32[58,8,128]{2,1,0:T(8,128)S(1)}, f32[58,8,128]{2,1,0:T(8,128)S(1)}, u32[]{:S(2)}, u32[]{:S(2)}) collective-permute-start(f32[58,8,128]{2,1,0:T(8,128)S(1)} %get-tuple-element.27), channel_id=1, source_target_pairs={{8,4},{16,12},{24,20},{9,5},{17,13},{25,21},{10,6},{18,14},{26,22}... | collective-permute-start | bytes 712712 | tf_op jit(solution)/shard_map/ppermute | solution.py:938
  9.8 7.9 %collective-permute-start.4 = (f32[58,8,128]{2,1,0:T(8,128)S(1)}, f32[58,8,128]{2,1,0:T(8,128)S(1)}, u32[]{:S(2)}, u32[]{:S(2)}) collective-permute-start(f32[58,8,128]{2,1,0:T(8,128)S(1)} %get-tuple-element.27), channel_id=1, source_target_pairs={{4,8},{12,16},{20,24},{5,9},{13,17},{21,25},{6,10},{14,18},{22,26}... | collective-permute-start | bytes 712712 | tf_op jit(solution)/shard_map/ppermute | solution.py:938
  10.5 7.2 %collective-permute-start.3 = (f32[57,8,128]{2,1,0:T(8,128)S(1)}, f32[57,8,128]{2,1,0:T(8,128)S(1)}, u32[]{:S(2)}, u32[]{:S(2)}) collective-permute-start(f32[57,8,128]{2,1,0:T(8,128)S(1)} %get-tuple-element.26), channel_id=1, source_target_pairs={{0,4},{4,0},{8,12},{12,8},{16,20},{20,16},{24,28},{28,24},{1,5},{5... | collective-permute-start | bytes 700424 | tf_op jit(solution)/shard_map/ppermute | solution.py:929
  15.8 1.4 %collective-permute-start.6 = (f32[35,8,128]{2,1,0:T(8,128)S(1)}, f32[35,8,128]{2,1,0:T(8,128)S(1)}, u32[]{:S(2)}, u32[]{:S(2)}) collective-permute-start(f32[35,8,128]{2,1,0:T(8,128)S(1)} %get-tuple-element.28), channel_id=1, source_target_pairs={{0,4},{4,0},{8,12},{12,8},{16,20},{20,16},{24,28},{28,24},{1,5},{5... | collective-permute-start | bytes 430088 | tf_op jit(solution)/shard_map/ppermute | solution.py:929

commit v18 on v16

--- a/solution.py
+++ b/solution.py
@@ -199,7 +199,14 @@
     return masks
 
 
-def stream_tile(load, sign, masks, lane):
+def stream_tile(get, sign, masks, lane):
+    loaded = {}
+
+    def load(*at):
+        if at not in loaded:
+            loaded[at] = get(*at)
+        return loaded[at]
+
     cross_low, cross_high = lane >= LANES - NZ, lane < NZ
     combined = {}
     out = []
@@ -746,8 +753,12 @@
 
         def load(i, tile_step, row_step, move):
             at = 5 * i + step[tile_step]
-            before, own, behind = (ref[at, pl.ds(ROWS * n + row_step, ROWS), :] for n in (1, 2, 3))
-            return (own, jnp.where(after, behind, before), before, behind)[r]
+            def part(n):
+                return ref[at, pl.ds(ROWS * n + row_step, ROWS), :]
+
+            if r == 1:
+                return jnp.where(after, part(3), part(1))
+            return part({0: 2, 2: 1, 3: 3}[r])
 
         return load
 

time: 37.7 us -> 37.7 us (level)
  no operation moved by 1% of the time
where the time goes in v18:
time: 37.7 us; the launch traced here: 37.4 us
  blocking collectives  18 us (48%)
  starting transfers between devices  8.33 us (22%)
  Pallas kernels  6.48 us (17%)
  waiting for transfers between devices  3.88 us (10%)
  between operations  0.68 us (2%)
    all_to_all x1, blocking collectives, on_device(): gathered = lax.all_to_all(sums, ('gx', 'gy'), 0, 0, tiled=True)  18 us
    ppermute x3, starting transfers between devices, swap(): lax.ppermute(value, axis, [(i, i ^ 1) for i in range(size) if i ^ 1 < size])  6.32 us
    ppermute x3, waiting for transfers between devices, swap(): lax.ppermute(value, axis, [(i, i ^ 1) for i in range(size) if i ^ 1 < size])  3.87 us
    pallas_call x1, Pallas kernels, on_device(): call(functools.partial(steps_kernel, sizes), (pltpu.VMEM((Q, ROWS, 2 * LA...  3.86 us
    ppermute x3, starting transfers between devices, swap_between(): return lax.ppermute(value, axis, pairs + [(j, i) for i, j in pairs])  2.01 us
    pallas_call x1, Pallas kernels, on_device(): call(pack_own, (tiles_of(y_layout.size),) * 2 + (tiles_of(side_layout.siz...  1.29 us
  transfers between devices with their start and end apart: 6, of which 2 were waited for; matrix products, arithmetic and copies ran while one was open for 0% of the time, Pallas kernels for 2%

profile of v18, /device:TPU:0, one launch (start us, length us, event | category | flops | bytes accessed | tf_op | source)
XLA Modules:
  0.0 37.4 jit_solution(13296057668102037470)
XLA Ops:
  0.6 1.3 %pack_own.1 = (f32[37,8,128]{2,1,0:T(8,128)S(1)}, f32[37,8,128]{2,1,0:T(8,128)S(1)}, f32[35,8,128]{2,1,0:T(8,128)S(1)}, f32[65,8,128]{2,1,0:T(8,128)S(1)}, f32[3...) custom-call(f32[19,8,256]{2,1,0:T(8,128)} %f_hbm.1, ...), custom_call_target="tpu_custom_call" | custom-call | tf_op jit(solution)/shard_map/pack_own/pallas_call | solution.py:946
  1.9 3.0 %collective-permute-start = (f32[37,8,128]{2,1,0:T(8,128)S(1)}, f32[37,8,128]{2,1,0:T(8,128)S(1)}, u32[]{:S(2)}, u32[]{:S(2)}) collective-permute-start(f32[37,8,128]{2,1,0:T(8,128)S(1)} %get-tuple-element.24), channel_id=1, source_target_pairs={{0,1},{1,0},{2,3},{3,2},{4,5},{5,4},{6,7},{7,6},{8,9},{9,8},{10,11... | collective-permute-start | bytes 454664 | tf_op jit(solution)/shard_map/ppermute | solution.py:936
  4.9 0.7 %collective-permute-start.1 = (f32[37,8,128]{2,1,0:T(8,128)S(1)}, f32[37,8,128]{2,1,0:T(8,128)S(1)}, u32[]{:S(2)}, u32[]{:S(2)}) collective-permute-start(f32[37,8,128]{2,1,0:T(8,128)S(1)} %get-tuple-element.25), channel_id=1, source_target_pairs={{1,2},{2,1},{5,6},{6,5},{9,10},{10,9},{13,14},{14,13},{17,18},{18,... | collective-permute-start | bytes 454664 | tf_op jit(solution)/shard_map/ppermute | solution.py:940
  5.6 0.7 %collective-permute-start.5 = (f32[65,8,128]{2,1,0:T(8,128)S(1)}, f32[65,8,128]{2,1,0:T(8,128)S(1)}, u32[]{:S(2)}, u32[]{:S(2)}) collective-permute-start(f32[65,8,128]{2,1,0:T(8,128)S(1)} %get-tuple-element.29), channel_id=1, source_target_pairs={{4,8},{12,16},{20,24},{8,4},{16,12},{24,20},{5,9},{13,17},{21,25},... | collective-permute-start | bytes 798728 | tf_op jit(solution)/shard_map/ppermute | solution.py:940
  6.3 2.6 %collective-permute-done.first_y_ref = f32[37,8,128]{2,1,0:T(8,128)S(1)} collective-permute-done((f32[37,8,128]{2,1,0:T(8,128)S(1)}, f32[37,8,128]{2,1,0:T(8,128)S(1)}, u32[]{:S(2)}, u32[]{:S(2)}) %collective-permute-start) | collective-permute-done | bytes 151584 | tf_op jit(solution)/shard_map/ppermute | solution.py:936
  8.9 0.0 collective-permute-done.1.second_y_ref
  8.9 0.2 pack_x.1
  9.1 0.7 %collective-permute-start.3 = (f32[58,8,128]{2,1,0:T(8,128)S(1)}, f32[58,8,128]{2,1,0:T(8,128)S(1)}, u32[]{:S(2)}, u32[]{:S(2)}) collective-permute-start(f32[58,8,128]{2,1,0:T(8,128)S(1)} %get-tuple-element.27), channel_id=1, source_target_pairs={{4,8},{12,16},{20,24},{8,4},{16,12},{24,20},{5,9},{13,17},{21,25},... | collective-permute-start | bytes 712712 | tf_op jit(solution)/shard_map/ppermute | solution.py:940
  9.8 3.2 %collective-permute-start.2 = (f32[57,8,128]{2,1,0:T(8,128)S(1)}, f32[57,8,128]{2,1,0:T(8,128)S(1)}, u32[]{:S(2)}, u32[]{:S(2)}) collective-permute-start(f32[57,8,128]{2,1,0:T(8,128)S(1)} %get-tuple-element.26), channel_id=1, source_target_pairs={{0,4},{4,0},{8,12},{12,8},{16,20},{20,16},{24,28},{28,24},{1,5},{5... | collective-permute-start | bytes 700424 | tf_op jit(solution)/shard_map/ppermute | solution.py:936
  13.0 0.1 collective-permute-start.4
  13.1 1.3 %collective-permute-done.4.first_side_ref = f32[35,8,128]{2,1,0:T(8,128)S(1)} collective-permute-done((f32[35,8,128]{2,1,0:T(8,128)S(1)}, f32[35,8,128]{2,1,0:T(8,128)S(1)}, u32[]{:S(2)}, u32[]{:S(2)}) %collective-permute-start.4) | collective-permute-done | bytes 143392 | tf_op jit(solution)/shard_map/ppermute | solution.py:936
  14.4 0.0 collective-permute-done.5.second_side_ref
  14.4 0.4 %lay_out.1 = (f32[95,40,128]{2,1,0:T(8,128)S(1)}, f32[76,24,128]{2,1,0:T(8,128)S(1)}, f32[2,5,3,8,128]{4,3,2,1,0:T(8,128)S(1)}, f32[4,4,2,8,128]{4,3,2,1,0:T(8,128)S(1)}) custom-call(f32[37,8,128]{2,1,0:T(8,128)S(1)} %collective-permute-done.first_y_ref, f32[37,8,128]{2,1,0:T(8,128)S(1)} %collective-permute-done.1.second_y_ref, ...), custom_call_target="tpu_custom_call" | custom-call | tf_op jit(solution)/shard_map/lay_out/pallas_call | solution.py:982
  14.8 0.0 collective-permute-done.2.first_x_ref
  14.8 0.0 collective-permute-done.3.second_x_ref
  14.8 3.9 %steps.1 = (f32[19,8,256]{2,1,0:T(8,128)S(1)}, f32[32,64]{1,0:T(8,128)S(1)}, f32[95,40,128]{2,1,0:T(8,128)S(1)}, f32[76,24,128]{2,1,0:T(8,128)S(1)}, f32[2,5,3,8...) custom-call(f32[38,8,128]{2,1,0:T(8,128)S(1)} %get-tuple-element.21., ...), custom_call_target="tpu_custom_call", output_to_operand_aliasing={{2}: (5, {}), {3}: (6, {}), {4}: (7, {}), {5}: (8, {})} | custom-call | tf_op jit(solution)/shard_map/steps/pallas_call | solution.py:985
  18.7 18.0 %all_to_all.9.parts_ref = f32[32,1,64]{2,1,0:T(1,128)S(1)} all-to-all(f32[32,1,64]{2,1,0:T(1,128)S(1)} %bitcast.2), channel_id=1, replica_groups=mesh['gx'=8,'gy'=4] {'gx','gy'}, dimensions={0} | all-to-all | bytes 16384 | tf_op jit(solution)/shard_map/all_to_all | solution.py:999
  36.7 0.7 %finish.1 = (f32[1,64]{1,0:T(1,128)}, f32[19,8,256]{2,1,0:T(8,128)}) custom-call(f32[32,1,64]{2,1,0:T(1,128)S(1)} %all_to_all.9.parts_ref, f32[19,8,256]{2,1,0:T(8,128)S(1)} %get-tuple-element.37.adjoint_ref), custom_call_target="tpu_custom_call" | custom-call | tf_op jit(solution)/shard_map/finish/pallas_call | solution.py:1000
Async XLA Ops:
  1.9 6.9 %collective-permute-start = (f32[37,8,128]{2,1,0:T(8,128)S(1)}, f32[37,8,128]{2,1,0:T(8,128)S(1)}, u32[]{:S(2)}, u32[]{:S(2)}) collective-permute-start(f32[37,8,128]{2,1,0:T(8,128)S(1)} %get-tuple-element.24), channel_id=1, source_target_pairs={{0,1},{1,0},{2,3},{3,2},{4,5},{5,4},{6,7},{7,6},{8,9},{9,8},{10,11... | collective-permute-start | bytes 454664 | tf_op jit(solution)/shard_map/ppermute | solution.py:936
  4.9 3.9 %collective-permute-start.1 = (f32[37,8,128]{2,1,0:T(8,128)S(1)}, f32[37,8,128]{2,1,0:T(8,128)S(1)}, u32[]{:S(2)}, u32[]{:S(2)}) collective-permute-start(f32[37,8,128]{2,1,0:T(8,128)S(1)} %get-tuple-element.25), channel_id=1, source_target_pairs={{1,2},{2,1},{5,6},{6,5},{9,10},{10,9},{13,14},{14,13},{17,18},{18,... | collective-permute-start | bytes 454664 | tf_op jit(solution)/shard_map/ppermute | solution.py:940
  5.6 8.8 %collective-permute-start.5 = (f32[65,8,128]{2,1,0:T(8,128)S(1)}, f32[65,8,128]{2,1,0:T(8,128)S(1)}, u32[]{:S(2)}, u32[]{:S(2)}) collective-permute-start(f32[65,8,128]{2,1,0:T(8,128)S(1)} %get-tuple-element.29), channel_id=1, source_target_pairs={{4,8},{12,16},{20,24},{8,4},{16,12},{24,20},{5,9},{13,17},{21,25},... | collective-permute-start | bytes 798728 | tf_op jit(solution)/shard_map/ppermute | solution.py:940
  9.1 5.7 %collective-permute-start.3 = (f32[58,8,128]{2,1,0:T(8,128)S(1)}, f32[58,8,128]{2,1,0:T(8,128)S(1)}, u32[]{:S(2)}, u32[]{:S(2)}) collective-permute-start(f32[58,8,128]{2,1,0:T(8,128)S(1)} %get-tuple-element.27), channel_id=1, source_target_pairs={{4,8},{12,16},{20,24},{8,4},{16,12},{24,20},{5,9},{13,17},{21,25},... | collective-permute-start | bytes 712712 | tf_op jit(solution)/shard_map/ppermute | solution.py:940
  9.8 5.0 %collective-permute-start.2 = (f32[57,8,128]{2,1,0:T(8,128)S(1)}, f32[57,8,128]{2,1,0:T(8,128)S(1)}, u32[]{:S(2)}, u32[]{:S(2)}) collective-permute-start(f32[57,8,128]{2,1,0:T(8,128)S(1)} %get-tuple-element.26), channel_id=1, source_target_pairs={{0,4},{4,0},{8,12},{12,8},{16,20},{20,16},{24,28},{28,24},{1,5},{5... | collective-permute-start | bytes 700424 | tf_op jit(solution)/shard_map/ppermute | solution.py:936
  13.0 1.4 %collective-permute-start.4 = (f32[35,8,128]{2,1,0:T(8,128)S(1)}, f32[35,8,128]{2,1,0:T(8,128)S(1)}, u32[]{:S(2)}, u32[]{:S(2)}) collective-permute-start(f32[35,8,128]{2,1,0:T(8,128)S(1)} %get-tuple-element.28), channel_id=1, source_target_pairs={{0,4},{4,0},{8,12},{12,8},{16,20},{20,16},{24,28},{28,24},{1,5},{5... | collective-permute-start | bytes 430088 | tf_op jit(solution)/shard_map/ppermute | solution.py:936

commit v19 on v16

--- a/solution.py
+++ b/solution.py
@@ -46,11 +46,16 @@
 Y_TILES = 43
 X_EXTRA = 19
 X_LANE = 20
-X_SIDE = 2 * X_LANE
-X_RING = 4 * X_LANE
-X_CODE13 = X_RING + Q + 1
-X_CODE2 = X_CODE13 + 4
-X_TILES = X_CODE2 + 2
+X_HALVES = 10
+
+
+def x_places(lanes):
+    ring = X_LANE * lanes
+    code13 = ring + X_HALVES
+    code2 = code13 + lanes
+    return ring, code13, code2, code2 + (lanes + 1) // 2
+
+
 EMPTY = 25
 FREE = NZ - EMPTY
 WEIGHTS = [W_REST] + [W_AXIS] * 6 + [W_DIAG] * 12
@@ -305,17 +310,15 @@
 def layouts():
     y_fills = {2 * i + t: WEIGHTS[i] for i in LEVEL for t in range(2)}
     y_fills.update({Y_POP: W_DIAG, Y_CODE2: 0.0})
-    x_fills = {X_LANE * n + i: WEIGHTS[i] for n in range(4) for i in LEVEL}
-    side = {at: fill for at, fill in x_fills.items() if at < X_SIDE}
-    rest = {at - X_SIDE: fill for at, fill in x_fills.items() if at >= X_SIDE}
-    rest.update({X_CODE2 - X_SIDE: 0.0, X_CODE2 + 1 - X_SIDE: 0.0})
-    rest.update({X_RING - X_SIDE + i: WEIGHTS[i] for i in range(Q)})
-    ring = [X_RING - X_SIDE + i for i in range(9)]
-    return (
-        Layout(Y_TILES, [2 * i for i in LEVEL[:6]], y_fills),
-        Layout(X_SIDE, LEVEL[:5], side),
-        Layout(X_TILES - X_SIDE, ring, rest),
-    )
+    out = [Layout(Y_TILES, [2 * i for i in LEVEL[:6]], y_fills)]
+    for lanes, count in ((3, 10), (1, 4)):
+        ring, _, code2, tiles = x_places(lanes)
+        fills = {ring + n: WEIGHTS[2 * n] for n in range(1, X_HALVES)}
+        fills.update({at: 0.0 for at in range(code2, tiles)})
+        fills.update({X_LANE * n + i: WEIGHTS[i] for n in range(lanes) for i in LEVEL})
+        guests = [X_LANE * (lanes - 1) + i for i in LEVEL[:count]]
+        out.append(Layout(tiles, guests, fills))
+    return out
 
 
 class Pick:
@@ -349,14 +352,6 @@
         self.second.finish()
 
 
-class Shifted:
-    def __init__(self, ref, start):
-        self.ref, self.start = ref, start
-
-    def __getitem__(self, at):
-        return self.ref[at - self.start]
-
-
 def is_even(axis):
     return lax.rem(lax.axis_index(axis), 2) == 0
 
@@ -369,8 +364,6 @@
     porosity_hbm,
     first_ref,
     second_ref,
-    first_side_ref,
-    second_side_ref,
     own_ref,
     state_ref,
     own_cot_ref,
@@ -398,9 +391,7 @@
         copy.start()
     for copy in copies[:4]:
         copy.wait()
-    y_layout, side_layout, _ = layouts()
-    deal = Deal(is_even("gy"), first_ref, second_ref, y_layout)
-    side = Deal(is_even("gx"), first_side_ref, second_side_ref, side_layout)
+    deal = Deal(is_even("gy"), first_ref, second_ref, layouts()[0])
     row, lane, column, depth = iotas()
     top = depth == NZ - 1
 
@@ -456,48 +447,51 @@
     for t in range(2):
         for i in range(Q):
             own_cot_ref[2 * i + t] = tile_of(cot_ref, i, t)
-        pack_lines(
-            side,
-            X_LANE * t,
-            lambda i: own_ref[2 * i + t],
-            lambda i: tile_of(cot_ref, i, t),
-        )
-    side.finish()
-
-
-def from_y(left_ref, right_ref):
+
+
+def is_right(near):
+    return is_even("gy") if near else jnp.logical_not(is_even("gy"))
+
+
+def half_lanes(right):
     row, lane, column, depth = iotas()
-    high = lane >= LANES // 2
-
-    def population(i, c):
-        if c == 1:
-            return left_ref[2 * i + 1]
-        if c == 4:
-            return right_ref[2 * i]
-        along_y = VELOCITIES[i][1]
-        left, right = left_ref[2 * i], right_ref[2 * i + 1]
-        if along_y == 1 and i in turned(1, 1):
-            right = columns(right_ref[Y_POP], -turned(1, 1).index(i))
-        if along_y == -1 and i in turned(1, -1):
-            left = columns(left_ref[Y_POP], 3 - turned(1, -1).index(i))
-        return jnp.where(high, left, right)
-
-    def cotangent(i, c):
-        ref, way, place, far = (left_ref, 1, 1, 0) if c == 1 else (right_ref, -1, 2, 1)
-        deep = 3 - way * VELOCITIES[i][1]
-        value = columns(ref[2 * i + far], way * (4 - deep))
-        if i in turned(1, way):
-            extra = columns(ref[Y_COT], place - turned(1, way).index(i))
-            value = jnp.where(column == place, extra, value)
-        return value
-
-    def codes(s, c):
-        if c == 0:
-            left, right = columns(left_ref[Y_CODE3], 3), columns(right_ref[Y_CODE3], 1)
-            return jnp.where(high, left, right)
-        return (left_ref if c == 1 else right_ref)[(Y_CODE1, Y_CODE2, Y_CODE3)[s - 1]]
-
-    return population, cotangent, codes
+    return lane // (LANES // 2) == jnp.where(right, 0, 1)
+
+
+def from_y(message_ref, near):
+    row, lane, column, depth = iotas()
+    ref = Unpacking(message_ref, layouts()[0])
+    right = is_right(near)
+
+    def population(i):
+        return jnp.where(right, ref[2 * i], ref[2 * i + 1])
+
+    def cotangent(i):
+        values = []
+        for way, place, far in ((1, 1, 0), (-1, 2, 1)):
+            deep = 3 - way * VELOCITIES[i][1]
+            value = columns(ref[2 * i + far], way * (4 - deep))
+            if i in turned(1, way):
+                extra = columns(ref[Y_COT], place - turned(1, way).index(i))
+                value = jnp.where(column == place, extra, value)
+            values.append(value)
+        return jnp.where(right, values[1], values[0])
+
+    def codes(s):
+        return ref[(Y_CODE1, Y_CODE2, Y_CODE3)[s - 1]]
+
+    def outer(i):
+        left, above = ref[2 * i], ref[2 * i + 1]
+        if i in turned(1, 1):
+            above = columns(ref[Y_POP], -turned(1, 1).index(i))
+        if i in turned(1, -1):
+            left = columns(ref[Y_POP], 3 - turned(1, -1).index(i))
+        return jnp.where(right, above, left)
+
+    def outer_code():
+        return jnp.where(right, columns(ref[Y_CODE3], 1), columns(ref[Y_CODE3], 3))
+
+    return population, cotangent, codes, outer, outer_code
 
 
 def mix_lines(deal, at, pop, cot, deep, way):
@@ -527,8 +521,49 @@
         deal.put(way, first + X_EXTRA, extra)
 
 
-def from_x(ref, n, way):
+def pack_neighbour(deal, lanes, message_ref, near):
+    ring, code13, code2, tiles = x_places(lanes)
+    population, cotangent, codes, outer, outer_code = from_y(message_ref, near)
+    pack_lines(deal, X_LANE * (lanes - 1), population, cotangent)
+    kept = half_lanes(is_right(near))
+    for n in range(X_HALVES):
+        first, second = (outer(2 * n - 1), outer(2 * n)) if n else (outer(0), outer_code())
+        deal.put_both(ring + n, jnp.where(kept, first, pltpu.roll(second, LANES // 2, 1)))
+    for way in (1, -1):
+        mix_lines(deal, code13 + lanes - 1, codes(1), codes(3), 3, way)
+    deal.put_both(tiles - 1, codes(2))
+
+
+def pack_near(own_ref, cot_ref, field_ref, message_ref, first_ref, second_ref):
     row, lane, column, depth = iotas()
+    deal = Deal(is_even("gx"), first_ref, second_ref, layouts()[1])
+    ring, code13, code2, tiles = x_places(3)
+    for t in range(2):
+        pack_lines(
+            deal,
+            X_LANE * t,
+            lambda i: own_ref[2 * i + t],
+            lambda i: cot_ref[2 * i + t],
+        )
+        code = jnp.where(depth == NZ - 1, field_ref[2 * OWN_PHI + t], field_ref[2 + t])
+        for way in (1, -1):
+            mix_lines(deal, code13 + t, code, field_ref[6 + t], 3, way)
+    first, second = field_ref[4], lines(field_ref[5], 4)
+    deal.put(1, code2, jnp.where(row >= 4, first, second))
+    deal.put(-1, code2, jnp.where(row < 4, first, second))
+    pack_neighbour(deal, 3, message_ref, True)
+    deal.finish()
+
+
+def pack_far(message_ref, first_ref, second_ref):
+    deal = Deal(is_even("gx"), first_ref, second_ref, layouts()[2])
+    pack_neighbour(deal, 1, message_ref, False)
+    deal.finish()
+
+
+def from_x(ref, n, way, lanes):
+    row, lane, column, depth = iotas()
+    ring, code13, code2, _ = x_places(lanes)
     first = X_LANE * n
 
     def population(i):
@@ -549,46 +584,18 @@
 
     def codes(s):
         if s == 2:
-            return lines(ref[X_CODE2 + n // 2], 4 * (n % 2))
-        value = ref[X_CODE13 + n]
+            return lines(ref[code2 + n // 2], 4 * (n % 2))
+        value = ref[code13 + n]
         return value if s == 1 else lines(value, -3 * way)
 
-    return population, cotangent, codes
-
-
-def pack_x(field_ref, first_y_ref, second_y_ref, first_ref, second_ref):
-    row, lane, column, depth = iotas()
-    y_layout, _, layout = layouts()
-    deal = Deal(is_even("gx"), first_ref, second_ref, layout, X_SIDE)
-    population, cotangent, codes = from_y(*sides(first_y_ref, second_y_ref, "gy", y_layout))
-
-    def both_codes(at, first, second):
-        second = lines(second, 4)
-        deal.put(1, at, jnp.where(row >= 4, first, second))
-        deal.put(-1, at, jnp.where(row < 4, first, second))
-
-    for n, c in ((2, 1), (3, 4)):
-        pack_lines(
-            deal,
-            X_LANE * n,
-            lambda i: population(i, c),
-            lambda i: cotangent(i, c),
-        )
-    for n in range(Q + 1):
-        value = population(n, 0) if n < Q else codes(1, 0)
-        deal.put_both(X_RING + n, value)
-    for n in range(4):
-        if n < 2:
-            first = jnp.where(depth == NZ - 1, field_ref[2 * OWN_PHI + n], field_ref[2 + n])
-            third = field_ref[6 + n]
-        else:
-            c = (1, 4)[n - 2]
-            first, third = codes(1, c), codes(3, c)
-        for way in (1, -1):
-            mix_lines(deal, X_CODE13 + n, first, third, 3, way)
-    both_codes(X_CODE2, field_ref[4], field_ref[5])
-    both_codes(X_CODE2 + 1, codes(2, 1), codes(2, 4))
-    deal.finish()
+    def outer(i):
+        value = ref[ring + (i + 1) // 2]
+        return pltpu.roll(value, LANES // 2, 1) if i and i % 2 == 0 else value
+
+    def outer_code():
+        return pltpu.roll(ref[ring], LANES // 2, 1)
+
+    return population, cotangent, codes, outer, outer_code
 
 
 def sides(first_ref, second_ref, axis, layout):
@@ -627,42 +634,42 @@
 def lay_own(c, population, cotangent, codes, code_phi, pop, cot, wide, field):
     for i in range(Q):
         pop[5 * i + c, pl.ds(2 * ROWS, ROWS), :] = population(i)
-        if c:
+        if cotangent is not None:
             cot[4 * i + c - 1, own_rows(), :] = cotangent(i)
     for n in range(2):
         wide[n, c, 1] = code_phi[n]
-    if c:
+    if cotangent is not None:
         field[0, c - 1, 0], field[1, c - 1, 0] = code_phi[1], code_phi[0]
         for s in (2, 3):
             field[s, c - 1, 0] = codes(s)
 
 
-def lay_halo(c, below, above, pop, cot):
+def lay_halo(c, below, above, pop, cot, wide, field):
     row, lane, column, depth = iotas()
+    before, behind = expand(below[2](1)), expand(above[2](1))
+    for n in range(2):
+        wide[n, c, 0], wide[n, c, 2] = before[n], behind[n]
     for i in range(Q):
         pop[5 * i + c, pl.ds(ROWS, ROWS), :] = below[0](i)
         pop[5 * i + c, pl.ds(3 * ROWS, ROWS), :] = above[0](i)
-        if c:
+        if below[1] is not None:
             put_halo(cot, 4 * i + c - 1, jnp.where(row < 4, above[1](i), below[1](i)))
-
-
-def lay_codes(c, below, above, wide, field):
-    row, lane, column, depth = iotas()
-    before, after = expand(below[2](1)), expand(above[2](1))
-    for n in range(2):
-        wide[n, c, 0], wide[n, c, 2] = before[n], after[n]
-    if c:
+    if below[1] is not None:
         for n, place in ((0, 1), (1, 0)):
-            field[place, c - 1, 1] = jnp.where(row < 4, after[n], before[n])
+            field[place, c - 1, 1] = jnp.where(row < 4, behind[n], before[n])
         for s in (2, 3):
             field[s, c - 1, 1] = jnp.where(row < 4, above[2](s), below[2](s))
 
 
+def near_tile():
+    return jnp.where(is_right(True), 4, 1)
+
+
 def lay_out(
-    first_y_ref,
-    second_y_ref,
-    first_side_ref,
-    second_side_ref,
+    near_y_ref,
+    far_y_ref,
+    first_near_ref,
+    second_near_ref,
     own_ref,
     field_ref,
     cot_ref,
@@ -671,41 +678,52 @@
     wide,
     field,
 ):
-    y_layout, side_layout, _ = layouts()
-    from_left = from_y(*sides(first_y_ref, second_y_ref, "gy", y_layout))
-    below, above = sides(first_side_ref, second_side_ref, "gx", side_layout)
-    for c in range(5):
-        t = c - 2
-        if t in (0, 1):
-            lay_own(
-                c,
-                lambda i: own_ref[2 * i + t],
-                lambda i: cot_ref[2 * i + t],
-                lambda s: field_ref[2 * s + t],
-                (field_ref[2 + t], field_ref[2 * OWN_PHI + t]),
-                pop,
-                cot,
-                wide,
-                field,
-            )
-            lay_halo(c, from_x(below, t, 1), from_x(above, t, -1), pop, cot)
-        else:
-            own = [functools.partial(lambda g, n: g(n, c), get) for get in from_left]
-            lay_own(c, *own, expand(own[2](1)), pop, cot, wide, field)
-
-
-def lay_halos(below, above, pop, cot, wide, field):
+    spaces = pop, cot, wide, field
+    below, above = sides(first_near_ref, second_near_ref, "gx", layouts()[1])
+    for t in range(2):
+        lay_own(
+            2 + t,
+            lambda i: own_ref[2 * i + t],
+            lambda i: cot_ref[2 * i + t],
+            lambda s: field_ref[2 * s + t],
+            (field_ref[2 + t], field_ref[2 * OWN_PHI + t]),
+            *spaces,
+        )
+        lay_halo(2 + t, from_x(below, t, 1, 3), from_x(above, t, -1, 3), *spaces)
+    near, far = from_y(near_y_ref, True), from_y(far_y_ref, False)
+    for c, (population, cotangent, codes, _, _) in ((near_tile(), near), (5 - near_tile(), far)):
+        lay_own(c, population, cotangent, codes, expand(codes(1)), *spaces)
+    kept = half_lanes(is_right(True))
+    lay_own(
+        0,
+        lambda i: jnp.where(kept, near[3](i), far[3](i)),
+        None,
+        None,
+        expand(jnp.where(kept, near[4](), far[4]())),
+        *spaces,
+    )
+    lay_halo(near_tile(), from_x(below, 2, 1, 3), from_x(above, 2, -1, 3), *spaces)
+
+
+def lay_far(near_refs, far_refs, spaces):
+    nears, fars = (
+        [
+            from_x(ref, lanes - 1, way, lanes)
+            for ref, way in zip(sides(*refs, "gx", layout), (1, -1))
+        ]
+        for refs, layout, lanes in zip((near_refs, far_refs), layouts()[1:], (3, 1))
+    )
+    lay_halo(5 - near_tile(), *fars, *spaces)
+    kept = half_lanes(is_right(True))
     ring = [
-        (lambda i, ref=ref: ref[X_RING + i], None, lambda s, ref=ref: ref[X_RING + Q])
-        for ref in (below, above)
+        (
+            lambda i, near=near, far=far: jnp.where(kept, near[3](i), far[3](i)),
+            None,
+            lambda s, near=near, far=far: jnp.where(kept, near[4](), far[4]()),
+        )
+        for near, far in zip(nears, fars)
     ]
-    lay_halo(0, *ring, pop, cot)
-    lay_codes(0, *ring, wide, field)
-    for n, c in enumerate((2, 3, 1, 4)):
-        halves = from_x(below, n, 1), from_x(above, n, -1)
-        if n > 1:
-            lay_halo(c, *halves, pop, cot)
-        lay_codes(c, *halves, wide, field)
+    lay_halo(0, *ring, *spaces)
 
 
 def steps_kernel(
@@ -713,15 +731,19 @@
     state_ref,
     own_field_ref,
     names_ref,
-    first_x_ref,
-    second_x_ref,
+    first_near_ref,
+    second_near_ref,
+    first_far_ref,
+    second_far_ref,
     *refs,
 ):
     adjoint_ref, panel_ref, pop_a, ring_a, wide, field, pop_b, ring_b, saved, mom, grad = refs[4:]
     size_x, size_y = sizes
-    halves = sides(first_x_ref, second_x_ref, "gx", layouts()[2])
-    below, above = (Shifted(ref, X_SIDE) for ref in halves)
-    lay_halos(below, above, pop_a, ring_a, wide, field)
+    lay_far(
+        (first_near_ref, second_near_ref),
+        (first_far_ref, second_far_ref),
+        (pop_a, ring_a, wide, field),
+    )
 
     at_x, at_y = lax.axis_index("gx"), lax.axis_index("gy")
     edges = (
@@ -905,7 +927,7 @@
     size_x, size_y = sizes
     panels = porosity.shape[0]
     devices = size_x * size_y
-    y_layout, side_layout, rest_layout = layouts()
+    y_layout, near_layout, far_layout = layouts()
 
     params = pltpu.CompilerParams(vmem_limit_bytes=32 * 1024 * 1024)
 
@@ -932,10 +954,9 @@
         pltpu.with_memory_space_constraint(value, pltpu.HBM)
         for value in (checkpoint, cotangent, cell_codes, baffle_index, porosity)
     ]
-    first_y, second_y, first_side, second_side, own, state, cot, field, names = call(
+    near_y, far_y, own, state, cot, field, names = call(
         pack_own,
         (tiles_of(y_layout.size),) * 2
-        + (tiles_of(side_layout.size), tiles_of(rest_layout.size + 8))
         + (tiles_of(2 * Q),) * 3
         + (tiles_of(2 * OWN_PHI + 2), jax.ShapeDtypeStruct((2, ROWS, LANES), jnp.int32)),
         [HBM] * 5,
@@ -949,19 +970,24 @@
         ],
         name="pack_own",
     )(*arguments)
-    second_y = swap_between(second_y, "gy", size_y)
-    first_y = swap(first_y, "gy", size_y)
-    second_side = swap_between(second_side, "gx", size_x)
-    first_side = swap(first_side, "gx", size_x)
-    first_x, second_x = call(
-        pack_x,
-        (tiles_of(rest_layout.size), tiles_of(rest_layout.size + 1)),
-        [VMEM] * 3,
-        name="pack_x",
-    )(field, first_y, second_y)
-    second_x = swap_between(second_x, "gx", size_x)
-    first_x = swap(first_x, "gx", size_x)
-
+    near_y = swap(near_y, "gy", size_y)
+    far_y = swap_between(far_y, "gy", size_y)
+    first_near, second_near = call(
+        pack_near,
+        (tiles_of(near_layout.size), tiles_of(near_layout.size + 1)),
+        [VMEM] * 4,
+        name="pack_near",
+    )(own, cot, field, near_y)
+    second_near = swap_between(second_near, "gx", size_x)
+    first_near = swap(first_near, "gx", size_x)
+    first_far, second_far = call(
+        pack_far,
+        (tiles_of(far_layout.size), tiles_of(far_layout.size + 1)),
+        [VMEM],
+        name="pack_far",
+    )(far_y)
+    second_far = swap_between(second_far, "gx", size_x)
+    first_far = swap(first_far, "gx", size_x)
     spaces = (
         shape_of(5 * Q, 5 * ROWS, LANES),
         shape_of(4 * Q, 3 * ROWS, LANES),
@@ -969,12 +995,12 @@
         shape_of(4, 4, 2, ROWS, LANES),
     )
     laid = call(lay_out, spaces, [VMEM] * 7, name="lay_out")(
-        first_y, second_y, first_side, second_side, own, field, cot
+        near_y, far_y, first_near, second_near, own, field, cot
     )
     adjoint, sums, *_ = call(
         functools.partial(steps_kernel, sizes),
         (pltpu.VMEM((Q, ROWS, 2 * LANES), jnp.float32), shape_of(devices, panels)) + spaces,
-        [VMEM] * 9,
+        [VMEM] * 11,
         [
             pltpu.VMEM((5 * Q, 5 * ROWS, LANES), jnp.float32),
             pltpu.VMEM((4 * Q, 3 * ROWS, LANES), jnp.float32),
@@ -983,8 +1009,8 @@
             pltpu.VMEM((4, ROWS, LANES), jnp.float32),
         ],
         name="steps",
-        aliases={5 + n: 2 + n for n in range(4)},
-    )(state, field, names, first_x, second_x, *laid)
+        aliases={7 + n: 2 + n for n in range(4)},
+    )(state, field, names, first_near, second_near, first_far, second_far, *laid)
     gathered = lax.all_to_all(sums, ("gx", "gy"), 0, 0, tiled=True)
     totals, adjoint = pl.pallas_call(
         finish,

time: 37.7 us -> 37.3 us (0.989)
  blocking collectives: 18 us -> 14.5 us
  starting transfers between devices: 8.33 us -> 11.2 us
  Pallas kernels: 6.48 us -> 7.17 us
  waiting for transfers between devices: 3.88 us -> 3.4 us
    all_to_all x1, blocking collectives: 18 us -> 14.5 us  [on_device(): gathered = lax.all_to_all(sums, ('gx', 'gy'), 0, 0, tiled=True)]
    ppermute x3, starting transfers between devices: 6.32 us -> 9.24 us  [swap(): lax.ppermute(value, axis, [(i, i ^ 1) for i in range(size) if i ^ 1 < size])]
    ppermute x3, waiting for transfers between devices: 3.87 us -> 3.4 us  [swap(): lax.ppermute(value, axis, [(i, i ^ 1) for i in range(size) if i ^ 1 < size])]
    pallas_call x1, Pallas kernels: 0.43 us -> 0.83 us  [on_device(): call(lay_out, spaces, [VMEM] * 7, name='lay_out')]
    pallas_call x2 -> x3, Pallas kernels: 1.51 us -> 1.77 us  [the longest x1 1.24 us: on_device(): call(pack_own, (tiles_of(y_layout.size),) * 2 + (tiles_of(2 * Q),) * 3 +...]
  transfers between devices with their start and end apart: 6 -> 6, of which waited for: 2 -> 2; matrix products, arithmetic and copies ran while one was open for 0% -> 0% of each run, Pallas kernels for 2% -> 4%
where the time goes in v19:
time: 37.3 us; the launch traced here: 37 us
  blocking collectives  14.5 us (39%)
  starting transfers between devices  11.2 us (30%)
  Pallas kernels  7.17 us (19%)
  waiting for transfers between devices  3.4 us (9%)
  between operations  0.69 us (2%)
    all_to_all x1, blocking collectives, on_device(): gathered = lax.all_to_all(sums, ('gx', 'gy'), 0, 0, tiled=True)  14.5 us
    ppermute x3, starting transfers between devices, swap(): lax.ppermute(value, axis, [(i, i ^ 1) for i in range(size) if i ^ 1 < size])  9.24 us
    pallas_call x1, Pallas kernels, on_device(): call(functools.partial(steps_kernel, sizes), (pltpu.VMEM((Q, ROWS, 2 * LA...  3.88 us
    ppermute x3, waiting for transfers between devices, swap(): lax.ppermute(value, axis, [(i, i ^ 1) for i in range(size) if i ^ 1 < size])  3.4 us
    ppermute x3, starting transfers between devices, swap_between(): return lax.ppermute(value, axis, pairs + [(j, i) for i, j in pairs])  2 us
    pallas_call x1, Pallas kernels, on_device(): call(pack_own, (tiles_of(y_layout.size),) * 2 + (tiles_of(2 * Q),) * 3 +...  1.24 us
    pallas_call x1, Pallas kernels, on_device(): call(lay_out, spaces, [VMEM] * 7, name='lay_out')  0.83 us
  transfers between devices with their start and end apart: 6, of which 2 were waited for; matrix products, arithmetic and copies ran while one was open for 0% of the time, Pallas kernels for 4%

profile of v19, /device:TPU:0, one launch (start us, length us, event | category | flops | bytes accessed | tf_op | source)
XLA Modules:
  0.0 37.0 jit_solution(6860796446222741167)
XLA Ops:
  0.6 1.2 %pack_own.1 = (f32[37,8,128]{2,1,0:T(8,128)S(1)}, f32[37,8,128]{2,1,0:T(8,128)S(1)}, f32[38,8,128]{2,1,0:T(8,128)S(1)}, f32[38,8,128]{2,1,0:T(8,128)S(1)}, f32[3...) custom-call(f32[19,8,256]{2,1,0:T(8,128)} %f_hbm.1, f32[19,8,256]{2,1,0:T(8,128)} %cot_hbm.1, ...), custom_call_target="tpu_custom_call" | custom-call | tf_op jit(solution)/shard_map/pack_own/pallas_call | solution.py:957
  1.9 3.0 %collective-permute-start = (f32[37,8,128]{2,1,0:T(8,128)S(1)}, f32[37,8,128]{2,1,0:T(8,128)S(1)}, u32[]{:S(2)}, u32[]{:S(2)}) collective-permute-start(f32[37,8,128]{2,1,0:T(8,128)S(1)} %get-tuple-element.26), channel_id=1, source_target_pairs={{0,1},{1,0},{2,3},{3,2},{4,5},{5,4},{6,7},{7,6},{8,9},{9,8},{10,11... | collective-permute-start | bytes 454664 | tf_op jit(solution)/shard_map/ppermute | solution.py:947
  4.9 0.7 %collective-permute-start.3 = (f32[37,8,128]{2,1,0:T(8,128)S(1)}, f32[37,8,128]{2,1,0:T(8,128)S(1)}, u32[]{:S(2)}, u32[]{:S(2)}) collective-permute-start(f32[37,8,128]{2,1,0:T(8,128)S(1)} %get-tuple-element.29), channel_id=1, source_target_pairs={{1,2},{2,1},{5,6},{6,5},{9,10},{10,9},{13,14},{14,13},{17,18},{18,... | collective-permute-start | bytes 454664 | tf_op jit(solution)/shard_map/ppermute | solution.py:951
  5.5 3.3 %collective-permute-done.message_ref.near_y_ref = f32[37,8,128]{2,1,0:T(8,128)S(1)} collective-permute-done((f32[37,8,128]{2,1,0:T(8,128)S(1)}, f32[37,8,128]{2,1,0:T(8,128)S(1)}, u32[]{:S(2)}, u32[]{:S(2)}) %collective-permute-start) | collective-permute-done | bytes 151584 | tf_op jit(solution)/shard_map/ppermute | solution.py:947
  8.8 0.3 pack_near.1
  9.1 0.7 %collective-permute-start.2 = (f32[66,8,128]{2,1,0:T(8,128)S(1)}, f32[66,8,128]{2,1,0:T(8,128)S(1)}, u32[]{:S(2)}, u32[]{:S(2)}) collective-permute-start(f32[66,8,128]{2,1,0:T(8,128)S(1)} %get-tuple-element.28), channel_id=1, source_target_pairs={{4,8},{12,16},{20,24},{8,4},{16,12},{24,20},{5,9},{13,17},{21,25},... | collective-permute-start | bytes 811016 | tf_op jit(solution)/shard_map/ppermute | solution.py:951
  9.8 3.2 %collective-permute-start.1 = (f32[65,8,128]{2,1,0:T(8,128)S(1)}, f32[65,8,128]{2,1,0:T(8,128)S(1)}, u32[]{:S(2)}, u32[]{:S(2)}) collective-permute-start(f32[65,8,128]{2,1,0:T(8,128)S(1)} %get-tuple-element.27), channel_id=1, source_target_pairs={{0,4},{4,0},{8,12},{12,8},{16,20},{20,16},{24,28},{28,24},{1,5},{5... | collective-permute-start | bytes 798728 | tf_op jit(solution)/shard_map/ppermute | solution.py:947
  13.0 0.0 collective-permute-done.3.message_ref.far_y_ref
  13.0 0.2 pack_far.1
  13.3 0.7 %collective-permute-start.5 = (f32[29,8,128]{2,1,0:T(8,128)S(1)}, f32[29,8,128]{2,1,0:T(8,128)S(1)}, u32[]{:S(2)}, u32[]{:S(2)}) collective-permute-start(f32[29,8,128]{2,1,0:T(8,128)S(1)} %get-tuple-element.31), channel_id=1, source_target_pairs={{4,8},{12,16},{20,24},{8,4},{16,12},{24,20},{5,9},{13,17},{21,25},... | collective-permute-start | bytes 356360 | tf_op jit(solution)/shard_map/ppermute | solution.py:951
  14.0 3.0 %collective-permute-start.4 = (f32[28,8,128]{2,1,0:T(8,128)S(1)}, f32[28,8,128]{2,1,0:T(8,128)S(1)}, u32[]{:S(2)}, u32[]{:S(2)}) collective-permute-start(f32[28,8,128]{2,1,0:T(8,128)S(1)} %get-tuple-element.30), channel_id=1, source_target_pairs={{0,4},{4,0},{8,12},{12,8},{16,20},{20,16},{24,28},{28,24},{1,5},{5... | collective-permute-start | bytes 344072 | tf_op jit(solution)/shard_map/ppermute | solution.py:947
  17.0 0.0 collective-permute-done.1.first_near_ref
  17.0 0.0 collective-permute-done.2.second_near_ref
  17.0 0.8 %lay_out.1 = (f32[95,40,128]{2,1,0:T(8,128)S(1)}, f32[76,24,128]{2,1,0:T(8,128)S(1)}, f32[2,5,3,8,128]{4,3,2,1,0:T(8,128)S(1)}, f32[4,4,2,8,128]{4,3,2,1,0:T(8,128)S(1)}) custom-call(f32[37,8,128]{2,1,0:T(8,128)S(1)} %collective-permute-done.message_ref.near_y_ref, f32[37,8,128]{2,1,0:T(8,128)S(1)} %collective-permute-done.3.message_ref.far_y_ref, ...), custom_call_target="tpu_custom_call" | custom-call | tf_op jit(solution)/shard_map/lay_out/pallas_call | solution.py:997
  17.8 0.1 collective-permute-done.4.first_far_ref
  17.9 0.0 collective-permute-done.5.second_far_ref
  17.9 3.9 %steps.1 = (f32[19,8,256]{2,1,0:T(8,128)S(1)}, f32[32,64]{1,0:T(8,128)S(1)}, f32[95,40,128]{2,1,0:T(8,128)S(1)}, f32[76,24,128]{2,1,0:T(8,128)S(1)}, f32[2,5,3,8...) custom-call(f32[38,8,128]{2,1,0:T(8,128)S(1)} %get-tuple-element.21., ...), custom_call_target="tpu_custom_call", output_to_operand_aliasing={{2}: (7, {}), {3}: (8, {}), {4}: (9, {}), {5}: (10, {})} | custom-call | tf_op jit(solution)/shard_map/steps/pallas_call | solution.py:1000
  21.8 14.5 %all_to_all.9.parts_ref = f32[32,1,64]{2,1,0:T(1,128)S(1)} all-to-all(f32[32,1,64]{2,1,0:T(1,128)S(1)} %bitcast.2), channel_id=1, replica_groups=mesh['gx'=8,'gy'=4] {'gx','gy'}, dimensions={0} | all-to-all | bytes 16384 | tf_op jit(solution)/shard_map/all_to_all | solution.py:1014
  36.3 0.7 %finish.1 = (f32[1,64]{1,0:T(1,128)}, f32[19,8,256]{2,1,0:T(8,128)}) custom-call(f32[32,1,64]{2,1,0:T(1,128)S(1)} %all_to_all.9.parts_ref, f32[19,8,256]{2,1,0:T(8,128)S(1)} %get-tuple-element.37.adjoint_ref), custom_call_target="tpu_custom_call" | custom-call | tf_op jit(solution)/shard_map/finish/pallas_call | solution.py:1015
Async XLA Ops:
  1.9 6.9 %collective-permute-start = (f32[37,8,128]{2,1,0:T(8,128)S(1)}, f32[37,8,128]{2,1,0:T(8,128)S(1)}, u32[]{:S(2)}, u32[]{:S(2)}) collective-permute-start(f32[37,8,128]{2,1,0:T(8,128)S(1)} %get-tuple-element.26), channel_id=1, source_target_pairs={{0,1},{1,0},{2,3},{3,2},{4,5},{5,4},{6,7},{7,6},{8,9},{9,8},{10,11... | collective-permute-start | bytes 454664 | tf_op jit(solution)/shard_map/ppermute | solution.py:947
  4.9 8.2 %collective-permute-start.3 = (f32[37,8,128]{2,1,0:T(8,128)S(1)}, f32[37,8,128]{2,1,0:T(8,128)S(1)}, u32[]{:S(2)}, u32[]{:S(2)}) collective-permute-start(f32[37,8,128]{2,1,0:T(8,128)S(1)} %get-tuple-element.29), channel_id=1, source_target_pairs={{1,2},{2,1},{5,6},{6,5},{9,10},{10,9},{13,14},{14,13},{17,18},{18,... | collective-permute-start | bytes 454664 | tf_op jit(solution)/shard_map/ppermute | solution.py:951
  9.1 7.9 %collective-permute-start.2 = (f32[66,8,128]{2,1,0:T(8,128)S(1)}, f32[66,8,128]{2,1,0:T(8,128)S(1)}, u32[]{:S(2)}, u32[]{:S(2)}) collective-permute-start(f32[66,8,128]{2,1,0:T(8,128)S(1)} %get-tuple-element.28), channel_id=1, source_target_pairs={{4,8},{12,16},{20,24},{8,4},{16,12},{24,20},{5,9},{13,17},{21,25},... | collective-permute-start | bytes 811016 | tf_op jit(solution)/shard_map/ppermute | solution.py:951
  9.8 7.2 %collective-permute-start.1 = (f32[65,8,128]{2,1,0:T(8,128)S(1)}, f32[65,8,128]{2,1,0:T(8,128)S(1)}, u32[]{:S(2)}, u32[]{:S(2)}) collective-permute-start(f32[65,8,128]{2,1,0:T(8,128)S(1)} %get-tuple-element.27), channel_id=1, source_target_pairs={{0,4},{4,0},{8,12},{12,8},{16,20},{20,16},{24,28},{28,24},{1,5},{5... | collective-permute-start | bytes 798728 | tf_op jit(solution)/shard_map/ppermute | solution.py:947
  13.3 4.6 %collective-permute-start.5 = (f32[29,8,128]{2,1,0:T(8,128)S(1)}, f32[29,8,128]{2,1,0:T(8,128)S(1)}, u32[]{:S(2)}, u32[]{:S(2)}) collective-permute-start(f32[29,8,128]{2,1,0:T(8,128)S(1)} %get-tuple-element.31), channel_id=1, source_target_pairs={{4,8},{12,16},{20,24},{8,4},{16,12},{24,20},{5,9},{13,17},{21,25},... | collective-permute-start | bytes 356360 | tf_op jit(solution)/shard_map/ppermute | solution.py:951
  14.0 4.0 %collective-permute-start.4 = (f32[28,8,128]{2,1,0:T(8,128)S(1)}, f32[28,8,128]{2,1,0:T(8,128)S(1)}, u32[]{:S(2)}, u32[]{:S(2)}) collective-permute-start(f32[28,8,128]{2,1,0:T(8,128)S(1)} %get-tuple-element.30), channel_id=1, source_target_pairs={{0,4},{4,0},{8,12},{12,8},{16,20},{20,16},{24,28},{28,24},{1,5},{5... | collective-permute-start | bytes 344072 | tf_op jit(solution)/shard_map/ppermute | solution.py:947

commit v20 on v19

--- a/solution.py
+++ b/solution.py
@@ -950,6 +950,14 @@
         pairs = [(i, i + 1) for i in range(1, size - 1, 2)]
         return lax.ppermute(value, axis, pairs + [(j, i) for i, j in pairs])
 
+    def swap_inner(value, start):
+        pairs = [
+            (i * size_y + y, (i + 1) * size_y + y)
+            for i in range(start, size_x - 1, 2)
+            for y in range(1, size_y - 1)
+        ]
+        return lax.ppermute(value, ("gx", "gy"), pairs + [(j, i) for i, j in pairs])
+
     arguments = [
         pltpu.with_memory_space_constraint(value, pltpu.HBM)
         for value in (checkpoint, cotangent, cell_codes, baffle_index, porosity)
@@ -986,8 +994,8 @@
         [VMEM],
         name="pack_far",
     )(far_y)
-    second_far = swap_between(second_far, "gx", size_x)
-    first_far = swap(first_far, "gx", size_x)
+    second_far = swap_inner(second_far, 1)
+    first_far = swap_inner(first_far, 0)
     spaces = (
         shape_of(5 * Q, 5 * ROWS, LANES),
         shape_of(4 * Q, 3 * ROWS, LANES),

time: 37.3 us -> 36.8 us (0.987)
  starting transfers between devices: 11.2 us -> 8.91 us
  blocking collectives: 14.5 us -> 16.4 us
    ppermute x3 -> x2, starting transfers between devices: 9.24 us -> 6.24 us  [swap(): lax.ppermute(value, axis, [(i, i ^ 1) for i in range(size) if i ^ 1 < size])]
    all_to_all x1, blocking collectives: 14.5 us -> 16.4 us  [on_device(): gathered = lax.all_to_all(sums, ('gx', 'gy'), 0, 0, tiled=True)]
    ppermute x0 -> x2, starting transfers between devices: none -> 1.34 us  [swap_inner(): return lax.ppermute(value, ('gx', 'gy'), pairs + [(j, i) for i, j in pairs])]
    ppermute x3 -> x2, starting transfers between devices: 2 us -> 1.34 us  [swap_between(): return lax.ppermute(value, axis, pairs + [(j, i) for i, j in pairs])]
    ppermute x3 -> x2, waiting for transfers between devices: 3.4 us -> 3.27 us  [swap(): lax.ppermute(value, axis, [(i, i ^ 1) for i in range(size) if i ^ 1 < size])]
  transfers between devices with their start and end apart: 6 -> 6, of which waited for: 2 -> 1; matrix products, arithmetic and copies ran while one was open for 0% -> 0% of each run, Pallas kernels for 4% -> 4%
where the time goes in v20:
time: 36.8 us; the launch traced here: 36.5 us
  blocking collectives  16.4 us (45%)
  starting transfers between devices  8.91 us (24%)
  Pallas kernels  7.18 us (20%)
  waiting for transfers between devices  3.28 us (9%)
  between operations  0.72 us (2%)
    all_to_all x1, blocking collectives, on_device(): gathered = lax.all_to_all(sums, ('gx', 'gy'), 0, 0, tiled=True)  16.4 us
    ppermute x2, starting transfers between devices, swap(): lax.ppermute(value, axis, [(i, i ^ 1) for i in range(size) if i ^ 1 < size])  6.24 us
    pallas_call x1, Pallas kernels, on_device(): call(functools.partial(steps_kernel, sizes), (pltpu.VMEM((Q, ROWS, 2 * LA...  3.89 us
    ppermute x2, waiting for transfers between devices, swap(): lax.ppermute(value, axis, [(i, i ^ 1) for i in range(size) if i ^ 1 < size])  3.27 us
    ppermute x2, starting transfers between devices, swap_inner(): return lax.ppermute(value, ('gx', 'gy'), pairs + [(j, i) for i, j in pairs])  1.34 us
    ppermute x2, starting transfers between devices, swap_between(): return lax.ppermute(value, axis, pairs + [(j, i) for i, j in pairs])  1.34 us
    pallas_call x1, Pallas kernels, on_device(): call(pack_own, (tiles_of(y_layout.size),) * 2 + (tiles_of(2 * Q),) * 3 +...  1.24 us
    pallas_call x1, Pallas kernels, on_device(): call(lay_out, spaces, [VMEM] * 7, name='lay_out')  0.83 us
  transfers between devices with their start and end apart: 6, of which 1 were waited for; matrix products, arithmetic and copies ran while one was open for 0% of the time, Pallas kernels for 4%

profile of v20, /device:TPU:0, one launch (start us, length us, event | category | flops | bytes accessed | tf_op | source)
XLA Modules:
  0.0 36.5 jit_solution(9715607606393879816)
XLA Ops:
  0.6 1.2 %pack_own.1 = (f32[37,8,128]{2,1,0:T(8,128)S(1)}, f32[37,8,128]{2,1,0:T(8,128)S(1)}, f32[38,8,128]{2,1,0:T(8,128)S(1)}, f32[38,8,128]{2,1,0:T(8,128)S(1)}, f32[3...) custom-call(f32[19,8,256]{2,1,0:T(8,128)} %f_hbm.1, f32[19,8,256]{2,1,0:T(8,128)} %cot_hbm.1, ...), custom_call_target="tpu_custom_call" | custom-call | tf_op jit(solution)/shard_map/pack_own/pallas_call | solution.py:965
  1.9 3.0 %collective-permute-start = (f32[37,8,128]{2,1,0:T(8,128)S(1)}, f32[37,8,128]{2,1,0:T(8,128)S(1)}, u32[]{:S(2)}, u32[]{:S(2)}) collective-permute-start(f32[37,8,128]{2,1,0:T(8,128)S(1)} %get-tuple-element.26), channel_id=1, source_target_pairs={{0,1},{1,0},{2,3},{3,2},{4,5},{5,4},{6,7},{7,6},{8,9},{9,8},{10,11... | collective-permute-start | bytes 454664 | tf_op jit(solution)/shard_map/ppermute | solution.py:947
  4.9 0.7 %collective-permute-start.3 = (f32[37,8,128]{2,1,0:T(8,128)S(1)}, f32[37,8,128]{2,1,0:T(8,128)S(1)}, u32[]{:S(2)}, u32[]{:S(2)}) collective-permute-start(f32[37,8,128]{2,1,0:T(8,128)S(1)} %get-tuple-element.29), channel_id=1, source_target_pairs={{1,2},{2,1},{5,6},{6,5},{9,10},{10,9},{13,14},{14,13},{17,18},{18,... | collective-permute-start | bytes 454664 | tf_op jit(solution)/shard_map/ppermute | solution.py:951
  5.5 3.3 %collective-permute-done.message_ref.near_y_ref = f32[37,8,128]{2,1,0:T(8,128)S(1)} collective-permute-done((f32[37,8,128]{2,1,0:T(8,128)S(1)}, f32[37,8,128]{2,1,0:T(8,128)S(1)}, u32[]{:S(2)}, u32[]{:S(2)}) %collective-permute-start) | collective-permute-done | bytes 151584 | tf_op jit(solution)/shard_map/ppermute | solution.py:947
  8.8 0.3 pack_near.1
  9.1 0.7 %collective-permute-start.2 = (f32[66,8,128]{2,1,0:T(8,128)S(1)}, f32[66,8,128]{2,1,0:T(8,128)S(1)}, u32[]{:S(2)}, u32[]{:S(2)}) collective-permute-start(f32[66,8,128]{2,1,0:T(8,128)S(1)} %get-tuple-element.28), channel_id=1, source_target_pairs={{4,8},{12,16},{20,24},{8,4},{16,12},{24,20},{5,9},{13,17},{21,25},... | collective-permute-start | bytes 811016 | tf_op jit(solution)/shard_map/ppermute | solution.py:951
  9.8 3.2 %collective-permute-start.1 = (f32[65,8,128]{2,1,0:T(8,128)S(1)}, f32[65,8,128]{2,1,0:T(8,128)S(1)}, u32[]{:S(2)}, u32[]{:S(2)}) collective-permute-start(f32[65,8,128]{2,1,0:T(8,128)S(1)} %get-tuple-element.27), channel_id=1, source_target_pairs={{0,4},{4,0},{8,12},{12,8},{16,20},{20,16},{24,28},{28,24},{1,5},{5... | collective-permute-start | bytes 798728 | tf_op jit(solution)/shard_map/ppermute | solution.py:947
  13.0 0.0 collective-permute-done.3.message_ref.far_y_ref
  13.0 0.2 pack_far.1
  13.3 0.7 %collective-permute-start.5 = (f32[29,8,128]{2,1,0:T(8,128)S(1)}, f32[29,8,128]{2,1,0:T(8,128)S(1)}, u32[]{:S(2)}, u32[]{:S(2)}) collective-permute-start(f32[29,8,128]{2,1,0:T(8,128)S(1)} %get-tuple-element.31), channel_id=1, source_target_pairs={{5,9},{6,10},{13,17},{14,18},{21,25},{22,26},{9,5},{10,6},{17,13},... | collective-permute-start | bytes 356360 | tf_op jit(solution)/shard_map/ppermute | solution.py:959
  14.0 0.7 %collective-permute-start.4 = (f32[28,8,128]{2,1,0:T(8,128)S(1)}, f32[28,8,128]{2,1,0:T(8,128)S(1)}, u32[]{:S(2)}, u32[]{:S(2)}) collective-permute-start(f32[28,8,128]{2,1,0:T(8,128)S(1)} %get-tuple-element.30), channel_id=1, source_target_pairs={{1,5},{2,6},{9,13},{10,14},{17,21},{18,22},{25,29},{26,30},{5,1},{... | collective-permute-start | bytes 344072 | tf_op jit(solution)/shard_map/ppermute | solution.py:959
  14.6 0.0 collective-permute-done.1.first_near_ref
  14.7 0.0 collective-permute-done.2.second_near_ref
  14.7 0.8 %lay_out.1 = (f32[95,40,128]{2,1,0:T(8,128)S(1)}, f32[76,24,128]{2,1,0:T(8,128)S(1)}, f32[2,5,3,8,128]{4,3,2,1,0:T(8,128)S(1)}, f32[4,4,2,8,128]{4,3,2,1,0:T(8,128)S(1)}) custom-call(f32[37,8,128]{2,1,0:T(8,128)S(1)} %collective-permute-done.message_ref.near_y_ref, f32[37,8,128]{2,1,0:T(8,128)S(1)} %collective-permute-done.3.message_ref.far_y_ref, ...), custom_call_target="tpu_custom_call" | custom-call | tf_op jit(solution)/shard_map/lay_out/pallas_call | solution.py:1005
  15.5 0.0 collective-permute-done.4.first_far_ref
  15.5 0.0 collective-permute-done.5.second_far_ref
  15.5 3.9 %steps.1 = (f32[19,8,256]{2,1,0:T(8,128)S(1)}, f32[32,64]{1,0:T(8,128)S(1)}, f32[95,40,128]{2,1,0:T(8,128)S(1)}, f32[76,24,128]{2,1,0:T(8,128)S(1)}, f32[2,5,3,8...) custom-call(f32[38,8,128]{2,1,0:T(8,128)S(1)} %get-tuple-element.21., ...), custom_call_target="tpu_custom_call", output_to_operand_aliasing={{2}: (7, {}), {3}: (8, {}), {4}: (9, {}), {5}: (10, {})} | custom-call | tf_op jit(solution)/shard_map/steps/pallas_call | solution.py:1008
  19.4 16.4 %all_to_all.9.parts_ref = f32[32,1,64]{2,1,0:T(1,128)S(1)} all-to-all(f32[32,1,64]{2,1,0:T(1,128)S(1)} %bitcast.2), channel_id=1, replica_groups=mesh['gx'=8,'gy'=4] {'gx','gy'}, dimensions={0} | all-to-all | bytes 16384 | tf_op jit(solution)/shard_map/all_to_all | solution.py:1022
  35.9 0.7 %finish.1 = (f32[1,64]{1,0:T(1,128)}, f32[19,8,256]{2,1,0:T(8,128)}) custom-call(f32[32,1,64]{2,1,0:T(1,128)S(1)} %all_to_all.9.parts_ref, f32[19,8,256]{2,1,0:T(8,128)S(1)} %get-tuple-element.37.adjoint_ref), custom_call_target="tpu_custom_call" | custom-call | tf_op jit(solution)/shard_map/finish/pallas_call | solution.py:1023
Async XLA Ops:
  1.9 6.9 %collective-permute-start = (f32[37,8,128]{2,1,0:T(8,128)S(1)}, f32[37,8,128]{2,1,0:T(8,128)S(1)}, u32[]{:S(2)}, u32[]{:S(2)}) collective-permute-start(f32[37,8,128]{2,1,0:T(8,128)S(1)} %get-tuple-element.26), channel_id=1, source_target_pairs={{0,1},{1,0},{2,3},{3,2},{4,5},{5,4},{6,7},{7,6},{8,9},{9,8},{10,11... | collective-permute-start | bytes 454664 | tf_op jit(solution)/shard_map/ppermute | solution.py:947
  4.9 8.2 %collective-permute-start.3 = (f32[37,8,128]{2,1,0:T(8,128)S(1)}, f32[37,8,128]{2,1,0:T(8,128)S(1)}, u32[]{:S(2)}, u32[]{:S(2)}) collective-permute-start(f32[37,8,128]{2,1,0:T(8,128)S(1)} %get-tuple-element.29), channel_id=1, source_target_pairs={{1,2},{2,1},{5,6},{6,5},{9,10},{10,9},{13,14},{14,13},{17,18},{18,... | collective-permute-start | bytes 454664 | tf_op jit(solution)/shard_map/ppermute | solution.py:951
  9.1 5.5 %collective-permute-start.2 = (f32[66,8,128]{2,1,0:T(8,128)S(1)}, f32[66,8,128]{2,1,0:T(8,128)S(1)}, u32[]{:S(2)}, u32[]{:S(2)}) collective-permute-start(f32[66,8,128]{2,1,0:T(8,128)S(1)} %get-tuple-element.28), channel_id=1, source_target_pairs={{4,8},{12,16},{20,24},{8,4},{16,12},{24,20},{5,9},{13,17},{21,25},... | collective-permute-start | bytes 811016 | tf_op jit(solution)/shard_map/ppermute | solution.py:951
  9.8 4.8 %collective-permute-start.1 = (f32[65,8,128]{2,1,0:T(8,128)S(1)}, f32[65,8,128]{2,1,0:T(8,128)S(1)}, u32[]{:S(2)}, u32[]{:S(2)}) collective-permute-start(f32[65,8,128]{2,1,0:T(8,128)S(1)} %get-tuple-element.27), channel_id=1, source_target_pairs={{0,4},{4,0},{8,12},{12,8},{16,20},{20,16},{24,28},{28,24},{1,5},{5... | collective-permute-start | bytes 798728 | tf_op jit(solution)/shard_map/ppermute | solution.py:947
  13.3 2.2 %collective-permute-start.5 = (f32[29,8,128]{2,1,0:T(8,128)S(1)}, f32[29,8,128]{2,1,0:T(8,128)S(1)}, u32[]{:S(2)}, u32[]{:S(2)}) collective-permute-start(f32[29,8,128]{2,1,0:T(8,128)S(1)} %get-tuple-element.31), channel_id=1, source_target_pairs={{5,9},{6,10},{13,17},{14,18},{21,25},{22,26},{9,5},{10,6},{17,13},... | collective-permute-start | bytes 356360 | tf_op jit(solution)/shard_map/ppermute | solution.py:959
  14.0 1.5 %collective-permute-start.4 = (f32[28,8,128]{2,1,0:T(8,128)S(1)}, f32[28,8,128]{2,1,0:T(8,128)S(1)}, u32[]{:S(2)}, u32[]{:S(2)}) collective-permute-start(f32[28,8,128]{2,1,0:T(8,128)S(1)} %get-tuple-element.30), channel_id=1, source_target_pairs={{1,5},{2,6},{9,13},{10,14},{17,21},{18,22},{25,29},{26,30},{5,1},{... | collective-permute-start | bytes 344072 | tf_op jit(solution)/shard_map/ppermute | solution.py:959

commit v21 on v20

--- a/solution.py
+++ b/solution.py
@@ -950,10 +950,10 @@
         pairs = [(i, i + 1) for i in range(1, size - 1, 2)]
         return lax.ppermute(value, axis, pairs + [(j, i) for i, j in pairs])
 
-    def swap_inner(value, start):
+    def swap_inner(value):
         pairs = [
             (i * size_y + y, (i + 1) * size_y + y)
-            for i in range(start, size_x - 1, 2)
+            for i in range(1, size_x - 1, 2)
             for y in range(1, size_y - 1)
         ]
         return lax.ppermute(value, ("gx", "gy"), pairs + [(j, i) for i, j in pairs])
@@ -994,8 +994,8 @@
         [VMEM],
         name="pack_far",
     )(far_y)
-    second_far = swap_inner(second_far, 1)
-    first_far = swap_inner(first_far, 0)
+    second_far = swap_inner(second_far)
+    first_far = swap(first_far, "gx", size_x)
     spaces = (
         shape_of(5 * Q, 5 * ROWS, LANES),
         shape_of(4 * Q, 3 * ROWS, LANES),

time: 36.8 us -> 36.8 us (level)
  starting transfers between devices: 8.91 us -> 8.33 us
  waiting for transfers between devices: 3.28 us -> 3.74 us
    ppermute x2 -> x1, starting transfers between devices: 1.34 us -> 0.67 us  [swap_inner(): return lax.ppermute(value, ('gx', 'gy'), pairs + [(j, i) for i, j in pairs])]
    ppermute x2 -> x3, waiting for transfers between devices: 3.27 us -> 3.74 us  [swap(): lax.ppermute(value, axis, [(i, i ^ 1) for i in range(size) if i ^ 1 < size])]
    ppermute x2 -> x3, starting transfers between devices: 6.24 us -> 6.33 us  [swap(): lax.ppermute(value, axis, [(i, i ^ 1) for i in range(size) if i ^ 1 < size])]
  transfers between devices with their start and end apart: 6 -> 6, of which waited for: 1 -> 3; matrix products, arithmetic and copies ran while one was open for 0% -> 0% of each run, Pallas kernels for 4% -> 4%
where the time goes in v21:
time: 36.8 us; the launch traced here: 36.5 us
  blocking collectives  16.6 us (45%)
  starting transfers between devices  8.33 us (23%)
  Pallas kernels  7.17 us (19%)
  waiting for transfers between devices  3.74 us (10%)
  between operations  0.69 us (2%)
    all_to_all x1, blocking collectives, on_device(): gathered = lax.all_to_all(sums, ('gx', 'gy'), 0, 0, tiled=True)  16.6 us
    ppermute x3, starting transfers between devices, swap(): lax.ppermute(value, axis, [(i, i ^ 1) for i in range(size) if i ^ 1 < size])  6.33 us
    pallas_call x1, Pallas kernels, on_device(): call(functools.partial(steps_kernel, sizes), (pltpu.VMEM((Q, ROWS, 2 * LA...  3.88 us
    ppermute x3, waiting for transfers between devices, swap(): lax.ppermute(value, axis, [(i, i ^ 1) for i in range(size) if i ^ 1 < size])  3.74 us
    ppermute x2, starting transfers between devices, swap_between(): return lax.ppermute(value, axis, pairs + [(j, i) for i, j in pairs])  1.34 us
    pallas_call x1, Pallas kernels, on_device(): call(pack_own, (tiles_of(y_layout.size),) * 2 + (tiles_of(2 * Q),) * 3 +...  1.24 us
    pallas_call x1, Pallas kernels, on_device(): call(lay_out, spaces, [VMEM] * 7, name='lay_out')  0.83 us
  transfers between devices with their start and end apart: 6, of which 3 were waited for; matrix products, arithmetic and copies ran while one was open for 0% of the time, Pallas kernels for 4%

profile of v21, /device:TPU:0, one launch (start us, length us, event | category | flops | bytes accessed | tf_op | source)
XLA Modules:
  0.0 36.5 jit_solution(9521280787538020107)
XLA Ops:
  0.6 1.2 %pack_own.1 = (f32[37,8,128]{2,1,0:T(8,128)S(1)}, f32[37,8,128]{2,1,0:T(8,128)S(1)}, f32[38,8,128]{2,1,0:T(8,128)S(1)}, f32[38,8,128]{2,1,0:T(8,128)S(1)}, f32[3...) custom-call(f32[19,8,256]{2,1,0:T(8,128)} %f_hbm.1, f32[19,8,256]{2,1,0:T(8,128)} %cot_hbm.1, ...), custom_call_target="tpu_custom_call" | custom-call | tf_op jit(solution)/shard_map/pack_own/pallas_call | solution.py:965
  1.9 3.0 %collective-permute-start = (f32[37,8,128]{2,1,0:T(8,128)S(1)}, f32[37,8,128]{2,1,0:T(8,128)S(1)}, u32[]{:S(2)}, u32[]{:S(2)}) collective-permute-start(f32[37,8,128]{2,1,0:T(8,128)S(1)} %get-tuple-element.26), channel_id=1, source_target_pairs={{0,1},{1,0},{2,3},{3,2},{4,5},{5,4},{6,7},{7,6},{8,9},{9,8},{10,11... | collective-permute-start | bytes 454664 | tf_op jit(solution)/shard_map/ppermute | solution.py:947
  4.9 0.7 %collective-permute-start.3 = (f32[37,8,128]{2,1,0:T(8,128)S(1)}, f32[37,8,128]{2,1,0:T(8,128)S(1)}, u32[]{:S(2)}, u32[]{:S(2)}) collective-permute-start(f32[37,8,128]{2,1,0:T(8,128)S(1)} %get-tuple-element.29), channel_id=1, source_target_pairs={{1,2},{2,1},{5,6},{6,5},{9,10},{10,9},{13,14},{14,13},{17,18},{18,... | collective-permute-start | bytes 454664 | tf_op jit(solution)/shard_map/ppermute | solution.py:951
  5.5 3.3 %collective-permute-done.message_ref.near_y_ref = f32[37,8,128]{2,1,0:T(8,128)S(1)} collective-permute-done((f32[37,8,128]{2,1,0:T(8,128)S(1)}, f32[37,8,128]{2,1,0:T(8,128)S(1)}, u32[]{:S(2)}, u32[]{:S(2)}) %collective-permute-start) | collective-permute-done | bytes 151584 | tf_op jit(solution)/shard_map/ppermute | solution.py:947
  8.8 0.3 pack_near.1
  9.1 0.7 %collective-permute-start.2 = (f32[66,8,128]{2,1,0:T(8,128)S(1)}, f32[66,8,128]{2,1,0:T(8,128)S(1)}, u32[]{:S(2)}, u32[]{:S(2)}) collective-permute-start(f32[66,8,128]{2,1,0:T(8,128)S(1)} %get-tuple-element.28), channel_id=1, source_target_pairs={{4,8},{12,16},{20,24},{8,4},{16,12},{24,20},{5,9},{13,17},{21,25},... | collective-permute-start | bytes 811016 | tf_op jit(solution)/shard_map/ppermute | solution.py:951
  9.8 3.2 %collective-permute-start.1 = (f32[65,8,128]{2,1,0:T(8,128)S(1)}, f32[65,8,128]{2,1,0:T(8,128)S(1)}, u32[]{:S(2)}, u32[]{:S(2)}) collective-permute-start(f32[65,8,128]{2,1,0:T(8,128)S(1)} %get-tuple-element.27), channel_id=1, source_target_pairs={{0,4},{4,0},{8,12},{12,8},{16,20},{20,16},{24,28},{28,24},{1,5},{5... | collective-permute-start | bytes 798728 | tf_op jit(solution)/shard_map/ppermute | solution.py:947
  13.0 0.0 collective-permute-done.3.message_ref.far_y_ref
  13.0 0.2 pack_far.1
  13.3 0.7 %collective-permute-start.5 = (f32[29,8,128]{2,1,0:T(8,128)S(1)}, f32[29,8,128]{2,1,0:T(8,128)S(1)}, u32[]{:S(2)}, u32[]{:S(2)}) collective-permute-start(f32[29,8,128]{2,1,0:T(8,128)S(1)} %get-tuple-element.31), channel_id=1, source_target_pairs={{5,9},{6,10},{13,17},{14,18},{21,25},{22,26},{9,5},{10,6},{17,13},... | collective-permute-start | bytes 356360 | tf_op jit(solution)/shard_map/ppermute | solution.py:959
  14.0 0.1 collective-permute-start.4
  14.1 0.1 collective-permute-done.1.first_near_ref
  14.2 0.0 collective-permute-done.2.second_near_ref
  14.2 0.8 %lay_out.1 = (f32[95,40,128]{2,1,0:T(8,128)S(1)}, f32[76,24,128]{2,1,0:T(8,128)S(1)}, f32[2,5,3,8,128]{4,3,2,1,0:T(8,128)S(1)}, f32[4,4,2,8,128]{4,3,2,1,0:T(8,128)S(1)}) custom-call(f32[37,8,128]{2,1,0:T(8,128)S(1)} %collective-permute-done.message_ref.near_y_ref, f32[37,8,128]{2,1,0:T(8,128)S(1)} %collective-permute-done.3.message_ref.far_y_ref, ...), custom_call_target="tpu_custom_call" | custom-call | tf_op jit(solution)/shard_map/lay_out/pallas_call | solution.py:1005
  15.0 0.3 collective-permute-done.4.first_far_ref
  15.4 0.0 collective-permute-done.5.second_far_ref
  15.4 3.9 %steps.1 = (f32[19,8,256]{2,1,0:T(8,128)S(1)}, f32[32,64]{1,0:T(8,128)S(1)}, f32[95,40,128]{2,1,0:T(8,128)S(1)}, f32[76,24,128]{2,1,0:T(8,128)S(1)}, f32[2,5,3,8...) custom-call(f32[38,8,128]{2,1,0:T(8,128)S(1)} %get-tuple-element.21., ...), custom_call_target="tpu_custom_call", output_to_operand_aliasing={{2}: (7, {}), {3}: (8, {}), {4}: (9, {}), {5}: (10, {})} | custom-call | tf_op jit(solution)/shard_map/steps/pallas_call | solution.py:1008
  19.2 16.6 %all_to_all.9.parts_ref = f32[32,1,64]{2,1,0:T(1,128)S(1)} all-to-all(f32[32,1,64]{2,1,0:T(1,128)S(1)} %bitcast.2), channel_id=1, replica_groups=mesh['gx'=8,'gy'=4] {'gx','gy'}, dimensions={0} | all-to-all | bytes 16384 | tf_op jit(solution)/shard_map/all_to_all | solution.py:1022
  35.9 0.7 %finish.1 = (f32[1,64]{1,0:T(1,128)}, f32[19,8,256]{2,1,0:T(8,128)}) custom-call(f32[32,1,64]{2,1,0:T(1,128)S(1)} %all_to_all.9.parts_ref, f32[19,8,256]{2,1,0:T(8,128)S(1)} %get-tuple-element.37.adjoint_ref), custom_call_target="tpu_custom_call" | custom-call | tf_op jit(solution)/shard_map/finish/pallas_call | solution.py:1023
Async XLA Ops:
  1.9 6.9 %collective-permute-start = (f32[37,8,128]{2,1,0:T(8,128)S(1)}, f32[37,8,128]{2,1,0:T(8,128)S(1)}, u32[]{:S(2)}, u32[]{:S(2)}) collective-permute-start(f32[37,8,128]{2,1,0:T(8,128)S(1)} %get-tuple-element.26), channel_id=1, source_target_pairs={{0,1},{1,0},{2,3},{3,2},{4,5},{5,4},{6,7},{7,6},{8,9},{9,8},{10,11... | collective-permute-start | bytes 454664 | tf_op jit(solution)/shard_map/ppermute | solution.py:947
  4.9 8.2 %collective-permute-start.3 = (f32[37,8,128]{2,1,0:T(8,128)S(1)}, f32[37,8,128]{2,1,0:T(8,128)S(1)}, u32[]{:S(2)}, u32[]{:S(2)}) collective-permute-start(f32[37,8,128]{2,1,0:T(8,128)S(1)} %get-tuple-element.29), channel_id=1, source_target_pairs={{1,2},{2,1},{5,6},{6,5},{9,10},{10,9},{13,14},{14,13},{17,18},{18,... | collective-permute-start | bytes 454664 | tf_op jit(solution)/shard_map/ppermute | solution.py:951
  9.1 5.1 %collective-permute-start.2 = (f32[66,8,128]{2,1,0:T(8,128)S(1)}, f32[66,8,128]{2,1,0:T(8,128)S(1)}, u32[]{:S(2)}, u32[]{:S(2)}) collective-permute-start(f32[66,8,128]{2,1,0:T(8,128)S(1)} %get-tuple-element.28), channel_id=1, source_target_pairs={{4,8},{12,16},{20,24},{8,4},{16,12},{24,20},{5,9},{13,17},{21,25},... | collective-permute-start | bytes 811016 | tf_op jit(solution)/shard_map/ppermute | solution.py:951
  9.8 4.4 %collective-permute-start.1 = (f32[65,8,128]{2,1,0:T(8,128)S(1)}, f32[65,8,128]{2,1,0:T(8,128)S(1)}, u32[]{:S(2)}, u32[]{:S(2)}) collective-permute-start(f32[65,8,128]{2,1,0:T(8,128)S(1)} %get-tuple-element.27), channel_id=1, source_target_pairs={{0,4},{4,0},{8,12},{12,8},{16,20},{20,16},{24,28},{28,24},{1,5},{5... | collective-permute-start | bytes 798728 | tf_op jit(solution)/shard_map/ppermute | solution.py:947
  13.3 2.1 %collective-permute-start.5 = (f32[29,8,128]{2,1,0:T(8,128)S(1)}, f32[29,8,128]{2,1,0:T(8,128)S(1)}, u32[]{:S(2)}, u32[]{:S(2)}) collective-permute-start(f32[29,8,128]{2,1,0:T(8,128)S(1)} %get-tuple-element.31), channel_id=1, source_target_pairs={{5,9},{6,10},{13,17},{14,18},{21,25},{22,26},{9,5},{10,6},{17,13},... | collective-permute-start | bytes 356360 | tf_op jit(solution)/shard_map/ppermute | solution.py:959
  14.0 1.4 %collective-permute-start.4 = (f32[28,8,128]{2,1,0:T(8,128)S(1)}, f32[28,8,128]{2,1,0:T(8,128)S(1)}, u32[]{:S(2)}, u32[]{:S(2)}) collective-permute-start(f32[28,8,128]{2,1,0:T(8,128)S(1)} %get-tuple-element.30), channel_id=1, source_target_pairs={{0,4},{4,0},{8,12},{12,8},{16,20},{20,16},{24,28},{28,24},{1,5},{5... | collective-permute-start | bytes 344072 | tf_op jit(solution)/shard_map/ppermute | solution.py:947

commit v22 on v21

--- a/solution.py
+++ b/solution.py
@@ -832,7 +832,7 @@
             put_ring(ring_b, 4 * i + tile, out[0][i], out[1][i])
         return carry
 
-    lax.fori_loop(0, 4, second_step, 0)
+    lax.fori_loop(0, 4, second_step, 0, unroll=2)
 
     def third_step(tile, carry):
         for r in range(2):
@@ -843,7 +843,7 @@
                     saved[2, i, tile] = f[i]
         return carry
 
-    lax.fori_loop(0, 4, third_step, 0)
+    lax.fori_loop(0, 4, third_step, 0, unroll=2)
 
     def back_tile(load, s, tile, r, own):
         b = stream_tile(load, -1, masks_of(4 if tile is None else tile, 1, r), lane)
@@ -865,7 +865,7 @@
             put_ring(ring_b, 4 * i + tile, out[0][i], out[1][i])
         return carry
 
-    lax.fori_loop(0, 4, last_step, 0)
+    lax.fori_loop(0, 4, last_step, 0, unroll=2)
 
     for k, tile in enumerate((1, 2, None)):
         out = []

time: 36.8 us -> 36.4 us (0.989)
  Pallas kernels: 7.17 us -> 6.72 us
    pallas_call x1, Pallas kernels: 3.88 us -> 3.43 us  [on_device(): call(functools.partial(steps_kernel, sizes), (pltpu.VMEM((Q, ROWS, 2 * LA...]
where the time goes in v22:
time: 36.4 us; the launch traced here: 36.1 us
  blocking collectives  16.6 us (46%)
  starting transfers between devices  8.33 us (23%)
  Pallas kernels  6.72 us (18%)
  waiting for transfers between devices  3.74 us (10%)
  between operations  0.69 us (2%)
    all_to_all x1, blocking collectives, on_device(): gathered = lax.all_to_all(sums, ('gx', 'gy'), 0, 0, tiled=True)  16.6 us
    ppermute x3, starting transfers between devices, swap(): lax.ppermute(value, axis, [(i, i ^ 1) for i in range(size) if i ^ 1 < size])  6.33 us
    ppermute x3, waiting for transfers between devices, swap(): lax.ppermute(value, axis, [(i, i ^ 1) for i in range(size) if i ^ 1 < size])  3.74 us
    pallas_call x1, Pallas kernels, on_device(): call(functools.partial(steps_kernel, sizes), (pltpu.VMEM((Q, ROWS, 2 * LA...  3.43 us
    ppermute x2, starting transfers between devices, swap_between(): return lax.ppermute(value, axis, pairs + [(j, i) for i, j in pairs])  1.34 us
    pallas_call x1, Pallas kernels, on_device(): call(pack_own, (tiles_of(y_layout.size),) * 2 + (tiles_of(2 * Q),) * 3 +...  1.24 us
    pallas_call x1, Pallas kernels, on_device(): call(lay_out, spaces, [VMEM] * 7, name='lay_out')  0.83 us
  transfers between devices with their start and end apart: 6, of which 3 were waited for; matrix products, arithmetic and copies ran while one was open for 0% of the time, Pallas kernels for 4%

profile of v22, /device:TPU:0, one launch (start us, length us, event | category | flops | bytes accessed | tf_op | source)
XLA Modules:
  0.0 36.1 jit_solution(5895618761510577748)
XLA Ops:
  0.6 1.2 %pack_own.1 = (f32[37,8,128]{2,1,0:T(8,128)S(1)}, f32[37,8,128]{2,1,0:T(8,128)S(1)}, f32[38,8,128]{2,1,0:T(8,128)S(1)}, f32[38,8,128]{2,1,0:T(8,128)S(1)}, f32[3...) custom-call(f32[19,8,256]{2,1,0:T(8,128)} %f_hbm.1, f32[19,8,256]{2,1,0:T(8,128)} %cot_hbm.1, ...), custom_call_target="tpu_custom_call" | custom-call | tf_op jit(solution)/shard_map/pack_own/pallas_call | solution.py:965
  1.9 3.0 %collective-permute-start = (f32[37,8,128]{2,1,0:T(8,128)S(1)}, f32[37,8,128]{2,1,0:T(8,128)S(1)}, u32[]{:S(2)}, u32[]{:S(2)}) collective-permute-start(f32[37,8,128]{2,1,0:T(8,128)S(1)} %get-tuple-element.26), channel_id=1, source_target_pairs={{0,1},{1,0},{2,3},{3,2},{4,5},{5,4},{6,7},{7,6},{8,9},{9,8},{10,11... | collective-permute-start | bytes 454664 | tf_op jit(solution)/shard_map/ppermute | solution.py:947
  4.9 0.7 %collective-permute-start.3 = (f32[37,8,128]{2,1,0:T(8,128)S(1)}, f32[37,8,128]{2,1,0:T(8,128)S(1)}, u32[]{:S(2)}, u32[]{:S(2)}) collective-permute-start(f32[37,8,128]{2,1,0:T(8,128)S(1)} %get-tuple-element.29), channel_id=1, source_target_pairs={{1,2},{2,1},{5,6},{6,5},{9,10},{10,9},{13,14},{14,13},{17,18},{18,... | collective-permute-start | bytes 454664 | tf_op jit(solution)/shard_map/ppermute | solution.py:951
  5.5 3.3 %collective-permute-done.message_ref.near_y_ref = f32[37,8,128]{2,1,0:T(8,128)S(1)} collective-permute-done((f32[37,8,128]{2,1,0:T(8,128)S(1)}, f32[37,8,128]{2,1,0:T(8,128)S(1)}, u32[]{:S(2)}, u32[]{:S(2)}) %collective-permute-start) | collective-permute-done | bytes 151584 | tf_op jit(solution)/shard_map/ppermute | solution.py:947
  8.8 0.3 pack_near.1
  9.1 0.7 %collective-permute-start.2 = (f32[66,8,128]{2,1,0:T(8,128)S(1)}, f32[66,8,128]{2,1,0:T(8,128)S(1)}, u32[]{:S(2)}, u32[]{:S(2)}) collective-permute-start(f32[66,8,128]{2,1,0:T(8,128)S(1)} %get-tuple-element.28), channel_id=1, source_target_pairs={{4,8},{12,16},{20,24},{8,4},{16,12},{24,20},{5,9},{13,17},{21,25},... | collective-permute-start | bytes 811016 | tf_op jit(solution)/shard_map/ppermute | solution.py:951
  9.8 3.2 %collective-permute-start.1 = (f32[65,8,128]{2,1,0:T(8,128)S(1)}, f32[65,8,128]{2,1,0:T(8,128)S(1)}, u32[]{:S(2)}, u32[]{:S(2)}) collective-permute-start(f32[65,8,128]{2,1,0:T(8,128)S(1)} %get-tuple-element.27), channel_id=1, source_target_pairs={{0,4},{4,0},{8,12},{12,8},{16,20},{20,16},{24,28},{28,24},{1,5},{5... | collective-permute-start | bytes 798728 | tf_op jit(solution)/shard_map/ppermute | solution.py:947
  13.0 0.0 collective-permute-done.3.message_ref.far_y_ref
  13.0 0.2 pack_far.1
  13.3 0.7 %collective-permute-start.5 = (f32[29,8,128]{2,1,0:T(8,128)S(1)}, f32[29,8,128]{2,1,0:T(8,128)S(1)}, u32[]{:S(2)}, u32[]{:S(2)}) collective-permute-start(f32[29,8,128]{2,1,0:T(8,128)S(1)} %get-tuple-element.31), channel_id=1, source_target_pairs={{5,9},{6,10},{13,17},{14,18},{21,25},{22,26},{9,5},{10,6},{17,13},... | collective-permute-start | bytes 356360 | tf_op jit(solution)/shard_map/ppermute | solution.py:959
  14.0 0.1 collective-permute-start.4
  14.1 0.1 collective-permute-done.1.first_near_ref
  14.2 0.0 collective-permute-done.2.second_near_ref
  14.2 0.8 %lay_out.1 = (f32[95,40,128]{2,1,0:T(8,128)S(1)}, f32[76,24,128]{2,1,0:T(8,128)S(1)}, f32[2,5,3,8,128]{4,3,2,1,0:T(8,128)S(1)}, f32[4,4,2,8,128]{4,3,2,1,0:T(8,128)S(1)}) custom-call(f32[37,8,128]{2,1,0:T(8,128)S(1)} %collective-permute-done.message_ref.near_y_ref, f32[37,8,128]{2,1,0:T(8,128)S(1)} %collective-permute-done.3.message_ref.far_y_ref, ...), custom_call_target="tpu_custom_call" | custom-call | tf_op jit(solution)/shard_map/lay_out/pallas_call | solution.py:1005
  15.0 0.3 collective-permute-done.4.first_far_ref
  15.4 0.0 collective-permute-done.5.second_far_ref
  15.4 3.4 %steps.1 = (f32[19,8,256]{2,1,0:T(8,128)S(1)}, f32[32,64]{1,0:T(8,128)S(1)}, f32[95,40,128]{2,1,0:T(8,128)S(1)}, f32[76,24,128]{2,1,0:T(8,128)S(1)}, f32[2,5,3,8...) custom-call(f32[38,8,128]{2,1,0:T(8,128)S(1)} %get-tuple-element.21., ...), custom_call_target="tpu_custom_call", output_to_operand_aliasing={{2}: (7, {}), {3}: (8, {}), {4}: (9, {}), {5}: (10, {})} | custom-call | tf_op jit(solution)/shard_map/steps/pallas_call | solution.py:1008
  18.8 16.6 %all_to_all.9.parts_ref = f32[32,1,64]{2,1,0:T(1,128)S(1)} all-to-all(f32[32,1,64]{2,1,0:T(1,128)S(1)} %bitcast.2), channel_id=1, replica_groups=mesh['gx'=8,'gy'=4] {'gx','gy'}, dimensions={0} | all-to-all | bytes 16384 | tf_op jit(solution)/shard_map/all_to_all | solution.py:1022
  35.4 0.7 %finish.1 = (f32[1,64]{1,0:T(1,128)}, f32[19,8,256]{2,1,0:T(8,128)}) custom-call(f32[32,1,64]{2,1,0:T(1,128)S(1)} %all_to_all.9.parts_ref, f32[19,8,256]{2,1,0:T(8,128)S(1)} %get-tuple-element.37.adjoint_ref), custom_call_target="tpu_custom_call" | custom-call | tf_op jit(solution)/shard_map/finish/pallas_call | solution.py:1023
Async XLA Ops:
  1.9 6.9 %collective-permute-start = (f32[37,8,128]{2,1,0:T(8,128)S(1)}, f32[37,8,128]{2,1,0:T(8,128)S(1)}, u32[]{:S(2)}, u32[]{:S(2)}) collective-permute-start(f32[37,8,128]{2,1,0:T(8,128)S(1)} %get-tuple-element.26), channel_id=1, source_target_pairs={{0,1},{1,0},{2,3},{3,2},{4,5},{5,4},{6,7},{7,6},{8,9},{9,8},{10,11... | collective-permute-start | bytes 454664 | tf_op jit(solution)/shard_map/ppermute | solution.py:947
  4.9 8.2 %collective-permute-start.3 = (f32[37,8,128]{2,1,0:T(8,128)S(1)}, f32[37,8,128]{2,1,0:T(8,128)S(1)}, u32[]{:S(2)}, u32[]{:S(2)}) collective-permute-start(f32[37,8,128]{2,1,0:T(8,128)S(1)} %get-tuple-element.29), channel_id=1, source_target_pairs={{1,2},{2,1},{5,6},{6,5},{9,10},{10,9},{13,14},{14,13},{17,18},{18,... | collective-permute-start | bytes 454664 | tf_op jit(solution)/shard_map/ppermute | solution.py:951
  9.1 5.1 %collective-permute-start.2 = (f32[66,8,128]{2,1,0:T(8,128)S(1)}, f32[66,8,128]{2,1,0:T(8,128)S(1)}, u32[]{:S(2)}, u32[]{:S(2)}) collective-permute-start(f32[66,8,128]{2,1,0:T(8,128)S(1)} %get-tuple-element.28), channel_id=1, source_target_pairs={{4,8},{12,16},{20,24},{8,4},{16,12},{24,20},{5,9},{13,17},{21,25},... | collective-permute-start | bytes 811016 | tf_op jit(solution)/shard_map/ppermute | solution.py:951
  9.8 4.4 %collective-permute-start.1 = (f32[65,8,128]{2,1,0:T(8,128)S(1)}, f32[65,8,128]{2,1,0:T(8,128)S(1)}, u32[]{:S(2)}, u32[]{:S(2)}) collective-permute-start(f32[65,8,128]{2,1,0:T(8,128)S(1)} %get-tuple-element.27), channel_id=1, source_target_pairs={{0,4},{4,0},{8,12},{12,8},{16,20},{20,16},{24,28},{28,24},{1,5},{5... | collective-permute-start | bytes 798728 | tf_op jit(solution)/shard_map/ppermute | solution.py:947
  13.3 2.1 %collective-permute-start.5 = (f32[29,8,128]{2,1,0:T(8,128)S(1)}, f32[29,8,128]{2,1,0:T(8,128)S(1)}, u32[]{:S(2)}, u32[]{:S(2)}) collective-permute-start(f32[29,8,128]{2,1,0:T(8,128)S(1)} %get-tuple-element.31), channel_id=1, source_target_pairs={{5,9},{6,10},{13,17},{14,18},{21,25},{22,26},{9,5},{10,6},{17,13},... | collective-permute-start | bytes 356360 | tf_op jit(solution)/shard_map/ppermute | solution.py:959
  14.0 1.4 %collective-permute-start.4 = (f32[28,8,128]{2,1,0:T(8,128)S(1)}, f32[28,8,128]{2,1,0:T(8,128)S(1)}, u32[]{:S(2)}, u32[]{:S(2)}) collective-permute-start(f32[28,8,128]{2,1,0:T(8,128)S(1)} %get-tuple-element.30), channel_id=1, source_target_pairs={{0,4},{4,0},{8,12},{12,8},{16,20},{20,16},{24,28},{28,24},{1,5},{5... | collective-permute-start | bytes 344072 | tf_op jit(solution)/shard_map/ppermute | solution.py:947

commit v23 on v22

--- a/solution.py
+++ b/solution.py
@@ -816,7 +816,7 @@
             mom[0, n, place, 1] = jnp.where(after, halo[1][n], halo[0][n])
         return carry
 
-    lax.fori_loop(0, 5, first_step, 0)
+    lax.fori_loop(0, 5, first_step, 0, unroll=True)
 
     def second_step(tile, carry):
         out = []
@@ -832,7 +832,7 @@
             put_ring(ring_b, 4 * i + tile, out[0][i], out[1][i])
         return carry
 
-    lax.fori_loop(0, 4, second_step, 0, unroll=2)
+    lax.fori_loop(0, 4, second_step, 0, unroll=True)
 
     def third_step(tile, carry):
         for r in range(2):
@@ -843,7 +843,7 @@
                     saved[2, i, tile] = f[i]
         return carry
 
-    lax.fori_loop(0, 4, third_step, 0, unroll=2)
+    lax.fori_loop(0, 4, third_step, 0, unroll=True)
 
     def back_tile(load, s, tile, r, own):
         b = stream_tile(load, -1, masks_of(4 if tile is None else tile, 1, r), lane)
@@ -865,7 +865,7 @@
             put_ring(ring_b, 4 * i + tile, out[0][i], out[1][i])
         return carry
 
-    lax.fori_loop(0, 4, last_step, 0, unroll=2)
+    lax.fori_loop(0, 4, last_step, 0, unroll=True)
 
     for k, tile in enumerate((1, 2, None)):
         out = []

time: 36.4 us -> 35.3 us (0.970)
  Pallas kernels: 6.72 us -> 5.66 us
    pallas_call x1, Pallas kernels: 3.43 us -> 2.37 us  [on_device(): call(functools.partial(steps_kernel, sizes), (pltpu.VMEM((Q, ROWS, 2 * LA...]
where the time goes in v23:
time: 35.3 us; the launch traced here: 35 us
  blocking collectives  16.6 us (47%)
  starting transfers between devices  8.33 us (24%)
  Pallas kernels  5.66 us (16%)
  waiting for transfers between devices  3.74 us (11%)
  between operations  0.69 us (2%)
    all_to_all x1, blocking collectives, on_device(): gathered = lax.all_to_all(sums, ('gx', 'gy'), 0, 0, tiled=True)  16.6 us
    ppermute x3, starting transfers between devices, swap(): lax.ppermute(value, axis, [(i, i ^ 1) for i in range(size) if i ^ 1 < size])  6.33 us
    ppermute x3, waiting for transfers between devices, swap(): lax.ppermute(value, axis, [(i, i ^ 1) for i in range(size) if i ^ 1 < size])  3.74 us
    pallas_call x1, Pallas kernels, on_device(): call(functools.partial(steps_kernel, sizes), (pltpu.VMEM((Q, ROWS, 2 * LA...  2.37 us
    ppermute x2, starting transfers between devices, swap_between(): return lax.ppermute(value, axis, pairs + [(j, i) for i, j in pairs])  1.34 us
    pallas_call x1, Pallas kernels, on_device(): call(pack_own, (tiles_of(y_layout.size),) * 2 + (tiles_of(2 * Q),) * 3 +...  1.24 us
    pallas_call x1, Pallas kernels, on_device(): call(lay_out, spaces, [VMEM] * 7, name='lay_out')  0.83 us
  transfers between devices with their start and end apart: 6, of which 3 were waited for; matrix products, arithmetic and copies ran while one was open for 0% of the time, Pallas kernels for 4%

profile of v23, /device:TPU:0, one launch (start us, length us, event | category | flops | bytes accessed | tf_op | source)
XLA Modules:
  0.0 35.0 jit_solution(14061298558558752640)
XLA Ops:
  0.6 1.2 %pack_own.1 = (f32[37,8,128]{2,1,0:T(8,128)S(1)}, f32[37,8,128]{2,1,0:T(8,128)S(1)}, f32[38,8,128]{2,1,0:T(8,128)S(1)}, f32[38,8,128]{2,1,0:T(8,128)S(1)}, f32[3...) custom-call(f32[19,8,256]{2,1,0:T(8,128)} %f_hbm.1, f32[19,8,256]{2,1,0:T(8,128)} %cot_hbm.1, ...), custom_call_target="tpu_custom_call" | custom-call | tf_op jit(solution)/shard_map/pack_own/pallas_call | solution.py:965
  1.9 3.0 %collective-permute-start = (f32[37,8,128]{2,1,0:T(8,128)S(1)}, f32[37,8,128]{2,1,0:T(8,128)S(1)}, u32[]{:S(2)}, u32[]{:S(2)}) collective-permute-start(f32[37,8,128]{2,1,0:T(8,128)S(1)} %get-tuple-element.26), channel_id=1, source_target_pairs={{0,1},{1,0},{2,3},{3,2},{4,5},{5,4},{6,7},{7,6},{8,9},{9,8},{10,11... | collective-permute-start | bytes 454664 | tf_op jit(solution)/shard_map/ppermute | solution.py:947
  4.9 0.7 %collective-permute-start.3 = (f32[37,8,128]{2,1,0:T(8,128)S(1)}, f32[37,8,128]{2,1,0:T(8,128)S(1)}, u32[]{:S(2)}, u32[]{:S(2)}) collective-permute-start(f32[37,8,128]{2,1,0:T(8,128)S(1)} %get-tuple-element.29), channel_id=1, source_target_pairs={{1,2},{2,1},{5,6},{6,5},{9,10},{10,9},{13,14},{14,13},{17,18},{18,... | collective-permute-start | bytes 454664 | tf_op jit(solution)/shard_map/ppermute | solution.py:951
  5.5 3.3 %collective-permute-done.message_ref.near_y_ref = f32[37,8,128]{2,1,0:T(8,128)S(1)} collective-permute-done((f32[37,8,128]{2,1,0:T(8,128)S(1)}, f32[37,8,128]{2,1,0:T(8,128)S(1)}, u32[]{:S(2)}, u32[]{:S(2)}) %collective-permute-start) | collective-permute-done | bytes 151584 | tf_op jit(solution)/shard_map/ppermute | solution.py:947
  8.8 0.3 pack_near.1
  9.1 0.7 %collective-permute-start.2 = (f32[66,8,128]{2,1,0:T(8,128)S(1)}, f32[66,8,128]{2,1,0:T(8,128)S(1)}, u32[]{:S(2)}, u32[]{:S(2)}) collective-permute-start(f32[66,8,128]{2,1,0:T(8,128)S(1)} %get-tuple-element.28), channel_id=1, source_target_pairs={{4,8},{12,16},{20,24},{8,4},{16,12},{24,20},{5,9},{13,17},{21,25},... | collective-permute-start | bytes 811016 | tf_op jit(solution)/shard_map/ppermute | solution.py:951
  9.8 3.2 %collective-permute-start.1 = (f32[65,8,128]{2,1,0:T(8,128)S(1)}, f32[65,8,128]{2,1,0:T(8,128)S(1)}, u32[]{:S(2)}, u32[]{:S(2)}) collective-permute-start(f32[65,8,128]{2,1,0:T(8,128)S(1)} %get-tuple-element.27), channel_id=1, source_target_pairs={{0,4},{4,0},{8,12},{12,8},{16,20},{20,16},{24,28},{28,24},{1,5},{5... | collective-permute-start | bytes 798728 | tf_op jit(solution)/shard_map/ppermute | solution.py:947
  13.0 0.0 collective-permute-done.3.message_ref.far_y_ref
  13.0 0.2 pack_far.1
  13.3 0.7 %collective-permute-start.5 = (f32[29,8,128]{2,1,0:T(8,128)S(1)}, f32[29,8,128]{2,1,0:T(8,128)S(1)}, u32[]{:S(2)}, u32[]{:S(2)}) collective-permute-start(f32[29,8,128]{2,1,0:T(8,128)S(1)} %get-tuple-element.31), channel_id=1, source_target_pairs={{5,9},{6,10},{13,17},{14,18},{21,25},{22,26},{9,5},{10,6},{17,13},... | collective-permute-start | bytes 356360 | tf_op jit(solution)/shard_map/ppermute | solution.py:959
  14.0 0.1 collective-permute-start.4
  14.1 0.1 collective-permute-done.1.first_near_ref
  14.2 0.0 collective-permute-done.2.second_near_ref
  14.2 0.8 %lay_out.1 = (f32[95,40,128]{2,1,0:T(8,128)S(1)}, f32[76,24,128]{2,1,0:T(8,128)S(1)}, f32[2,5,3,8,128]{4,3,2,1,0:T(8,128)S(1)}, f32[4,4,2,8,128]{4,3,2,1,0:T(8,128)S(1)}) custom-call(f32[37,8,128]{2,1,0:T(8,128)S(1)} %collective-permute-done.message_ref.near_y_ref, f32[37,8,128]{2,1,0:T(8,128)S(1)} %collective-permute-done.3.message_ref.far_y_ref, ...), custom_call_target="tpu_custom_call" | custom-call | tf_op jit(solution)/shard_map/lay_out/pallas_call | solution.py:1005
  15.0 0.3 collective-permute-done.4.first_far_ref
  15.4 0.0 collective-permute-done.5.second_far_ref
  15.4 2.4 %steps.1 = (f32[19,8,256]{2,1,0:T(8,128)S(1)}, f32[32,64]{1,0:T(8,128)S(1)}, f32[95,40,128]{2,1,0:T(8,128)S(1)}, f32[76,24,128]{2,1,0:T(8,128)S(1)}, f32[2,5,3,8...) custom-call(f32[38,8,128]{2,1,0:T(8,128)S(1)} %get-tuple-element.21., ...), custom_call_target="tpu_custom_call", output_to_operand_aliasing={{2}: (7, {}), {3}: (8, {}), {4}: (9, {}), {5}: (10, {})} | custom-call | tf_op jit(solution)/shard_map/steps/pallas_call | solution.py:1008
  17.7 16.6 %all_to_all.9.parts_ref = f32[32,1,64]{2,1,0:T(1,128)S(1)} all-to-all(f32[32,1,64]{2,1,0:T(1,128)S(1)} %bitcast.2), channel_id=1, replica_groups=mesh['gx'=8,'gy'=4] {'gx','gy'}, dimensions={0} | all-to-all | bytes 16384 | tf_op jit(solution)/shard_map/all_to_all | solution.py:1022
  34.4 0.7 %finish.1 = (f32[1,64]{1,0:T(1,128)}, f32[19,8,256]{2,1,0:T(8,128)}) custom-call(f32[32,1,64]{2,1,0:T(1,128)S(1)} %all_to_all.9.parts_ref, f32[19,8,256]{2,1,0:T(8,128)S(1)} %get-tuple-element.37.adjoint_ref), custom_call_target="tpu_custom_call" | custom-call | tf_op jit(solution)/shard_map/finish/pallas_call | solution.py:1023
Async XLA Ops:
  1.9 6.9 %collective-permute-start = (f32[37,8,128]{2,1,0:T(8,128)S(1)}, f32[37,8,128]{2,1,0:T(8,128)S(1)}, u32[]{:S(2)}, u32[]{:S(2)}) collective-permute-start(f32[37,8,128]{2,1,0:T(8,128)S(1)} %get-tuple-element.26), channel_id=1, source_target_pairs={{0,1},{1,0},{2,3},{3,2},{4,5},{5,4},{6,7},{7,6},{8,9},{9,8},{10,11... | collective-permute-start | bytes 454664 | tf_op jit(solution)/shard_map/ppermute | solution.py:947
  4.9 8.2 %collective-permute-start.3 = (f32[37,8,128]{2,1,0:T(8,128)S(1)}, f32[37,8,128]{2,1,0:T(8,128)S(1)}, u32[]{:S(2)}, u32[]{:S(2)}) collective-permute-start(f32[37,8,128]{2,1,0:T(8,128)S(1)} %get-tuple-element.29), channel_id=1, source_target_pairs={{1,2},{2,1},{5,6},{6,5},{9,10},{10,9},{13,14},{14,13},{17,18},{18,... | collective-permute-start | bytes 454664 | tf_op jit(solution)/shard_map/ppermute | solution.py:951
  9.1 5.1 %collective-permute-start.2 = (f32[66,8,128]{2,1,0:T(8,128)S(1)}, f32[66,8,128]{2,1,0:T(8,128)S(1)}, u32[]{:S(2)}, u32[]{:S(2)}) collective-permute-start(f32[66,8,128]{2,1,0:T(8,128)S(1)} %get-tuple-element.28), channel_id=1, source_target_pairs={{4,8},{12,16},{20,24},{8,4},{16,12},{24,20},{5,9},{13,17},{21,25},... | collective-permute-start | bytes 811016 | tf_op jit(solution)/shard_map/ppermute | solution.py:951
  9.8 4.4 %collective-permute-start.1 = (f32[65,8,128]{2,1,0:T(8,128)S(1)}, f32[65,8,128]{2,1,0:T(8,128)S(1)}, u32[]{:S(2)}, u32[]{:S(2)}) collective-permute-start(f32[65,8,128]{2,1,0:T(8,128)S(1)} %get-tuple-element.27), channel_id=1, source_target_pairs={{0,4},{4,0},{8,12},{12,8},{16,20},{20,16},{24,28},{28,24},{1,5},{5... | collective-permute-start | bytes 798728 | tf_op jit(solution)/shard_map/ppermute | solution.py:947
  13.3 2.1 %collective-permute-start.5 = (f32[29,8,128]{2,1,0:T(8,128)S(1)}, f32[29,8,128]{2,1,0:T(8,128)S(1)}, u32[]{:S(2)}, u32[]{:S(2)}) collective-permute-start(f32[29,8,128]{2,1,0:T(8,128)S(1)} %get-tuple-element.31), channel_id=1, source_target_pairs={{5,9},{6,10},{13,17},{14,18},{21,25},{22,26},{9,5},{10,6},{17,13},... | collective-permute-start | bytes 356360 | tf_op jit(solution)/shard_map/ppermute | solution.py:959
  14.0 1.4 %collective-permute-start.4 = (f32[28,8,128]{2,1,0:T(8,128)S(1)}, f32[28,8,128]{2,1,0:T(8,128)S(1)}, u32[]{:S(2)}, u32[]{:S(2)}) collective-permute-start(f32[28,8,128]{2,1,0:T(8,128)S(1)} %get-tuple-element.30), channel_id=1, source_target_pairs={{0,4},{4,0},{8,12},{12,8},{16,20},{20,16},{24,28},{28,24},{1,5},{5... | collective-permute-start | bytes 344072 | tf_op jit(solution)/shard_map/ppermute | solution.py:947

commit v24 on v23

--- a/solution.py
+++ b/solution.py
@@ -449,47 +449,43 @@
             own_cot_ref[2 * i + t] = tile_of(cot_ref, i, t)
 
 
-def is_right(near):
-    return is_even("gy") if near else jnp.logical_not(is_even("gy"))
+def by_parity(body):
+    even = is_even("gy")
+    pl.when(even)(lambda: body(True))
+    pl.when(jnp.logical_not(even))(lambda: body(False))
 
 
 def half_lanes(right):
     row, lane, column, depth = iotas()
-    return lane // (LANES // 2) == jnp.where(right, 0, 1)
-
-
-def from_y(message_ref, near):
+    return lane < LANES // 2 if right else lane >= LANES // 2
+
+
+def from_y(message_ref, right):
     row, lane, column, depth = iotas()
     ref = Unpacking(message_ref, layouts()[0])
-    right = is_right(near)
+    way, place, far = (-1, 2, 1) if right else (1, 1, 0)
 
     def population(i):
-        return jnp.where(right, ref[2 * i], ref[2 * i + 1])
+        return ref[2 * i + 1 - far]
 
     def cotangent(i):
-        values = []
-        for way, place, far in ((1, 1, 0), (-1, 2, 1)):
-            deep = 3 - way * VELOCITIES[i][1]
-            value = columns(ref[2 * i + far], way * (4 - deep))
-            if i in turned(1, way):
-                extra = columns(ref[Y_COT], place - turned(1, way).index(i))
-                value = jnp.where(column == place, extra, value)
-            values.append(value)
-        return jnp.where(right, values[1], values[0])
+        deep = 3 - way * VELOCITIES[i][1]
+        value = columns(ref[2 * i + far], way * (4 - deep))
+        if i in turned(1, way):
+            extra = columns(ref[Y_COT], place - turned(1, way).index(i))
+            value = jnp.where(column == place, extra, value)
+        return value
 
     def codes(s):
         return ref[(Y_CODE1, Y_CODE2, Y_CODE3)[s - 1]]
 
     def outer(i):
-        left, above = ref[2 * i], ref[2 * i + 1]
-        if i in turned(1, 1):
-            above = columns(ref[Y_POP], -turned(1, 1).index(i))
-        if i in turned(1, -1):
-            left = columns(ref[Y_POP], 3 - turned(1, -1).index(i))
-        return jnp.where(right, above, left)
+        if i in turned(1, -way):
+            return columns(ref[Y_POP], (0 if right else 3) - turned(1, -way).index(i))
+        return ref[2 * i + far]
 
     def outer_code():
-        return jnp.where(right, columns(ref[Y_CODE3], 1), columns(ref[Y_CODE3], 3))
+        return columns(ref[Y_CODE3], 1 if right else 3)
 
     return population, cotangent, codes, outer, outer_code
 
@@ -521,11 +517,11 @@
         deal.put(way, first + X_EXTRA, extra)
 
 
-def pack_neighbour(deal, lanes, message_ref, near):
+def pack_neighbour(deal, lanes, message_ref, right):
     ring, code13, code2, tiles = x_places(lanes)
-    population, cotangent, codes, outer, outer_code = from_y(message_ref, near)
+    population, cotangent, codes, outer, outer_code = from_y(message_ref, right)
     pack_lines(deal, X_LANE * (lanes - 1), population, cotangent)
-    kept = half_lanes(is_right(near))
+    kept = half_lanes(right)
     for n in range(X_HALVES):
         first, second = (outer(2 * n - 1), outer(2 * n)) if n else (outer(0), outer_code())
         deal.put_both(ring + n, jnp.where(kept, first, pltpu.roll(second, LANES // 2, 1)))
@@ -551,14 +547,23 @@
     first, second = field_ref[4], lines(field_ref[5], 4)
     deal.put(1, code2, jnp.where(row >= 4, first, second))
     deal.put(-1, code2, jnp.where(row < 4, first, second))
-    pack_neighbour(deal, 3, message_ref, True)
-    deal.finish()
+
+    def neighbour(even):
+        pack_neighbour(deal, 3, message_ref, even)
+        deal.finish()
+
+    by_parity(neighbour)
 
 
 def pack_far(message_ref, first_ref, second_ref):
-    deal = Deal(is_even("gx"), first_ref, second_ref, layouts()[2])
-    pack_neighbour(deal, 1, message_ref, False)
-    deal.finish()
+    even_x = is_even("gx")
+
+    def neighbour(even):
+        deal = Deal(even_x, first_ref, second_ref, layouts()[2])
+        pack_neighbour(deal, 1, message_ref, not even)
+        deal.finish()
+
+    by_parity(neighbour)
 
 
 def from_x(ref, n, way, lanes):
@@ -661,8 +666,8 @@
             field[s, c - 1, 1] = jnp.where(row < 4, above[2](s), below[2](s))
 
 
-def near_tile():
-    return jnp.where(is_right(True), 4, 1)
+def near_tile(even):
+    return 4 if even else 1
 
 
 def lay_out(
@@ -690,22 +695,28 @@
             *spaces,
         )
         lay_halo(2 + t, from_x(below, t, 1, 3), from_x(above, t, -1, 3), *spaces)
-    near, far = from_y(near_y_ref, True), from_y(far_y_ref, False)
-    for c, (population, cotangent, codes, _, _) in ((near_tile(), near), (5 - near_tile(), far)):
-        lay_own(c, population, cotangent, codes, expand(codes(1)), *spaces)
-    kept = half_lanes(is_right(True))
-    lay_own(
-        0,
-        lambda i: jnp.where(kept, near[3](i), far[3](i)),
-        None,
-        None,
-        expand(jnp.where(kept, near[4](), far[4]())),
-        *spaces,
-    )
-    lay_halo(near_tile(), from_x(below, 2, 1, 3), from_x(above, 2, -1, 3), *spaces)
-
-
-def lay_far(near_refs, far_refs, spaces):
+
+    def neighbours(even):
+        place = near_tile(even)
+        below, above = sides(first_near_ref, second_near_ref, "gx", layouts()[1])
+        near, far = from_y(near_y_ref, even), from_y(far_y_ref, not even)
+        for c, (population, cotangent, codes, _, _) in ((place, near), (5 - place, far)):
+            lay_own(c, population, cotangent, codes, expand(codes(1)), *spaces)
+        kept = half_lanes(even)
+        lay_own(
+            0,
+            lambda i: jnp.where(kept, near[3](i), far[3](i)),
+            None,
+            None,
+            expand(jnp.where(kept, near[4](), far[4]())),
+            *spaces,
+        )
+        lay_halo(place, from_x(below, 2, 1, 3), from_x(above, 2, -1, 3), *spaces)
+
+    by_parity(neighbours)
+
+
+def lay_far(even, near_refs, far_refs, spaces):
     nears, fars = (
         [
             from_x(ref, lanes - 1, way, lanes)
@@ -713,8 +724,8 @@
         ]
         for refs, layout, lanes in zip((near_refs, far_refs), layouts()[1:], (3, 1))
     )
-    lay_halo(5 - near_tile(), *fars, *spaces)
-    kept = half_lanes(is_right(True))
+    lay_halo(5 - near_tile(even), *fars, *spaces)
+    kept = half_lanes(even)
     ring = [
         (
             lambda i, near=near, far=far: jnp.where(kept, near[3](i), far[3](i)),
@@ -739,10 +750,13 @@
 ):
     adjoint_ref, panel_ref, pop_a, ring_a, wide, field, pop_b, ring_b, saved, mom, grad = refs[4:]
     size_x, size_y = sizes
-    lay_far(
-        (first_near_ref, second_near_ref),
-        (first_far_ref, second_far_ref),
-        (pop_a, ring_a, wide, field),
+    by_parity(
+        lambda even: lay_far(
+            even,
+            (first_near_ref, second_near_ref),
+            (first_far_ref, second_far_ref),
+            (pop_a, ring_a, wide, field),
+        )
     )
 
     at_x, at_y = lax.axis_index("gx"), lax.axis_index("gy")

time: 35.3 us -> 35.6 us (level)
  Pallas kernels: 5.66 us -> 6.05 us
where the time goes in v24:
time: 35.6 us; the launch traced here: 35.3 us
  blocking collectives  16.6 us (47%)
  starting transfers between devices  8.34 us (23%)
  Pallas kernels  6.05 us (17%)
  waiting for transfers between devices  3.62 us (10%)
  between operations  0.7 us (2%)
    all_to_all x1, blocking collectives, on_device(): gathered = lax.all_to_all(sums, ('gx', 'gy'), 0, 0, tiled=True)  16.6 us
    ppermute x3, starting transfers between devices, swap(): lax.ppermute(value, axis, [(i, i ^ 1) for i in range(size) if i ^ 1 < size])  6.34 us
    ppermute x3, waiting for transfers between devices, swap(): lax.ppermute(value, axis, [(i, i ^ 1) for i in range(size) if i ^ 1 < size])  3.62 us
    pallas_call x1, Pallas kernels, on_device(): call(functools.partial(steps_kernel, sizes), (pltpu.VMEM((Q, ROWS, 2 * LA...  2.62 us
    ppermute x2, starting transfers between devices, swap_between(): return lax.ppermute(value, axis, pairs + [(j, i) for i, j in pairs])  1.34 us
    pallas_call x1, Pallas kernels, on_device(): call(pack_own, (tiles_of(y_layout.size),) * 2 + (tiles_of(2 * Q),) * 3 +...  1.24 us
    pallas_call x1, Pallas kernels, on_device(): call(lay_out, spaces, [VMEM] * 7, name='lay_out')  0.93 us
  transfers between devices with their start and end apart: 6, of which 3 were waited for; matrix products, arithmetic and copies ran while one was open for 0% of the time, Pallas kernels for 4%

profile of v24, /device:TPU:0, one launch (start us, length us, event | category | flops | bytes accessed | tf_op | source)
XLA Modules:
  0.0 35.3 jit_solution(5390186605012454748)
XLA Ops:
  0.6 1.2 %pack_own.1 = (f32[37,8,128]{2,1,0:T(8,128)S(1)}, f32[37,8,128]{2,1,0:T(8,128)S(1)}, f32[38,8,128]{2,1,0:T(8,128)S(1)}, f32[38,8,128]{2,1,0:T(8,128)S(1)}, f32[3...) custom-call(f32[19,8,256]{2,1,0:T(8,128)} %f_hbm.1, f32[19,8,256]{2,1,0:T(8,128)} %cot_hbm.1, ...), custom_call_target="tpu_custom_call" | custom-call | tf_op jit(solution)/shard_map/pack_own/pallas_call | solution.py:979
  1.9 3.0 %collective-permute-start = (f32[37,8,128]{2,1,0:T(8,128)S(1)}, f32[37,8,128]{2,1,0:T(8,128)S(1)}, u32[]{:S(2)}, u32[]{:S(2)}) collective-permute-start(f32[37,8,128]{2,1,0:T(8,128)S(1)} %get-tuple-element.26), channel_id=1, source_target_pairs={{0,1},{1,0},{2,3},{3,2},{4,5},{5,4},{6,7},{7,6},{8,9},{9,8},{10,11... | collective-permute-start | bytes 454664 | tf_op jit(solution)/shard_map/ppermute | solution.py:961
  4.9 0.7 %collective-permute-start.3 = (f32[37,8,128]{2,1,0:T(8,128)S(1)}, f32[37,8,128]{2,1,0:T(8,128)S(1)}, u32[]{:S(2)}, u32[]{:S(2)}) collective-permute-start(f32[37,8,128]{2,1,0:T(8,128)S(1)} %get-tuple-element.29), channel_id=1, source_target_pairs={{1,2},{2,1},{5,6},{6,5},{9,10},{10,9},{13,14},{14,13},{17,18},{18,... | collective-permute-start | bytes 454664 | tf_op jit(solution)/shard_map/ppermute | solution.py:965
  5.5 3.3 %collective-permute-done.message_ref.near_y_ref = f32[37,8,128]{2,1,0:T(8,128)S(1)} collective-permute-done((f32[37,8,128]{2,1,0:T(8,128)S(1)}, f32[37,8,128]{2,1,0:T(8,128)S(1)}, u32[]{:S(2)}, u32[]{:S(2)}) %collective-permute-start) | collective-permute-done | bytes 151584 | tf_op jit(solution)/shard_map/ppermute | solution.py:961
  8.8 0.3 pack_near.1
  9.1 0.7 %collective-permute-start.2 = (f32[66,8,128]{2,1,0:T(8,128)S(1)}, f32[66,8,128]{2,1,0:T(8,128)S(1)}, u32[]{:S(2)}, u32[]{:S(2)}) collective-permute-start(f32[66,8,128]{2,1,0:T(8,128)S(1)} %get-tuple-element.28), channel_id=1, source_target_pairs={{4,8},{12,16},{20,24},{8,4},{16,12},{24,20},{5,9},{13,17},{21,25},... | collective-permute-start | bytes 811016 | tf_op jit(solution)/shard_map/ppermute | solution.py:965
  9.8 3.2 %collective-permute-start.1 = (f32[65,8,128]{2,1,0:T(8,128)S(1)}, f32[65,8,128]{2,1,0:T(8,128)S(1)}, u32[]{:S(2)}, u32[]{:S(2)}) collective-permute-start(f32[65,8,128]{2,1,0:T(8,128)S(1)} %get-tuple-element.27), channel_id=1, source_target_pairs={{0,4},{4,0},{8,12},{12,8},{16,20},{20,16},{24,28},{28,24},{1,5},{5... | collective-permute-start | bytes 798728 | tf_op jit(solution)/shard_map/ppermute | solution.py:961
  13.1 0.0 collective-permute-done.3.message_ref.far_y_ref
  13.1 0.3 pack_far.1
  13.3 0.7 %collective-permute-start.5 = (f32[29,8,128]{2,1,0:T(8,128)S(1)}, f32[29,8,128]{2,1,0:T(8,128)S(1)}, u32[]{:S(2)}, u32[]{:S(2)}) collective-permute-start(f32[29,8,128]{2,1,0:T(8,128)S(1)} %get-tuple-element.31), channel_id=1, source_target_pairs={{5,9},{6,10},{13,17},{14,18},{21,25},{22,26},{9,5},{10,6},{17,13},... | collective-permute-start | bytes 356360 | tf_op jit(solution)/shard_map/ppermute | solution.py:973
  14.0 0.1 collective-permute-start.4
  14.1 0.1 collective-permute-done.1.first_near_ref
  14.2 0.0 collective-permute-done.2.second_near_ref
  14.2 0.9 %lay_out.1 = (f32[95,40,128]{2,1,0:T(8,128)S(1)}, f32[76,24,128]{2,1,0:T(8,128)S(1)}, f32[2,5,3,8,128]{4,3,2,1,0:T(8,128)S(1)}, f32[4,4,2,8,128]{4,3,2,1,0:T(8,128)S(1)}) custom-call(f32[37,8,128]{2,1,0:T(8,128)S(1)} %collective-permute-done.message_ref.near_y_ref, f32[37,8,128]{2,1,0:T(8,128)S(1)} %collective-permute-done.3.message_ref.far_y_ref, ...), custom_call_target="tpu_custom_call" | custom-call | tf_op jit(solution)/shard_map/lay_out/pallas_call | solution.py:1019
  15.2 0.2 collective-permute-done.4.first_far_ref
  15.4 0.0 collective-permute-done.5.second_far_ref
  15.4 2.6 %steps.1 = (f32[19,8,256]{2,1,0:T(8,128)S(1)}, f32[32,64]{1,0:T(8,128)S(1)}, f32[95,40,128]{2,1,0:T(8,128)S(1)}, f32[76,24,128]{2,1,0:T(8,128)S(1)}, f32[2,5,3,8...) custom-call(f32[38,8,128]{2,1,0:T(8,128)S(1)} %get-tuple-element.21., ...), custom_call_target="tpu_custom_call", output_to_operand_aliasing={{2}: (7, {}), {3}: (8, {}), {4}: (9, {}), {5}: (10, {})} | custom-call | tf_op jit(solution)/shard_map/steps/pallas_call | solution.py:1022
  18.0 16.6 %all_to_all.9.parts_ref = f32[32,1,64]{2,1,0:T(1,128)S(1)} all-to-all(f32[32,1,64]{2,1,0:T(1,128)S(1)} %bitcast.2), channel_id=1, replica_groups=mesh['gx'=8,'gy'=4] {'gx','gy'}, dimensions={0} | all-to-all | bytes 16384 | tf_op jit(solution)/shard_map/all_to_all | solution.py:1036
  34.6 0.7 %finish.1 = (f32[1,64]{1,0:T(1,128)}, f32[19,8,256]{2,1,0:T(8,128)}) custom-call(f32[32,1,64]{2,1,0:T(1,128)S(1)} %all_to_all.9.parts_ref, f32[19,8,256]{2,1,0:T(8,128)S(1)} %get-tuple-element.37.adjoint_ref), custom_call_target="tpu_custom_call" | custom-call | tf_op jit(solution)/shard_map/finish/pallas_call | solution.py:1037
Async XLA Ops:
  1.9 6.9 %collective-permute-start = (f32[37,8,128]{2,1,0:T(8,128)S(1)}, f32[37,8,128]{2,1,0:T(8,128)S(1)}, u32[]{:S(2)}, u32[]{:S(2)}) collective-permute-start(f32[37,8,128]{2,1,0:T(8,128)S(1)} %get-tuple-element.26), channel_id=1, source_target_pairs={{0,1},{1,0},{2,3},{3,2},{4,5},{5,4},{6,7},{7,6},{8,9},{9,8},{10,11... | collective-permute-start | bytes 454664 | tf_op jit(solution)/shard_map/ppermute | solution.py:961
  4.9 8.2 %collective-permute-start.3 = (f32[37,8,128]{2,1,0:T(8,128)S(1)}, f32[37,8,128]{2,1,0:T(8,128)S(1)}, u32[]{:S(2)}, u32[]{:S(2)}) collective-permute-start(f32[37,8,128]{2,1,0:T(8,128)S(1)} %get-tuple-element.29), channel_id=1, source_target_pairs={{1,2},{2,1},{5,6},{6,5},{9,10},{10,9},{13,14},{14,13},{17,18},{18,... | collective-permute-start | bytes 454664 | tf_op jit(solution)/shard_map/ppermute | solution.py:965
  9.1 5.1 %collective-permute-start.2 = (f32[66,8,128]{2,1,0:T(8,128)S(1)}, f32[66,8,128]{2,1,0:T(8,128)S(1)}, u32[]{:S(2)}, u32[]{:S(2)}) collective-permute-start(f32[66,8,128]{2,1,0:T(8,128)S(1)} %get-tuple-element.28), channel_id=1, source_target_pairs={{4,8},{12,16},{20,24},{8,4},{16,12},{24,20},{5,9},{13,17},{21,25},... | collective-permute-start | bytes 811016 | tf_op jit(solution)/shard_map/ppermute | solution.py:965
  9.8 4.4 %collective-permute-start.1 = (f32[65,8,128]{2,1,0:T(8,128)S(1)}, f32[65,8,128]{2,1,0:T(8,128)S(1)}, u32[]{:S(2)}, u32[]{:S(2)}) collective-permute-start(f32[65,8,128]{2,1,0:T(8,128)S(1)} %get-tuple-element.27), channel_id=1, source_target_pairs={{0,4},{4,0},{8,12},{12,8},{16,20},{20,16},{24,28},{28,24},{1,5},{5... | collective-permute-start | bytes 798728 | tf_op jit(solution)/shard_map/ppermute | solution.py:961
  13.3 2.1 %collective-permute-start.5 = (f32[29,8,128]{2,1,0:T(8,128)S(1)}, f32[29,8,128]{2,1,0:T(8,128)S(1)}, u32[]{:S(2)}, u32[]{:S(2)}) collective-permute-start(f32[29,8,128]{2,1,0:T(8,128)S(1)} %get-tuple-element.31), channel_id=1, source_target_pairs={{5,9},{6,10},{13,17},{14,18},{21,25},{22,26},{9,5},{10,6},{17,13},... | collective-permute-start | bytes 356360 | tf_op jit(solution)/shard_map/ppermute | solution.py:973
  14.0 1.4 %collective-permute-start.4 = (f32[28,8,128]{2,1,0:T(8,128)S(1)}, f32[28,8,128]{2,1,0:T(8,128)S(1)}, u32[]{:S(2)}, u32[]{:S(2)}) collective-permute-start(f32[28,8,128]{2,1,0:T(8,128)S(1)} %get-tuple-element.30), channel_id=1, source_target_pairs={{0,4},{4,0},{8,12},{12,8},{16,20},{20,16},{24,28},{28,24},{1,5},{5... | collective-permute-start | bytes 344072 | tf_op jit(solution)/shard_map/ppermute | solution.py:961

commit v25 on v23

--- a/solution.py
+++ b/solution.py
@@ -631,11 +631,18 @@
     return jnp.where(top, 0.0, code), phi
 
 
+def in_groups(size=8):
+    return [range(first, min(first + size, Q)) for first in range(0, Q, size)]
+
+
 def lay_own(c, population, cotangent, codes, code_phi, pop, cot, wide, field):
-    for i in range(Q):
-        pop[5 * i + c, pl.ds(2 * ROWS, ROWS), :] = population(i)
-        if cotangent is not None:
-            cot[4 * i + c - 1, own_rows(), :] = cotangent(i)
+    for group in in_groups():
+        pops = [population(i) for i in group]
+        cots = [cotangent(i) for i in group] if cotangent is not None else []
+        for i, value in zip(group, pops):
+            pop[5 * i + c, pl.ds(2 * ROWS, ROWS), :] = value
+        for i, value in zip(group, cots):
+            cot[4 * i + c - 1, own_rows(), :] = value
     for n in range(2):
         wide[n, c, 1] = code_phi[n]
     if cotangent is not None:
@@ -646,14 +653,19 @@
 
 def lay_halo(c, below, above, pop, cot, wide, field):
     row, lane, column, depth = iotas()
+    for group in in_groups():
+        pops = [(below[0](i), above[0](i)) for i in group]
+        cots = []
+        if below[1] is not None:
+            cots = [jnp.where(row < 4, above[1](i), below[1](i)) for i in group]
+        for i, (before, behind) in zip(group, pops):
+            pop[5 * i + c, pl.ds(ROWS, ROWS), :] = before
+            pop[5 * i + c, pl.ds(3 * ROWS, ROWS), :] = behind
+        for i, value in zip(group, cots):
+            put_halo(cot, 4 * i + c - 1, value)
     before, behind = expand(below[2](1)), expand(above[2](1))
     for n in range(2):
         wide[n, c, 0], wide[n, c, 2] = before[n], behind[n]
-    for i in range(Q):
-        pop[5 * i + c, pl.ds(ROWS, ROWS), :] = below[0](i)
-        pop[5 * i + c, pl.ds(3 * ROWS, ROWS), :] = above[0](i)
-        if below[1] is not None:
-            put_halo(cot, 4 * i + c - 1, jnp.where(row < 4, above[1](i), below[1](i)))
     if below[1] is not None:
         for n, place in ((0, 1), (1, 0)):
             field[place, c - 1, 1] = jnp.where(row < 4, behind[n], before[n])

time: 35.3 us -> 35.1 us (level)
  transfers between devices with their start and end apart: 6 -> 6, of which waited for: 3 -> 3; matrix products, arithmetic and copies ran while one was open for 0% -> 0% of each run, Pallas kernels for 4% -> 3%
where the time goes in v25:
time: 35.1 us; the launch traced here: 34.8 us
  blocking collectives  16.3 us (46%)
  starting transfers between devices  8.33 us (24%)
  Pallas kernels  5.41 us (15%)
  waiting for transfers between devices  4.03 us (11%)
  between operations  0.69 us (2%)
    all_to_all x1, blocking collectives, on_device(): gathered = lax.all_to_all(sums, ('gx', 'gy'), 0, 0, tiled=True)  16.3 us
    ppermute x3, starting transfers between devices, swap(): lax.ppermute(value, axis, [(i, i ^ 1) for i in range(size) if i ^ 1 < size])  6.33 us
    ppermute x3, waiting for transfers between devices, swap(): lax.ppermute(value, axis, [(i, i ^ 1) for i in range(size) if i ^ 1 < size])  4.02 us
    pallas_call x1, Pallas kernels, on_device(): call(functools.partial(steps_kernel, sizes), (pltpu.VMEM((Q, ROWS, 2 * LA...  2.41 us
    ppermute x2, starting transfers between devices, swap_between(): return lax.ppermute(value, axis, pairs + [(j, i) for i, j in pairs])  1.34 us
    pallas_call x1, Pallas kernels, on_device(): call(pack_own, (tiles_of(y_layout.size),) * 2 + (tiles_of(2 * Q),) * 3 +...  1.24 us
  transfers between devices with their start and end apart: 6, of which 3 were waited for; matrix products, arithmetic and copies ran while one was open for 0% of the time, Pallas kernels for 3%

profile of v25, /device:TPU:0, one launch (start us, length us, event | category | flops | bytes accessed | tf_op | source)
XLA Modules:
  0.0 34.8 jit_solution(18365564022307100194)
XLA Ops:
  0.6 1.2 %pack_own.1 = (f32[37,8,128]{2,1,0:T(8,128)S(1)}, f32[37,8,128]{2,1,0:T(8,128)S(1)}, f32[38,8,128]{2,1,0:T(8,128)S(1)}, f32[38,8,128]{2,1,0:T(8,128)S(1)}, f32[3...) custom-call(f32[19,8,256]{2,1,0:T(8,128)} %f_hbm.1, f32[19,8,256]{2,1,0:T(8,128)} %cot_hbm.1, ...), custom_call_target="tpu_custom_call" | custom-call | tf_op jit(solution)/shard_map/pack_own/pallas_call | solution.py:977
  1.9 3.0 %collective-permute-start = (f32[37,8,128]{2,1,0:T(8,128)S(1)}, f32[37,8,128]{2,1,0:T(8,128)S(1)}, u32[]{:S(2)}, u32[]{:S(2)}) collective-permute-start(f32[37,8,128]{2,1,0:T(8,128)S(1)} %get-tuple-element.26), channel_id=1, source_target_pairs={{0,1},{1,0},{2,3},{3,2},{4,5},{5,4},{6,7},{7,6},{8,9},{9,8},{10,11... | collective-permute-start | bytes 454664 | tf_op jit(solution)/shard_map/ppermute | solution.py:959
  4.9 0.7 %collective-permute-start.3 = (f32[37,8,128]{2,1,0:T(8,128)S(1)}, f32[37,8,128]{2,1,0:T(8,128)S(1)}, u32[]{:S(2)}, u32[]{:S(2)}) collective-permute-start(f32[37,8,128]{2,1,0:T(8,128)S(1)} %get-tuple-element.29), channel_id=1, source_target_pairs={{1,2},{2,1},{5,6},{6,5},{9,10},{10,9},{13,14},{14,13},{17,18},{18,... | collective-permute-start | bytes 454664 | tf_op jit(solution)/shard_map/ppermute | solution.py:963
  5.5 3.3 %collective-permute-done.message_ref.near_y_ref = f32[37,8,128]{2,1,0:T(8,128)S(1)} collective-permute-done((f32[37,8,128]{2,1,0:T(8,128)S(1)}, f32[37,8,128]{2,1,0:T(8,128)S(1)}, u32[]{:S(2)}, u32[]{:S(2)}) %collective-permute-start) | collective-permute-done | bytes 151584 | tf_op jit(solution)/shard_map/ppermute | solution.py:959
  8.8 0.3 pack_near.1
  9.1 0.7 %collective-permute-start.2 = (f32[66,8,128]{2,1,0:T(8,128)S(1)}, f32[66,8,128]{2,1,0:T(8,128)S(1)}, u32[]{:S(2)}, u32[]{:S(2)}) collective-permute-start(f32[66,8,128]{2,1,0:T(8,128)S(1)} %get-tuple-element.28), channel_id=1, source_target_pairs={{4,8},{12,16},{20,24},{8,4},{16,12},{24,20},{5,9},{13,17},{21,25},... | collective-permute-start | bytes 811016 | tf_op jit(solution)/shard_map/ppermute | solution.py:963
  9.8 3.2 %collective-permute-start.1 = (f32[65,8,128]{2,1,0:T(8,128)S(1)}, f32[65,8,128]{2,1,0:T(8,128)S(1)}, u32[]{:S(2)}, u32[]{:S(2)}) collective-permute-start(f32[65,8,128]{2,1,0:T(8,128)S(1)} %get-tuple-element.27), channel_id=1, source_target_pairs={{0,4},{4,0},{8,12},{12,8},{16,20},{20,16},{24,28},{28,24},{1,5},{5... | collective-permute-start | bytes 798728 | tf_op jit(solution)/shard_map/ppermute | solution.py:959
  13.0 0.0 collective-permute-done.3.message_ref.far_y_ref
  13.0 0.2 pack_far.1
  13.3 0.7 %collective-permute-start.5 = (f32[29,8,128]{2,1,0:T(8,128)S(1)}, f32[29,8,128]{2,1,0:T(8,128)S(1)}, u32[]{:S(2)}, u32[]{:S(2)}) collective-permute-start(f32[29,8,128]{2,1,0:T(8,128)S(1)} %get-tuple-element.31), channel_id=1, source_target_pairs={{5,9},{6,10},{13,17},{14,18},{21,25},{22,26},{9,5},{10,6},{17,13},... | collective-permute-start | bytes 356360 | tf_op jit(solution)/shard_map/ppermute | solution.py:971
  14.0 0.1 collective-permute-start.4
  14.1 0.1 collective-permute-done.1.first_near_ref
  14.2 0.0 collective-permute-done.2.second_near_ref
  14.2 0.6 %lay_out.1 = (f32[95,40,128]{2,1,0:T(8,128)S(1)}, f32[76,24,128]{2,1,0:T(8,128)S(1)}, f32[2,5,3,8,128]{4,3,2,1,0:T(8,128)S(1)}, f32[4,4,2,8,128]{4,3,2,1,0:T(8,128)S(1)}) custom-call(f32[37,8,128]{2,1,0:T(8,128)S(1)} %collective-permute-done.message_ref.near_y_ref, f32[37,8,128]{2,1,0:T(8,128)S(1)} %collective-permute-done.3.message_ref.far_y_ref, ...), custom_call_target="tpu_custom_call" | custom-call | tf_op jit(solution)/shard_map/lay_out/pallas_call | solution.py:1017
  14.8 0.6 %collective-permute-done.4.first_far_ref = f32[28,8,128]{2,1,0:T(8,128)S(1)} collective-permute-done((f32[28,8,128]{2,1,0:T(8,128)S(1)}, f32[28,8,128]{2,1,0:T(8,128)S(1)}, u32[]{:S(2)}, u32[]{:S(2)}) %collective-permute-start.4) | collective-permute-done | bytes 114720 | tf_op jit(solution)/shard_map/ppermute | solution.py:959
  15.4 0.0 collective-permute-done.5.second_far_ref
  15.4 2.4 %steps.1 = (f32[19,8,256]{2,1,0:T(8,128)S(1)}, f32[32,64]{1,0:T(8,128)S(1)}, f32[95,40,128]{2,1,0:T(8,128)S(1)}, f32[76,24,128]{2,1,0:T(8,128)S(1)}, f32[2,5,3,8...) custom-call(f32[38,8,128]{2,1,0:T(8,128)S(1)} %get-tuple-element.21., ...), custom_call_target="tpu_custom_call", output_to_operand_aliasing={{2}: (7, {}), {3}: (8, {}), {4}: (9, {}), {5}: (10, {})} | custom-call | tf_op jit(solution)/shard_map/steps/pallas_call | solution.py:1020
  17.8 16.3 %all_to_all.9.parts_ref = f32[32,1,64]{2,1,0:T(1,128)S(1)} all-to-all(f32[32,1,64]{2,1,0:T(1,128)S(1)} %bitcast.2), channel_id=1, replica_groups=mesh['gx'=8,'gy'=4] {'gx','gy'}, dimensions={0} | all-to-all | bytes 16384 | tf_op jit(solution)/shard_map/all_to_all | solution.py:1034
  34.1 0.7 %finish.1 = (f32[1,64]{1,0:T(1,128)}, f32[19,8,256]{2,1,0:T(8,128)}) custom-call(f32[32,1,64]{2,1,0:T(1,128)S(1)} %all_to_all.9.parts_ref, f32[19,8,256]{2,1,0:T(8,128)S(1)} %get-tuple-element.37.adjoint_ref), custom_call_target="tpu_custom_call" | custom-call | tf_op jit(solution)/shard_map/finish/pallas_call | solution.py:1035
Async XLA Ops:
  1.9 6.9 %collective-permute-start = (f32[37,8,128]{2,1,0:T(8,128)S(1)}, f32[37,8,128]{2,1,0:T(8,128)S(1)}, u32[]{:S(2)}, u32[]{:S(2)}) collective-permute-start(f32[37,8,128]{2,1,0:T(8,128)S(1)} %get-tuple-element.26), channel_id=1, source_target_pairs={{0,1},{1,0},{2,3},{3,2},{4,5},{5,4},{6,7},{7,6},{8,9},{9,8},{10,11... | collective-permute-start | bytes 454664 | tf_op jit(solution)/shard_map/ppermute | solution.py:959
  4.9 8.2 %collective-permute-start.3 = (f32[37,8,128]{2,1,0:T(8,128)S(1)}, f32[37,8,128]{2,1,0:T(8,128)S(1)}, u32[]{:S(2)}, u32[]{:S(2)}) collective-permute-start(f32[37,8,128]{2,1,0:T(8,128)S(1)} %get-tuple-element.29), channel_id=1, source_target_pairs={{1,2},{2,1},{5,6},{6,5},{9,10},{10,9},{13,14},{14,13},{17,18},{18,... | collective-permute-start | bytes 454664 | tf_op jit(solution)/shard_map/ppermute | solution.py:963
  9.1 5.1 %collective-permute-start.2 = (f32[66,8,128]{2,1,0:T(8,128)S(1)}, f32[66,8,128]{2,1,0:T(8,128)S(1)}, u32[]{:S(2)}, u32[]{:S(2)}) collective-permute-start(f32[66,8,128]{2,1,0:T(8,128)S(1)} %get-tuple-element.28), channel_id=1, source_target_pairs={{4,8},{12,16},{20,24},{8,4},{16,12},{24,20},{5,9},{13,17},{21,25},... | collective-permute-start | bytes 811016 | tf_op jit(solution)/shard_map/ppermute | solution.py:963
  9.8 4.4 %collective-permute-start.1 = (f32[65,8,128]{2,1,0:T(8,128)S(1)}, f32[65,8,128]{2,1,0:T(8,128)S(1)}, u32[]{:S(2)}, u32[]{:S(2)}) collective-permute-start(f32[65,8,128]{2,1,0:T(8,128)S(1)} %get-tuple-element.27), channel_id=1, source_target_pairs={{0,4},{4,0},{8,12},{12,8},{16,20},{20,16},{24,28},{28,24},{1,5},{5... | collective-permute-start | bytes 798728 | tf_op jit(solution)/shard_map/ppermute | solution.py:959
  13.3 2.1 %collective-permute-start.5 = (f32[29,8,128]{2,1,0:T(8,128)S(1)}, f32[29,8,128]{2,1,0:T(8,128)S(1)}, u32[]{:S(2)}, u32[]{:S(2)}) collective-permute-start(f32[29,8,128]{2,1,0:T(8,128)S(1)} %get-tuple-element.31), channel_id=1, source_target_pairs={{5,9},{6,10},{13,17},{14,18},{21,25},{22,26},{9,5},{10,6},{17,13},... | collective-permute-start | bytes 356360 | tf_op jit(solution)/shard_map/ppermute | solution.py:971
  14.0 1.4 %collective-permute-start.4 = (f32[28,8,128]{2,1,0:T(8,128)S(1)}, f32[28,8,128]{2,1,0:T(8,128)S(1)}, u32[]{:S(2)}, u32[]{:S(2)}) collective-permute-start(f32[28,8,128]{2,1,0:T(8,128)S(1)} %get-tuple-element.30), channel_id=1, source_target_pairs={{0,4},{4,0},{8,12},{12,8},{16,20},{20,16},{24,28},{28,24},{1,5},{5... | collective-permute-start | bytes 344072 | tf_op jit(solution)/shard_map/ppermute | solution.py:959

commit v26 on v25

--- a/solution.py
+++ b/solution.py
@@ -330,8 +330,8 @@
 
 
 class Deal:
-    def __init__(self, even, first, second, layout, skip=0):
-        self.even, self.skip, self.held = even, skip, {}
+    def __init__(self, even, first, second, layout):
+        self.even, self.held, self.ready = even, {}, []
         self.first, self.second = Packing(first, layout), Packing(second, layout)
 
     def put(self, way, at, value):
@@ -340,14 +340,24 @@
             return
         other = self.held.pop((-way, at))
         up, down = (value, other) if way == 1 else (other, value)
-        self.first[at - self.skip] = jnp.where(self.even, up, down)
-        self.second[at - self.skip] = jnp.where(self.even, down, up)
+        self.add(at, jnp.where(self.even, up, down), jnp.where(self.even, down, up))
 
     def put_both(self, at, value):
-        self.first[at - self.skip] = value
-        self.second[at - self.skip] = value
+        self.add(at, value, value)
+
+    def add(self, *entry):
+        self.ready.append(entry)
+        if len(self.ready) == 8:
+            self.write()
+
+    def write(self):
+        for at, first, second in self.ready:
+            self.first[at] = first
+            self.second[at] = second
+        self.ready = []
 
     def finish(self):
+        self.write()
         self.first.finish()
         self.second.finish()
 
@@ -814,14 +824,14 @@
         for r in (2, 0, 3):
             f = stream_tile(from_wide(pop_a, tile, r), 1, masks_of(tile, 2, r), lane)
             parts = moments(f)
+            at = {2: 0, 0: 1, 3: 2}[r]
+            g = collide(f, wide[0, tile, at], wide[1, tile, at], parts)
             if r == 0:
                 note(1, place, 0, parts)
                 for i in range(Q):
                     saved[0, i, place] = f[i]
             else:
                 halo.append(parts[2:4] + tuple(parts[4]))
-            at = {2: 0, 0: 1, 3: 2}[r]
-            g = collide(f, wide[0, tile, at], wide[1, tile, at], parts)
             for i in range(Q):
                 pop_b[5 * i + tile, pl.ds(ROWS * (at + 1), ROWS), :] = g[i]
         for n in range(5):
@@ -835,24 +845,25 @@
         for r in range(2):
             f = stream_tile(from_wide(pop_b, tile + 1, r), 1, masks_of(tile, 1, r), lane)
             parts = moments(f)
-            note(2, tile, r, parts)
-            if r == 0:
-                for i in range(Q):
-                    saved[1, i, tile] = f[i]
-            out.append(collide(f, field[2, tile, r], field[0, tile, r], parts))
+            out.append((f, parts, collide(f, field[2, tile, r], field[0, tile, r], parts)))
+        for r in range(2):
+            note(2, tile, r, out[r][1])
         for i in range(Q):
-            put_ring(ring_b, 4 * i + tile, out[0][i], out[1][i])
+            saved[1, i, tile] = out[0][0][i]
+            put_ring(ring_b, 4 * i + tile, out[0][2][i], out[1][2][i])
         return carry
 
     lax.fori_loop(0, 4, second_step, 0, unroll=True)
 
     def third_step(tile, carry):
+        out = []
         for r in range(2):
             f = stream_tile(from_ring(ring_b, tile, 4, r), 1, masks_of(tile, 1, r), lane)
-            note(3, tile, r, moments(f))
-            if r == 0:
-                for i in range(Q):
-                    saved[2, i, tile] = f[i]
+            out.append((f, moments(f)))
+        for r in range(2):
+            note(3, tile, r, out[r][1])
+        for i in range(Q):
+            saved[2, i, tile] = out[0][0][i]
         return carry
 
     lax.fori_loop(0, 4, third_step, 0, unroll=True)

time: 35.1 us -> 35.1 us (level)
  no operation moved by 1% of the time
where the time goes in v26:
time: 35.1 us; the launch traced here: 34.8 us
  blocking collectives  16.3 us (46%)
  starting transfers between devices  8.33 us (24%)
  Pallas kernels  5.41 us (15%)
  waiting for transfers between devices  4.03 us (11%)
  between operations  0.69 us (2%)
    all_to_all x1, blocking collectives, on_device(): gathered = lax.all_to_all(sums, ('gx', 'gy'), 0, 0, tiled=True)  16.3 us
    ppermute x3, starting transfers between devices, swap(): lax.ppermute(value, axis, [(i, i ^ 1) for i in range(size) if i ^ 1 < size])  6.33 us
    ppermute x3, waiting for transfers between devices, swap(): lax.ppermute(value, axis, [(i, i ^ 1) for i in range(size) if i ^ 1 < size])  4.02 us
    pallas_call x1, Pallas kernels, on_device(): call(functools.partial(steps_kernel, sizes), (pltpu.VMEM((Q, ROWS, 2 * LA...  2.41 us
    ppermute x2, starting transfers between devices, swap_between(): return lax.ppermute(value, axis, pairs + [(j, i) for i, j in pairs])  1.34 us
    pallas_call x1, Pallas kernels, on_device(): call(pack_own, (tiles_of(y_layout.size),) * 2 + (tiles_of(2 * Q),) * 3 +...  1.24 us
  transfers between devices with their start and end apart: 6, of which 3 were waited for; matrix products, arithmetic and copies ran while one was open for 0% of the time, Pallas kernels for 3%

profile of v26, /device:TPU:0, one launch (start us, length us, event | category | flops | bytes accessed | tf_op | source)
XLA Modules:
  0.0 34.8 jit_solution(13068017254976330679)
XLA Ops:
  0.6 1.2 %pack_own.1 = (f32[37,8,128]{2,1,0:T(8,128)S(1)}, f32[37,8,128]{2,1,0:T(8,128)S(1)}, f32[38,8,128]{2,1,0:T(8,128)S(1)}, f32[38,8,128]{2,1,0:T(8,128)S(1)}, f32[3...) custom-call(f32[19,8,256]{2,1,0:T(8,128)} %f_hbm.1, f32[19,8,256]{2,1,0:T(8,128)} %cot_hbm.1, ...), custom_call_target="tpu_custom_call" | custom-call | tf_op jit(solution)/shard_map/pack_own/pallas_call | solution.py:988
  1.9 3.0 %collective-permute-start = (f32[37,8,128]{2,1,0:T(8,128)S(1)}, f32[37,8,128]{2,1,0:T(8,128)S(1)}, u32[]{:S(2)}, u32[]{:S(2)}) collective-permute-start(f32[37,8,128]{2,1,0:T(8,128)S(1)} %get-tuple-element.26), channel_id=1, source_target_pairs={{0,1},{1,0},{2,3},{3,2},{4,5},{5,4},{6,7},{7,6},{8,9},{9,8},{10,11... | collective-permute-start | bytes 454664 | tf_op jit(solution)/shard_map/ppermute | solution.py:970
  4.9 0.7 %collective-permute-start.3 = (f32[37,8,128]{2,1,0:T(8,128)S(1)}, f32[37,8,128]{2,1,0:T(8,128)S(1)}, u32[]{:S(2)}, u32[]{:S(2)}) collective-permute-start(f32[37,8,128]{2,1,0:T(8,128)S(1)} %get-tuple-element.29), channel_id=1, source_target_pairs={{1,2},{2,1},{5,6},{6,5},{9,10},{10,9},{13,14},{14,13},{17,18},{18,... | collective-permute-start | bytes 454664 | tf_op jit(solution)/shard_map/ppermute | solution.py:974
  5.5 3.3 %collective-permute-done.message_ref.near_y_ref = f32[37,8,128]{2,1,0:T(8,128)S(1)} collective-permute-done((f32[37,8,128]{2,1,0:T(8,128)S(1)}, f32[37,8,128]{2,1,0:T(8,128)S(1)}, u32[]{:S(2)}, u32[]{:S(2)}) %collective-permute-start) | collective-permute-done | bytes 151584 | tf_op jit(solution)/shard_map/ppermute | solution.py:970
  8.8 0.3 pack_near.1
  9.1 0.7 %collective-permute-start.2 = (f32[66,8,128]{2,1,0:T(8,128)S(1)}, f32[66,8,128]{2,1,0:T(8,128)S(1)}, u32[]{:S(2)}, u32[]{:S(2)}) collective-permute-start(f32[66,8,128]{2,1,0:T(8,128)S(1)} %get-tuple-element.28), channel_id=1, source_target_pairs={{4,8},{12,16},{20,24},{8,4},{16,12},{24,20},{5,9},{13,17},{21,25},... | collective-permute-start | bytes 811016 | tf_op jit(solution)/shard_map/ppermute | solution.py:974
  9.8 3.2 %collective-permute-start.1 = (f32[65,8,128]{2,1,0:T(8,128)S(1)}, f32[65,8,128]{2,1,0:T(8,128)S(1)}, u32[]{:S(2)}, u32[]{:S(2)}) collective-permute-start(f32[65,8,128]{2,1,0:T(8,128)S(1)} %get-tuple-element.27), channel_id=1, source_target_pairs={{0,4},{4,0},{8,12},{12,8},{16,20},{20,16},{24,28},{28,24},{1,5},{5... | collective-permute-start | bytes 798728 | tf_op jit(solution)/shard_map/ppermute | solution.py:970
  13.0 0.0 collective-permute-done.3.message_ref.far_y_ref
  13.0 0.2 pack_far.1
  13.3 0.7 %collective-permute-start.5 = (f32[29,8,128]{2,1,0:T(8,128)S(1)}, f32[29,8,128]{2,1,0:T(8,128)S(1)}, u32[]{:S(2)}, u32[]{:S(2)}) collective-permute-start(f32[29,8,128]{2,1,0:T(8,128)S(1)} %get-tuple-element.31), channel_id=1, source_target_pairs={{5,9},{6,10},{13,17},{14,18},{21,25},{22,26},{9,5},{10,6},{17,13},... | collective-permute-start | bytes 356360 | tf_op jit(solution)/shard_map/ppermute | solution.py:982
  14.0 0.1 collective-permute-start.4
  14.1 0.1 collective-permute-done.1.first_near_ref
  14.2 0.0 collective-permute-done.2.second_near_ref
  14.2 0.6 %lay_out.1 = (f32[95,40,128]{2,1,0:T(8,128)S(1)}, f32[76,24,128]{2,1,0:T(8,128)S(1)}, f32[2,5,3,8,128]{4,3,2,1,0:T(8,128)S(1)}, f32[4,4,2,8,128]{4,3,2,1,0:T(8,128)S(1)}) custom-call(f32[37,8,128]{2,1,0:T(8,128)S(1)} %collective-permute-done.message_ref.near_y_ref, f32[37,8,128]{2,1,0:T(8,128)S(1)} %collective-permute-done.3.message_ref.far_y_ref, ...), custom_call_target="tpu_custom_call" | custom-call | tf_op jit(solution)/shard_map/lay_out/pallas_call | solution.py:1028
  14.8 0.6 %collective-permute-done.4.first_far_ref = f32[28,8,128]{2,1,0:T(8,128)S(1)} collective-permute-done((f32[28,8,128]{2,1,0:T(8,128)S(1)}, f32[28,8,128]{2,1,0:T(8,128)S(1)}, u32[]{:S(2)}, u32[]{:S(2)}) %collective-permute-start.4) | collective-permute-done | bytes 114720 | tf_op jit(solution)/shard_map/ppermute | solution.py:970
  15.4 0.0 collective-permute-done.5.second_far_ref
  15.4 2.4 %steps.1 = (f32[19,8,256]{2,1,0:T(8,128)S(1)}, f32[32,64]{1,0:T(8,128)S(1)}, f32[95,40,128]{2,1,0:T(8,128)S(1)}, f32[76,24,128]{2,1,0:T(8,128)S(1)}, f32[2,5,3,8...) custom-call(f32[38,8,128]{2,1,0:T(8,128)S(1)} %get-tuple-element.21., ...), custom_call_target="tpu_custom_call", output_to_operand_aliasing={{2}: (7, {}), {3}: (8, {}), {4}: (9, {}), {5}: (10, {})} | custom-call | tf_op jit(solution)/shard_map/steps/pallas_call | solution.py:1031
  17.8 16.3 %all_to_all.9.parts_ref = f32[32,1,64]{2,1,0:T(1,128)S(1)} all-to-all(f32[32,1,64]{2,1,0:T(1,128)S(1)} %bitcast.2), channel_id=1, replica_groups=mesh['gx'=8,'gy'=4] {'gx','gy'}, dimensions={0} | all-to-all | bytes 16384 | tf_op jit(solution)/shard_map/all_to_all | solution.py:1045
  34.1 0.7 %finish.1 = (f32[1,64]{1,0:T(1,128)}, f32[19,8,256]{2,1,0:T(8,128)}) custom-call(f32[32,1,64]{2,1,0:T(1,128)S(1)} %all_to_all.9.parts_ref, f32[19,8,256]{2,1,0:T(8,128)S(1)} %get-tuple-element.37.adjoint_ref), custom_call_target="tpu_custom_call" | custom-call | tf_op jit(solution)/shard_map/finish/pallas_call | solution.py:1046
Async XLA Ops:
  1.9 6.9 %collective-permute-start = (f32[37,8,128]{2,1,0:T(8,128)S(1)}, f32[37,8,128]{2,1,0:T(8,128)S(1)}, u32[]{:S(2)}, u32[]{:S(2)}) collective-permute-start(f32[37,8,128]{2,1,0:T(8,128)S(1)} %get-tuple-element.26), channel_id=1, source_target_pairs={{0,1},{1,0},{2,3},{3,2},{4,5},{5,4},{6,7},{7,6},{8,9},{9,8},{10,11... | collective-permute-start | bytes 454664 | tf_op jit(solution)/shard_map/ppermute | solution.py:970
  4.9 8.2 %collective-permute-start.3 = (f32[37,8,128]{2,1,0:T(8,128)S(1)}, f32[37,8,128]{2,1,0:T(8,128)S(1)}, u32[]{:S(2)}, u32[]{:S(2)}) collective-permute-start(f32[37,8,128]{2,1,0:T(8,128)S(1)} %get-tuple-element.29), channel_id=1, source_target_pairs={{1,2},{2,1},{5,6},{6,5},{9,10},{10,9},{13,14},{14,13},{17,18},{18,... | collective-permute-start | bytes 454664 | tf_op jit(solution)/shard_map/ppermute | solution.py:974
  9.1 5.1 %collective-permute-start.2 = (f32[66,8,128]{2,1,0:T(8,128)S(1)}, f32[66,8,128]{2,1,0:T(8,128)S(1)}, u32[]{:S(2)}, u32[]{:S(2)}) collective-permute-start(f32[66,8,128]{2,1,0:T(8,128)S(1)} %get-tuple-element.28), channel_id=1, source_target_pairs={{4,8},{12,16},{20,24},{8,4},{16,12},{24,20},{5,9},{13,17},{21,25},... | collective-permute-start | bytes 811016 | tf_op jit(solution)/shard_map/ppermute | solution.py:974
  9.8 4.4 %collective-permute-start.1 = (f32[65,8,128]{2,1,0:T(8,128)S(1)}, f32[65,8,128]{2,1,0:T(8,128)S(1)}, u32[]{:S(2)}, u32[]{:S(2)}) collective-permute-start(f32[65,8,128]{2,1,0:T(8,128)S(1)} %get-tuple-element.27), channel_id=1, source_target_pairs={{0,4},{4,0},{8,12},{12,8},{16,20},{20,16},{24,28},{28,24},{1,5},{5... | collective-permute-start | bytes 798728 | tf_op jit(solution)/shard_map/ppermute | solution.py:970
  13.3 2.1 %collective-permute-start.5 = (f32[29,8,128]{2,1,0:T(8,128)S(1)}, f32[29,8,128]{2,1,0:T(8,128)S(1)}, u32[]{:S(2)}, u32[]{:S(2)}) collective-permute-start(f32[29,8,128]{2,1,0:T(8,128)S(1)} %get-tuple-element.31), channel_id=1, source_target_pairs={{5,9},{6,10},{13,17},{14,18},{21,25},{22,26},{9,5},{10,6},{17,13},... | collective-permute-start | bytes 356360 | tf_op jit(solution)/shard_map/ppermute | solution.py:982
  14.0 1.4 %collective-permute-start.4 = (f32[28,8,128]{2,1,0:T(8,128)S(1)}, f32[28,8,128]{2,1,0:T(8,128)S(1)}, u32[]{:S(2)}, u32[]{:S(2)}) collective-permute-start(f32[28,8,128]{2,1,0:T(8,128)S(1)} %get-tuple-element.30), channel_id=1, source_target_pairs={{0,4},{4,0},{8,12},{12,8},{16,20},{20,16},{24,28},{28,24},{1,5},{5... | collective-permute-start | bytes 344072 | tf_op jit(solution)/shard_map/ppermute | solution.py:970

commit v27 on v26

--- a/solution.py
+++ b/solution.py
@@ -468,38 +468,45 @@
     return lane // (LANES // 2) == jnp.where(right, 0, 1)
 
 
-def from_y(message_ref, near):
+def choose(flag, first, second):
+    if isinstance(flag, bool):
+        return first() if flag else second()
+    return jnp.where(flag, first(), second())
+
+
+def from_y(message_ref, right):
     row, lane, column, depth = iotas()
     ref = Unpacking(message_ref, layouts()[0])
-    right = is_right(near)
 
     def population(i):
-        return jnp.where(right, ref[2 * i], ref[2 * i + 1])
+        return choose(right, lambda: ref[2 * i], lambda: ref[2 * i + 1])
 
     def cotangent(i):
-        values = []
-        for way, place, far in ((1, 1, 0), (-1, 2, 1)):
+        def of(way, place, far):
             deep = 3 - way * VELOCITIES[i][1]
             value = columns(ref[2 * i + far], way * (4 - deep))
             if i in turned(1, way):
                 extra = columns(ref[Y_COT], place - turned(1, way).index(i))
                 value = jnp.where(column == place, extra, value)
-            values.append(value)
-        return jnp.where(right, values[1], values[0])
+            return value
+
+        return choose(right, lambda: of(-1, 2, 1), lambda: of(1, 1, 0))
 
     def codes(s):
         return ref[(Y_CODE1, Y_CODE2, Y_CODE3)[s - 1]]
 
     def outer(i):
-        left, above = ref[2 * i], ref[2 * i + 1]
-        if i in turned(1, 1):
-            above = columns(ref[Y_POP], -turned(1, 1).index(i))
-        if i in turned(1, -1):
-            left = columns(ref[Y_POP], 3 - turned(1, -1).index(i))
-        return jnp.where(right, above, left)
+        def of(way, far):
+            if i in turned(1, -way):
+                first = 0 if way == -1 else 3
+                return columns(ref[Y_POP], first - turned(1, -way).index(i))
+            return ref[2 * i + far]
+
+        return choose(right, lambda: of(-1, 1), lambda: of(1, 0))
 
     def outer_code():
-        return jnp.where(right, columns(ref[Y_CODE3], 1), columns(ref[Y_CODE3], 3))
+        tile = ref[Y_CODE3]
+        return choose(right, lambda: columns(tile, 1), lambda: columns(tile, 3))
 
     return population, cotangent, codes, outer, outer_code
 
@@ -531,11 +538,11 @@
         deal.put(way, first + X_EXTRA, extra)
 
 
-def pack_neighbour(deal, lanes, message_ref, near):
+def pack_neighbour(deal, lanes, message_ref, right):
     ring, code13, code2, tiles = x_places(lanes)
-    population, cotangent, codes, outer, outer_code = from_y(message_ref, near)
+    population, cotangent, codes, outer, outer_code = from_y(message_ref, right)
     pack_lines(deal, X_LANE * (lanes - 1), population, cotangent)
-    kept = half_lanes(is_right(near))
+    kept = half_lanes(right)
     for n in range(X_HALVES):
         first, second = (outer(2 * n - 1), outer(2 * n)) if n else (outer(0), outer_code())
         deal.put_both(ring + n, jnp.where(kept, first, pltpu.roll(second, LANES // 2, 1)))
@@ -561,14 +568,21 @@
     first, second = field_ref[4], lines(field_ref[5], 4)
     deal.put(1, code2, jnp.where(row >= 4, first, second))
     deal.put(-1, code2, jnp.where(row < 4, first, second))
-    pack_neighbour(deal, 3, message_ref, True)
+    pack_neighbour(deal, 3, message_ref, is_right(True))
     deal.finish()
 
 
 def pack_far(message_ref, first_ref, second_ref):
-    deal = Deal(is_even("gx"), first_ref, second_ref, layouts()[2])
-    pack_neighbour(deal, 1, message_ref, False)
-    deal.finish()
+    even_x = is_even("gx")
+
+    def pack(right):
+        deal = Deal(even_x, first_ref, second_ref, layouts()[2])
+        pack_neighbour(deal, 1, message_ref, right)
+        deal.finish()
+
+    above = is_right(False)
+    pl.when(above)(lambda: pack(True))
+    pl.when(jnp.logical_not(above))(lambda: pack(False))
 
 
 def from_x(ref, n, way, lanes):
@@ -641,7 +655,7 @@
     return jnp.where(top, 0.0, code), phi
 
 
-def in_groups(size=8):
+def in_groups(size=10):
     return [range(first, min(first + size, Q)) for first in range(0, Q, size)]
 
 
@@ -712,7 +726,7 @@
             *spaces,
         )
         lay_halo(2 + t, from_x(below, t, 1, 3), from_x(above, t, -1, 3), *spaces)
-    near, far = from_y(near_y_ref, True), from_y(far_y_ref, False)
+    near, far = from_y(near_y_ref, is_right(True)), from_y(far_y_ref, is_right(False))
     for c, (population, cotangent, codes, _, _) in ((near_tile(), near), (5 - near_tile(), far)):
         lay_own(c, population, cotangent, codes, expand(codes(1)), *spaces)
     kept = half_lanes(is_right(True))

time: 35.1 us -> 35.1 us (level)
  no operation moved by 1% of the time
where the time goes in v27:
time: 35.1 us; the launch traced here: 34.8 us
  blocking collectives  16.3 us (46%)
  starting transfers between devices  8.35 us (24%)
  Pallas kernels  5.46 us (16%)
  waiting for transfers between devices  4.01 us (11%)
  between operations  0.69 us (2%)
    all_to_all x1, blocking collectives, on_device(): gathered = lax.all_to_all(sums, ('gx', 'gy'), 0, 0, tiled=True)  16.3 us
    ppermute x3, starting transfers between devices, swap(): lax.ppermute(value, axis, [(i, i ^ 1) for i in range(size) if i ^ 1 < size])  6.34 us
    ppermute x3, waiting for transfers between devices, swap(): lax.ppermute(value, axis, [(i, i ^ 1) for i in range(size) if i ^ 1 < size])  4 us
    pallas_call x1, Pallas kernels, on_device(): call(functools.partial(steps_kernel, sizes), (pltpu.VMEM((Q, ROWS, 2 * LA...  2.41 us
    ppermute x2, starting transfers between devices, swap_between(): return lax.ppermute(value, axis, pairs + [(j, i) for i, j in pairs])  1.34 us
    pallas_call x1, Pallas kernels, on_device(): call(pack_own, (tiles_of(y_layout.size),) * 2 + (tiles_of(2 * Q),) * 3 +...  1.24 us
  transfers between devices with their start and end apart: 6, of which 3 were waited for; matrix products, arithmetic and copies ran while one was open for 0% of the time, Pallas kernels for 3%

profile of v27, /device:TPU:0, one launch (start us, length us, event | category | flops | bytes accessed | tf_op | source)
XLA Modules:
  0.0 34.8 jit_solution(14081732536472293592)
XLA Ops:
  0.6 1.2 %pack_own.1 = (f32[37,8,128]{2,1,0:T(8,128)S(1)}, f32[37,8,128]{2,1,0:T(8,128)S(1)}, f32[38,8,128]{2,1,0:T(8,128)S(1)}, f32[38,8,128]{2,1,0:T(8,128)S(1)}, f32[3...) custom-call(f32[19,8,256]{2,1,0:T(8,128)} %f_hbm.1, f32[19,8,256]{2,1,0:T(8,128)} %cot_hbm.1, ...), custom_call_target="tpu_custom_call" | custom-call | tf_op jit(solution)/shard_map/pack_own/pallas_call | solution.py:1002
  1.9 3.0 %collective-permute-start = (f32[37,8,128]{2,1,0:T(8,128)S(1)}, f32[37,8,128]{2,1,0:T(8,128)S(1)}, u32[]{:S(2)}, u32[]{:S(2)}) collective-permute-start(f32[37,8,128]{2,1,0:T(8,128)S(1)} %get-tuple-element.26), channel_id=1, source_target_pairs={{0,1},{1,0},{2,3},{3,2},{4,5},{5,4},{6,7},{7,6},{8,9},{9,8},{10,11... | collective-permute-start | bytes 454664 | tf_op jit(solution)/shard_map/ppermute | solution.py:984
  4.9 0.7 %collective-permute-start.3 = (f32[37,8,128]{2,1,0:T(8,128)S(1)}, f32[37,8,128]{2,1,0:T(8,128)S(1)}, u32[]{:S(2)}, u32[]{:S(2)}) collective-permute-start(f32[37,8,128]{2,1,0:T(8,128)S(1)} %get-tuple-element.29), channel_id=1, source_target_pairs={{1,2},{2,1},{5,6},{6,5},{9,10},{10,9},{13,14},{14,13},{17,18},{18,... | collective-permute-start | bytes 454664 | tf_op jit(solution)/shard_map/ppermute | solution.py:988
  5.5 3.3 %collective-permute-done.message_ref.near_y_ref = f32[37,8,128]{2,1,0:T(8,128)S(1)} collective-permute-done((f32[37,8,128]{2,1,0:T(8,128)S(1)}, f32[37,8,128]{2,1,0:T(8,128)S(1)}, u32[]{:S(2)}, u32[]{:S(2)}) %collective-permute-start) | collective-permute-done | bytes 151584 | tf_op jit(solution)/shard_map/ppermute | solution.py:984
  8.8 0.3 pack_near.1
  9.1 0.7 %collective-permute-start.2 = (f32[66,8,128]{2,1,0:T(8,128)S(1)}, f32[66,8,128]{2,1,0:T(8,128)S(1)}, u32[]{:S(2)}, u32[]{:S(2)}) collective-permute-start(f32[66,8,128]{2,1,0:T(8,128)S(1)} %get-tuple-element.28), channel_id=1, source_target_pairs={{4,8},{12,16},{20,24},{8,4},{16,12},{24,20},{5,9},{13,17},{21,25},... | collective-permute-start | bytes 811016 | tf_op jit(solution)/shard_map/ppermute | solution.py:988
  9.8 3.2 %collective-permute-start.1 = (f32[65,8,128]{2,1,0:T(8,128)S(1)}, f32[65,8,128]{2,1,0:T(8,128)S(1)}, u32[]{:S(2)}, u32[]{:S(2)}) collective-permute-start(f32[65,8,128]{2,1,0:T(8,128)S(1)} %get-tuple-element.27), channel_id=1, source_target_pairs={{0,4},{4,0},{8,12},{12,8},{16,20},{20,16},{24,28},{28,24},{1,5},{5... | collective-permute-start | bytes 798728 | tf_op jit(solution)/shard_map/ppermute | solution.py:984
  13.1 0.0 collective-permute-done.3.message_ref.far_y_ref
  13.1 0.3 pack_far.1
  13.3 0.7 %collective-permute-start.5 = (f32[29,8,128]{2,1,0:T(8,128)S(1)}, f32[29,8,128]{2,1,0:T(8,128)S(1)}, u32[]{:S(2)}, u32[]{:S(2)}) collective-permute-start(f32[29,8,128]{2,1,0:T(8,128)S(1)} %get-tuple-element.31), channel_id=1, source_target_pairs={{5,9},{6,10},{13,17},{14,18},{21,25},{22,26},{9,5},{10,6},{17,13},... | collective-permute-start | bytes 356360 | tf_op jit(solution)/shard_map/ppermute | solution.py:996
  14.0 0.1 collective-permute-start.4
  14.1 0.1 collective-permute-done.1.first_near_ref
  14.2 0.0 collective-permute-done.2.second_near_ref
  14.2 0.6 %lay_out.1 = (f32[95,40,128]{2,1,0:T(8,128)S(1)}, f32[76,24,128]{2,1,0:T(8,128)S(1)}, f32[2,5,3,8,128]{4,3,2,1,0:T(8,128)S(1)}, f32[4,4,2,8,128]{4,3,2,1,0:T(8,128)S(1)}) custom-call(f32[37,8,128]{2,1,0:T(8,128)S(1)} %collective-permute-done.message_ref.near_y_ref, f32[37,8,128]{2,1,0:T(8,128)S(1)} %collective-permute-done.3.message_ref.far_y_ref, ...), custom_call_target="tpu_custom_call" | custom-call | tf_op jit(solution)/shard_map/lay_out/pallas_call | solution.py:1042
  14.8 0.6 %collective-permute-done.4.first_far_ref = f32[28,8,128]{2,1,0:T(8,128)S(1)} collective-permute-done((f32[28,8,128]{2,1,0:T(8,128)S(1)}, f32[28,8,128]{2,1,0:T(8,128)S(1)}, u32[]{:S(2)}, u32[]{:S(2)}) %collective-permute-start.4) | collective-permute-done | bytes 114720 | tf_op jit(solution)/shard_map/ppermute | solution.py:984
  15.4 0.0 collective-permute-done.5.second_far_ref
  15.4 2.4 %steps.1 = (f32[19,8,256]{2,1,0:T(8,128)S(1)}, f32[32,64]{1,0:T(8,128)S(1)}, f32[95,40,128]{2,1,0:T(8,128)S(1)}, f32[76,24,128]{2,1,0:T(8,128)S(1)}, f32[2,5,3,8...) custom-call(f32[38,8,128]{2,1,0:T(8,128)S(1)} %get-tuple-element.21., ...), custom_call_target="tpu_custom_call", output_to_operand_aliasing={{2}: (7, {}), {3}: (8, {}), {4}: (9, {}), {5}: (10, {})} | custom-call | tf_op jit(solution)/shard_map/steps/pallas_call | solution.py:1045
  17.8 16.3 %all_to_all.9.parts_ref = f32[32,1,64]{2,1,0:T(1,128)S(1)} all-to-all(f32[32,1,64]{2,1,0:T(1,128)S(1)} %bitcast.2), channel_id=1, replica_groups=mesh['gx'=8,'gy'=4] {'gx','gy'}, dimensions={0} | all-to-all | bytes 16384 | tf_op jit(solution)/shard_map/all_to_all | solution.py:1059
  34.1 0.7 %finish.1 = (f32[1,64]{1,0:T(1,128)}, f32[19,8,256]{2,1,0:T(8,128)}) custom-call(f32[32,1,64]{2,1,0:T(1,128)S(1)} %all_to_all.9.parts_ref, f32[19,8,256]{2,1,0:T(8,128)S(1)} %get-tuple-element.37.adjoint_ref), custom_call_target="tpu_custom_call" | custom-call | tf_op jit(solution)/shard_map/finish/pallas_call | solution.py:1060
Async XLA Ops:
  1.9 6.9 %collective-permute-start = (f32[37,8,128]{2,1,0:T(8,128)S(1)}, f32[37,8,128]{2,1,0:T(8,128)S(1)}, u32[]{:S(2)}, u32[]{:S(2)}) collective-permute-start(f32[37,8,128]{2,1,0:T(8,128)S(1)} %get-tuple-element.26), channel_id=1, source_target_pairs={{0,1},{1,0},{2,3},{3,2},{4,5},{5,4},{6,7},{7,6},{8,9},{9,8},{10,11... | collective-permute-start | bytes 454664 | tf_op jit(solution)/shard_map/ppermute | solution.py:984
  4.9 8.2 %collective-permute-start.3 = (f32[37,8,128]{2,1,0:T(8,128)S(1)}, f32[37,8,128]{2,1,0:T(8,128)S(1)}, u32[]{:S(2)}, u32[]{:S(2)}) collective-permute-start(f32[37,8,128]{2,1,0:T(8,128)S(1)} %get-tuple-element.29), channel_id=1, source_target_pairs={{1,2},{2,1},{5,6},{6,5},{9,10},{10,9},{13,14},{14,13},{17,18},{18,... | collective-permute-start | bytes 454664 | tf_op jit(solution)/shard_map/ppermute | solution.py:988
  9.1 5.1 %collective-permute-start.2 = (f32[66,8,128]{2,1,0:T(8,128)S(1)}, f32[66,8,128]{2,1,0:T(8,128)S(1)}, u32[]{:S(2)}, u32[]{:S(2)}) collective-permute-start(f32[66,8,128]{2,1,0:T(8,128)S(1)} %get-tuple-element.28), channel_id=1, source_target_pairs={{4,8},{12,16},{20,24},{8,4},{16,12},{24,20},{5,9},{13,17},{21,25},... | collective-permute-start | bytes 811016 | tf_op jit(solution)/shard_map/ppermute | solution.py:988
  9.8 4.4 %collective-permute-start.1 = (f32[65,8,128]{2,1,0:T(8,128)S(1)}, f32[65,8,128]{2,1,0:T(8,128)S(1)}, u32[]{:S(2)}, u32[]{:S(2)}) collective-permute-start(f32[65,8,128]{2,1,0:T(8,128)S(1)} %get-tuple-element.27), channel_id=1, source_target_pairs={{0,4},{4,0},{8,12},{12,8},{16,20},{20,16},{24,28},{28,24},{1,5},{5... | collective-permute-start | bytes 798728 | tf_op jit(solution)/shard_map/ppermute | solution.py:984
  13.3 2.1 %collective-permute-start.5 = (f32[29,8,128]{2,1,0:T(8,128)S(1)}, f32[29,8,128]{2,1,0:T(8,128)S(1)}, u32[]{:S(2)}, u32[]{:S(2)}) collective-permute-start(f32[29,8,128]{2,1,0:T(8,128)S(1)} %get-tuple-element.31), channel_id=1, source_target_pairs={{5,9},{6,10},{13,17},{14,18},{21,25},{22,26},{9,5},{10,6},{17,13},... | collective-permute-start | bytes 356360 | tf_op jit(solution)/shard_map/ppermute | solution.py:996
  14.0 1.4 %collective-permute-start.4 = (f32[28,8,128]{2,1,0:T(8,128)S(1)}, f32[28,8,128]{2,1,0:T(8,128)S(1)}, u32[]{:S(2)}, u32[]{:S(2)}) collective-permute-start(f32[28,8,128]{2,1,0:T(8,128)S(1)} %get-tuple-element.30), channel_id=1, source_target_pairs={{0,4},{4,0},{8,12},{12,8},{16,20},{20,16},{24,28},{28,24},{1,5},{5... | collective-permute-start | bytes 344072 | tf_op jit(solution)/shard_map/ppermute | solution.py:984

commit v28 on v27

--- a/solution.py
+++ b/solution.py
@@ -474,7 +474,7 @@
     return jnp.where(flag, first(), second())
 
 
-def from_y(message_ref, right):
+def from_side(message_ref, right):
     row, lane, column, depth = iotas()
     ref = Unpacking(message_ref, layouts()[0])
 
@@ -507,6 +507,43 @@
     def outer_code():
         tile = ref[Y_CODE3]
         return choose(right, lambda: columns(tile, 1), lambda: columns(tile, 3))
+
+    return population, cotangent, codes, outer, outer_code
+
+
+def from_y(message_ref, right):
+    row, lane, column, depth = iotas()
+    ref = Unpacking(message_ref, layouts()[0])
+    if isinstance(right, bool):
+        return from_side(message_ref, right)
+
+    def population(i):
+        return jnp.where(right, ref[2 * i], ref[2 * i + 1])
+
+    def cotangent(i):
+        values = []
+        for way, place, far in ((1, 1, 0), (-1, 2, 1)):
+            deep = 3 - way * VELOCITIES[i][1]
+            value = columns(ref[2 * i + far], way * (4 - deep))
+            if i in turned(1, way):
+                extra = columns(ref[Y_COT], place - turned(1, way).index(i))
+                value = jnp.where(column == place, extra, value)
+            values.append(value)
+        return jnp.where(right, values[1], values[0])
+
+    def codes(s):
+        return ref[(Y_CODE1, Y_CODE2, Y_CODE3)[s - 1]]
+
+    def outer(i):
+        left, above = ref[2 * i], ref[2 * i + 1]
+        if i in turned(1, 1):
+            above = columns(ref[Y_POP], -turned(1, 1).index(i))
+        if i in turned(1, -1):
+            left = columns(ref[Y_POP], 3 - turned(1, -1).index(i))
+        return jnp.where(right, above, left)
+
+    def outer_code():
+        return jnp.where(right, columns(ref[Y_CODE3], 1), columns(ref[Y_CODE3], 3))
 
     return population, cotangent, codes, outer, outer_code
 
@@ -655,7 +692,7 @@
     return jnp.where(top, 0.0, code), phi
 
 
-def in_groups(size=10):
+def in_groups(size=8):
     return [range(first, min(first + size, Q)) for first in range(0, Q, size)]
 
 

time: 35.1 us -> 35.1 us (level)
  no operation moved by 1% of the time
where the time goes in v28:
time: 35.1 us; the launch traced here: 34.8 us
  blocking collectives  16.3 us (46%)
  starting transfers between devices  8.35 us (24%)
  Pallas kernels  5.42 us (15%)
  waiting for transfers between devices  4.01 us (11%)
  between operations  0.69 us (2%)
    all_to_all x1, blocking collectives, on_device(): gathered = lax.all_to_all(sums, ('gx', 'gy'), 0, 0, tiled=True)  16.3 us
    ppermute x3, starting transfers between devices, swap(): lax.ppermute(value, axis, [(i, i ^ 1) for i in range(size) if i ^ 1 < size])  6.34 us
    ppermute x3, waiting for transfers between devices, swap(): lax.ppermute(value, axis, [(i, i ^ 1) for i in range(size) if i ^ 1 < size])  4 us
    pallas_call x1, Pallas kernels, on_device(): call(functools.partial(steps_kernel, sizes), (pltpu.VMEM((Q, ROWS, 2 * LA...  2.41 us
    ppermute x2, starting transfers between devices, swap_between(): return lax.ppermute(value, axis, pairs + [(j, i) for i, j in pairs])  1.34 us
    pallas_call x1, Pallas kernels, on_device(): call(pack_own, (tiles_of(y_layout.size),) * 2 + (tiles_of(2 * Q),) * 3 +...  1.24 us
  transfers between devices with their start and end apart: 6, of which 3 were waited for; matrix products, arithmetic and copies ran while one was open for 0% of the time, Pallas kernels for 3%

profile of v28, /device:TPU:0, one launch (start us, length us, event | category | flops | bytes accessed | tf_op | source)
XLA Modules:
  0.0 34.8 jit_solution(11032050146376962745)
XLA Ops:
  0.6 1.2 %pack_own.1 = (f32[37,8,128]{2,1,0:T(8,128)S(1)}, f32[37,8,128]{2,1,0:T(8,128)S(1)}, f32[38,8,128]{2,1,0:T(8,128)S(1)}, f32[38,8,128]{2,1,0:T(8,128)S(1)}, f32[3...) custom-call(f32[19,8,256]{2,1,0:T(8,128)} %f_hbm.1, f32[19,8,256]{2,1,0:T(8,128)} %cot_hbm.1, ...), custom_call_target="tpu_custom_call" | custom-call | tf_op jit(solution)/shard_map/pack_own/pallas_call | solution.py:1039
  1.9 3.0 %collective-permute-start = (f32[37,8,128]{2,1,0:T(8,128)S(1)}, f32[37,8,128]{2,1,0:T(8,128)S(1)}, u32[]{:S(2)}, u32[]{:S(2)}) collective-permute-start(f32[37,8,128]{2,1,0:T(8,128)S(1)} %get-tuple-element.26), channel_id=1, source_target_pairs={{0,1},{1,0},{2,3},{3,2},{4,5},{5,4},{6,7},{7,6},{8,9},{9,8},{10,11... | collective-permute-start | bytes 454664 | tf_op jit(solution)/shard_map/ppermute | solution.py:1021
  4.9 0.7 %collective-permute-start.3 = (f32[37,8,128]{2,1,0:T(8,128)S(1)}, f32[37,8,128]{2,1,0:T(8,128)S(1)}, u32[]{:S(2)}, u32[]{:S(2)}) collective-permute-start(f32[37,8,128]{2,1,0:T(8,128)S(1)} %get-tuple-element.29), channel_id=1, source_target_pairs={{1,2},{2,1},{5,6},{6,5},{9,10},{10,9},{13,14},{14,13},{17,18},{18,... | collective-permute-start | bytes 454664 | tf_op jit(solution)/shard_map/ppermute | solution.py:1025
  5.5 3.3 %collective-permute-done.message_ref.near_y_ref = f32[37,8,128]{2,1,0:T(8,128)S(1)} collective-permute-done((f32[37,8,128]{2,1,0:T(8,128)S(1)}, f32[37,8,128]{2,1,0:T(8,128)S(1)}, u32[]{:S(2)}, u32[]{:S(2)}) %collective-permute-start) | collective-permute-done | bytes 151584 | tf_op jit(solution)/shard_map/ppermute | solution.py:1021
  8.8 0.3 pack_near.1
  9.1 0.7 %collective-permute-start.2 = (f32[66,8,128]{2,1,0:T(8,128)S(1)}, f32[66,8,128]{2,1,0:T(8,128)S(1)}, u32[]{:S(2)}, u32[]{:S(2)}) collective-permute-start(f32[66,8,128]{2,1,0:T(8,128)S(1)} %get-tuple-element.28), channel_id=1, source_target_pairs={{4,8},{12,16},{20,24},{8,4},{16,12},{24,20},{5,9},{13,17},{21,25},... | collective-permute-start | bytes 811016 | tf_op jit(solution)/shard_map/ppermute | solution.py:1025
  9.8 3.2 %collective-permute-start.1 = (f32[65,8,128]{2,1,0:T(8,128)S(1)}, f32[65,8,128]{2,1,0:T(8,128)S(1)}, u32[]{:S(2)}, u32[]{:S(2)}) collective-permute-start(f32[65,8,128]{2,1,0:T(8,128)S(1)} %get-tuple-element.27), channel_id=1, source_target_pairs={{0,4},{4,0},{8,12},{12,8},{16,20},{20,16},{24,28},{28,24},{1,5},{5... | collective-permute-start | bytes 798728 | tf_op jit(solution)/shard_map/ppermute | solution.py:1021
  13.0 0.0 collective-permute-done.3.message_ref.far_y_ref
  13.0 0.3 pack_far.1
  13.3 0.7 %collective-permute-start.5 = (f32[29,8,128]{2,1,0:T(8,128)S(1)}, f32[29,8,128]{2,1,0:T(8,128)S(1)}, u32[]{:S(2)}, u32[]{:S(2)}) collective-permute-start(f32[29,8,128]{2,1,0:T(8,128)S(1)} %get-tuple-element.31), channel_id=1, source_target_pairs={{5,9},{6,10},{13,17},{14,18},{21,25},{22,26},{9,5},{10,6},{17,13},... | collective-permute-start | bytes 356360 | tf_op jit(solution)/shard_map/ppermute | solution.py:1033
  14.0 0.1 collective-permute-start.4
  14.1 0.1 collective-permute-done.1.first_near_ref
  14.2 0.0 collective-permute-done.2.second_near_ref
  14.2 0.6 %lay_out.1 = (f32[95,40,128]{2,1,0:T(8,128)S(1)}, f32[76,24,128]{2,1,0:T(8,128)S(1)}, f32[2,5,3,8,128]{4,3,2,1,0:T(8,128)S(1)}, f32[4,4,2,8,128]{4,3,2,1,0:T(8,128)S(1)}) custom-call(f32[37,8,128]{2,1,0:T(8,128)S(1)} %collective-permute-done.message_ref.near_y_ref, f32[37,8,128]{2,1,0:T(8,128)S(1)} %collective-permute-done.3.message_ref.far_y_ref, ...), custom_call_target="tpu_custom_call" | custom-call | tf_op jit(solution)/shard_map/lay_out/pallas_call | solution.py:1079
  14.8 0.6 %collective-permute-done.4.first_far_ref = f32[28,8,128]{2,1,0:T(8,128)S(1)} collective-permute-done((f32[28,8,128]{2,1,0:T(8,128)S(1)}, f32[28,8,128]{2,1,0:T(8,128)S(1)}, u32[]{:S(2)}, u32[]{:S(2)}) %collective-permute-start.4) | collective-permute-done | bytes 114720 | tf_op jit(solution)/shard_map/ppermute | solution.py:1021
  15.4 0.0 collective-permute-done.5.second_far_ref
  15.4 2.4 %steps.1 = (f32[19,8,256]{2,1,0:T(8,128)S(1)}, f32[32,64]{1,0:T(8,128)S(1)}, f32[95,40,128]{2,1,0:T(8,128)S(1)}, f32[76,24,128]{2,1,0:T(8,128)S(1)}, f32[2,5,3,8...) custom-call(f32[38,8,128]{2,1,0:T(8,128)S(1)} %get-tuple-element.21., ...), custom_call_target="tpu_custom_call", output_to_operand_aliasing={{2}: (7, {}), {3}: (8, {}), {4}: (9, {}), {5}: (10, {})} | custom-call | tf_op jit(solution)/shard_map/steps/pallas_call | solution.py:1082
  17.8 16.3 %all_to_all.9.parts_ref = f32[32,1,64]{2,1,0:T(1,128)S(1)} all-to-all(f32[32,1,64]{2,1,0:T(1,128)S(1)} %bitcast.2), channel_id=1, replica_groups=mesh['gx'=8,'gy'=4] {'gx','gy'}, dimensions={0} | all-to-all | bytes 16384 | tf_op jit(solution)/shard_map/all_to_all | solution.py:1096
  34.1 0.7 %finish.1 = (f32[1,64]{1,0:T(1,128)}, f32[19,8,256]{2,1,0:T(8,128)}) custom-call(f32[32,1,64]{2,1,0:T(1,128)S(1)} %all_to_all.9.parts_ref, f32[19,8,256]{2,1,0:T(8,128)S(1)} %get-tuple-element.37.adjoint_ref), custom_call_target="tpu_custom_call" | custom-call | tf_op jit(solution)/shard_map/finish/pallas_call | solution.py:1097
Async XLA Ops:
  1.9 6.9 %collective-permute-start = (f32[37,8,128]{2,1,0:T(8,128)S(1)}, f32[37,8,128]{2,1,0:T(8,128)S(1)}, u32[]{:S(2)}, u32[]{:S(2)}) collective-permute-start(f32[37,8,128]{2,1,0:T(8,128)S(1)} %get-tuple-element.26), channel_id=1, source_target_pairs={{0,1},{1,0},{2,3},{3,2},{4,5},{5,4},{6,7},{7,6},{8,9},{9,8},{10,11... | collective-permute-start | bytes 454664 | tf_op jit(solution)/shard_map/ppermute | solution.py:1021
  4.9 8.2 %collective-permute-start.3 = (f32[37,8,128]{2,1,0:T(8,128)S(1)}, f32[37,8,128]{2,1,0:T(8,128)S(1)}, u32[]{:S(2)}, u32[]{:S(2)}) collective-permute-start(f32[37,8,128]{2,1,0:T(8,128)S(1)} %get-tuple-element.29), channel_id=1, source_target_pairs={{1,2},{2,1},{5,6},{6,5},{9,10},{10,9},{13,14},{14,13},{17,18},{18,... | collective-permute-start | bytes 454664 | tf_op jit(solution)/shard_map/ppermute | solution.py:1025
  9.1 5.1 %collective-permute-start.2 = (f32[66,8,128]{2,1,0:T(8,128)S(1)}, f32[66,8,128]{2,1,0:T(8,128)S(1)}, u32[]{:S(2)}, u32[]{:S(2)}) collective-permute-start(f32[66,8,128]{2,1,0:T(8,128)S(1)} %get-tuple-element.28), channel_id=1, source_target_pairs={{4,8},{12,16},{20,24},{8,4},{16,12},{24,20},{5,9},{13,17},{21,25},... | collective-permute-start | bytes 811016 | tf_op jit(solution)/shard_map/ppermute | solution.py:1025
  9.8 4.4 %collective-permute-start.1 = (f32[65,8,128]{2,1,0:T(8,128)S(1)}, f32[65,8,128]{2,1,0:T(8,128)S(1)}, u32[]{:S(2)}, u32[]{:S(2)}) collective-permute-start(f32[65,8,128]{2,1,0:T(8,128)S(1)} %get-tuple-element.27), channel_id=1, source_target_pairs={{0,4},{4,0},{8,12},{12,8},{16,20},{20,16},{24,28},{28,24},{1,5},{5... | collective-permute-start | bytes 798728 | tf_op jit(solution)/shard_map/ppermute | solution.py:1021
  13.3 2.1 %collective-permute-start.5 = (f32[29,8,128]{2,1,0:T(8,128)S(1)}, f32[29,8,128]{2,1,0:T(8,128)S(1)}, u32[]{:S(2)}, u32[]{:S(2)}) collective-permute-start(f32[29,8,128]{2,1,0:T(8,128)S(1)} %get-tuple-element.31), channel_id=1, source_target_pairs={{5,9},{6,10},{13,17},{14,18},{21,25},{22,26},{9,5},{10,6},{17,13},... | collective-permute-start | bytes 356360 | tf_op jit(solution)/shard_map/ppermute | solution.py:1033
  14.0 1.4 %collective-permute-start.4 = (f32[28,8,128]{2,1,0:T(8,128)S(1)}, f32[28,8,128]{2,1,0:T(8,128)S(1)}, u32[]{:S(2)}, u32[]{:S(2)}) collective-permute-start(f32[28,8,128]{2,1,0:T(8,128)S(1)} %get-tuple-element.30), channel_id=1, source_target_pairs={{0,4},{4,0},{8,12},{12,8},{16,20},{20,16},{24,28},{28,24},{1,5},{5... | collective-permute-start | bytes 344072 | tf_op jit(solution)/shard_map/ppermute | solution.py:1021
